TPU v7x, 128 devices: a whole 4x4x4 slice. The times are simulated.
128 devices in a mesh: grp: 8 (over y, z_hi), dev: 16 (over z_lo, x, core).
Axes of the slice: x: 4, y: 4, z: 4 (z_hi: 2, z_lo: 2; z = z_hi * 2 + z_lo), core: 2. Of those that a mesh axis runs over, the one named last changes fastest.
Arguments:
- line_pos: float32 [3, 256, 16384], P(None, None, ('grp', 'dev')), may hold values from -6 to 6
- line_vel: float32 [3, 256, 16384], P(None, None, ('grp', 'dev')), may hold values from -2 to 2
- stiffness: float32 [16384], P(('grp', 'dev')), may hold values from 0.1 to 0.9
- contact: int32 [8, 256, 16384], P(None, None, ('grp', 'dev')), may hold values 0 or 1
- offset: float32 [3, 16384], P(None, ('grp', 'dev')), may hold values from -3 to 3
- attach: int32 [16384], P(('grp', 'dev')), may hold values from 0 to 127
- plat_pos: float32 [3, 1024], P(None, 'grp'), may hold values from -6 to 6
- plat_vel: float32 [3, 1024], P(None, 'grp'), may hold values from -2 to 2
- inv_mass: float32 [3, 1024], P(None, 'grp'), may hold values from 0.05 to 0.3
- restoring: float32 [3, 1024], P(None, 'grp'), may hold values from 0.05 to 0.5
- kernel: float32 [8, 3, 1024], P(None, None, 'grp'), may hold values from -2.4 to 2.4
- vel_hist: float32 [8, 3, 1024], P(None, None, 'grp'), may hold values from -3 to 3
- wave: float32 [8, 3, 1024], P(None, None, 'grp'), may hold values from -6 to 6
- sample_pick: int32 [8192], P(('grp', 'dev')), may hold values from 0 to 1023
- sample_dest: int32 [8192, 1], P(('grp', 'dev')), may hold values from 0 to 15; in each aligned block of 64 rows (0 to 63, 64 to 127, ...) at most 8 rows name the same one
- w_in: bfloat16 [768, 2048], replicated, may hold values from -0.21875 to 0.21875
- gain: float32 [2048], replicated, may hold values from 0.25 to 1.75
- w_gate: bfloat16 [2048, 8192], P(None, 'dev'), may hold values from -0.125 to 0.125
- w_up: bfloat16 [2048, 8192], P(None, 'dev'), may hold values from -0.125 to 0.125
- w_down: bfloat16 [8192, 2048], P('dev'), may hold values from -0.0625 to 0.0625
- w_out: bfloat16 [2048, 768], replicated, may hold values from -0.125 to 0.125
Outputs:
- final_pos: float32 [3, 256, 16384], P(None, None, ('grp', 'dev'))
- final_plat: float32 [3, 1024], P(None, 'grp')
- slot_error: bfloat16 [16384, 768], P(('grp', 'dev'))
- grad_gate: float32 [2048, 8192], P('grp', 'dev')
- grad_up: float32 [2048, 8192], P('grp', 'dev')
Inputs may be any that keep to these rules, and one draw needn't show every extreme that they name: `sample_dest`: at most 8 samples of one device name the same learner shard; some device and shard reach 8.
All inputs are finite; a program needn't handle non-finite values. No bound on the sum of `contact` on one device may be relied on, other than what follows from the above.
Results may differ from a plain program's by a relative error of at most 0.012.
Values may be sent and summed in bfloat16 or wider, within the bound.
No kernel may reach another device: no remote copies, remote signals or barrier semaphores. Data moves between devices by JAX's collectives and lax.ppermute only.
A program may use at most 128 MiB of HBM per device.

v0:
```python
import functools
import jax
import jax.numpy as jnp
from jax import lax
from jax.experimental import pallas as pl
from jax.experimental.pallas import tpu as pltpu
from jax.sharding import Mesh, PartitionSpec as P

STEPS = 8
CAP = 8
NODES = 256
TAIL = 8
LANES = 128
COUNT = 64
FEATS = 768
ROWS = 72
ONES_ROW = 24
CODE_ROW = 67
HIGH = lax.Precision.HIGHEST
F32 = jnp.float32
BF16 = jnp.bfloat16
DEV = ("zl", "x", "core")
CHIP = ("zl", "x")
GRP = ("y", "zh")
ALL = GRP + DEV
PAIRS = [(s, t) for s in range(2, STEPS) for t in range(1, s)]
SWAP = [(0, 1), (1, 0)]


def nt(left, right, precision=None):
    return lax.dot_general(
        left, right, (((1,), (1,)), ((), ())), precision=precision, preferred_element_type=F32
    )


def iota(shape, dim):
    return lax.broadcasted_iota(jnp.int32, shape, dim)


def pick_matrix(pick_ref):
    count = pick_ref.shape[1]
    eye = iota((count, count), 0) == iota((count, count), 1)
    pick = jnp.sum(jnp.where(eye, pick_ref[...].astype(F32), 0.0), axis=1, keepdims=True).astype(jnp.int32)
    at = (pick >> 3) + LANES * (pick & 7)
    at = jnp.concatenate([at, at + LANES], axis=0)
    return (iota((2 * count, LANES * (STEPS + 1)), 1) == at).astype(F32).astype(BF16)


def evolve_kernel(
    pos_ref, vel_ref, stiff_ref, contact_ref, off_ref, attach_ref, plat_ref, pick_ref, dest_ref,
    pay_ref, rows_ref, bound_ref, fpos_ref, stack, lin,
):
    k = stiff_ref[...]
    onehot = (attach_ref[...] == iota((LANES, LANES), 0)).astype(F32)
    off = off_ref[...]
    fair = jnp.dot(plat_ref[...], onehot, precision=HIGH, preferred_element_type=F32) + off
    row = iota((NODES, LANES), 0)
    first, last, bulk = row == 0, row == NODES - 1, row < NODES - TAIL
    lin[...] = jnp.zeros_like(lin)
    lin[ONES_ROW : ONES_ROW + 1] = jnp.ones((1, LANES), F32)
    pos = [jnp.where(last, fair[c : c + 1], pos_ref[c]) for c in range(3)]
    vel = [vel_ref[c] for c in range(3)]
    for step in range(STEPS):
        touch = contact_ref[step].astype(F32)
        damp = 0.02 + 0.1 * touch
        for c in range(3):
            p = pos[c]
            stack[c * NODES : (c + 1) * NODES, step * LANES : (step + 1) * LANES] = jnp.where(bulk, p, 0.0).astype(BF16)
            bound_ref[step * 3 + c : step * 3 + c + 1] = p[NODES - TAIL - 1 : NODES - TAIL]
            lin[step * 3 + c : step * 3 + c + 1] = p[NODES - 2 : NODES - 1] - p[NODES - 1 : NODES]
            accel = k * (pltpu.roll(p, NODES - 1, 0) - 2.0 * p + pltpu.roll(p, 1, 0)) - damp * vel[c]
            if c == 2:
                accel = accel + (-0.05 - 0.3 * touch * (p + 2.0))
            vel[c] = vel[c] + accel
            pos[c] = jnp.where(first, p, jnp.where(last, off[c : c + 1], p + vel[c]))
    for c in range(3):
        stack[c * NODES : (c + 1) * NODES, STEPS * LANES :] = jnp.where(bulk, pos[c], 0.0).astype(BF16)
        fpos_ref[c] = pos[c]
    rows_ref[...] = nt(pick_matrix(pick_ref), stack[...]).astype(BF16)
    trow = iota((TAIL, LANES), 0)
    zero = jnp.zeros((TAIL, LANES), F32)
    for kind in range(2):
        rp, rv = [zero] * 6, [zero] * 6
        for step in range(1, STEPS):
            for t in range(1, step):
                at = ONES_ROW + 1 + 2 * PAIRS.index((step, t)) + kind
                lin[at : at + 1] = rp[t - 1][TAIL - 2 : TAIL - 1]
            if step == STEPS - 1:
                break
            touch = contact_ref[step, NODES - TAIL : NODES].astype(F32)
            damp = 0.02 + 0.1 * touch
            for t in range(1, step + 1):
                p = jnp.where(trow == TAIL - 1, 1.0 if t == step else 0.0, rp[t - 1])
                up = pltpu.roll(p, TAIL - 1, 0)
                down = jnp.where(trow == 0, 0.0, pltpu.roll(p, 1, 0))
                accel = k * (up - 2.0 * p + down) - damp * rv[t - 1]
                if kind == 1:
                    accel = accel - 0.3 * touch * p
                rv[t - 1] = rv[t - 1] + accel
                rp[t - 1] = p + rv[t - 1]
    sums = nt(lin[...] * k, onehot, HIGH)
    count = dest_ref.shape[0]
    lane, sub = iota((count, LANES), 1), iota((count, LANES), 0)
    dest_col = dest_ref[...].astype(F32)
    dest = jnp.sum(jnp.where(lane == sub, dest_col, 0.0), axis=0, keepdims=True)
    rank = jnp.sum(jnp.where((dest_col == dest) & (sub < lane), 1.0, 0.0), axis=0, keepdims=True)
    codes = jnp.where(iota((1, LANES), 1) < count, dest * CAP + rank, -1.0)
    pay_ref[...] = jnp.where(iota((ROWS, LANES), 0) == CODE_ROW, codes, sums)


def finish_kernel(
    recv_ref, plat_ref, plat_vel_ref, inv_ref, rest_ref, kern_ref, hist_ref, wave_ref,
    pos_ref, vel_ref, contact_ref, stiff_ref, off_ref, attach_ref, pick_ref, bound_ref, rows_ref, fpos_in,
    x_ref, t_ref, plat_out, fpos_ref, tails, final, sem,
):
    total = recv_ref[0]
    for d in range(1, recv_ref.shape[0]):
        total = total + recv_ref[d]
    q, u = plat_ref[...], plat_vel_ref[...]
    hist = [hist_ref[m] for m in range(STEPS)]
    ones = total[ONES_ROW : ONES_ROW + 1]
    qs = [q]
    for step in range(STEPS):
        force = total[3 * step : 3 * step + 3]
        if step > 0:
            force = force - ones * q
        for t in range(1, step):
            at = ONES_ROW + 1 + 2 * PAIRS.index((step, t))
            coef = jnp.concatenate([total[at : at + 1], total[at : at + 2]], axis=0)
            force = force + coef * qs[t]
        memory = kern_ref[0] * hist[0]
        for m in range(1, STEPS):
            memory = memory + kern_ref[m] * hist[m]
        u = u + inv_ref[...] * (force - rest_ref[...] * q - memory + wave_ref[step])
        q = q + u
        hist = [u] + hist[:-1]
        qs.append(q)
    plat_out[...] = q
    k = stiff_ref[...]
    onehot = (attach_ref[...] == iota((LANES, LANES), 0)).astype(F32)
    fair = jnp.dot(jnp.concatenate(qs, axis=0), onehot, precision=HIGH, preferred_element_type=F32)
    trow = iota((TAIL, LANES), 0)
    pos = [pos_ref[c] for c in range(3)]
    vel = [vel_ref[c] for c in range(3)]
    for step in range(STEPS + 1):
        for c in range(3):
            here = fair[step * 3 + c : step * 3 + c + 1] + off_ref[c : c + 1]
            p = jnp.where(trow == TAIL - 1, here, pos[c])
            tails[c * TAIL : (c + 1) * TAIL, step * LANES : (step + 1) * LANES] = p
            if step == STEPS:
                final[c] = p
                continue
            touch = contact_ref[step].astype(F32)
            up = pltpu.roll(p, TAIL - 1, 0)
            bound = bound_ref[step * 3 + c : step * 3 + c + 1]
            down = jnp.where(trow == 0, bound, pltpu.roll(p, 1, 0))
            accel = k * (up - 2.0 * p + down) - (0.02 + 0.1 * touch) * vel[c]
            if c == 2:
                accel = accel + (-0.05 - 0.3 * touch * (p + 2.0))
            vel[c] = vel[c] + accel
            pos[c] = p + vel[c]
    copy = pltpu.make_async_copy(final, fpos_ref.at[:, NODES - TAIL : NODES, :], sem)
    copy.start()
    picked = nt(pick_matrix(pick_ref), tails[...].astype(BF16)).astype(BF16)
    at = iota((3 * TAIL, FEATS), 0)
    where = (at // TAIL) * NODES + (NODES - TAIL) + at % TAIL
    place = (iota((3 * TAIL, FEATS), 1) == where).astype(F32).astype(BF16)
    rows = rows_ref[...].astype(F32) + jnp.dot(picked, place, preferred_element_type=F32)
    count = x_ref.shape[0]
    x_ref[...] = rows[:count].astype(BF16)
    t_ref[...] = rows[count:].astype(BF16)
    copy.wait()


VM = pl.BlockSpec(memory_space=pltpu.VMEM)


def evolve(line_pos, line_vel, stiff, contact, offset, attach, plat_pos, pick, dest):
    sds = jax.ShapeDtypeStruct
    return pl.pallas_call(
        evolve_kernel,
        out_shape=(
            sds((ROWS, LANES), F32),
            sds((2 * COUNT, FEATS), BF16),
            sds((3 * STEPS, LANES), F32),
            sds((3, NODES, LANES), F32),
        ),
        in_specs=[VM] * 9,
        out_specs=(VM,) * 4,
        scratch_shapes=[
            pltpu.VMEM((3 * NODES, LANES * (STEPS + 1)), BF16),
            pltpu.VMEM((ROWS, LANES), F32),
        ],
        compiler_params=pltpu.CompilerParams(vmem_limit_bytes=40 * 1024 * 1024),
        name="evolve",
    )(line_pos, line_vel, stiff, contact, offset, attach, plat_pos, pick, dest)


def finish(recv, plats, lines, bound, rows, fpos):
    sds = jax.ShapeDtypeStruct
    whole = lambda a: pl.BlockSpec(a.shape, lambda i: (0,) * a.ndim)
    tail = lambda a: pl.BlockSpec((a.shape[0], TAIL, LANES), lambda i: (0, NODES // TAIL - 1, 0))
    line_pos, line_vel, contact, stiff, offset, attach, pick = lines
    args = (recv, *plats, line_pos, line_vel, contact, stiff, offset, attach, pick, bound, rows)
    specs = [whole(a) for a in args]
    at = 1 + len(plats)
    for i in range(at, at + 3):
        specs[i] = tail(args[i])
    out = (sds((COUNT, FEATS), BF16), sds((COUNT, FEATS), BF16), sds((3, LANES), F32))
    return pl.pallas_call(
        finish_kernel,
        grid=(1,),
        out_shape=out + (sds(fpos.shape, F32),),
        in_specs=specs + [pl.BlockSpec(memory_space=pl.ANY)],
        out_specs=tuple(whole(a) for a in out) + (pl.BlockSpec(memory_space=pl.ANY),),
        scratch_shapes=[
            pltpu.VMEM((3 * TAIL, LANES * (STEPS + 1)), F32),
            pltpu.VMEM((3, TAIL, LANES), F32),
            pltpu.SemaphoreType.DMA,
        ],
        input_output_aliases={len(args): 3},
        compiler_params=pltpu.CompilerParams(vmem_limit_bytes=40 * 1024 * 1024),
        name="finish",
    )(*args, fpos)


def exchange(x, axes):
    return lax.all_to_all(x, axes, split_axis=0, concat_axis=0, tiled=True)


def spread(x, axes):
    return exchange(jnp.broadcast_to(x[None], (lax.axis_size(axes),) + x.shape), axes)


def body(
    line_pos, line_vel, stiffness, contact, offset, attach, plat_pos, plat_vel, inv_mass, restoring,
    kernel, vel_hist, wave, sample_pick, sample_dest, w_in, gain, w_gate, w_up, w_down, w_out,
):
    chips = lax.axis_size(CHIP)
    half = chips * COUNT
    stiff, att, pick = stiffness[None], attach[None], sample_pick[None]
    pay, rows, bound, fpos = evolve(
        line_pos, line_vel, stiff, contact, offset, att, plat_pos, pick, sample_dest
    )
    recv = spread(pay, DEV)
    x_own, target, final_plat, final_pos = finish(
        recv,
        (plat_pos, plat_vel, inv_mass, restoring, kernel, vel_hist, wave),
        (line_pos, line_vel, contact, stiff, offset, att, pick),
        bound, rows, fpos,
    )
    x_mine = spread(x_own, CHIP).reshape(half, FEATS)
    x_other = lax.ppermute(x_mine, "core", SWAP)
    x_all = jnp.concatenate([x_mine, x_other], axis=0)
    fused = jnp.dot(w_down, w_out, preferred_element_type=F32).astype(BF16)
    hidden = jnp.dot(x_all, w_in, preferred_element_type=F32).astype(BF16)
    wide = hidden.astype(F32)
    normed = (wide * lax.rsqrt(jnp.mean(wide * wide, axis=1, keepdims=True) + 1e-06) * gain).astype(BF16)
    gate = jnp.dot(normed, w_gate, preferred_element_type=F32)
    upper = jnp.dot(normed, w_up, preferred_element_type=F32)
    sigma = jax.nn.sigmoid(gate)
    act = (gate * sigma * upper).astype(BF16)
    part = jnp.dot(act, fused, preferred_element_type=F32)
    from_core = lax.ppermute(part[half:].astype(BF16), "core", SWAP)
    both = (part[:half] + from_core.astype(F32)).astype(BF16)
    parts = exchange(both.reshape(chips, COUNT, FEATS), CHIP)
    chip = lax.axis_index(CHIP)
    core = lax.axis_index("core")
    own_hidden = lax.dynamic_slice_in_dim(hidden, chip * COUNT, COUNT, 0)
    err = (
        jnp.dot(own_hidden, w_out, preferred_element_type=F32)
        + jnp.sum(parts.astype(F32), axis=0)
        - target.astype(F32)
    ).astype(BF16)
    err_mine = spread(err, CHIP).reshape(half, FEATS)
    err_other = lax.ppermute(err_mine, "core", SWAP)
    err_all = jnp.concatenate([err_mine, err_other], axis=0)
    dpred = (err_all.astype(F32) / 64.0).astype(BF16)
    dact = nt(dpred, fused)
    dgate = (dact * upper * sigma * (1.0 + gate * (1.0 - sigma))).astype(BF16)
    dup = (dact * gate * sigma).astype(BF16)
    joined = jnp.concatenate([dgate, dup], axis=1)
    width = dgate.shape[1]
    grads = lax.dot_general(normed, joined, (((0,), (0,)), ((), ())), preferred_element_type=F32).astype(BF16)
    groups = lax.axis_size(GRP)
    grads = exchange(grads.reshape(groups, -1, 2 * width), GRP)
    grads = jnp.sum(grads.astype(F32), axis=0)
    codes = recv[:, CODE_ROW, :COUNT].reshape(chips, 2, COUNT)
    codes = lax.dynamic_slice_in_dim(jnp.concatenate([codes, codes], axis=1), core, 2, 1)
    codes = codes.transpose(1, 0, 2).reshape(1, 2 * half)
    me = chip * 2 + core
    number = jnp.arange(2 * half, dtype=jnp.int32)
    source = ((number // COUNT) % chips) * 2 + (number // half + core) % 2
    slot = jnp.arange(2 * chips * CAP, dtype=jnp.int32)[:, None]
    match = (source[None] == slot // CAP) & (codes == (me * CAP + slot % CAP).astype(F32))
    slot_error = jnp.dot(match.astype(BF16), err_all, preferred_element_type=F32).astype(BF16)
    return (final_pos, final_plat, slot_error, grads[:, :width], grads[:, width:])


def solution(mesh):
    sizes = (4, 2, 2, 4, 2)
    if mesh.devices.shape[0] == 1:
        sizes = (1, 1, 2, 4, 2)
    fine = Mesh(mesh.devices.reshape(sizes), ALL)
    in_specs = (
        P(None, None, ALL),
        P(None, None, ALL),
        P(ALL),
        P(None, None, ALL),
        P(None, ALL),
        P(ALL),
        P(None, GRP),
        P(None, GRP),
        P(None, GRP),
        P(None, GRP),
        P(None, None, GRP),
        P(None, None, GRP),
        P(None, None, GRP),
        P(ALL),
        P(ALL, None),
        P(),
        P(),
        P(None, DEV),
        P(None, DEV),
        P(DEV, None),
        P(),
    )
    out_specs = (
        P(None, None, ALL),
        P(None, GRP),
        P(ALL, None),
        P(GRP, DEV),
        P(GRP, DEV),
    )
    return jax.shard_map(body, mesh=fine, in_specs=in_specs, out_specs=out_specs, check_vma=False)
```

profile of v0, /device:TPU:0, one launch (start us, length us, event | category | flops | bytes accessed | tf_op | source)
XLA Modules:
  0.0 199.7 jit_solution(8389634480455340487)
XLA Ops:
  0.6 1.5 copy.31.dest_ref
  2.2 1.2 copy-done.1
  3.4 1.0 copy-done.3
  4.4 1.0 copy-done.5
  5.4 0.8 copy-done.9
  6.1 0.7 copy-done.16
  6.8 0.7 copy-done.18
  7.5 0.7 copy-done.23
  8.2 0.7 copy-done.25
  8.8 0.7 copy-done.27
  9.5 3.3 %evolve.1 = (f32[72,128]{1,0:T(8,128)S(1)}, bf16[128,768]{1,0:T(8,128)(2,1)S(1)}, f32[24,128]{1,0:T(8,128)S(1)}, f32[3,256,128]{2,1,0:T(8,128)}) custom-call(f32[3,256,128]{2,1,0:T(8,128)S(1)} %copy-done.3, f32[3,256,128]{2,1,0:T(8,128)S(1)} %copy-done.5, f32[1,128]{1,0:T(1,128)S(1)} %bitcast.18, s32[8,256,128]{2,1,0:T(8,128)S(1)} %copy-done.1, ...), custom_call_target="tpu_custom_call" | custom-call | tf_op jit(solution)/shard_map/evolve/pallas_call | solution.py:180
  12.7 0.7 copy-done.7
  13.4 0.6 copy-done.14
  14.0 0.9 broadcast_in_dim.15
  14.9 5.9 %all-to-all-start = ((f32[16,72,128]{2,1,0:T(8,128)}), f32[16,72,128]{2,1,0:T(8,128)}, u32[]{:S(2)}, u32[]{:S(2)}) async-start(f32[16,72,128]{2,1,0:T(8,128)} %broadcast_in_dim.15), calls=%async_computation | async-start | bytes 1179648 | tf_op jit(solution)/shard_map/all_to_all | solution.py:228
  20.8 0.7 copy.32.kern_ref
  21.5 1.3 copy.33.hist_ref
  22.8 1.3 copy.34.wave_ref
  24.1 8.3 %all-to-all-done.recv_ref = f32[16,72,128]{2,1,0:T(8,128)} async-done(((f32[16,72,128]{2,1,0:T(8,128)}), f32[16,72,128]{2,1,0:T(8,128)}, u32[]{:S(2)}, u32[]{:S(2)}) %all-to-all-start) | async-done | bytes 589856 | tf_op jit(solution)/shard_map/all_to_all | solution.py:228
  32.4 1.2 copy-done.2
  33.6 1.0 copy-done.6
  34.6 0.9 copy-done.8
  35.5 0.7 copy-done.12
  36.3 0.7 copy-done.13
  37.0 0.7 copy-done.15
  37.7 0.7 copy-done.17
  38.4 0.7 copy-done.19
  39.0 0.7 copy-done.20
  39.7 0.7 copy-done.21
  40.4 0.7 copy-done.22
  41.1 0.7 copy-done.24
  41.7 0.7 copy-done.26
  42.4 0.7 copy-done.28
  43.1 2.8 %finish.1 = (bf16[64,768]{1,0:T(8,128)(2,1)S(1)}, bf16[64,768]{1,0:T(8,128)(2,1)S(1)}, f32[3,128]{1,0:T(4,128)}, f32[3,256,128]{2,1,0:T(8,128)}) custom-call(f32[16,72,128]{2,1,0:T(8,128)} %all-to-all-done.recv_ref, f32[3,128]{1,0:T(4,128)S(1)} %copy-done.19, f32[3,128]{1,0:T(4,128)S(1)} %copy-done.20, ...), custom_call_target="tpu_custom_call", output_to_operand_aliasing={{3}: (17, {})} | custom-call | tf_op jit(solution)/shard_map/finish/pallas_call | solution.py:210
  45.9 0.1 broadcast_in_dim.16
  46.0 15.4 %all_to_all.25 = bf16[8,64,768]{2,1,0:T(8,128)(2,1)S(1)} all-to-all(bf16[8,64,768]{2,1,0:T(8,128)(2,1)S(1)} %broadcast_in_dim.16), channel_id=1, replica_groups=mesh['y'=4,'zh'=2,'zl'=2,'x'=4,'core'=2] {'zl','x'}, dimensions={0} | all-to-all | bytes 1572864 | tf_op jit(solution)/shard_map/all_to_all | solution.py:228
  61.4 1.8 convolution_convert_fusion.2
  63.2 0.4 collective-permute-done
  63.7 4.5 %fusion = (f32[1024]{0:T(1024)S(1)}, bf16[1024,2048]{1,0:T(8,128)(2,1)S(1)}) fusion(bf16[768,2048]{1,0:T(8,128)(2,1)S(1)} %copy-done, bf16[512,768]{1,0:T(8,128)(2,1)S(1)} %collective-permute-done, bf16[512,768]{1,0:T(8,128)(2,1)S(1)} %bitcast.30), kind=kOutput, calls=%fused_computation.2 | convolution fusion | flops 3232758784 | bytes 8916992 | tf_op jit(solution)/shard_map/dot_general | solution.py:256
  68.2 2.6 %fusion.45 = f32[1024,512]{0,1:T(8,128)S(1)} fusion(bf16[2048,512]{1,0:T(8,128)(2,1)S(1)} %copy-done.34, bf16[1024,2048]{1,0:T(8,128)(2,1)S(1)} %get-tuple-element.26, f32[2048]{0:T(1024)S(1)} %copy-done.37, f32[1024]{0:T(1024)S(1)} %add_rsqrt_fusion), kind=kOutput, calls=%fused_computation.82 | convolution fusion | flops 2155872256 | bytes 8400896 | tf_op jit(solution)/shard_map/dot_general | solution.py:260
  70.8 0.5 copy-done.35
  71.3 2.6 %fusion.47 = f32[1024,512]{0,1:T(8,128)S(1)} fusion(bf16[2048,512]{1,0:T(8,128)(2,1)S(1)} %copy-done.35, bf16[1024,2048]{1,0:T(8,128)(2,1)S(1)} %get-tuple-element.26, f32[2048]{0:T(1024)S(1)} %copy-done.37, f32[1024]{0:T(1024)S(1)} %add_rsqrt_fusion), kind=kOutput, calls=%fused_computation.83 | convolution fusion | flops 2155872256 | bytes 8400896 | tf_op jit(solution)/shard_map/dot_general | solution.py:259
  73.9 1.2 fusion.14
  75.1 0.2 copy-done.42
  75.3 0.1 slice.30
  75.4 0.2 collective-permute-start.1
  75.6 2.1 %collective-permute-done.1 = bf16[512,768]{1,0:T(8,128)(2,1)S(1)} collective-permute-done((bf16[512,768]{1,0:T(8,128)(2,1)S(1)}, bf16[512,768]{1,0:T(8,128)(2,1)S(1)}, u32[]{:S(2)}, u32[]{:S(2)}) %collective-permute-start.1) | collective-permute-done | bytes 786464 | tf_op jit(solution)/shard_map/ppermute | solution.py:264
  77.7 1.1 fusion.7
  78.8 4.2 %all-to-all-start.2 = ((bf16[8,64,768]{2,1,0:T(8,128)(2,1)}), bf16[8,64,768]{2,1,0:T(8,128)(2,1)}, u32[]{:S(2)}, u32[]{:S(2)}) async-start(bf16[8,64,768]{2,1,0:T(8,128)(2,1)} %bitcast.25), calls=%async_computation.2 | async-start | bytes 1572864 | tf_op jit(solution)/shard_map/all_to_all | solution.py:228
  83.0 13.5 %all-to-all-done.2 = bf16[8,64,768]{2,1,0:T(8,128)(2,1)} async-done(((bf16[8,64,768]{2,1,0:T(8,128)(2,1)}), bf16[8,64,768]{2,1,0:T(8,128)(2,1)}, u32[]{:S(2)}, u32[]{:S(2)}) %all-to-all-start.2) | async-done | bytes 786464 | tf_op jit(solution)/shard_map/all_to_all | solution.py:228
  96.5 1.3 convert_reduce_fusion.1
  97.8 2.8 %fusion.13 = bf16[64,768]{1,0:T(8,128)(2,1)S(1)} fusion(f32[64,768]{1,0:T(8,128)S(1)} %convert_reduce_fusion.1, bf16[2048,768]{1,0:T(8,128)(2,1)} %param.41, bf16[1024,2048]{1,0:T(8,128)(2,1)} %copy-done.31, s32[]{:T(128)S(6)} %select_n.69, bf16[64,768]{1,0:T(8,128)(2,1)S(1)} %copy-done.11), kind=kOutput, calls=%fused_computation.30 | convolution fusion | flops 201523200 | bytes 3801092 | tf_op jit(solution)/shard_map/dot_general | solution.py:271
  100.6 0.1 broadcast_in_dim.17
  100.7 15.5 %all_to_all.26 = bf16[8,64,768]{2,1,0:T(8,128)(2,1)S(1)} all-to-all(bf16[8,64,768]{2,1,0:T(8,128)(2,1)S(1)} %broadcast_in_dim.17), channel_id=1, replica_groups=mesh['y'=4,'zh'=2,'zl'=2,'x'=4,'core'=2] {'zl','x'}, dimensions={0} | all-to-all | bytes 1572864 | tf_op jit(solution)/shard_map/all_to_all | solution.py:228
  116.2 2.3 %collective-permute-done.2 = bf16[512,768]{1,0:T(8,128)(2,1)S(1)} collective-permute-done((bf16[512,768]{1,0:T(8,128)(2,1)S(1)}, bf16[512,768]{1,0:T(8,128)(2,1)S(1)}, u32[]{:S(2)}, u32[]{:S(2)}) %collective-permute-start.2) | collective-permute-done | bytes 786464 | tf_op jit(solution)/shard_map/ppermute | solution.py:276
  118.5 1.7 multiply_convert_fusion.2
  120.2 7.8 %convolution_convert_fusion.1 = bf16[2048,1024]{1,0:T(8,128)(2,1)} fusion(bf16[1024,512]{0,1:T(8,128)(2,1)S(1)} %get-tuple-element.22, bf16[1024,512]{0,1:T(8,128)(2,1)S(1)} %get-tuple-element.21, bf16[1024,2048]{1,0:T(8,128)(2,1)S(1)} %copy-done.32, f32[2048]{0:T(1024)S(1)} %copy-done.37, f32[1024]{0:T(1024)S(1)} %add_rsqrt_fusion), kind=kOutput, calls=%fused_computation.7 | convolution fusion | flops 4309647360 | bytes 10498048 | tf_op jit(solution)/shard_map/dot_general | solution.py:284
  128.0 7.5 %all-to-all-start.4 = ((bf16[8,256,1024]{2,1,0:T(8,128)(2,1)}), bf16[8,256,1024]{2,1,0:T(8,128)(2,1)}, u32[]{:S(2)}, u32[]{:S(2)}) async-start(bf16[8,256,1024]{2,1,0:T(8,128)(2,1)} %bitcast.24), calls=%async_computation.4 | async-start | bytes 8388608 | tf_op jit(solution)/shard_map/all_to_all | solution.py:228
  135.6 0.8 slice.21
  136.4 0.1 eq.36
  136.5 2.5 %convolution_convert_fusion.3 = bf16[128,768]{1,0:T(8,128)(2,1)} fusion(bf16[512,768]{1,0:T(8,128)(2,1)} %copy-done.36, bf16[512,768]{1,0:T(8,128)(2,1)} %bitcast.28, f32[1024]{0:T(1024)S(1)} %eq.36, s32[1024]{0:T(1024)S(1)} %fusion.27, f32[128]{0:T(128)S(1)} %get-tuple-element.28, s32[128]{0:T(128)S(1)} %get-tuple-element.27), kind=kOutput, calls=%fused_computation.27 | convolution fusion | flops 204963840 | bytes 1778688 | tf_op jit(solution)/shard_map/dot_general | solution.py:296
  139.0 56.5 %all-to-all-done.4 = bf16[8,256,1024]{2,1,0:T(8,128)(2,1)} async-done(((bf16[8,256,1024]{2,1,0:T(8,128)(2,1)}), bf16[8,256,1024]{2,1,0:T(8,128)(2,1)}, u32[]{:S(2)}, u32[]{:S(2)}) %all-to-all-start.4) | async-done | bytes 4194336 | tf_op jit(solution)/shard_map/all_to_all | solution.py:228
  195.4 3.2 %convert_reduce_fusion = f32[256,1024]{1,0:T(8,128)S(1)} fusion(bf16[8,256,1024]{2,1,0:T(8,128)(2,1)} %all-to-all-done.4), kind=kLoop, calls=%fused_computation.5 | loop fusion | flops 3932160 | bytes 5242880 | tf_op jit(solution)/shard_map/reduce_sum | solution.py:287
  198.6 1.0 fusion.49
  (68 shorter events, 0.2 us)
Async XLA Ops:
  0.6 63.0 %copy-start = (bf16[768,2048]{1,0:T(8,128)(2,1)S(1)}, bf16[768,2048]{1,0:T(8,128)(2,1)}, u32[]{:S(2)}) copy-start(bf16[768,2048]{1,0:T(8,128)(2,1)} %param.36) | copy-start | bytes 9437188
  2.2 1.2 copy-start.1
  3.4 1.0 copy-start.3
  4.4 1.0 copy-start.5
  5.4 0.8 copy-start.9
  6.1 0.7 copy-start.16
  6.8 0.7 copy-start.18
  7.5 0.7 copy-start.23
  8.2 0.7 copy-start.25
  8.8 0.7 copy-start.27
  9.5 22.9 %copy-start.4 = (f32[3,256,128]{2,1,0:T(8,128)S(1)}, f32[3,256,128]{2,1,0:T(8,128)}, u32[]{:S(2)}) copy-start(f32[3,256,128]{2,1,0:T(8,128)} %pos_ref.3) | copy-start | bytes 1179652
  12.7 0.7 copy-start.7
  13.4 0.6 copy-start.14
  14.9 17.5 %all-to-all-start = ((f32[16,72,128]{2,1,0:T(8,128)}), f32[16,72,128]{2,1,0:T(8,128)}, u32[]{:S(2)}, u32[]{:S(2)}) async-start(f32[16,72,128]{2,1,0:T(8,128)} %broadcast_in_dim.15), calls=%async_computation | async-start | bytes 1179648 | tf_op jit(solution)/shard_map/all_to_all | solution.py:228
  32.4 1.2 copy-start.2
  33.6 1.0 copy-start.6
  34.6 0.9 copy-start.8
  35.5 0.7 copy-start.12
  36.3 0.7 copy-start.13
  37.0 0.7 copy-start.15
  37.7 0.7 copy-start.17
  38.4 0.7 copy-start.19
  39.0 0.7 copy-start.20
  39.7 0.7 copy-start.21
  40.4 0.7 copy-start.22
  41.1 0.7 copy-start.24
  41.7 0.7 copy-start.26
  42.4 0.7 copy-start.28
  43.1 18.3 %copy-start.29 = (bf16[2048,768]{1,0:T(8,128)(2,1)S(1)}, bf16[2048,768]{1,0:T(8,128)(2,1)}, u32[]{:S(2)}) copy-start(bf16[2048,768]{1,0:T(8,128)(2,1)} %param.41) | copy-start | bytes 9437188
  43.1 18.3 %copy-start.33 = (bf16[512,2048]{1,0:T(8,128)(2,1)S(1)}, bf16[512,2048]{1,0:T(8,128)(2,1)}, u32[]{:S(2)}) copy-start(bf16[512,2048]{1,0:T(8,128)(2,1)} %param.40) | copy-start | bytes 6291460
  45.9 17.3 %copy-start.10 = (bf16[64,768]{1,0:T(8,128)(2,1)}, bf16[64,768]{1,0:T(8,128)(2,1)S(1)}, u32[]{:S(2)}) copy-start(bf16[64,768]{1,0:T(8,128)(2,1)S(1)} %get-tuple-element.20) | copy-start | bytes 294916
  61.4 2.3 %collective-permute-start = (bf16[512,768]{1,0:T(8,128)(2,1)S(1)}, bf16[512,768]{1,0:T(8,128)(2,1)S(1)}, u32[]{:S(2)}, u32[]{:S(2)}) collective-permute-start(bf16[512,768]{1,0:T(8,128)(2,1)S(1)} %bitcast.29), channel_id=1, source_target_pairs={{0,1},{1,0},{2,3},{3,2},{4,5},{5,4},{6,7},{7,6},{8,9},{9,8},{10,11... | collective-permute-start | bytes 2359304 | tf_op jit(solution)/shard_map/ppermute | solution.py:253
  63.2 10.7 %copy-start.38 = (bf16[512,768]{1,0:T(8,128)(2,1)}, bf16[512,768]{1,0:T(8,128)(2,1)S(1)}, u32[]{:S(2)}) copy-start(bf16[512,768]{1,0:T(8,128)(2,1)S(1)} %convolution_convert_fusion.2) | copy-start | bytes 2359300
  63.2 5.0 %copy-start.34 = (bf16[2048,512]{1,0:T(8,128)(2,1)S(1)}, bf16[2048,512]{1,0:T(8,128)(2,1)}, u32[]{:S(2)}) copy-start(bf16[2048,512]{1,0:T(8,128)(2,1)} %param.39) | copy-start | bytes 6291460
  63.2 5.0 %copy-start.37 = (f32[2048]{0:T(1024)S(1)}, f32[2048]{0:T(1024)}, u32[]{:S(2)}) copy-start(f32[2048]{0:T(1024)} %param.37) | copy-start | bytes 24580
  68.2 2.7 %copy-start.31 = (bf16[1024,2048]{1,0:T(8,128)(2,1)}, bf16[1024,2048]{1,0:T(8,128)(2,1)S(1)}, u32[]{:S(2)}) copy-start(bf16[1024,2048]{1,0:T(8,128)(2,1)S(1)} %get-tuple-element.26) | copy-start | bytes 12582916
  68.2 3.1 %copy-start.35 = (bf16[2048,512]{1,0:T(8,128)(2,1)S(1)}, bf16[2048,512]{1,0:T(8,128)(2,1)}, u32[]{:S(2)}) copy-start(bf16[2048,512]{1,0:T(8,128)(2,1)} %param.38) | copy-start | bytes 6291460
  71.3 2.6 %copy-start.40 = (f32[1024,512]{0,1:T(8,128)}, f32[1024,512]{0,1:T(8,128)S(1)}, u32[]{:S(2)}) copy-start(f32[1024,512]{0,1:T(8,128)S(1)} %fusion.45) | copy-start | bytes 6291460
  73.9 1.4 copy-start.42
  75.4 22.5 %copy-start.11 = (bf16[64,768]{1,0:T(8,128)(2,1)S(1)}, bf16[64,768]{1,0:T(8,128)(2,1)}, u32[]{:S(2)}) copy-start(bf16[64,768]{1,0:T(8,128)(2,1)} %copy-done.10) | copy-start | bytes 294916
  75.4 2.4 %collective-permute-start.1 = (bf16[512,768]{1,0:T(8,128)(2,1)S(1)}, bf16[512,768]{1,0:T(8,128)(2,1)S(1)}, u32[]{:S(2)}, u32[]{:S(2)}) collective-permute-start(bf16[512,768]{1,0:T(8,128)(2,1)S(1)} %slice.30), channel_id=1, source_target_pairs={{0,1},{1,0},{2,3},{3,2},{4,5},{5,4},{6,7},{7,6},{8,9},{9,8},{10,11... | collective-permute-start | bytes 2359304 | tf_op jit(solution)/shard_map/ppermute | solution.py:264
  78.8 17.7 %all-to-all-start.2 = ((bf16[8,64,768]{2,1,0:T(8,128)(2,1)}), bf16[8,64,768]{2,1,0:T(8,128)(2,1)}, u32[]{:S(2)}, u32[]{:S(2)}) async-start(bf16[8,64,768]{2,1,0:T(8,128)(2,1)} %bitcast.25), calls=%async_computation.2 | async-start | bytes 1572864 | tf_op jit(solution)/shard_map/all_to_all | solution.py:228
  97.8 20.7 %copy-start.39 = (bf16[512,768]{1,0:T(8,128)(2,1)S(1)}, bf16[512,768]{1,0:T(8,128)(2,1)}, u32[]{:S(2)}) copy-start(bf16[512,768]{1,0:T(8,128)(2,1)} %copy-done.38) | copy-start | bytes 2359300
  97.8 20.7 %copy-start.41 = (f32[1024,512]{0,1:T(8,128)S(1)}, f32[1024,512]{0,1:T(8,128)}, u32[]{:S(2)}) copy-start(f32[1024,512]{0,1:T(8,128)} %copy-done.40) | copy-start | bytes 6291460
  97.8 20.7 %copy-start.43 = (f32[1024,512]{0,1:T(8,128)S(1)}, f32[1024,512]{0,1:T(8,128)}, u32[]{:S(2)}) copy-start(f32[1024,512]{0,1:T(8,128)} %copy-done.42) | copy-start | bytes 6291460
  116.2 4.0 %copy-start.30 = (bf16[8,64,768]{2,1,0:T(8,128)(2,1)}, bf16[8,64,768]{2,1,0:T(8,128)(2,1)S(1)}, u32[]{:S(2)}) copy-start(bf16[8,64,768]{2,1,0:T(8,128)(2,1)S(1)} %all_to_all.26) | copy-start | bytes 2359300
  116.2 4.0 %copy-start.32 = (bf16[1024,2048]{1,0:T(8,128)(2,1)S(1)}, bf16[1024,2048]{1,0:T(8,128)(2,1)}, u32[]{:S(2)}) copy-start(bf16[1024,2048]{1,0:T(8,128)(2,1)} %copy-done.31) | copy-start | bytes 12582916
  116.2 2.3 %collective-permute-start.2 = (bf16[512,768]{1,0:T(8,128)(2,1)S(1)}, bf16[512,768]{1,0:T(8,128)(2,1)S(1)}, u32[]{:S(2)}, u32[]{:S(2)}) collective-permute-start(bf16[512,768]{1,0:T(8,128)(2,1)S(1)} %bitcast.26), channel_id=1, source_target_pairs={{0,1},{1,0},{2,3},{3,2},{4,5},{5,4},{6,7},{7,6},{8,9},{9,8},{10,11... | collective-permute-start | bytes 2359304 | tf_op jit(solution)/shard_map/ppermute | solution.py:276
  118.5 1.7 copy-start.36
  128.0 67.4 %all-to-all-start.4 = ((bf16[8,256,1024]{2,1,0:T(8,128)(2,1)}), bf16[8,256,1024]{2,1,0:T(8,128)(2,1)}, u32[]{:S(2)}, u32[]{:S(2)}) async-start(bf16[8,256,1024]{2,1,0:T(8,128)(2,1)} %bitcast.24), calls=%async_computation.4 | async-start | bytes 8388608 | tf_op jit(solution)/shard_map/all_to_all | solution.py:228
where the time goes:
time: 201 us; the launch traced here: 200 us
  waiting for transfers between devices  83.1 us (41%)
  blocking collectives  30.9 us (15%)
  local copies, waits for them, and re-layouts  27.8 us (14%)
  matrix products  27.4 us (14%)
  starting transfers between devices  17.9 us (9%)
  Pallas kernels  6.07 us (3%)
  other arithmetic  5.52 us (3%)
    all_to_all x3, waiting for transfers between devices, exchange(): return lax.all_to_all(x, axes, split_axis=0, concat_axis=0, tiled=True)  78.2 us
    all_to_all x2, blocking collectives, exchange(): return lax.all_to_all(x, axes, split_axis=0, concat_axis=0, tiled=True)  30.9 us
    unnamed x92, local copies, waits for them, and re-layouts  24.8 us
    all_to_all x3, starting transfers between devices, exchange(): return lax.all_to_all(x, axes, split_axis=0, concat_axis=0, tiled=True)  17.6 us
    dot_general x1, matrix products, body(): lax.dot_general(normed, joined, (((0,), (0,)), ((), ())), preferred_eleme...  7.82 us
    dot_general x1, matrix products, body(): hidden = jnp.dot(x_all, w_in, preferred_element_type=F32).astype(BF16)  4.52 us
  transfers between devices with their start and end apart: 6, of which 6 were waited for; matrix products, arithmetic and copies ran while one was open for 4% of the time, Pallas kernels for 0%

commit v1 on v0

v1 whole, which is shorter than its diff:
```python
import functools
import jax
import jax.numpy as jnp
from jax import lax
from jax.experimental import pallas as pl
from jax.experimental.pallas import tpu as pltpu
from jax.sharding import Mesh, PartitionSpec as P

STEPS = 8
CAP = 8
NODES = 256
TAIL = 8
LANES = 128
COUNT = 64
FEATS = 768
ROWS = 72
ONES_ROW = 24
CODE_ROW = 67
HIGH = lax.Precision.HIGHEST
F32 = jnp.float32
BF16 = jnp.bfloat16
DEV = ("zl", "x", "core")
CHIP = ("zl", "x")
GRP = ("y", "zh")
ALL = GRP + DEV
PAIRS = [(s, t) for s in range(2, STEPS) for t in range(1, s)]
SWAP = [(0, 1), (1, 0)]


def nt(left, right, precision=None):
    return lax.dot_general(
        left, right, (((1,), (1,)), ((), ())), precision=precision, preferred_element_type=F32
    )


def iota(shape, dim):
    return lax.broadcasted_iota(jnp.int32, shape, dim)


def pick_matrix(pick_ref):
    count = pick_ref.shape[1]
    eye = iota((count, count), 0) == iota((count, count), 1)
    pick = jnp.sum(jnp.where(eye, pick_ref[...].astype(F32), 0.0), axis=1, keepdims=True).astype(jnp.int32)
    at = (pick >> 3) + LANES * (pick & 7)
    at = jnp.concatenate([at, at + LANES], axis=0)
    return (iota((2 * count, LANES * (STEPS + 1)), 1) == at).astype(F32).astype(BF16)


def fetch(refs, bufs, sem):
    copies = [pltpu.make_async_copy(r, b, sem.at[i]) for i, (r, b) in enumerate(zip(refs, bufs))]
    for c in copies:
        c.start()
    return copies


def evolve_kernel(
    pos_ref, vel_ref, stiff_ref, contact_ref, off_ref, attach_ref, plat_ref, pick_ref, dest_ref,
    pay_ref, rows_ref, bound_ref, fpos_ref,
    posb, velb, contactb, stiffb, offb, attachb, platb, pickb, destb, stack, lin, sem,
):
    small = fetch(
        (stiff_ref, off_ref, attach_ref, plat_ref, pick_ref, dest_ref),
        (stiffb, offb, attachb, platb, pickb, destb),
        sem.at[0],
    )
    large = fetch(
        (pos_ref, vel_ref) + tuple(contact_ref.at[s] for s in range(STEPS)),
        (posb, velb) + tuple(contactb.at[s] for s in range(STEPS)),
        sem.at[1],
    )
    for c in small:
        c.wait()
    k = stiffb[...]
    onehot = (attachb[...] == iota((LANES, LANES), 0)).astype(F32)
    off = offb[...]
    fair = jnp.dot(platb[...], onehot, precision=HIGH, preferred_element_type=F32) + off
    picks = pick_matrix(pickb)
    row = iota((NODES, LANES), 0)
    first, last, bulk = row == 0, row == NODES - 1, row < NODES - TAIL
    lin[...] = jnp.zeros_like(lin)
    lin[ONES_ROW : ONES_ROW + 1] = jnp.ones((1, LANES), F32)
    large[0].wait()
    large[1].wait()
    pos = [jnp.where(last, fair[c : c + 1], posb[c]) for c in range(3)]
    vel = [velb[c] for c in range(3)]
    for step in range(STEPS):
        large[2 + step].wait()
        touch = contactb[step].astype(F32)
        damp = 0.02 + 0.1 * touch
        for c in range(3):
            p = pos[c]
            stack[c * NODES : (c + 1) * NODES, step * LANES : (step + 1) * LANES] = jnp.where(bulk, p, 0.0).astype(BF16)
            bound_ref[step * 3 + c : step * 3 + c + 1] = p[NODES - TAIL - 1 : NODES - TAIL]
            lin[step * 3 + c : step * 3 + c + 1] = p[NODES - 2 : NODES - 1] - p[NODES - 1 : NODES]
            accel = k * (pltpu.roll(p, NODES - 1, 0) - 2.0 * p + pltpu.roll(p, 1, 0)) - damp * vel[c]
            if c == 2:
                accel = accel + (-0.05 - 0.3 * touch * (p + 2.0))
            vel[c] = vel[c] + accel
            pos[c] = jnp.where(first, p, jnp.where(last, off[c : c + 1], p + vel[c]))
    for c in range(3):
        stack[c * NODES : (c + 1) * NODES, STEPS * LANES :] = jnp.where(bulk, pos[c], 0.0).astype(BF16)
        fpos_ref[c] = pos[c]
    rows_ref[...] = nt(picks, stack[...]).astype(BF16)
    trow = iota((TAIL, LANES), 0)
    zero = jnp.zeros((TAIL, LANES), F32)
    for kind in range(2):
        rp, rv = [zero] * 6, [zero] * 6
        for step in range(1, STEPS):
            for t in range(1, step):
                at = ONES_ROW + 1 + 2 * PAIRS.index((step, t)) + kind
                lin[at : at + 1] = rp[t - 1][TAIL - 2 : TAIL - 1]
            if step == STEPS - 1:
                break
            touch = contactb[step, NODES - TAIL : NODES].astype(F32)
            damp = 0.02 + 0.1 * touch
            for t in range(1, step + 1):
                p = jnp.where(trow == TAIL - 1, 1.0 if t == step else 0.0, rp[t - 1])
                up = pltpu.roll(p, TAIL - 1, 0)
                down = jnp.where(trow == 0, 0.0, pltpu.roll(p, 1, 0))
                accel = k * (up - 2.0 * p + down) - damp * rv[t - 1]
                if kind == 1:
                    accel = accel - 0.3 * touch * p
                rv[t - 1] = rv[t - 1] + accel
                rp[t - 1] = p + rv[t - 1]
    sums = nt(lin[...] * k, onehot, HIGH)
    count = destb.shape[1]
    lane, sub = iota((count, count), 1), iota((count, count), 0)
    dest = destb[...].astype(F32)
    dest_col = jnp.sum(jnp.where(lane == sub, dest, 0.0), axis=1, keepdims=True)
    rank = jnp.sum(jnp.where((dest_col == dest) & (sub < lane), 1.0, 0.0), axis=0, keepdims=True)
    codes = jnp.concatenate([dest * CAP + rank, jnp.full((1, LANES - count), -1.0, F32)], axis=1)
    pay_ref[...] = jnp.where(iota((ROWS, LANES), 0) == CODE_ROW, codes, sums)


def finish_kernel(
    recv_ref, bound_ref, rows_ref, plat_ref, plat_vel_ref, inv_ref, rest_ref, kern_ref, hist_ref, wave_ref,
    pos_ref, vel_ref, contact_ref, stiff_ref, off_ref, attach_ref, pick_ref, w_in_ref, fpos_in,
    x_ref, t_ref, h_ref, plat_out, fpos_ref,
    recvb, boundb, rowsb, platb, plat_velb, invb, restb, kernb, histb, waveb,
    posb, velb, contactb, stiffb, offb, attachb, pickb, w_inb, tails, final, sem, out_sem,
):
    at = pl.ds(NODES - TAIL, TAIL)
    copies = fetch(
        (
            recv_ref, plat_ref, plat_vel_ref, inv_ref, rest_ref, kern_ref, hist_ref, wave_ref,
            stiff_ref, off_ref, attach_ref, pick_ref, bound_ref, rows_ref,
            pos_ref.at[:, at, :], vel_ref.at[:, at, :], contact_ref.at[:, at, :], w_in_ref,
        ),
        (
            recvb, platb, plat_velb, invb, restb, kernb, histb, waveb,
            stiffb, offb, attachb, pickb, boundb, rowsb, posb, velb, contactb, w_inb,
        ),
        sem,
    )
    for c in copies[:-1]:
        c.wait()
    total = recvb[0]
    for d in range(1, recvb.shape[0]):
        total = total + recvb[d]
    q, u = platb[...], plat_velb[...]
    hist = [histb[:, m] for m in range(STEPS)]
    kern = [kernb[:, m] for m in range(STEPS)]
    ones = total[ONES_ROW : ONES_ROW + 1]
    qs = [q]
    for step in range(STEPS):
        force = total[3 * step : 3 * step + 3]
        if step > 0:
            force = force - ones * q
        for t in range(1, step):
            at = ONES_ROW + 1 + 2 * PAIRS.index((step, t))
            coef = jnp.concatenate([total[at : at + 1], total[at : at + 2]], axis=0)
            force = force + coef * qs[t]
        memory = kern[0] * hist[0]
        for m in range(1, STEPS):
            memory = memory + kern[m] * hist[m]
        u = u + invb[...] * (force - restb[...] * q - memory + waveb[:, step])
        q = q + u
        hist = [u] + hist[:-1]
        qs.append(q)
    plat_out[...] = q
    k = stiffb[...]
    onehot = (attachb[...] == iota((LANES, LANES), 0)).astype(F32)
    fair = jnp.dot(jnp.concatenate(qs, axis=0), onehot, precision=HIGH, preferred_element_type=F32)
    trow = iota((TAIL, LANES), 0)
    pos = [posb[c] for c in range(3)]
    vel = [velb[c] for c in range(3)]
    for step in range(STEPS + 1):
        for c in range(3):
            here = fair[step * 3 + c : step * 3 + c + 1] + offb[c : c + 1]
            p = jnp.where(trow == TAIL - 1, here, pos[c])
            tails[c * TAIL : (c + 1) * TAIL, step * LANES : (step + 1) * LANES] = p
            if step == STEPS:
                final[c] = p
                continue
            touch = contactb[step].astype(F32)
            up = pltpu.roll(p, TAIL - 1, 0)
            bound = boundb[step * 3 + c : step * 3 + c + 1]
            down = jnp.where(trow == 0, bound, pltpu.roll(p, 1, 0))
            accel = k * (up - 2.0 * p + down) - (0.02 + 0.1 * touch) * vel[c]
            if c == 2:
                accel = accel + (-0.05 - 0.3 * touch * (p + 2.0))
            vel[c] = vel[c] + accel
            pos[c] = p + vel[c]
    copy = pltpu.make_async_copy(final, fpos_ref.at[:, NODES - TAIL : NODES, :], out_sem)
    copy.start()
    picked = nt(pick_matrix(pickb), tails[...].astype(BF16)).astype(BF16)
    at = iota((3 * TAIL, FEATS), 0)
    where = (at // TAIL) * NODES + (NODES - TAIL) + at % TAIL
    place = (iota((3 * TAIL, FEATS), 1) == where).astype(F32).astype(BF16)
    rows = rowsb[...].astype(F32) + jnp.dot(picked, place, preferred_element_type=F32)
    count = x_ref.shape[0]
    t_ref[...] = rows[count:].astype(BF16)
    copies[-1].wait()
    hidden = jnp.dot(rows[:count].astype(BF16), w_inb[...], preferred_element_type=F32).astype(BF16)
    h_ref[...] = hidden
    wide = hidden.astype(F32)
    scale = lax.rsqrt(jnp.mean(wide * wide, axis=1, keepdims=True) + 1e-06)
    x_ref[...] = (rows[:count] * scale).astype(BF16)
    copy.wait()


VM = pl.BlockSpec(memory_space=pltpu.VMEM)
HB = pl.BlockSpec(memory_space=pltpu.HBM)


def vmem_like(a, tail=False):
    shape = (a.shape[0], TAIL, LANES) if tail else a.shape
    return pltpu.VMEM(shape, a.dtype)


def evolve(line_pos, line_vel, stiff, contact, offset, attach, plat_pos, pick, dest):
    sds = jax.ShapeDtypeStruct
    large = (line_pos, line_vel, contact)
    small = (stiff, offset, attach, plat_pos, pick, dest)
    return pl.pallas_call(
        evolve_kernel,
        out_shape=(
            sds((ROWS, LANES), F32),
            sds((2 * COUNT, FEATS), BF16),
            sds((3 * STEPS, LANES), F32),
            sds((3, NODES, LANES), F32),
        ),
        in_specs=[HB] * 9,
        out_specs=(VM,) * 4,
        scratch_shapes=[vmem_like(a) for a in large + small]
        + [
            pltpu.VMEM((3 * NODES, LANES * (STEPS + 1)), BF16),
            pltpu.VMEM((ROWS, LANES), F32),
            pltpu.SemaphoreType.DMA((2, 2 + STEPS)),
        ],
        compiler_params=pltpu.CompilerParams(vmem_limit_bytes=32 * 1024 * 1024),
        cost_estimate=pl.CostEstimate(flops=260000000, bytes_accessed=3000000, transcendentals=0),
        name="evolve",
    )(line_pos, line_vel, stiff, contact, offset, attach, plat_pos, pick, dest)


def finish(recv, bound, rows, plats, lines, w_in, fpos):
    sds = jax.ShapeDtypeStruct
    args = (recv, bound, rows, *plats, *lines, w_in)
    at = 3 + len(plats)
    bufs = [vmem_like(a, at <= i < at + 3) for i, a in enumerate(args)]
    out = (
        sds((COUNT, FEATS), BF16),
        sds((COUNT, FEATS), BF16),
        sds((COUNT, w_in.shape[1]), BF16),
        sds((3, LANES), F32),
    )
    return pl.pallas_call(
        finish_kernel,
        out_shape=out + (sds(fpos.shape, F32),),
        in_specs=[HB] * (len(args) + 1),
        out_specs=(VM,) * len(out) + (HB,),
        scratch_shapes=bufs
        + [
            pltpu.VMEM((3 * TAIL, LANES * (STEPS + 1)), F32),
            pltpu.VMEM((3, TAIL, LANES), F32),
            pltpu.SemaphoreType.DMA((len(args),)),
            pltpu.SemaphoreType.DMA,
        ],
        input_output_aliases={len(args): len(out)},
        compiler_params=pltpu.CompilerParams(vmem_limit_bytes=32 * 1024 * 1024),
        cost_estimate=pl.CostEstimate(flops=300000000, bytes_accessed=4000000, transcendentals=0),
        name="finish",
    )(*args, fpos)


def exchange(x, axes):
    return lax.all_to_all(x, axes, split_axis=0, concat_axis=0, tiled=True)


def spread(x, axes):
    return exchange(jnp.broadcast_to(x[None], (lax.axis_size(axes),) + x.shape), axes)


def dot(left, right):
    return jnp.dot(left, right, preferred_element_type=F32)


def tn(left, right):
    return lax.dot_general(left, right, (((0,), (0,)), ((), ())), preferred_element_type=F32)


def swap(x):
    return lax.ppermute(x, "core", SWAP)


def body(
    line_pos, line_vel, stiffness, contact, offset, attach, plat_pos, plat_vel, inv_mass, restoring,
    kernel, vel_hist, wave, sample_pick, sample_dest, w_in, gain, w_gate, w_up, w_down, w_out,
):
    chips = lax.axis_size(CHIP)
    groups = lax.axis_size(GRP)
    half = chips * COUNT
    width = w_gate.shape[1]
    stiff, att, pick, dest = stiffness[None], attach[None], sample_pick[None], sample_dest.reshape(1, -1)
    pay, rows, bound, fpos = evolve(
        line_pos, line_vel, stiff, contact, offset, att, plat_pos, pick, dest
    )
    other = swap(pay)
    pay = jnp.concatenate(
        [pay[:CODE_ROW] + other[:CODE_ROW], pay[CODE_ROW : CODE_ROW + 1], other[CODE_ROW : CODE_ROW + 1], pay[CODE_ROW + 2 :]],
        axis=0,
    )
    recv = spread(pay, CHIP)
    scaled = (w_in.astype(F32) * gain).astype(BF16)
    gate_w = dot(scaled, w_gate).astype(BF16)
    up_w = dot(scaled, w_up).astype(BF16)
    down_w = dot(w_down, w_out).astype(BF16)
    gate_w = jnp.concatenate([gate_w, swap(gate_w)], axis=1)
    up_w = jnp.concatenate([up_w, swap(up_w)], axis=1)
    down_w = jnp.concatenate([down_w, swap(down_w)], axis=0)
    turned = lambda a: a.transpose(1, 0, 2)
    x_own, target, hidden, final_plat, final_pos = finish(
        recv, bound, rows,
        (plat_pos, plat_vel, inv_mass, restoring, turned(kernel), turned(vel_hist), turned(wave)),
        (line_pos, line_vel, contact, stiff, offset, att, pick),
        w_in, fpos,
    )
    x = spread(x_own, CHIP).reshape(half, FEATS)
    base = lax.optimization_barrier(dot(hidden, w_out) - target.astype(F32))
    gate = dot(x, gate_w)
    upper = dot(x, up_w)
    sigma = jax.nn.sigmoid(gate)
    act = (gate * sigma * upper).astype(BF16)
    part = dot(act, down_w).astype(BF16)
    parts = exchange(part.reshape(chips, COUNT, FEATS), CHIP)
    err = (base + jnp.sum(parts.astype(F32), axis=0)).astype(BF16)
    err_mine = spread(err, CHIP).reshape(half, FEATS)
    dpred = (err_mine.astype(F32) / 64.0).astype(BF16)
    dact = nt(dpred, down_w)
    dgate = (dact * upper * sigma * (1.0 + gate * (1.0 - sigma))).astype(BF16)
    dup = (dact * gate * sigma).astype(BF16)
    theirs = swap(tn(x, jnp.concatenate([dgate[:, width:], dup[:, width:]], axis=1)).astype(BF16))
    mine = tn(x, jnp.concatenate([dgate[:, :width], dup[:, :width]], axis=1))
    feat_grads = (mine + theirs.astype(F32)).astype(BF16)
    feat_grads = exchange(feat_grads.reshape(groups, FEATS // groups, 2 * width), GRP)
    feat_grads = jnp.sum(feat_grads.astype(F32), axis=0).astype(BF16)
    feat_grads = spread(feat_grads, GRP).reshape(FEATS, 2 * width)
    at = lax.axis_index(GRP)
    block = w_in.shape[1] // groups
    w_in_own = lax.dynamic_slice_in_dim(w_in, at * block, block, 1)
    gain_own = lax.dynamic_slice_in_dim(gain, at * block, block, 0)[:, None]
    grad_gate = gain_own * tn(w_in_own, feat_grads[:, :width])
    grad_up = gain_own * tn(w_in_own, feat_grads[:, width:])
    err_all = jnp.concatenate([err_mine, swap(err_mine)], axis=0)
    codes = recv[:, CODE_ROW : CODE_ROW + 2, :COUNT].transpose(1, 0, 2).reshape(1, 2 * half)
    core = lax.axis_index("core")
    me = lax.axis_index(CHIP) * 2 + core
    number = jnp.arange(2 * half, dtype=jnp.int32)
    source = ((number // COUNT) % chips) * 2 + (number // half + core) % 2
    slot = jnp.arange(2 * chips * CAP, dtype=jnp.int32)[:, None]
    match = (source[None] == slot // CAP) & (codes == (me * CAP + slot % CAP).astype(F32))
    slot_error = dot(match.astype(BF16), err_all).astype(BF16)
    return (final_pos, final_plat, slot_error, grad_gate, grad_up)


def solution(mesh):
    sizes = (4, 2, 2, 4, 2)
    if mesh.devices.shape[0] == 1:
        sizes = (1, 1, 2, 4, 2)
    fine = Mesh(mesh.devices.reshape(sizes), ALL)
    in_specs = (
        P(None, None, ALL),
        P(None, None, ALL),
        P(ALL),
        P(None, None, ALL),
        P(None, ALL),
        P(ALL),
        P(None, GRP),
        P(None, GRP),
        P(None, GRP),
        P(None, GRP),
        P(None, None, GRP),
        P(None, None, GRP),
        P(None, None, GRP),
        P(ALL),
        P(ALL, None),
        P(),
        P(),
        P(None, DEV),
        P(None, DEV),
        P(DEV, None),
        P(),
    )
    out_specs = (
        P(None, None, ALL),
        P(None, GRP),
        P(ALL, None),
        P(GRP, DEV),
        P(GRP, DEV),
    )
    return jax.shard_map(body, mesh=fine, in_specs=in_specs, out_specs=out_specs, check_vma=False)
```

time: 201 us -> 192 us (0.955)
  waiting for transfers between devices: 83.1 us -> 43.5 us
  matrix products: 27.4 us -> 42.2 us
  blocking collectives: 30.9 us -> 45.6 us
  Pallas kernels: 6.07 us -> 9.15 us
  local copies, waits for them, and re-layouts: 27.8 us -> 25.4 us
    all_to_all x3 -> x4, waiting for transfers between devices: 78.2 us -> 39.1 us  [exchange(): return lax.all_to_all(x, axes, split_axis=0, concat_axis=0, tiled=True)]
    all_to_all x2, blocking collectives: 30.9 us -> 45.6 us  [exchange(): return lax.all_to_all(x, axes, split_axis=0, concat_axis=0, tiled=True)]
    dot_general x8 -> x12, matrix products: 25.7 us -> 38.3 us  [the longest x8 29.1 us: dot(): return jnp.dot(left, right, preferred_element_type=F32)]
    unnamed x92 -> x74, local copies, waits for them, and re-layouts: 24.8 us -> 20.6 us
    pallas_call x1, Pallas kernels: 3.26 us -> 5.88 us  [evolve(): pl.pallas_call(evolve_kernel, out_shape=(sds((ROWS, LANES), F32), sds((2...]
    dot_general x1, matrix products: 1.68 us -> 3.96 us  [nt(): lax.dot_general(left, right, (((1,), (1,)), ((), ())), precision=precisio...]
    broadcast_in_dim x3 -> x4, local copies, waits for them, and re-layouts: 0.97 us -> 3.08 us  [spread(): jnp.broadcast_to(x[None], (lax.axis_size(axes),) + x.shape)]
    all_to_all x3 -> x4, starting transfers between devices: 17.6 us -> 18.5 us  [exchange(): return lax.all_to_all(x, axes, split_axis=0, concat_axis=0, tiled=True)]
  transfers between devices with their start and end apart: 6 -> 10, of which waited for: 6 -> 6; matrix products, arithmetic and copies ran while one was open for 4% -> 15% of each run, Pallas kernels for 0% -> 2%
where the time goes in v1:
time: 192 us; the launch traced here: 190 us
  blocking collectives  45.6 us (24%)
  waiting for transfers between devices  43.5 us (23%)
  matrix products  42.2 us (22%)
  local copies, waits for them, and re-layouts  25.4 us (13%)
  starting transfers between devices  19.2 us (10%)
  Pallas kernels  9.15 us (5%)
  other arithmetic  4.08 us (2%)
    all_to_all x2, blocking collectives, exchange(): return lax.all_to_all(x, axes, split_axis=0, concat_axis=0, tiled=True)  45.6 us
    all_to_all x4, waiting for transfers between devices, exchange(): return lax.all_to_all(x, axes, split_axis=0, concat_axis=0, tiled=True)  39.1 us
    dot_general x8, matrix products, dot(): return jnp.dot(left, right, preferred_element_type=F32)  29.1 us
    unnamed x74, local copies, waits for them, and re-layouts  20.6 us
    all_to_all x4, starting transfers between devices, exchange(): return lax.all_to_all(x, axes, split_axis=0, concat_axis=0, tiled=True)  18.5 us
    dot_general x4, matrix products, tn(): lax.dot_general(left, right, (((0,), (0,)), ((), ())), preferred_element_...  9.19 us
    pallas_call x1, Pallas kernels, evolve(): pl.pallas_call(evolve_kernel, out_shape=(sds((ROWS, LANES), F32), sds((2...  5.88 us
    ppermute x6, waiting for transfers between devices, swap(): return lax.ppermute(x, 'core', SWAP)  4.38 us
  transfers between devices with their start and end apart: 10, of which 6 were waited for; matrix products, arithmetic and copies ran while one was open for 15% of the time, Pallas kernels for 2%

profile of v1, /device:TPU:0, one launch (start us, length us, event | category | flops | bytes accessed | tf_op | source)
XLA Modules:
  0.0 190.2 jit_solution(10251666406960108959)
XLA Ops:
  0.7 1.4 copy-done.1
  2.0 1.0 copy-done.4
  3.0 1.0 copy-done.6
  4.0 0.7 copy-done.19
  4.7 0.7 copy-done.21
  5.4 0.7 copy-done.26
  6.0 0.7 copy-done.28
  6.7 0.7 copy-done.30
  7.4 0.7 copy-done.32
  8.0 5.9 %evolve.1 = (f32[72,128]{1,0:T(8,128)S(1)}, bf16[128,768]{1,0:T(8,128)(2,1)S(1)}, f32[24,128]{1,0:T(8,128)S(1)}, f32[3,256,128]{2,1,0:T(8,128)}) custom-call(f32[3,256,128]{2,1,0:T(8,128)S(1)} %copy-done.4, f32[3,256,128]{2,1,0:T(8,128)S(1)} %copy-done.6, f32[1,128]{1,0:T(1,128)S(1)} %bitcast.27, s32[8,256,128]{2,1,0:T(8,128)S(1)} %copy-done.1, ...), custom_call_target="tpu_custom_call" | custom-call | flops 260000000 | bytes 3000000 | tf_op jit(solution)/shard_map/evolve/pallas_call | solution.py:235
  13.9 0.1 collective-permute-start
  14.0 5.3 %fusion.15 = bf16[768,512]{0,1:T(8,128)(2,1)} fusion(bf16[2048,512]{1,0:T(8,128)(2,1)} %param.39, bf16[768,2048]{1,0:T(8,128)(2,1)} %w_in_ref.1, f32[2048]{0:T(1024)} %param.37), kind=kOutput, calls=%fused_computation.25 | convolution fusion | flops 1615724544 | bytes 6037504 | tf_op jit(solution)/shard_map/dot_general | solution.py:296
  19.3 0.5 collective-permute-start.2
  19.9 0.7 broadcast_in_dim.17
  20.6 5.7 %all-to-all-start = ((f32[8,72,128]{2,1,0:T(8,128)}), f32[8,72,128]{2,1,0:T(8,128)}, u32[]{:S(2)}, u32[]{:S(2)}) async-start(f32[8,72,128]{2,1,0:T(8,128)} %broadcast_in_dim.17), calls=%async_computation | async-start | bytes 589824 | tf_op jit(solution)/shard_map/all_to_all | solution.py:288
  26.4 5.3 %fusion.14 = bf16[768,512]{0,1:T(8,128)(2,1)} fusion(bf16[2048,512]{1,0:T(8,128)(2,1)} %param.38, bf16[768,2048]{1,0:T(8,128)(2,1)} %w_in_ref.1, f32[2048]{0:T(1024)} %param.37), kind=kOutput, calls=%fused_computation.24 | convolution fusion | flops 1615724544 | bytes 6037504 | tf_op jit(solution)/shard_map/dot_general | solution.py:296
  31.7 2.6 %all-to-all-done.recv_ref = f32[8,72,128]{2,1,0:T(8,128)} async-done(((f32[8,72,128]{2,1,0:T(8,128)}), f32[8,72,128]{2,1,0:T(8,128)}, u32[]{:S(2)}, u32[]{:S(2)}) %all-to-all-start) | async-done | bytes 294944 | tf_op jit(solution)/shard_map/all_to_all | solution.py:288
  34.3 1.2 copy-done.2
  35.5 1.9 copy-done.3
  37.4 1.0 copy-done.7
  38.4 0.9 copy-done.11
  39.3 0.7 copy-done.15
  40.0 0.7 copy-done.16
  40.7 0.7 copy-done.18
  41.4 0.7 copy-done.22
  42.1 0.7 copy-done.23
  42.8 0.7 copy-done.24
  43.5 0.7 copy-done.25
  44.2 0.7 copy-done.27
  44.8 0.7 copy-done.29
  45.5 0.7 copy-done.31
  46.1 3.3 %finish.1 = (bf16[64,768]{1,0:T(8,128)(2,1)S(1)}, bf16[64,768]{1,0:T(8,128)(2,1)S(1)}, bf16[64,2048]{1,0:T(8,128)(2,1)S(1)}, f32[3,128]{1,0:T(4,128)}, f32[3,256,128]{2,1,0:T(8,128)}) custom-call(f32[8,72,128]{2,1,0:T(8,128)} %all-to-all-done.recv_ref, f32[24,128]{1,0:T(8,128)S(1)} %copy-done.18, ...), custom_call_target="tpu_custom_call", output_to_operand_aliasing={{4}: (18, {})} | custom-call | flops 300000000 | bytes 4000000 | tf_op jit(solution)/shard_map/finish/pallas_call | solution.py:268
  49.4 0.7 copy-done.8
  50.1 0.6 copy-done.12
  50.8 0.9 broadcast_in_dim.18
  51.7 4.2 %all-to-all-start.1 = ((bf16[8,64,768]{2,1,0:T(8,128)(2,1)}), bf16[8,64,768]{2,1,0:T(8,128)(2,1)}, u32[]{:S(2)}, u32[]{:S(2)}) async-start(bf16[8,64,768]{2,1,0:T(8,128)(2,1)} %broadcast_in_dim.18), calls=%async_computation.1 | async-start | bytes 1572864 | tf_op jit(solution)/shard_map/all_to_all | solution.py:288
  55.9 4.3 %convolution_convert_fusion.1 = bf16[512,768]{1,0:T(8,128)(2,1)} fusion(bf16[512,2048]{1,0:T(8,128)(2,1)} %param.40, bf16[2048,768]{1,0:T(8,128)(2,1)S(1)} %copy-done), kind=kOutput, calls=%fused_computation.26 | convolution fusion | flops 1611005952 | bytes 6029312 | tf_op jit(solution)/shard_map/dot_general | solution.py:296
  60.2 8.7 %all-to-all-done.1 = bf16[8,64,768]{2,1,0:T(8,128)(2,1)} async-done(((bf16[8,64,768]{2,1,0:T(8,128)(2,1)}), bf16[8,64,768]{2,1,0:T(8,128)(2,1)}, u32[]{:S(2)}, u32[]{:S(2)}) %all-to-all-start.1) | async-done | bytes 786464 | tf_op jit(solution)/shard_map/all_to_all | solution.py:288
  68.9 2.6 %fusion.6 = f32[512,1024]{1,0:T(8,128)S(1)} fusion(bf16[512,768]{1,0:T(8,128)(2,1)} %bitcast.8, bf16[768,512]{0,1:T(8,128)(2,1)} %collective-permute-done.2, bf16[768,512]{0,1:T(8,128)(2,1)} %fusion.15), kind=kOutput, calls=%fused_computation.13 | convolution fusion | flops 808452096 | bytes 4456448 | tf_op jit(solution)/shard_map/dot_general | solution.py:296
  71.5 3.4 %fusion.2 = f32[512,1024]{1,0:T(8,128)S(1)} fusion(bf16[512,768]{1,0:T(8,128)(2,1)} %bitcast.8, bf16[768,512]{0,1:T(8,128)(2,1)} %collective-permute-done.1, bf16[768,512]{0,1:T(8,128)(2,1)} %fusion.14), kind=kOutput, calls=%fused_computation.9 | convolution fusion | flops 808452096 | bytes 4456448 | tf_op jit(solution)/shard_map/dot_general | solution.py:296
  75.0 4.4 %convolution_convert_fusion.2 = bf16[512,768]{1,0:T(8,128)(2,1)} fusion(f32[512,1024]{1,0:T(8,128)S(1)} %fusion.6, f32[512,1024]{1,0:T(8,128)S(1)} %fusion.2, bf16[512,768]{1,0:T(8,128)(2,1)} %collective-permute-done.3, bf16[512,768]{1,0:T(8,128)(2,1)} %convolution_convert_fusion.1), kind=kOutput, calls=%fused_computation.27 | convolution fusion | flops 811991040 | bytes 6553600 | tf_op jit(solution)/shard_map/dot_general | solution.py:296
  79.4 4.2 %all-to-all-start.2 = ((bf16[8,64,768]{2,1,0:T(8,128)(2,1)}), bf16[8,64,768]{2,1,0:T(8,128)(2,1)}, u32[]{:S(2)}, u32[]{:S(2)}) async-start(bf16[8,64,768]{2,1,0:T(8,128)(2,1)} %bitcast.38), calls=%async_computation.2 | async-start | bytes 1572864 | tf_op jit(solution)/shard_map/all_to_all | solution.py:288
  83.6 1.3 convolution_subtract_fusion
  84.9 11.7 %all-to-all-done.2 = bf16[8,64,768]{2,1,0:T(8,128)(2,1)} async-done(((bf16[8,64,768]{2,1,0:T(8,128)(2,1)}), bf16[8,64,768]{2,1,0:T(8,128)(2,1)}, u32[]{:S(2)}, u32[]{:S(2)}) %all-to-all-start.2) | async-done | bytes 786464 | tf_op jit(solution)/shard_map/all_to_all | solution.py:288
  96.6 1.4 convert_reduce_fusion
  98.0 1.0 add_convert_fusion.1
  99.0 15.4 %all_to_all.30 = bf16[8,64,768]{2,1,0:T(8,128)(2,1)S(1)} all-to-all(bf16[8,64,768]{2,1,0:T(8,128)(2,1)S(1)} %broadcast_in_dim.19), channel_id=1, replica_groups=mesh['y'=4,'zh'=2,'zl'=2,'x'=4,'core'=2] {'zl','x'}, dimensions={0} | all-to-all | bytes 1572864 | tf_op jit(solution)/shard_map/all_to_all | solution.py:288
  114.5 4.0 %multiply_convert_fusion.4 = (bf16[512,1024]{1,0:T(8,128)(2,1)S(1)}, bf16[512,1024]{1,0:T(8,128)(2,1)S(1)}) fusion(f32[512,1024]{1,0:T(8,128)} %copy-done.36, f32[512,1024]{1,0:T(8,128)S(1)} %copy-done.35, bf16[512,768]{1,0:T(8,128)(2,1)} %collective-permute-done.3, bf16[512,768]{1,0:T(8,128)(2,1)} %convolution_convert_fusion.1, ...), kind=kOutput, calls=%fused_computation.5 | convolution fusion | flops 816447488 | bytes 8650752 | tf_op jit(solution)/shard_map/dot_general | solution.py:31
  118.5 0.2 fusion.64
  118.6 2.1 %convolution_convert_fusion = bf16[768,1024]{1,0:T(8,128)(2,1)S(1)} fusion(bf16[512,768]{1,0:T(8,128)(2,1)} %bitcast.8, bf16[512,512]{1,0:T(8,128)(2,1)S(1)} %get-tuple-element.31, bf16[512,512]{1,0:T(8,128)(2,1)S(1)} %get-tuple-element.26), kind=kOutput, calls=%fused_computation.8 | convolution fusion | flops 808189952 | bytes 3407872 | tf_op jit(solution)/shard_map/dot_general | solution.py:300
  120.9 3.4 %collective-permute-done.5 = bf16[768,1024]{1,0:T(8,128)(2,1)S(1)} collective-permute-done((bf16[768,1024]{1,0:T(8,128)(2,1)S(1)}, bf16[768,1024]{1,0:T(8,128)(2,1)S(1)}, u32[]{:S(2)}, u32[]{:S(2)}) %collective-permute-start.5) | collective-permute-done | bytes 1572896 | tf_op jit(solution)/shard_map/ppermute | solution.py:304
  124.3 2.2 %add_convert_fusion = bf16[768,1024]{1,0:T(8,128)(2,1)S(1)} fusion(bf16[768,1024]{1,0:T(8,128)(2,1)S(1)} %collective-permute-done.5, bf16[512,768]{1,0:T(8,128)(2,1)} %bitcast.8, bf16[512,512]{1,0:T(8,128)(2,1)S(1)} %get-tuple-element.32, bf16[512,512]{1,0:T(8,128)(2,1)S(1)} %get-tuple-element.25), kind=kOutput, calls=%fused_computation.1 | convolution fusion | flops 809762816 | bytes 4980736 | tf_op jit(solution)/shard_map/dot_general | solution.py:300
  126.4 30.2 %all_to_all.31 = bf16[8,96,1024]{2,1,0:T(8,128)(2,1)} all-to-all(bf16[8,96,1024]{2,1,0:T(8,128)(2,1)S(1)} %bitcast.34), channel_id=1, replica_groups=mesh['y'=4,'zh'=2,'zl'=2,'x'=4,'core'=2] {'y','zh'}, dimensions={0} | all-to-all | bytes 3145728 | tf_op jit(solution)/shard_map/all_to_all | solution.py:288
  156.6 1.7 reduce_sum.22
  158.3 1.3 broadcast_in_dim.20
  159.6 4.3 %all-to-all-start.5 = ((bf16[8,96,1024]{2,1,0:T(8,128)(2,1)}), bf16[8,96,1024]{2,1,0:T(8,128)(2,1)}, u32[]{:S(2)}, u32[]{:S(2)}) async-start(bf16[8,96,1024]{2,1,0:T(8,128)(2,1)} %broadcast_in_dim.20), calls=%async_computation.5 | async-start | bytes 3145728 | tf_op jit(solution)/shard_map/all_to_all | solution.py:288
  164.0 0.1 collective-permute-start.4
  164.1 0.8 dynamic_slice.6
  164.9 0.8 slice_bitcast_fusion
  165.7 1.0 collective-permute-done.4
  166.7 2.5 %fusion.16 = bf16[128,768]{1,0:T(8,128)(2,1)} fusion(bf16[512,768]{1,0:T(8,128)(2,1)} %collective-permute-done.4, bf16[512,768]{1,0:T(8,128)(2,1)} %bitcast.37, f32[1024]{0:T(1024)S(1)} %eq.36, s32[1024]{0:T(1024)S(1)} %fusion.43, f32[128]{0:T(128)S(1)} %get-tuple-element.30, s32[128]{0:T(128)S(1)} %get-tuple-element.29), kind=kOutput, calls=%fused_computation.30 | convolution fusion | flops 204963840 | bytes 1778688 | tf_op jit(solution)/shard_map/dot_general | solution.py:296
  169.1 16.2 %all-to-all-done.5 = bf16[8,96,1024]{2,1,0:T(8,128)(2,1)} async-done(((bf16[8,96,1024]{2,1,0:T(8,128)(2,1)}), bf16[8,96,1024]{2,1,0:T(8,128)(2,1)}, u32[]{:S(2)}, u32[]{:S(2)}) %all-to-all-start.5) | async-done | bytes 1572896 | tf_op jit(solution)/shard_map/all_to_all | solution.py:288
  185.3 2.4 %convolution_multiply_fusion = f32[256,512]{1,0:T(8,128)} fusion(bf16[768,1024]{1,0:T(8,128)(2,1)} %bitcast.12, bf16[768,2048]{1,0:T(8,128)(2,1)} %w_in_ref.1, s32[]{:T(128)S(6)} %select_n.66, f32[256]{0:T(256)S(1)} %dynamic_slice.6), kind=kOutput, calls=%fused_computation.28 | convolution fusion | flops 201457664 | bytes 1704964 | tf_op jit(solution)/shard_map/dot_general | solution.py:300
  187.8 2.4 %convolution_multiply_fusion.1 = f32[256,512]{1,0:T(8,128)} fusion(bf16[768,1024]{1,0:T(8,128)(2,1)} %bitcast.12, bf16[768,2048]{1,0:T(8,128)(2,1)} %w_in_ref.1, s32[]{:T(128)S(6)} %select_n.66, f32[256]{0:T(256)S(1)} %dynamic_slice.6), kind=kOutput, calls=%fused_computation.29 | convolution fusion | flops 201457664 | bytes 1704964 | tf_op jit(solution)/shard_map/dot_general | solution.py:300
  (66 shorter events, 0.4 us)
Async XLA Ops:
  0.6 55.3 %copy-start = (bf16[2048,768]{1,0:T(8,128)(2,1)S(1)}, bf16[2048,768]{1,0:T(8,128)(2,1)}, u32[]{:S(2)}) copy-start(bf16[2048,768]{1,0:T(8,128)(2,1)} %param.41) | copy-start | bytes 9437188
  0.6 1.4 copy-start.1
  2.0 1.0 copy-start.4
  3.0 1.0 copy-start.6
  4.0 0.7 copy-start.19
  4.7 0.7 copy-start.21
  5.4 0.7 copy-start.26
  6.0 0.7 copy-start.28
  6.7 0.7 copy-start.30
  7.3 0.7 copy-start.32
  13.9 5.4 %copy-start.10 = (bf16[128,768]{1,0:T(8,128)(2,1)}, bf16[128,768]{1,0:T(8,128)(2,1)S(1)}, u32[]{:S(2)}) copy-start(bf16[128,768]{1,0:T(8,128)(2,1)S(1)} %get-tuple-element.16.rows_ref) | copy-start | bytes 589828
  13.9 5.4 %copy-start.17 = (f32[24,128]{1,0:T(8,128)}, f32[24,128]{1,0:T(8,128)S(1)}, u32[]{:S(2)}) copy-start(f32[24,128]{1,0:T(8,128)S(1)} %get-tuple-element.15.bound_ref) | copy-start | bytes 36868
  13.9 5.9 %collective-permute-start = (f32[72,128]{1,0:T(8,128)S(1)}, f32[72,128]{1,0:T(8,128)S(1)}, u32[]{:S(2)}, u32[]{:S(2)}) collective-permute-start(f32[72,128]{1,0:T(8,128)S(1)} %get-tuple-element.14), channel_id=1, source_target_pairs={{0,1},{1,0},{2,3},{3,2},{4,5},{5,4},{6,7},{7,6},{8,9},{9,8},{10,11... | collective-permute-start | bytes 110600 | tf_op jit(solution)/shard_map/ppermute | solution.py:304
  19.3 40.9 %collective-permute-start.2 = (bf16[768,512]{0,1:T(8,128)(2,1)}, bf16[768,512]{0,1:T(8,128)(2,1)}, u32[]{:S(2)}, u32[]{:S(2)}) collective-permute-start(bf16[768,512]{0,1:T(8,128)(2,1)} %fusion.15), channel_id=1, source_target_pairs={{0,1},{1,0},{2,3},{3,2},{4,5},{5,4},{6,7},{7,6},{8,9},{9,8},{10,11... | collective-permute-start | bytes 2359304 | tf_op jit(solution)/shard_map/ppermute | solution.py:304
  20.6 13.7 %all-to-all-start = ((f32[8,72,128]{2,1,0:T(8,128)}), f32[8,72,128]{2,1,0:T(8,128)}, u32[]{:S(2)}, u32[]{:S(2)}) async-start(f32[8,72,128]{2,1,0:T(8,128)} %broadcast_in_dim.17), calls=%async_computation | async-start | bytes 589824 | tf_op jit(solution)/shard_map/all_to_all | solution.py:288
  26.3 7.9 %copy-start.5 = (f32[3,256,128]{2,1,0:T(8,128)S(1)}, f32[3,256,128]{2,1,0:T(8,128)}, u32[]{:S(2)}) copy-start(f32[3,256,128]{2,1,0:T(8,128)} %pos_ref.3) | copy-start | bytes 1179652
  26.3 7.9 %copy-start.14 = (f32[8,3,128]{2,0,1:T(8,128)S(1)}, f32[8,3,128]{2,0,1:T(8,128)}, u32[]{:S(2)}) copy-start(f32[8,3,128]{2,0,1:T(8,128)} %param.31) | copy-start | bytes 36868
  26.4 7.9 %copy-start.20 = (f32[3,128]{1,0:T(4,128)S(1)}, f32[3,128]{1,0:T(4,128)}, u32[]{:S(2)}) copy-start(f32[3,128]{1,0:T(4,128)} %off_ref.3) | copy-start | bytes 4612
  31.7 39.8 %collective-permute-start.1 = (bf16[768,512]{0,1:T(8,128)(2,1)}, bf16[768,512]{0,1:T(8,128)(2,1)}, u32[]{:S(2)}, u32[]{:S(2)}) collective-permute-start(bf16[768,512]{0,1:T(8,128)(2,1)} %fusion.14), channel_id=1, source_target_pairs={{0,1},{1,0},{2,3},{3,2},{4,5},{5,4},{6,7},{7,6},{8,9},{9,8},{10,11... | collective-permute-start | bytes 2359304 | tf_op jit(solution)/shard_map/ppermute | solution.py:304
  34.3 1.2 copy-start.2
  35.5 1.9 copy-start.3
  37.4 1.0 copy-start.7
  38.4 0.9 copy-start.11
  39.3 0.7 copy-start.15
  40.0 0.7 copy-start.16
  40.7 0.7 copy-start.18
  41.4 0.7 copy-start.22
  42.1 0.7 copy-start.23
  42.8 0.7 copy-start.24
  43.5 0.7 copy-start.25
  44.2 0.7 copy-start.27
  44.8 0.7 copy-start.29
  45.5 0.7 copy-start.31
  49.4 0.7 copy-start.8
  50.1 0.6 copy-start.12
  51.7 17.2 %all-to-all-start.1 = ((bf16[8,64,768]{2,1,0:T(8,128)(2,1)}), bf16[8,64,768]{2,1,0:T(8,128)(2,1)}, u32[]{:S(2)}, u32[]{:S(2)}) async-start(bf16[8,64,768]{2,1,0:T(8,128)(2,1)} %broadcast_in_dim.18), calls=%async_computation.1 | async-start | bytes 1572864 | tf_op jit(solution)/shard_map/all_to_all | solution.py:288
  60.2 14.7 %collective-permute-start.3 = (bf16[512,768]{1,0:T(8,128)(2,1)}, bf16[512,768]{1,0:T(8,128)(2,1)}, u32[]{:S(2)}, u32[]{:S(2)}) collective-permute-start(bf16[512,768]{1,0:T(8,128)(2,1)} %convolution_convert_fusion.1), channel_id=1, source_target_pairs={{0,1},{1,0},{2,3},{3,2},{4,5},{5,4},{6,7},{7,6},{8,9},{9,8},{10,11... | collective-permute-start | bytes 2359304 | tf_op jit(solution)/shard_map/ppermute | solution.py:304
  71.5 3.4 %copy-start.34 = (f32[512,1024]{1,0:T(8,128)}, f32[512,1024]{1,0:T(8,128)S(1)}, u32[]{:S(2)}) copy-start(f32[512,1024]{1,0:T(8,128)S(1)} %fusion.6) | copy-start | bytes 6291460
  74.9 4.4 %copy-start.36 = (f32[512,1024]{1,0:T(8,128)}, f32[512,1024]{1,0:T(8,128)S(1)}, u32[]{:S(2)}) copy-start(f32[512,1024]{1,0:T(8,128)S(1)} %fusion.2) | copy-start | bytes 6291460
  74.9 8.7 %copy-start.9 = (bf16[64,2048]{1,0:T(8,128)(2,1)S(1)}, bf16[64,2048]{1,0:T(8,128)(2,1)}, u32[]{:S(2)}) copy-start(bf16[64,2048]{1,0:T(8,128)(2,1)} %copy-done.8) | copy-start | bytes 786436
  74.9 8.7 %copy-start.13 = (bf16[64,768]{1,0:T(8,128)(2,1)S(1)}, bf16[64,768]{1,0:T(8,128)(2,1)}, u32[]{:S(2)}) copy-start(bf16[64,768]{1,0:T(8,128)(2,1)} %copy-done.12) | copy-start | bytes 294916
  79.4 17.3 %all-to-all-start.2 = ((bf16[8,64,768]{2,1,0:T(8,128)(2,1)}), bf16[8,64,768]{2,1,0:T(8,128)(2,1)}, u32[]{:S(2)}, u32[]{:S(2)}) async-start(bf16[8,64,768]{2,1,0:T(8,128)(2,1)} %bitcast.38), calls=%async_computation.2 | async-start | bytes 1572864 | tf_op jit(solution)/shard_map/all_to_all | solution.py:288
  96.6 17.9 %copy-start.35 = (f32[512,1024]{1,0:T(8,128)S(1)}, f32[512,1024]{1,0:T(8,128)}, u32[]{:S(2)}) copy-start(f32[512,1024]{1,0:T(8,128)} %copy-done.34) | copy-start | bytes 6291460
  114.5 4.0 %copy-start.33 = (bf16[8,64,768]{2,1,0:T(8,128)(2,1)}, bf16[8,64,768]{2,1,0:T(8,128)(2,1)S(1)}, u32[]{:S(2)}) copy-start(bf16[8,64,768]{2,1,0:T(8,128)(2,1)S(1)} %all_to_all.30) | copy-start | bytes 2359300
  120.8 3.5 %collective-permute-start.5 = (bf16[768,1024]{1,0:T(8,128)(2,1)S(1)}, bf16[768,1024]{1,0:T(8,128)(2,1)S(1)}, u32[]{:S(2)}, u32[]{:S(2)}) collective-permute-start(bf16[768,1024]{1,0:T(8,128)(2,1)S(1)} %convolution_convert_fusion), channel_id=1, source_target_pairs={{0,1},{1,0},{2,3},{3,2},{4,5},{5,4},{6,7},{7,6},{8,9},{9,8},{10,11... | collective-permute-start | bytes 4718600 | tf_op jit(solution)/shard_map/ppermute | solution.py:304
  159.6 25.7 %all-to-all-start.5 = ((bf16[8,96,1024]{2,1,0:T(8,128)(2,1)}), bf16[8,96,1024]{2,1,0:T(8,128)(2,1)}, u32[]{:S(2)}, u32[]{:S(2)}) async-start(bf16[8,96,1024]{2,1,0:T(8,128)(2,1)} %broadcast_in_dim.20), calls=%async_computation.5 | async-start | bytes 3145728 | tf_op jit(solution)/shard_map/all_to_all | solution.py:288
  164.0 2.7 %collective-permute-start.4 = (bf16[512,768]{1,0:T(8,128)(2,1)}, bf16[512,768]{1,0:T(8,128)(2,1)}, u32[]{:S(2)}, u32[]{:S(2)}) collective-permute-start(bf16[512,768]{1,0:T(8,128)(2,1)} %bitcast.36), channel_id=1, source_target_pairs={{0,1},{1,0},{2,3},{3,2},{4,5},{5,4},{6,7},{7,6},{8,9},{9,8},{10,11... | collective-permute-start | bytes 2359304 | tf_op jit(solution)/shard_map/ppermute | solution.py:304

commit v2 on v1

--- a/solution.py
+++ b/solution.py
@@ -16,6 +16,7 @@
 ROWS = 72
 ONES_ROW = 24
 CODE_ROW = 67
+LIMIT = 60 * 1024 * 1024
 HIGH = lax.Precision.HIGHEST
 F32 = jnp.float32
 BF16 = jnp.bfloat16
@@ -129,7 +130,7 @@
     dest_col = jnp.sum(jnp.where(lane == sub, dest, 0.0), axis=1, keepdims=True)
     rank = jnp.sum(jnp.where((dest_col == dest) & (sub < lane), 1.0, 0.0), axis=0, keepdims=True)
     codes = jnp.concatenate([dest * CAP + rank, jnp.full((1, LANES - count), -1.0, F32)], axis=1)
-    pay_ref[...] = jnp.where(iota((ROWS, LANES), 0) == CODE_ROW, codes, sums)
+    pay_ref[...] = jnp.where(iota((ROWS, LANES), 0) == CODE_ROW + lax.axis_index("core"), codes, sums)
 
 
 def finish_kernel(
@@ -208,15 +209,83 @@
     where = (at // TAIL) * NODES + (NODES - TAIL) + at % TAIL
     place = (iota((3 * TAIL, FEATS), 1) == where).astype(F32).astype(BF16)
     rows = rowsb[...].astype(F32) + jnp.dot(picked, place, preferred_element_type=F32)
-    count = x_ref.shape[0]
+    count = t_ref.shape[0]
     t_ref[...] = rows[count:].astype(BF16)
     copies[-1].wait()
     hidden = jnp.dot(rows[:count].astype(BF16), w_inb[...], preferred_element_type=F32).astype(BF16)
     h_ref[...] = hidden
     wide = hidden.astype(F32)
     scale = lax.rsqrt(jnp.mean(wide * wide, axis=1, keepdims=True) + 1e-06)
-    x_ref[...] = (rows[:count] * scale).astype(BF16)
+    scaled = (rows[:count] * scale).astype(BF16)
+    for d in range(x_ref.shape[0]):
+        x_ref[d] = scaled
     copy.wait()
+
+
+def forward_kernel(
+    x_ref, g0_ref, u0_ref, d0_ref, g1_ref, u1_ref, d1_ref, part_ref, a_ref, b_ref,
+    xb, g0b, u0b, d0b, g1b, u1b, d1b, sem,
+):
+    copies = fetch(
+        (x_ref, g0_ref, u0_ref, d0_ref, g1_ref, u1_ref, d1_ref), (xb, g0b, u0b, d0b, g1b, u1b, d1b), sem
+    )
+    copies[0].wait()
+    x = xb[...].reshape(-1, xb.shape[-1])
+    part = None
+    for side, (g, u, d) in enumerate(((g0b, u0b, d0b), (g1b, u1b, d1b))):
+        copies[1 + 3 * side].wait()
+        gate = dot(x, g[...])
+        copies[2 + 3 * side].wait()
+        upper = dot(x, u[...])
+        sigma = jax.nn.sigmoid(gate)
+        silu = gate * sigma
+        a_ref[side] = (upper * sigma * (1.0 + gate * (1.0 - sigma))).astype(BF16)
+        b_ref[side] = silu.astype(BF16)
+        copies[3 + 3 * side].wait()
+        term = dot((silu * upper).astype(BF16), d[...])
+        part = term if part is None else part + term
+    part_ref[...] = part.astype(BF16).reshape(part_ref.shape)
+
+
+def error_kernel(parts_ref, base_ref, err_ref):
+    total = base_ref[...]
+    for d in range(parts_ref.shape[0]):
+        total = total + parts_ref[d].astype(F32)
+    total = total.astype(BF16)
+    for d in range(err_ref.shape[0]):
+        err_ref[d] = total
+
+
+def backward_kernel(side, err_ref, d_ref, a_ref, b_ref, xt_ref, y_ref, errb, db, ab, bb, xtb, sem):
+    copies = fetch((err_ref, d_ref, a_ref.at[side], b_ref.at[side], xt_ref), (errb, db, ab, bb, xtb), sem)
+    copies[0].wait()
+    dpred = (errb[...].astype(F32) / 64.0).astype(BF16).reshape(-1, errb.shape[-1])
+    copies[1].wait()
+    dact = nt(dpred, db[...])
+    copies[2].wait()
+    dgate = (dact * ab[...].astype(F32)).astype(BF16)
+    copies[3].wait()
+    dup = (dact * bb[...].astype(F32)).astype(BF16)
+    copies[4].wait()
+    width = dgate.shape[1]
+    y_ref[:, :width] = dot(xtb[...], dgate).astype(y_ref.dtype)
+    y_ref[:, width:] = dot(xtb[...], dup).astype(y_ref.dtype)
+
+
+def sum_kernel(parts_ref, out_ref):
+    total = parts_ref[0].astype(F32)
+    for d in range(1, parts_ref.shape[0]):
+        total = total + parts_ref[d].astype(F32)
+    total = total.astype(BF16)
+    for d in range(out_ref.shape[0]):
+        out_ref[d] = total
+
+
+def last_kernel(y_ref, w_ref, gate_ref, up_ref):
+    width = gate_ref.shape[1]
+    y = y_ref[...].reshape(w_ref.shape[1], 2 * width)
+    gate_ref[...] = dot(w_ref[...], y[:, :width])
+    up_ref[...] = dot(w_ref[...], y[:, width:])
 
 
 VM = pl.BlockSpec(memory_space=pltpu.VMEM)
@@ -248,7 +317,7 @@
             pltpu.VMEM((ROWS, LANES), F32),
             pltpu.SemaphoreType.DMA((2, 2 + STEPS)),
         ],
-        compiler_params=pltpu.CompilerParams(vmem_limit_bytes=32 * 1024 * 1024),
+        compiler_params=pltpu.CompilerParams(vmem_limit_bytes=LIMIT),
         cost_estimate=pl.CostEstimate(flops=260000000, bytes_accessed=3000000, transcendentals=0),
         name="evolve",
     )(line_pos, line_vel, stiff, contact, offset, attach, plat_pos, pick, dest)
@@ -260,7 +329,7 @@
     at = 3 + len(plats)
     bufs = [vmem_like(a, at <= i < at + 3) for i, a in enumerate(args)]
     out = (
-        sds((COUNT, FEATS), BF16),
+        sds((recv.shape[0], COUNT, FEATS), BF16),
         sds((COUNT, FEATS), BF16),
         sds((COUNT, w_in.shape[1]), BF16),
         sds((3, LANES), F32),
@@ -278,36 +347,73 @@
             pltpu.SemaphoreType.DMA,
         ],
         input_output_aliases={len(args): len(out)},
-        compiler_params=pltpu.CompilerParams(vmem_limit_bytes=32 * 1024 * 1024),
+        compiler_params=pltpu.CompilerParams(vmem_limit_bytes=LIMIT),
         cost_estimate=pl.CostEstimate(flops=300000000, bytes_accessed=4000000, transcendentals=0),
         name="finish",
     )(*args, fpos)
 
 
+def forward(x, weights):
+    sds = jax.ShapeDtypeStruct
+    args = (x, *weights)
+    rows, width = x.shape[0] * x.shape[1], weights[0].shape[1]
+    return pl.pallas_call(
+        forward_kernel,
+        out_shape=(sds(x.shape, BF16), sds((2, rows, width), BF16), sds((2, rows, width), BF16)),
+        in_specs=[HB] * len(args),
+        out_specs=(VM,) * 3,
+        scratch_shapes=[vmem_like(a) for a in args] + [pltpu.SemaphoreType.DMA((len(args),))],
+        compiler_params=pltpu.CompilerParams(vmem_limit_bytes=LIMIT),
+        cost_estimate=pl.CostEstimate(flops=2400000000, bytes_accessed=9000000, transcendentals=500000),
+        name="forward",
+    )(*args)
+
+
+def backward(side, err, down, a, b, xt, kind):
+    args = (err, down, a, b, xt)
+    bufs = [vmem_like(v) for v in (err, down)] + [pltpu.VMEM(a.shape[1:], BF16)] * 2 + [vmem_like(xt)]
+    return pl.pallas_call(
+        functools.partial(backward_kernel, side),
+        out_shape=jax.ShapeDtypeStruct((xt.shape[0], 2 * a.shape[2]), kind),
+        in_specs=[HB] * len(args),
+        out_specs=VM,
+        scratch_shapes=bufs + [pltpu.SemaphoreType.DMA((len(args),))],
+        compiler_params=pltpu.CompilerParams(vmem_limit_bytes=LIMIT),
+        cost_estimate=pl.CostEstimate(flops=1200000000, bytes_accessed=6000000, transcendentals=0),
+        name="backward",
+    )(*args)
+
+
+def simple(kernel, name, out_shape, *args):
+    return pl.pallas_call(
+        kernel,
+        out_shape=out_shape,
+        compiler_params=pltpu.CompilerParams(vmem_limit_bytes=LIMIT),
+        name=name,
+    )(*args)
+
+
 def exchange(x, axes):
     return lax.all_to_all(x, axes, split_axis=0, concat_axis=0, tiled=True)
 
 
-def spread(x, axes):
-    return exchange(jnp.broadcast_to(x[None], (lax.axis_size(axes),) + x.shape), axes)
-
-
 def dot(left, right):
     return jnp.dot(left, right, preferred_element_type=F32)
 
 
-def tn(left, right):
-    return lax.dot_general(left, right, (((0,), (0,)), ((), ())), preferred_element_type=F32)
-
-
 def swap(x):
     return lax.ppermute(x, "core", SWAP)
+
+
+def after(x, *others):
+    return lax.optimization_barrier((x,) + others)[0]
 
 
 def body(
     line_pos, line_vel, stiffness, contact, offset, attach, plat_pos, plat_vel, inv_mass, restoring,
     kernel, vel_hist, wave, sample_pick, sample_dest, w_in, gain, w_gate, w_up, w_down, w_out,
 ):
+    sds = jax.ShapeDtypeStruct
     chips = lax.axis_size(CHIP)
     groups = lax.axis_size(GRP)
     half = chips * COUNT
@@ -316,19 +422,14 @@
     pay, rows, bound, fpos = evolve(
         line_pos, line_vel, stiff, contact, offset, att, plat_pos, pick, dest
     )
-    other = swap(pay)
-    pay = jnp.concatenate(
-        [pay[:CODE_ROW] + other[:CODE_ROW], pay[CODE_ROW : CODE_ROW + 1], other[CODE_ROW : CODE_ROW + 1], pay[CODE_ROW + 2 :]],
-        axis=0,
-    )
-    recv = spread(pay, CHIP)
-    scaled = (w_in.astype(F32) * gain).astype(BF16)
+    pay = jnp.broadcast_to((pay + swap(pay))[None], (chips,) + pay.shape)
+    pay, w_in_late, w_down_late = lax.optimization_barrier((pay, w_in, w_down))
+    recv = exchange(pay, CHIP)
+    scaled = lax.optimization_barrier((w_in_late.astype(F32) * gain).astype(BF16))
     gate_w = dot(scaled, w_gate).astype(BF16)
+    gate_o = swap(gate_w)
     up_w = dot(scaled, w_up).astype(BF16)
-    down_w = dot(w_down, w_out).astype(BF16)
-    gate_w = jnp.concatenate([gate_w, swap(gate_w)], axis=1)
-    up_w = jnp.concatenate([up_w, swap(up_w)], axis=1)
-    down_w = jnp.concatenate([down_w, swap(down_w)], axis=0)
+    up_o = swap(up_w)
     turned = lambda a: a.transpose(1, 0, 2)
     x_own, target, hidden, final_plat, final_pos = finish(
         recv, bound, rows,
@@ -336,35 +437,35 @@
         (line_pos, line_vel, contact, stiff, offset, att, pick),
         w_in, fpos,
     )
-    x = spread(x_own, CHIP).reshape(half, FEATS)
+    x_own, w_down_late = lax.optimization_barrier((x_own, w_down_late))
+    x = exchange(x_own, CHIP)
+    down_w = dot(w_down_late, w_out).astype(BF16)
+    down_o = swap(down_w)
+    part, slope_a, slope_b = forward(x, (gate_w, up_w, down_w, gate_o, up_o, down_o))
+    part, hidden, x_late, scaled_late = lax.optimization_barrier((part, hidden, x, scaled))
+    parts = exchange(part, CHIP)
     base = lax.optimization_barrier(dot(hidden, w_out) - target.astype(F32))
-    gate = dot(x, gate_w)
-    upper = dot(x, up_w)
-    sigma = jax.nn.sigmoid(gate)
-    act = (gate * sigma * upper).astype(BF16)
-    part = dot(act, down_w).astype(BF16)
-    parts = exchange(part.reshape(chips, COUNT, FEATS), CHIP)
-    err = (base + jnp.sum(parts.astype(F32), axis=0)).astype(BF16)
-    err_mine = spread(err, CHIP).reshape(half, FEATS)
-    dpred = (err_mine.astype(F32) / 64.0).astype(BF16)
-    dact = nt(dpred, down_w)
-    dgate = (dact * upper * sigma * (1.0 + gate * (1.0 - sigma))).astype(BF16)
-    dup = (dact * gate * sigma).astype(BF16)
-    theirs = swap(tn(x, jnp.concatenate([dgate[:, width:], dup[:, width:]], axis=1)).astype(BF16))
-    mine = tn(x, jnp.concatenate([dgate[:, :width], dup[:, :width]], axis=1))
+    xt = lax.optimization_barrier(x_late.reshape(half, FEATS).T)
+    at = lax.axis_index(GRP)
+    block = w_in.shape[1] // groups
+    w_own = lax.optimization_barrier(lax.dynamic_slice_in_dim(scaled_late, at * block, block, 1).T)
+    err_own = simple(error_kernel, "error", sds((chips, COUNT, FEATS), BF16), parts, base)
+    err = exchange(err_own, CHIP)
+    theirs = swap(backward(1, err, down_o, slope_a, slope_b, xt, BF16))
+    mine = backward(0, err, down_w, slope_a, slope_b, xt, F32)
     feat_grads = (mine + theirs.astype(F32)).astype(BF16)
     feat_grads = exchange(feat_grads.reshape(groups, FEATS // groups, 2 * width), GRP)
-    feat_grads = jnp.sum(feat_grads.astype(F32), axis=0).astype(BF16)
-    feat_grads = spread(feat_grads, GRP).reshape(FEATS, 2 * width)
-    at = lax.axis_index(GRP)
-    block = w_in.shape[1] // groups
-    w_in_own = lax.dynamic_slice_in_dim(w_in, at * block, block, 1)
-    gain_own = lax.dynamic_slice_in_dim(gain, at * block, block, 0)[:, None]
-    grad_gate = gain_own * tn(w_in_own, feat_grads[:, :width])
-    grad_up = gain_own * tn(w_in_own, feat_grads[:, width:])
-    err_all = jnp.concatenate([err_mine, swap(err_mine)], axis=0)
-    codes = recv[:, CODE_ROW : CODE_ROW + 2, :COUNT].transpose(1, 0, 2).reshape(1, 2 * half)
+    feat_grads = simple(sum_kernel, "total", sds(feat_grads.shape, BF16), feat_grads)
+    feat_grads, err_late = lax.optimization_barrier((feat_grads, err))
+    feat_grads = exchange(feat_grads, GRP)
+    grad_gate, grad_up = simple(
+        last_kernel, "last", (sds((block, width), F32), sds((block, width), F32)), feat_grads, w_own
+    )
+    err_late = err_late.reshape(half, FEATS)
+    err_all = jnp.concatenate([err_late, swap(err_late)], axis=0)
     core = lax.axis_index("core")
+    codes = recv[:, CODE_ROW : CODE_ROW + 2, :COUNT]
+    codes = jnp.where(core == 0, codes, codes[:, ::-1]).transpose(1, 0, 2).reshape(1, 2 * half)
     me = lax.axis_index(CHIP) * 2 + core
     number = jnp.arange(2 * half, dtype=jnp.int32)
     source = ((number // COUNT) % chips) * 2 + (number // half + core) % 2

time: 192 us -> 178 us (0.927)
  matrix products: 42.2 us -> 13.5 us
  Pallas kernels: 9.15 us -> 33.5 us
  blocking collectives: 45.6 us -> 30.5 us
  local copies, waits for them, and re-layouts: 25.4 us -> 11.1 us
  waiting for transfers between devices: 43.5 us -> 55 us
  starting transfers between devices: 19.2 us -> 25 us
  other arithmetic: 4.08 us -> 7.1 us
    pallas_call x0 -> x6, Pallas kernels: none -> 23.9 us  [the longest x2 9.45 us: backward(): pl.pallas_call(functools.partial(backward_kernel, side), out_shape=jax.Sh...]
    unnamed x74 -> x16, local copies, waits for them, and re-layouts: 20.6 us -> 0.76 us
    dot_general x8 -> x5, matrix products: 29.1 us -> 13.5 us  [dot(): return jnp.dot(left, right, preferred_element_type=F32)]
    all_to_all x2 -> x1, blocking collectives: 45.6 us -> 30.5 us  [exchange(): return lax.all_to_all(x, axes, split_axis=0, concat_axis=0, tiled=True)]
    all_to_all x4 -> x5, waiting for transfers between devices: 39.1 us -> 53.6 us  [exchange(): return lax.all_to_all(x, axes, split_axis=0, concat_axis=0, tiled=True)]
    dot_general x5 -> x0, matrix products: 13.1 us -> none  [the longest x4 9.19 us: tn(): lax.dot_general(left, right, (((0,), (0,)), ((), ())), preferred_element_...]
    all_to_all x4 -> x5, starting transfers between devices: 18.5 us -> 24.2 us  [exchange(): return lax.all_to_all(x, axes, split_axis=0, concat_axis=0, tiled=True)]
    optimization_barrier x0 -> x1, local copies, waits for them, and re-layouts: none -> 4.67 us  [body(): pay, w_in_late, w_down_late = lax.optimization_barrier((pay, w_in, w_down))]
  transfers between devices with their start and end apart: 10 -> 11, of which waited for: 6 -> 5; matrix products, arithmetic and copies ran while one was open for 15% -> 15% of each run, Pallas kernels for 2% -> 5%
where the time goes in v2:
time: 178 us; the launch traced here: 177 us
  waiting for transfers between devices  55 us (31%)
  Pallas kernels  33.5 us (19%)
  blocking collectives  30.5 us (17%)
  starting transfers between devices  25 us (14%)
  matrix products  13.5 us (8%)
  local copies, waits for them, and re-layouts  11.1 us (6%)
  other arithmetic  7.1 us (4%)
    all_to_all x5, waiting for transfers between devices, exchange(): return lax.all_to_all(x, axes, split_axis=0, concat_axis=0, tiled=True)  53.6 us
    all_to_all x1, blocking collectives, exchange(): return lax.all_to_all(x, axes, split_axis=0, concat_axis=0, tiled=True)  30.5 us
    all_to_all x5, starting transfers between devices, exchange(): return lax.all_to_all(x, axes, split_axis=0, concat_axis=0, tiled=True)  24.2 us
    dot_general x5, matrix products, dot(): return jnp.dot(left, right, preferred_element_type=F32)  13.5 us
    pallas_call x2, Pallas kernels, backward(): pl.pallas_call(functools.partial(backward_kernel, side), out_shape=jax.Sh...  9.45 us
    pallas_call x3, Pallas kernels, simple(): pl.pallas_call(kernel, out_shape=out_shape, compiler_params=pltpu.Compile...  7.79 us
    pallas_call x1, Pallas kernels, forward(): pl.pallas_call(forward_kernel, out_shape=(sds(x.shape, BF16), sds((2, row...  6.66 us
    pallas_call x1, Pallas kernels, evolve(): pl.pallas_call(evolve_kernel, out_shape=(sds((ROWS, LANES), F32), sds((2...  5.39 us
  transfers between devices with their start and end apart: 11, of which 5 were waited for; matrix products, arithmetic and copies ran while one was open for 15% of the time, Pallas kernels for 5%

profile of v2, /device:TPU:0, one launch (start us, length us, event | category | flops | bytes accessed | tf_op | source)
XLA Modules:
  0.0 176.5 jit_solution(8973484756332752742)
XLA Ops:
  0.6 0.0 copy-start
  0.6 5.4 %evolve.1 = (f32[72,128]{1,0:T(8,128)}, bf16[128,768]{1,0:T(8,128)(2,1)}, f32[24,128]{1,0:T(8,128)}, f32[3,256,128]{2,1,0:T(8,128)}) custom-call(f32[3,256,128]{2,1,0:T(8,128)} %pos_ref.3, f32[3,256,128]{2,1,0:T(8,128)} %vel_ref.3, f32[1,128]{1,0:T(1,128)} %bitcast.29, s32[8,256,128]{2,1,0:T(8,128)} %contact_ref.3, f32[3,128]{1,0:T(4,128)} %off_ref.3, ...), custom_call_target="tpu_custom_call" | custom-call | flops 260000000 | bytes 3000000 | tf_op jit(solution)/shard_map/evolve/pallas_call | solution.py:304
  6.0 0.1 collective-permute-start
  6.1 1.4 collective-permute-done
  7.5 0.8 add.91
  8.3 0.7 broadcast_in_dim.21
  9.1 5.7 %all-to-all-start = ((f32[8,72,128]{2,1,0:T(8,128)}), f32[8,72,128]{2,1,0:T(8,128)S(1)}, u32[]{:S(2)}, u32[]{:S(2)}) async-start(f32[8,72,128]{2,1,0:T(8,128)} %broadcast_in_dim.21), calls=%async_computation | async-start | bytes 589824 | tf_op jit(solution)/shard_map/all_to_all | solution.py:397
  14.8 0.0 copy-start.7
  14.8 4.7 %copy.30 = bf16[768,2048]{0,1:T(8,128)(2,1)} copy(bf16[768,2048]{1,0:T(8,128)(2,1)} %w_in_ref.1) | data formatting | bytes 6291456 | tf_op jit(solution)/shard_map/optimization_barrier | solution.py:426
  19.5 0.0 copy-done.7
  19.5 0.0 copy-start.2
  19.5 2.6 %multiply_convert_fusion = bf16[768,2048]{0,1:T(8,128)(2,1)S(1)} fusion(bf16[768,2048]{0,1:T(8,128)(2,1)} %copy.30, f32[2048]{0:T(1024)S(1)} %copy-done.7), kind=kLoop, calls=%fused_computation | loop fusion | flops 4718592 | bytes 6299648 | tf_op jit(solution)/shard_map/convert_element_type | solution.py:428
  22.1 0.0 copy-done.2
  22.1 0.0 copy-start.1
  22.1 0.0 copy-start.3
  22.1 2.7 %convolution_convert_fusion.1.u0_ref = bf16[768,512]{1,0:T(8,128)(2,1)} fusion(bf16[768,2048]{0,1:T(8,128)(2,1)S(1)} %multiply_convert_fusion, bf16[2048,512]{1,0:T(8,128)(2,1)S(1)} %copy-done.2), kind=kOutput, calls=%fused_computation.7 | convolution fusion | flops 1611005952 | bytes 6029312 | tf_op jit(solution)/shard_map/dot_general | solution.py:401
  24.8 0.0 copy-done.3
  24.8 2.7 %convolution_convert_fusion.2.g0_ref = bf16[768,512]{1,0:T(8,128)(2,1)} fusion(bf16[768,2048]{0,1:T(8,128)(2,1)S(1)} %multiply_convert_fusion, bf16[2048,512]{1,0:T(8,128)(2,1)S(1)} %copy-done.3), kind=kOutput, calls=%fused_computation.8 | convolution fusion | flops 1611005952 | bytes 6029312 | tf_op jit(solution)/shard_map/dot_general | solution.py:401
  27.5 0.0 copy-done.1
  27.5 0.0 collective-permute-start.1
  27.5 0.5 collective-permute-start.2
  28.1 0.0 all-to-all-done.recv_ref
  28.1 0.0 copy-start.4
  28.1 0.7 copy-done.4
  28.8 4.2 %finish.1 = (bf16[8,64,768]{2,1,0:T(8,128)(2,1)}, bf16[64,768]{1,0:T(8,128)(2,1)}, bf16[64,2048]{1,0:T(8,128)(2,1)}, f32[3,128]{1,0:T(4,128)}, f32[3,256,128]{2,1,0:T(8,128)}) custom-call(f32[8,72,128]{2,1,0:T(8,128)} %copy-done.4, f32[24,128]{1,0:T(8,128)} %get-tuple-element.32.bound_ref, ...), custom_call_target="tpu_custom_call", output_to_operand_aliasing={{4}: (18, {})} | custom-call | flops 300000000 | bytes 4000000 | tf_op jit(solution)/shard_map/finish/pallas_call | solution.py:337
  33.0 0.0 copy-done
  33.0 4.3 %convolution_convert_fusion.d0_ref.d_ref = bf16[512,768]{1,0:T(8,128)(2,1)} fusion(bf16[512,2048]{1,0:T(8,128)(2,1)} %param.40, bf16[2048,768]{1,0:T(8,128)(2,1)S(1)} %copy-done), kind=kOutput, calls=%fused_computation.6 | convolution fusion | flops 1611005952 | bytes 6029312 | tf_op jit(solution)/shard_map/dot_general | solution.py:401
  37.3 0.0 collective-permute-start.3
  37.3 5.7 %all-to-all-start.1 = ((bf16[8,64,768]{2,1,0:T(8,128)(2,1)}), bf16[8,64,768]{2,1,0:T(8,128)(2,1)}, u32[]{:S(2)}, u32[]{:S(2)}) async-start(bf16[8,64,768]{2,1,0:T(8,128)(2,1)} %get-tuple-element.39), calls=%async_computation.1 | async-start | bytes 1572864 | tf_op jit(solution)/shard_map/all_to_all | solution.py:397
  43.0 0.0 copy-start.5
  43.0 0.0 copy-start.6
  43.0 0.0 collective-permute-done.1.g1_ref
  43.0 0.0 collective-permute-done.2.u1_ref
  43.0 13.6 %all-to-all-done.1.x_ref = bf16[8,64,768]{2,1,0:T(8,128)(2,1)} async-done(((bf16[8,64,768]{2,1,0:T(8,128)(2,1)}), bf16[8,64,768]{2,1,0:T(8,128)(2,1)}, u32[]{:S(2)}, u32[]{:S(2)}) %all-to-all-start.1) | async-done | bytes 786464 | tf_op jit(solution)/shard_map/all_to_all | solution.py:397
  56.6 0.0 collective-permute-done.3.d1_ref.d_ref
  56.7 6.7 %forward.1 = (bf16[8,64,768]{2,1,0:T(8,128)(2,1)}, bf16[2,512,512]{2,1,0:T(8,128)(2,1)}, bf16[2,512,512]{2,1,0:T(8,128)(2,1)}) custom-call(bf16[8,64,768]{2,1,0:T(8,128)(2,1)} %all-to-all-done.1.x_ref, bf16[768,512]{1,0:T(8,128)(2,1)} %convolution_convert_fusion.2.g0_ref, bf16[768,512]{1,0:T(8,128)(2,1)} %convolution_convert_fusion.1.u0_ref, ...), custom_call_target="tpu_custom_call" | custom-call | flops 2400000000 | bytes 9000000 | tf_op jit(solution)/shard_map/forward/pallas_call | solution.py:360
  63.3 4.2 %all-to-all-start.2 = ((bf16[8,64,768]{2,1,0:T(8,128)(2,1)}), bf16[8,64,768]{2,1,0:T(8,128)(2,1)}, u32[]{:S(2)}, u32[]{:S(2)}) async-start(bf16[8,64,768]{2,1,0:T(8,128)(2,1)} %get-tuple-element.44), calls=%async_computation.2 | async-start | bytes 1572864 | tf_op jit(solution)/shard_map/all_to_all | solution.py:397
  67.6 0.0 copy-done.5
  67.6 0.0 copy-done.6
  67.6 1.3 convolution_subtract_fusion.base_ref
  68.9 11.8 %all-to-all-done.2.parts_ref = bf16[8,64,768]{2,1,0:T(8,128)(2,1)} async-done(((bf16[8,64,768]{2,1,0:T(8,128)(2,1)}), bf16[8,64,768]{2,1,0:T(8,128)(2,1)}, u32[]{:S(2)}, u32[]{:S(2)}) %all-to-all-start.2) | async-done | bytes 786464 | tf_op jit(solution)/shard_map/all_to_all | solution.py:397
  80.7 2.2 %error.1 = bf16[8,64,768]{2,1,0:T(8,128)(2,1)} custom-call(bf16[8,64,768]{2,1,0:T(8,128)(2,1)} %all-to-all-done.2.parts_ref, f32[64,768]{1,0:T(8,128)} %convolution_subtract_fusion.base_ref), custom_call_target="tpu_custom_call" | custom-call | tf_op jit(solution)/shard_map/error/pallas_call | solution.py:388
  82.8 4.2 %all-to-all-start.3 = ((bf16[8,64,768]{2,1,0:T(8,128)(2,1)}), bf16[8,64,768]{2,1,0:T(8,128)(2,1)}, u32[]{:S(2)}, u32[]{:S(2)}) async-start(bf16[8,64,768]{2,1,0:T(8,128)(2,1)} %error.1), calls=%async_computation.3 | async-start | bytes 1572864 | tf_op jit(solution)/shard_map/all_to_all | solution.py:397
  87.1 2.3 %copy.31 = bf16[512,768]{0,1:T(8,128)(2,1)} copy(bf16[512,768]{1,0:T(8,128)(2,1)} %bitcast.8) | data formatting | bytes 1572864 | tf_op jit(solution)/shard_map/reshape | solution.py:448
  89.4 10.8 %all-to-all-done.3.err_ref = bf16[8,64,768]{2,1,0:T(8,128)(2,1)} async-done(((bf16[8,64,768]{2,1,0:T(8,128)(2,1)}), bf16[8,64,768]{2,1,0:T(8,128)(2,1)}, u32[]{:S(2)}, u32[]{:S(2)}) %all-to-all-start.3) | async-done | bytes 786464 | tf_op jit(solution)/shard_map/all_to_all | solution.py:397
  100.1 4.5 %backward.3 = bf16[768,1024]{1,0:T(8,128)(2,1)} custom-call(bf16[8,64,768]{2,1,0:T(8,128)(2,1)} %all-to-all-done.3.err_ref, bf16[512,768]{1,0:T(8,128)(2,1)} %collective-permute-done.3.d1_ref.d_ref, bf16[2,512,512]{2,1,0:T(8,128)(2,1)} %get-tuple-element.47.a_ref, bf16[2,512,512]{2,1,0:T(8,128)(2,1)} %get-tuple-element.48.b_ref, bf16[768,512]{1,0:T(8,128)(2,1)} %bitcast.23), custom_call_target="tpu_custom_call" | custom-call | flops 1200000000 | bytes 6000000 | tf_op jit(solution)/shard_map/backward/pallas_call | solution.py:375
  104.6 0.1 collective-permute-start.4
  104.7 5.0 %backward.2 = f32[768,1024]{1,0:T(8,128)} custom-call(bf16[8,64,768]{2,1,0:T(8,128)(2,1)} %all-to-all-done.3.err_ref, bf16[512,768]{1,0:T(8,128)(2,1)} %convolution_convert_fusion.d0_ref.d_ref, bf16[2,512,512]{2,1,0:T(8,128)(2,1)} %get-tuple-element.47.a_ref, bf16[2,512,512]{2,1,0:T(8,128)(2,1)} %get-tuple-element.48.b_ref, bf16[768,512]{1,0:T(8,128)(2,1)} %bitcast.24), custom_call_target="tpu_custom_call" | custom-call | flops 1200000000 | bytes 6000000 | tf_op jit(solution)/shard_map/backward/pallas_call | solution.py:375
  109.7 0.0 collective-permute-done.4
  109.7 2.9 %add_convert_fusion = bf16[768,1024]{1,0:T(8,128)(2,1)S(1)} fusion(f32[768,1024]{1,0:T(8,128)} %backward.2, bf16[768,1024]{1,0:T(8,128)(2,1)} %collective-permute-done.4), kind=kLoop, calls=%fused_computation.1 | loop fusion | flops 2359296 | bytes 6291456 | tf_op jit(solution)/shard_map/convert_element_type | solution.py:456
  112.6 30.5 %all_to_all.30.parts_ref = bf16[8,96,1024]{2,1,0:T(8,128)(2,1)} all-to-all(bf16[8,96,1024]{2,1,0:T(8,128)(2,1)S(1)} %bitcast.25), channel_id=1, replica_groups=mesh['y'=4,'zh'=2,'zl'=2,'x'=4,'core'=2] {'y','zh'}, dimensions={0} | all-to-all | bytes 3145728 | tf_op jit(solution)/shard_map/all_to_all | solution.py:397
  143.2 2.8 %total.1 = bf16[8,96,1024]{2,1,0:T(8,128)(2,1)} custom-call(bf16[8,96,1024]{2,1,0:T(8,128)(2,1)} %all_to_all.30.parts_ref), custom_call_target="tpu_custom_call" | custom-call | tf_op jit(solution)/shard_map/total/pallas_call | solution.py:388
  145.9 4.3 %all-to-all-start.5 = ((bf16[8,96,1024]{2,1,0:T(8,128)(2,1)}), bf16[8,96,1024]{2,1,0:T(8,128)(2,1)}, u32[]{:S(2)}, u32[]{:S(2)}) async-start(bf16[8,96,1024]{2,1,0:T(8,128)(2,1)} %total.1), calls=%async_computation.5 | async-start | bytes 3145728 | tf_op jit(solution)/shard_map/all_to_all | solution.py:397
  150.2 0.1 collective-permute-start.5
  150.4 0.8 slice.4
  151.2 0.8 select_bitcast_fusion
  152.0 0.1 eq.40
  152.0 1.8 dynamic-slice_bitcast_fusion.w_ref
  153.8 0.0 collective-permute-done.5
  153.8 2.5 %fusion.4 = bf16[128,768]{1,0:T(8,128)(2,1)} fusion(bf16[512,768]{1,0:T(8,128)(2,1)} %collective-permute-done.5, bf16[512,768]{1,0:T(8,128)(2,1)} %bitcast.11, f32[1024]{0:T(1024)S(1)} %eq.40, s32[1024]{0:T(1024)S(1)} %fusion.16, f32[128]{0:T(128)S(1)} %get-tuple-element.56, s32[128]{0:T(128)S(1)} %get-tuple-element.55), kind=kOutput, calls=%fused_computation.9 | convolution fusion | flops 204963840 | bytes 1778688 | tf_op jit(solution)/shard_map/dot_general | solution.py:401
  156.3 17.4 %all-to-all-done.5.y_ref = bf16[8,96,1024]{2,1,0:T(8,128)(2,1)} async-done(((bf16[8,96,1024]{2,1,0:T(8,128)(2,1)}), bf16[8,96,1024]{2,1,0:T(8,128)(2,1)}, u32[]{:S(2)}, u32[]{:S(2)}) %all-to-all-start.5) | async-done | bytes 1572896 | tf_op jit(solution)/shard_map/all_to_all | solution.py:397
  173.7 2.8 %last.1 = (f32[256,512]{1,0:T(8,128)}, f32[256,512]{1,0:T(8,128)}) custom-call(bf16[8,96,1024]{2,1,0:T(8,128)(2,1)} %all-to-all-done.5.y_ref, bf16[256,768]{1,0:T(8,128)(2,1)} %dynamic-slice_bitcast_fusion.w_ref), custom_call_target="tpu_custom_call" | custom-call | tf_op jit(solution)/shard_map/last/pallas_call | solution.py:388
  (4 shorter events, 0.1 us)
Async XLA Ops:
  0.6 32.4 %copy-start = (bf16[2048,768]{1,0:T(8,128)(2,1)S(1)}, bf16[2048,768]{1,0:T(8,128)(2,1)}, u32[]{:S(2)}) copy-start(bf16[2048,768]{1,0:T(8,128)(2,1)} %param.41) | copy-start | bytes 9437188
  6.0 1.5 collective-permute-start
  9.1 19.0 %all-to-all-start = ((f32[8,72,128]{2,1,0:T(8,128)}), f32[8,72,128]{2,1,0:T(8,128)S(1)}, u32[]{:S(2)}, u32[]{:S(2)}) async-start(f32[8,72,128]{2,1,0:T(8,128)} %broadcast_in_dim.21), calls=%async_computation | async-start | bytes 589824 | tf_op jit(solution)/shard_map/all_to_all | solution.py:397
  14.8 4.7 %copy-start.7 = (f32[2048]{0:T(1024)S(1)}, f32[2048]{0:T(1024)}, u32[]{:S(2)}) copy-start(f32[2048]{0:T(1024)} %param.37) | copy-start | bytes 24580
  19.5 2.6 %copy-start.2 = (bf16[2048,512]{1,0:T(8,128)(2,1)S(1)}, bf16[2048,512]{1,0:T(8,128)(2,1)}, u32[]{:S(2)}) copy-start(bf16[2048,512]{1,0:T(8,128)(2,1)} %param.39) | copy-start | bytes 6291460
  22.1 5.4 %copy-start.1 = (bf16[768,2048]{0,1:T(8,128)(2,1)}, bf16[768,2048]{0,1:T(8,128)(2,1)S(1)}, u32[]{:S(2)}) copy-start(bf16[768,2048]{0,1:T(8,128)(2,1)S(1)} %multiply_convert_fusion) | copy-start | bytes 9437188
  22.1 2.7 %copy-start.3 = (bf16[2048,512]{1,0:T(8,128)(2,1)S(1)}, bf16[2048,512]{1,0:T(8,128)(2,1)}, u32[]{:S(2)}) copy-start(bf16[2048,512]{1,0:T(8,128)(2,1)} %param.38) | copy-start | bytes 6291460
  27.5 15.5 %collective-permute-start.1 = (bf16[768,512]{1,0:T(8,128)(2,1)}, bf16[768,512]{1,0:T(8,128)(2,1)}, u32[]{:S(2)}, u32[]{:S(2)}) collective-permute-start(bf16[768,512]{1,0:T(8,128)(2,1)} %convolution_convert_fusion.2.g0_ref), channel_id=1, source_target_pairs={{0,1},{1,0},{2,3},{3,2},{4,5},{5,4},{6,7},{7,6},{8,9},{9,8},{10,11... | collective-permute-start | bytes 2359304 | tf_op jit(solution)/shard_map/ppermute | solution.py:405
  27.5 15.5 %collective-permute-start.2 = (bf16[768,512]{1,0:T(8,128)(2,1)}, bf16[768,512]{1,0:T(8,128)(2,1)}, u32[]{:S(2)}, u32[]{:S(2)}) collective-permute-start(bf16[768,512]{1,0:T(8,128)(2,1)} %convolution_convert_fusion.1.u0_ref), channel_id=1, source_target_pairs={{0,1},{1,0},{2,3},{3,2},{4,5},{5,4},{6,7},{7,6},{8,9},{9,8},{10,11... | collective-permute-start | bytes 2359304 | tf_op jit(solution)/shard_map/ppermute | solution.py:405
  28.1 0.7 copy-start.4
  37.3 19.4 %collective-permute-start.3 = (bf16[512,768]{1,0:T(8,128)(2,1)}, bf16[512,768]{1,0:T(8,128)(2,1)}, u32[]{:S(2)}, u32[]{:S(2)}) collective-permute-start(bf16[512,768]{1,0:T(8,128)(2,1)} %convolution_convert_fusion.d0_ref.d_ref), channel_id=1, source_target_pairs={{0,1},{1,0},{2,3},{3,2},{4,5},{5,4},{6,7},{7,6},{8,9},{9,8},{10,11... | collective-permute-start | bytes 2359304 | tf_op jit(solution)/shard_map/ppermute | solution.py:405
  37.3 19.4 %all-to-all-start.1 = ((bf16[8,64,768]{2,1,0:T(8,128)(2,1)}), bf16[8,64,768]{2,1,0:T(8,128)(2,1)}, u32[]{:S(2)}, u32[]{:S(2)}) async-start(bf16[8,64,768]{2,1,0:T(8,128)(2,1)} %get-tuple-element.39), calls=%async_computation.1 | async-start | bytes 1572864 | tf_op jit(solution)/shard_map/all_to_all | solution.py:397
  43.0 24.6 %copy-start.5 = (bf16[64,2048]{1,0:T(8,128)(2,1)S(1)}, bf16[64,2048]{1,0:T(8,128)(2,1)}, u32[]{:S(2)}) copy-start(bf16[64,2048]{1,0:T(8,128)(2,1)} %get-tuple-element.45) | copy-start | bytes 786436
  43.0 24.6 %copy-start.6 = (bf16[64,768]{1,0:T(8,128)(2,1)S(1)}, bf16[64,768]{1,0:T(8,128)(2,1)}, u32[]{:S(2)}) copy-start(bf16[64,768]{1,0:T(8,128)(2,1)} %get-tuple-element.46) | copy-start | bytes 294916
  63.3 17.4 %all-to-all-start.2 = ((bf16[8,64,768]{2,1,0:T(8,128)(2,1)}), bf16[8,64,768]{2,1,0:T(8,128)(2,1)}, u32[]{:S(2)}, u32[]{:S(2)}) async-start(bf16[8,64,768]{2,1,0:T(8,128)(2,1)} %get-tuple-element.44), calls=%async_computation.2 | async-start | bytes 1572864 | tf_op jit(solution)/shard_map/all_to_all | solution.py:397
  82.8 17.3 %all-to-all-start.3 = ((bf16[8,64,768]{2,1,0:T(8,128)(2,1)}), bf16[8,64,768]{2,1,0:T(8,128)(2,1)}, u32[]{:S(2)}, u32[]{:S(2)}) async-start(bf16[8,64,768]{2,1,0:T(8,128)(2,1)} %error.1), calls=%async_computation.3 | async-start | bytes 1572864 | tf_op jit(solution)/shard_map/all_to_all | solution.py:397
  104.6 5.1 %collective-permute-start.4 = (bf16[768,1024]{1,0:T(8,128)(2,1)}, bf16[768,1024]{1,0:T(8,128)(2,1)}, u32[]{:S(2)}, u32[]{:S(2)}) collective-permute-start(bf16[768,1024]{1,0:T(8,128)(2,1)} %backward.3), channel_id=1, source_target_pairs={{0,1},{1,0},{2,3},{3,2},{4,5},{5,4},{6,7},{7,6},{8,9},{9,8},{10,11... | collective-permute-start | bytes 4718600 | tf_op jit(solution)/shard_map/ppermute | solution.py:405
  145.9 27.7 %all-to-all-start.5 = ((bf16[8,96,1024]{2,1,0:T(8,128)(2,1)}), bf16[8,96,1024]{2,1,0:T(8,128)(2,1)}, u32[]{:S(2)}, u32[]{:S(2)}) async-start(bf16[8,96,1024]{2,1,0:T(8,128)(2,1)} %total.1), calls=%async_computation.5 | async-start | bytes 3145728 | tf_op jit(solution)/shard_map/all_to_all | solution.py:397
  150.2 3.5 %collective-permute-start.5 = (bf16[512,768]{1,0:T(8,128)(2,1)}, bf16[512,768]{1,0:T(8,128)(2,1)}, u32[]{:S(2)}, u32[]{:S(2)}) collective-permute-start(bf16[512,768]{1,0:T(8,128)(2,1)} %bitcast.11), channel_id=1, source_target_pairs={{0,1},{1,0},{2,3},{3,2},{4,5},{5,4},{6,7},{7,6},{8,9},{9,8},{10,11... | collective-permute-start | bytes 2359304 | tf_op jit(solution)/shard_map/ppermute | solution.py:405

commit v3 on v2

--- a/solution.py
+++ b/solution.py
@@ -222,29 +222,66 @@
     copy.wait()
 
 
+def products_kernel(w_in_ref, gain_ref, gate_ref, up_ref, g_ref, u_ref, w_inb, gainb, gateb, upb, scaled, sem):
+    copies = fetch((gain_ref, w_in_ref, gate_ref, up_ref), (gainb, w_inb, gateb, upb), sem)
+    copies[0].wait()
+    copies[1].wait()
+    rows = 256
+    for i in range(w_inb.shape[0] // rows):
+        at = pl.ds(i * rows, rows)
+        scaled[at] = (w_inb[at].astype(F32) * gainb[...]).astype(BF16)
+        if i == 0:
+            copies[2].wait()
+        g_ref[at] = dot(scaled[at], gateb[...]).astype(BF16)
+        if i == 0:
+            copies[3].wait()
+        u_ref[at] = dot(scaled[at], upb[...]).astype(BF16)
+
+
+def down_kernel(w0_ref, w1_ref, out_ref, d0_ref, d1_ref, w0b, w1b, outb, sem):
+    copies = fetch((w0_ref, out_ref, w1_ref), (w0b, outb, w1b), sem)
+    copies[0].wait()
+    copies[1].wait()
+    d0_ref[...] = dot(w0b[...], outb[...]).astype(BF16)
+    copies[2].wait()
+    d1_ref[...] = dot(w1b[...], outb[...]).astype(BF16)
+
+
 def forward_kernel(
-    x_ref, g0_ref, u0_ref, d0_ref, g1_ref, u1_ref, d1_ref, part_ref, a_ref, b_ref,
-    xb, g0b, u0b, d0b, g1b, u1b, d1b, sem,
+    x_ref, g0_ref, u0_ref, d0_ref, g1_ref, u1_ref, d1_ref, part_ref, gate_ref, up_ref,
+    xb, g0b, u0b, d0b, g1b, u1b, d1b, gateb, upb, sem, out_sem,
 ):
     copies = fetch(
         (x_ref, g0_ref, u0_ref, d0_ref, g1_ref, u1_ref, d1_ref), (xb, g0b, u0b, d0b, g1b, u1b, d1b), sem
     )
     copies[0].wait()
     x = xb[...].reshape(-1, xb.shape[-1])
-    part = None
+    part, outs = None, []
     for side, (g, u, d) in enumerate(((g0b, u0b, d0b), (g1b, u1b, d1b))):
         copies[1 + 3 * side].wait()
         gate = dot(x, g[...])
+        gateb[side] = gate
         copies[2 + 3 * side].wait()
         upper = dot(x, u[...])
-        sigma = jax.nn.sigmoid(gate)
-        silu = gate * sigma
-        a_ref[side] = (upper * sigma * (1.0 + gate * (1.0 - sigma))).astype(BF16)
-        b_ref[side] = silu.astype(BF16)
+        upb[side] = upper
+        for i, (buf, ref) in enumerate(((gateb, gate_ref), (upb, up_ref))):
+            out = pltpu.make_async_copy(buf.at[side], ref.at[side], out_sem.at[2 * side + i])
+            out.start()
+            outs.append(out)
+        act = (gate * jax.nn.sigmoid(gate) * upper).astype(BF16)
         copies[3 + 3 * side].wait()
-        term = dot((silu * upper).astype(BF16), d[...])
+        term = dot(act, d[...])
         part = term if part is None else part + term
     part_ref[...] = part.astype(BF16).reshape(part_ref.shape)
+    for out in outs:
+        out.wait()
+
+
+def slopes_kernel(gate_ref, up_ref, a_ref, b_ref):
+    gate, upper = gate_ref[...], up_ref[...]
+    sigma = jax.nn.sigmoid(gate)
+    a_ref[...] = (upper * sigma * (1.0 + gate * (1.0 - sigma))).astype(BF16)
+    b_ref[...] = (gate * sigma).astype(BF16)
 
 
 def error_kernel(parts_ref, base_ref, err_ref):
@@ -256,20 +293,33 @@
         err_ref[d] = total
 
 
-def backward_kernel(side, err_ref, d_ref, a_ref, b_ref, xt_ref, y_ref, errb, db, ab, bb, xtb, sem):
-    copies = fetch((err_ref, d_ref, a_ref.at[side], b_ref.at[side], xt_ref), (errb, db, ab, bb, xtb), sem)
-    copies[0].wait()
-    dpred = (errb[...].astype(F32) / 64.0).astype(BF16).reshape(-1, errb.shape[-1])
-    copies[1].wait()
-    dact = nt(dpred, db[...])
-    copies[2].wait()
-    dgate = (dact * ab[...].astype(F32)).astype(BF16)
-    copies[3].wait()
-    dup = (dact * bb[...].astype(F32)).astype(BF16)
-    copies[4].wait()
-    width = dgate.shape[1]
-    y_ref[:, :width] = dot(xtb[...], dgate).astype(y_ref.dtype)
-    y_ref[:, width:] = dot(xtb[...], dup).astype(y_ref.dtype)
+def backward_kernel(
+    e0_ref, e1_ref, d_ref, a0_ref, b0_ref, a1_ref, b1_ref, x0_ref, x1_ref, y_ref,
+    e0b, e1b, db, a0b, b0b, a1b, b1b, x0b, x1b, grads, sem,
+):
+    copies = fetch(
+        (e0_ref, d_ref, a0_ref.at[0], b0_ref.at[0], e1_ref, a1_ref, b1_ref, x0_ref, x1_ref),
+        (e0b, db, a0b, b0b, e1b, a1b, b1b, x0b, x1b),
+        sem,
+    )
+    width = a0b.shape[1]
+    order = ((e0b, a0b, b0b, 0), (e1b, a1b, b1b, 4))
+    for side, (eb, ab, bb, first) in enumerate(order):
+        for i in range(3 if side else 4):
+            copies[first + i].wait()
+        dpred = (eb[...].astype(F32) / 64.0).astype(BF16).reshape(-1, eb.shape[-1])
+        dact = nt(dpred, db[...])
+        rows = pl.ds(side * dact.shape[0], dact.shape[0])
+        grads[rows, :width] = (dact * ab[...].astype(F32)).astype(BF16)
+        grads[rows, width:] = (dact * bb[...].astype(F32)).astype(BF16)
+    copies[7].wait()
+    copies[8].wait()
+    half = x0b.shape[1]
+    tall = 256
+    for i in range(y_ref.shape[0] // tall):
+        at = pl.ds(i * tall, tall)
+        y = dot(x0b[at], grads[:half]) + dot(x1b[at], grads[half:])
+        y_ref[at] = y.astype(BF16)
 
 
 def sum_kernel(parts_ref, out_ref):
@@ -281,15 +331,16 @@
         out_ref[d] = total
 
 
-def last_kernel(y_ref, w_ref, gate_ref, up_ref):
-    width = gate_ref.shape[1]
-    y = y_ref[...].reshape(w_ref.shape[1], 2 * width)
-    gate_ref[...] = dot(w_ref[...], y[:, :width])
-    up_ref[...] = dot(w_ref[...], y[:, width:])
+def last_kernel(yg_ref, yu_ref, w_ref, gate_ref, up_ref):
+    for y_ref, out_ref in ((yg_ref, gate_ref), (yu_ref, up_ref)):
+        y = y_ref[...].reshape(w_ref.shape[0], out_ref.shape[1])
+        out_ref[...] = lax.dot_general(
+            w_ref[...], y, (((0,), (0,)), ((), ())), preferred_element_type=F32
+        )
 
 
 VM = pl.BlockSpec(memory_space=pltpu.VMEM)
-HB = pl.BlockSpec(memory_space=pltpu.HBM)
+HB = pl.BlockSpec(memory_space=pl.ANY)
 
 
 def vmem_like(a, tail=False):
@@ -353,44 +404,27 @@
     )(*args, fpos)
 
 
-def forward(x, weights):
-    sds = jax.ShapeDtypeStruct
-    args = (x, *weights)
-    rows, width = x.shape[0] * x.shape[1], weights[0].shape[1]
-    return pl.pallas_call(
-        forward_kernel,
-        out_shape=(sds(x.shape, BF16), sds((2, rows, width), BF16), sds((2, rows, width), BF16)),
-        in_specs=[HB] * len(args),
-        out_specs=(VM,) * 3,
-        scratch_shapes=[vmem_like(a) for a in args] + [pltpu.SemaphoreType.DMA((len(args),))],
-        compiler_params=pltpu.CompilerParams(vmem_limit_bytes=LIMIT),
-        cost_estimate=pl.CostEstimate(flops=2400000000, bytes_accessed=9000000, transcendentals=500000),
-        name="forward",
-    )(*args)
-
-
-def backward(side, err, down, a, b, xt, kind):
-    args = (err, down, a, b, xt)
-    bufs = [vmem_like(v) for v in (err, down)] + [pltpu.VMEM(a.shape[1:], BF16)] * 2 + [vmem_like(xt)]
-    return pl.pallas_call(
-        functools.partial(backward_kernel, side),
-        out_shape=jax.ShapeDtypeStruct((xt.shape[0], 2 * a.shape[2]), kind),
-        in_specs=[HB] * len(args),
-        out_specs=VM,
-        scratch_shapes=bufs + [pltpu.SemaphoreType.DMA((len(args),))],
-        compiler_params=pltpu.CompilerParams(vmem_limit_bytes=LIMIT),
-        cost_estimate=pl.CostEstimate(flops=1200000000, bytes_accessed=6000000, transcendentals=0),
-        name="backward",
-    )(*args)
-
-
-def simple(kernel, name, out_shape, *args):
+PARAMS = pltpu.CompilerParams(vmem_limit_bytes=LIMIT)
+SMALL = pltpu.CompilerParams(vmem_limit_bytes=16 * 1024 * 1024)
+
+
+def staged(kernel, name, args, out_shape, scratch, flops, sems, out_specs=VM, bufs=None):
+    bufs = [vmem_like(a) for a in args] if bufs is None else bufs
     return pl.pallas_call(
         kernel,
         out_shape=out_shape,
-        compiler_params=pltpu.CompilerParams(vmem_limit_bytes=LIMIT),
+        in_specs=[HB] * len(args),
+        out_specs=out_specs,
+        scratch_shapes=bufs + scratch + [pltpu.SemaphoreType.DMA((n,)) for n in sems],
+        compiler_params=PARAMS,
+        cost_estimate=pl.CostEstimate(flops=flops, bytes_accessed=8000000, transcendentals=0),
         name=name,
     )(*args)
+
+
+def cut(shape, parts, offset=0):
+    block = shape[:-1] + (shape[-1] // parts,)
+    return pl.BlockSpec(block, lambda i: (0,) * (len(shape) - 1) + (i + offset,))
 
 
 def exchange(x, axes):
@@ -425,11 +459,13 @@
     pay = jnp.broadcast_to((pay + swap(pay))[None], (chips,) + pay.shape)
     pay, w_in_late, w_down_late = lax.optimization_barrier((pay, w_in, w_down))
     recv = exchange(pay, CHIP)
-    scaled = lax.optimization_barrier((w_in_late.astype(F32) * gain).astype(BF16))
-    gate_w = dot(scaled, w_gate).astype(BF16)
-    gate_o = swap(gate_w)
-    up_w = dot(scaled, w_up).astype(BF16)
-    up_o = swap(up_w)
+    product = sds((FEATS, width), BF16)
+    gate_w, up_w = staged(
+        products_kernel, "products", (w_in_late, gain[None], w_gate, w_up), (product, product),
+        [pltpu.VMEM(w_in.shape, BF16)], 3300000000, (4,), (VM,) * 2,
+    )
+    gate_o, up_o = swap(gate_w), swap(up_w)
+    w_down_o = swap(w_down)
     turned = lambda a: a.transpose(1, 0, 2)
     x_own, target, hidden, final_plat, final_pos = finish(
         recv, bound, rows,
@@ -437,32 +473,67 @@
         (line_pos, line_vel, contact, stiff, offset, att, pick),
         w_in, fpos,
     )
-    x_own, w_down_late = lax.optimization_barrier((x_own, w_down_late))
+    x_own, w_down_late, w_down_o, hidden = lax.optimization_barrier((x_own, w_down_late, w_down_o, hidden))
     x = exchange(x_own, CHIP)
-    down_w = dot(w_down_late, w_out).astype(BF16)
-    down_o = swap(down_w)
-    part, slope_a, slope_b = forward(x, (gate_w, up_w, down_w, gate_o, up_o, down_o))
-    part, hidden, x_late, scaled_late = lax.optimization_barrier((part, hidden, x, scaled))
+    product = sds((width, FEATS), BF16)
+    down_w, down_o = staged(
+        down_kernel, "down", (w_down_late, w_down_o, w_out), (product, product), [], 3300000000, (3,), (VM,) * 2
+    )
+    base = lax.optimization_barrier(dot(hidden, w_out) - target.astype(F32))
+    args = (x, gate_w, up_w, down_w, gate_o, up_o, down_o)
+    wide = sds((2, half, width), F32)
+    part, gate, upper = staged(
+        forward_kernel, "forward", args, (sds(x.shape, BF16), wide, wide),
+        [pltpu.VMEM(wide.shape, F32)] * 2, 2500000000, (7, 4), (VM, HB, HB),
+    )
+    part, gate, upper, x_late, w_in_late = lax.optimization_barrier((part, gate, upper, x, w_in_late))
     parts = exchange(part, CHIP)
-    base = lax.optimization_barrier(dot(hidden, w_out) - target.astype(F32))
-    xt = lax.optimization_barrier(x_late.reshape(half, FEATS).T)
+    slope = sds(wide.shape, BF16)
+    rows_of = lambda: pl.BlockSpec((2, half // 4, width), lambda i: (0, i, 0))
+    slope_a, slope_b = pl.pallas_call(
+        slopes_kernel, grid=(4,), out_shape=(slope, slope), in_specs=[rows_of(), rows_of()],
+        out_specs=(rows_of(), rows_of()), compiler_params=PARAMS, name="slopes",
+        cost_estimate=pl.CostEstimate(flops=8000000, bytes_accessed=6000000, transcendentals=1000000),
+    )(gate, upper)
+    slope_ao, slope_bo = swap(slope_a[1]), swap(slope_b[1])
+    x_late = lax.optimization_barrier(x_late.reshape(half, FEATS).T)
+    x_other = swap(x_late)
     at = lax.axis_index(GRP)
     block = w_in.shape[1] // groups
-    w_own = lax.optimization_barrier(lax.dynamic_slice_in_dim(scaled_late, at * block, block, 1).T)
-    err_own = simple(error_kernel, "error", sds((chips, COUNT, FEATS), BF16), parts, base)
+    w_own = lax.optimization_barrier(lax.dynamic_slice_in_dim(w_in_late, at * block, block, 1))
+    gain_own = lax.dynamic_slice_in_dim(gain, at * block, block, 0)
+    w_own = lax.optimization_barrier((w_own.astype(F32) * gain_own).astype(BF16))
+    err_own = pl.pallas_call(
+        error_kernel, grid=(3,), out_shape=sds((chips, COUNT, FEATS), BF16),
+        in_specs=[cut(parts.shape, 3), cut(base.shape, 3)], out_specs=cut(parts.shape, 3),
+        compiler_params=SMALL, name="error",
+    )(parts, base)
+    err_own, slope_ao, slope_bo, x_other = lax.optimization_barrier((err_own, slope_ao, slope_bo, x_other))
     err = exchange(err_own, CHIP)
-    theirs = swap(backward(1, err, down_o, slope_a, slope_b, xt, BF16))
-    mine = backward(0, err, down_w, slope_a, slope_b, xt, F32)
-    feat_grads = (mine + theirs.astype(F32)).astype(BF16)
+    err_other = swap(err)
+    args = (err, err_other, down_w, slope_a, slope_b, slope_ao, slope_bo, x_late, x_other)
+    part_like = pltpu.VMEM((half, width), BF16)
+    bufs = [vmem_like(err)] * 2 + [vmem_like(down_w)] + [part_like] * 4 + [vmem_like(x_late)] * 2
+    feat_grads = staged(
+        backward_kernel, "backward", args, sds((FEATS, 2 * width), BF16),
+        [pltpu.VMEM((2 * half, 2 * width), BF16)], 2500000000, (9,), bufs=bufs,
+    )
     feat_grads = exchange(feat_grads.reshape(groups, FEATS // groups, 2 * width), GRP)
-    feat_grads = simple(sum_kernel, "total", sds(feat_grads.shape, BF16), feat_grads)
-    feat_grads, err_late = lax.optimization_barrier((feat_grads, err))
+    feat_grads = pl.pallas_call(
+        sum_kernel, grid=(4,), out_shape=sds(feat_grads.shape, BF16), in_specs=[cut(feat_grads.shape, 4)],
+        out_specs=cut(feat_grads.shape, 4), compiler_params=SMALL, name="total",
+    )(feat_grads)
+    feat_grads, err_late, err_other = lax.optimization_barrier((feat_grads, err, err_other))
     feat_grads = exchange(feat_grads, GRP)
-    grad_gate, grad_up = simple(
-        last_kernel, "last", (sds((block, width), F32), sds((block, width), F32)), feat_grads, w_own
-    )
-    err_late = err_late.reshape(half, FEATS)
-    err_all = jnp.concatenate([err_late, swap(err_late)], axis=0)
+    grad = sds((block, width), F32)
+    grad_gate, grad_up = pl.pallas_call(
+        last_kernel, grid=(2,), out_shape=(grad, grad),
+        in_specs=[
+            cut(feat_grads.shape, 4), cut(feat_grads.shape, 4, 2), pl.BlockSpec(w_own.shape, lambda i: (0, 0))
+        ],
+        out_specs=(cut(grad.shape, 2),) * 2, compiler_params=SMALL, name="last",
+    )(feat_grads, feat_grads, w_own)
+    err_all = jnp.concatenate([err_late, err_other], axis=0).reshape(2 * half, FEATS)
     core = lax.axis_index("core")
     codes = recv[:, CODE_ROW : CODE_ROW + 2, :COUNT]
     codes = jnp.where(core == 0, codes, codes[:, ::-1]).transpose(1, 0, 2).reshape(1, 2 * half)

time: 178 us -> 157 us (0.88)
  waiting for transfers between devices: 55 us -> 27.5 us
  blocking collectives: 30.5 us -> 46.5 us
  Pallas kernels: 33.5 us -> 45.6 us
  matrix products: 13.5 us -> 3.65 us
  other arithmetic: 7.1 us -> 2.28 us
  starting transfers between devices: 25 us -> 20.3 us
    all_to_all x5 -> x4, waiting for transfers between devices: 53.6 us -> 24.2 us  [exchange(): return lax.all_to_all(x, axes, split_axis=0, concat_axis=0, tiled=True)]
    all_to_all x1 -> x2, blocking collectives: 30.5 us -> 46.5 us  [exchange(): return lax.all_to_all(x, axes, split_axis=0, concat_axis=0, tiled=True)]
    pallas_call x6 -> x8, Pallas kernels: 23.9 us -> 36.2 us  [the longest x4 27.3 us: staged(): pl.pallas_call(kernel, out_shape=out_shape, in_specs=[HB] * len(args), ou...]
    dot_general x5 -> x2, matrix products: 13.5 us -> 3.65 us  [dot(): return jnp.dot(left, right, preferred_element_type=F32)]
    all_to_all x5 -> x4, starting transfers between devices: 24.2 us -> 18.4 us  [exchange(): return lax.all_to_all(x, axes, split_axis=0, concat_axis=0, tiled=True)]
    convert_element_type x2 -> x1, other arithmetic: 5.54 us -> 0.08 us  [body(): (w_own.astype(F32) * gain_own).astype(BF16)]
    optimization_barrier x1 -> x0, local copies, waits for them, and re-layouts: 4.67 us -> none  [body(): pay, w_in_late, w_down_late = lax.optimization_barrier((pay, w_in, w_down))]
    unnamed x16 -> x26, local copies, waits for them, and re-layouts: 0.76 us -> 3.7 us
  transfers between devices with their start and end apart: 11 -> 12, of which waited for: 5 -> 6; matrix products, arithmetic and copies ran while one was open for 15% -> 8% of each run, Pallas kernels for 5% -> 19%
where the time goes in v3:
time: 157 us; the launch traced here: 156 us
  blocking collectives  46.5 us (30%)
  Pallas kernels  45.6 us (29%)
  waiting for transfers between devices  27.5 us (18%)
  starting transfers between devices  20.3 us (13%)
  local copies, waits for them, and re-layouts  9.57 us (6%)
  matrix products  3.65 us (2%)
  other arithmetic  2.28 us (1%)
    all_to_all x2, blocking collectives, exchange(): return lax.all_to_all(x, axes, split_axis=0, concat_axis=0, tiled=True)  46.5 us
    pallas_call x4, Pallas kernels, staged(): pl.pallas_call(kernel, out_shape=out_shape, in_specs=[HB] * len(args), ou...  27.3 us
    all_to_all x4, waiting for transfers between devices, exchange(): return lax.all_to_all(x, axes, split_axis=0, concat_axis=0, tiled=True)  24.2 us
    all_to_all x4, starting transfers between devices, exchange(): return lax.all_to_all(x, axes, split_axis=0, concat_axis=0, tiled=True)  18.4 us
    pallas_call x1, Pallas kernels, evolve(): pl.pallas_call(evolve_kernel, out_shape=(sds((ROWS, LANES), F32), sds((2...  5.24 us
    pallas_call x1, Pallas kernels, body(): pl.pallas_call(slopes_kernel, grid=(4,), out_shape=(slope, slope), in_spe...  4.67 us
    pallas_call x1, Pallas kernels, finish(): pl.pallas_call(finish_kernel, out_shape=out + (sds(fpos.shape, F32),), in...  4.2 us
    unnamed x26, local copies, waits for them, and re-layouts  3.7 us
  transfers between devices with their start and end apart: 12, of which 6 were waited for; matrix products, arithmetic and copies ran while one was open for 8% of the time, Pallas kernels for 19%

profile of v3, /device:TPU:0, one launch (start us, length us, event | category | flops | bytes accessed | tf_op | source)
XLA Modules:
  0.0 156.4 jit_solution(12070945348873166652)
XLA Ops:
  0.6 0.1 collective-permute-start.1
  0.7 5.2 %evolve.1 = (f32[72,128]{1,0:T(8,128)}, bf16[128,768]{1,0:T(8,128)(2,1)}, f32[24,128]{1,0:T(8,128)}, f32[3,256,128]{2,1,0:T(8,128)}) custom-call(f32[3,256,128]{2,1,0:T(8,128)} %pos_ref.3, f32[3,256,128]{2,1,0:T(8,128)} %vel_ref.3, f32[1,128]{1,0:T(1,128)} %bitcast.29, s32[8,256,128]{2,1,0:T(8,128)} %contact_ref.3, f32[3,128]{1,0:T(4,128)} %off_ref.3, ...), custom_call_target="tpu_custom_call" | custom-call | flops 260000000 | bytes 3000000 | tf_op jit(solution)/shard_map/evolve/pallas_call | solution.py:355
  6.0 0.6 collective-permute-start
  6.5 1.1 collective-permute-done
  7.6 0.8 add.89
  8.4 0.7 broadcast_in_dim.24
  9.1 5.7 %all-to-all-start = ((f32[8,72,128]{2,1,0:T(8,128)}), f32[8,72,128]{2,1,0:T(8,128)S(1)}, u32[]{:S(2)}, u32[]{:S(2)}) async-start(f32[8,72,128]{2,1,0:T(8,128)} %broadcast_in_dim.24), calls=%async_computation | async-start | bytes 589824 | tf_op jit(solution)/shard_map/all_to_all | solution.py:431
  14.9 7.1 %products.1 = (bf16[768,512]{1,0:T(8,128)(2,1)}, bf16[768,512]{1,0:T(8,128)(2,1)}) custom-call(bf16[768,2048]{1,0:T(8,128)(2,1)} %w_in_ref.2, f32[1,2048]{1,0:T(1,128)} %bitcast.36, bf16[2048,512]{1,0:T(8,128)(2,1)} %gate_ref.1, bf16[2048,512]{1,0:T(8,128)(2,1)} %up_ref.1), custom_call_target="tpu_custom_call" | custom-call | flops 3300000000 | bytes 8000000 | tf_op jit(solution)/shard_map/products/pallas_call | solution.py:413
  21.9 0.1 collective-permute-start.2
  22.1 0.4 collective-permute-start.3
  22.5 0.5 all-to-all-done.recv_ref
  23.0 0.7 copy-done.4
  23.7 4.2 %finish.1 = (bf16[8,64,768]{2,1,0:T(8,128)(2,1)}, bf16[64,768]{1,0:T(8,128)(2,1)}, bf16[64,2048]{1,0:T(8,128)(2,1)}, f32[3,128]{1,0:T(4,128)}, f32[3,256,128]{2,1,0:T(8,128)}) custom-call(f32[8,72,128]{2,1,0:T(8,128)} %copy-done.4, f32[24,128]{1,0:T(8,128)} %get-tuple-element.46.bound_ref, ...), custom_call_target="tpu_custom_call", output_to_operand_aliasing={{4}: (18, {})} | custom-call | flops 300000000 | bytes 4000000 | tf_op jit(solution)/shard_map/finish/pallas_call | solution.py:388
  27.9 0.0 collective-permute-done.1.w1_ref
  27.9 0.0 copy-start.10
  28.0 5.2 %all-to-all-start.1 = ((bf16[8,64,768]{2,1,0:T(8,128)(2,1)}), bf16[8,64,768]{2,1,0:T(8,128)(2,1)S(1)}, u32[]{:S(2)}, u32[]{:S(2)}) async-start(bf16[8,64,768]{2,1,0:T(8,128)(2,1)} %get-tuple-element.54), calls=%async_computation.1 | async-start | bytes 1572864 | tf_op jit(solution)/shard_map/all_to_all | solution.py:431
  33.2 8.1 %down.1 = (bf16[512,768]{1,0:T(8,128)(2,1)}, bf16[512,768]{1,0:T(8,128)(2,1)}) custom-call(bf16[512,2048]{1,0:T(8,128)(2,1)} %w0_ref, bf16[512,2048]{1,0:T(8,128)(2,1)} %copy-done.10, bf16[2048,768]{1,0:T(8,128)(2,1)} %out_ref.1), custom_call_target="tpu_custom_call" | custom-call | flops 3300000000 | bytes 8000000 | tf_op jit(solution)/shard_map/down/pallas_call | solution.py:413
  41.3 0.0 collective-permute-done.2.g1_ref
  41.3 0.0 collective-permute-done.3.u1_ref
  41.3 5.0 %all-to-all-done.1.x_ref = bf16[8,64,768]{2,1,0:T(8,128)(2,1)S(1)} async-done(((bf16[8,64,768]{2,1,0:T(8,128)(2,1)}), bf16[8,64,768]{2,1,0:T(8,128)(2,1)S(1)}, u32[]{:S(2)}, u32[]{:S(2)}) %all-to-all-start.1) | async-done | bytes 786464 | tf_op jit(solution)/shard_map/all_to_all | solution.py:431
  46.3 0.9 copy-done
  47.2 6.2 %forward.1 = (bf16[8,64,768]{2,1,0:T(8,128)(2,1)}, f32[2,512,512]{2,1,0:T(8,128)}, f32[2,512,512]{2,1,0:T(8,128)}) custom-call(bf16[8,64,768]{2,1,0:T(8,128)(2,1)} %copy-done, bf16[768,512]{1,0:T(8,128)(2,1)} %get-tuple-element.56.g0_ref, bf16[768,512]{1,0:T(8,128)(2,1)} %get-tuple-element.57.u0_ref, bf16[512,768]{1,0:T(8,128)(2,1)} %get-tuple-element.60.d0_ref.d_ref, ...), custom_call_target="tpu_custom_call" | custom-call | flops 2500000000 | bytes 8000000 | tf_op jit(solution)/shard_map/forward/pallas_call | solution.py:413
  53.5 0.0 copy-start.1
  53.5 3.7 %all-to-all-start.2 = ((bf16[8,64,768]{2,1,0:T(8,128)(2,1)}), bf16[8,64,768]{2,1,0:T(8,128)(2,1)S(1)}, u32[]{:S(2)}, u32[]{:S(2)}) async-start(bf16[8,64,768]{2,1,0:T(8,128)(2,1)} %get-tuple-element.65), calls=%async_computation.2 | async-start | bytes 1572864 | tf_op jit(solution)/shard_map/all_to_all | solution.py:431
  57.2 0.3 copy.29
  57.5 0.1 collective-permute-start.6
  57.6 4.7 %slopes.1 = (bf16[2,512,512]{2,1,0:T(8,128)(2,1)}, bf16[2,512,512]{2,1,0:T(8,128)(2,1)}) custom-call(f32[2,512,512]{2,1,0:T(8,128)} %get-tuple-element.68.gate_ref, f32[2,512,512]{2,1,0:T(8,128)} %get-tuple-element.69.up_ref), custom_call_target="tpu_custom_call" | custom-call | flops 8000000 | bytes 6000000 | tf_op jit(solution)/shard_map/slopes/pallas_call | solution.py:493
  62.2 0.0 copy-start.9
  62.2 1.1 slice_bitcast_fusion.1
  63.4 1.1 slice_bitcast_fusion
  64.5 0.4 collective-permute-start.5
  64.8 0.2 collective-permute-start.4
  65.1 2.5 %convolution_subtract_fusion.base_ref = f32[64,768]{1,0:T(8,128)S(1)} fusion(bf16[64,2048]{1,0:T(8,128)(2,1)S(1)} %copy-done.8, bf16[2048,768]{1,0:T(8,128)(2,1)} %out_ref.1, bf16[64,768]{1,0:T(8,128)(2,1)S(1)} %copy-done.9), kind=kOutput, calls=%fused_computation.2 | convolution fusion | flops 201424896 | bytes 3702784 | tf_op jit(solution)/shard_map/dot_general | solution.py:435
  67.6 2.6 %all-to-all-done.2.parts_ref = bf16[8,64,768]{2,1,0:T(8,128)(2,1)S(1)} async-done(((bf16[8,64,768]{2,1,0:T(8,128)(2,1)}), bf16[8,64,768]{2,1,0:T(8,128)(2,1)S(1)}, u32[]{:S(2)}, u32[]{:S(2)}) %all-to-all-start.2) | async-done | bytes 786464 | tf_op jit(solution)/shard_map/all_to_all | solution.py:431
  70.1 0.3 error.1
  70.5 0.0 collective-permute-done.5.b1_ref
  70.5 0.0 copy-start.11
  70.5 0.0 collective-permute-done.4.a1_ref
  70.5 0.0 collective-permute-done.6.x1_ref
  70.5 0.8 copy-done.11
  71.3 16.2 %all_to_all.30.e0_ref = bf16[8,64,768]{2,1,0:T(8,128)(2,1)S(1)} all-to-all(bf16[8,64,768]{2,1,0:T(8,128)(2,1)S(1)} %error.1), channel_id=1, replica_groups=mesh['y'=4,'zh'=2,'zl'=2,'x'=4,'core'=2] {'zl','x'}, dimensions={0} | all-to-all | bytes 1572864 | tf_op jit(solution)/shard_map/all_to_all | solution.py:431
  87.5 0.0 collective-permute-start.7
  87.5 2.3 %collective-permute-done.7.e1_ref = bf16[8,64,768]{2,1,0:T(8,128)(2,1)S(1)} collective-permute-done((bf16[8,64,768]{2,1,0:T(8,128)(2,1)S(1)}, bf16[8,64,768]{2,1,0:T(8,128)(2,1)S(1)}, u32[]{:S(2)}, u32[]{:S(2)}) %collective-permute-start.7) | collective-permute-done | bytes 786464 | tf_op jit(solution)/shard_map/ppermute | solution.py:439
  89.8 0.0 copy-done.2
  89.8 0.9 copy-done.6
  90.7 5.9 %backward.1 = bf16[768,1024]{1,0:T(8,128)(2,1)} custom-call(bf16[8,64,768]{2,1,0:T(8,128)(2,1)} %copy-done.2, bf16[8,64,768]{2,1,0:T(8,128)(2,1)} %copy-done.6, bf16[512,768]{1,0:T(8,128)(2,1)} %get-tuple-element.60.d0_ref.d_ref, bf16[2,512,512]{2,1,0:T(8,128)(2,1)} %get-tuple-element.70.a0_ref, bf16[2,512,512]{2,1,0:T(8,128)(2,1)} %get-tuple-element.71.b0_ref, ...), custom_call_target="tpu_custom_call" | custom-call | flops 2500000000 | bytes 8000000 | tf_op jit(solution)/shard_map/backward/pallas_call | solution.py:413
  96.6 30.3 %all_to_all.31.parts_ref = bf16[8,96,1024]{2,1,0:T(8,128)(2,1)S(1)} all-to-all(bf16[8,96,1024]{2,1,0:T(8,128)(2,1)} %bitcast.22), channel_id=1, replica_groups=mesh['y'=4,'zh'=2,'zl'=2,'x'=4,'core'=2] {'y','zh'}, dimensions={0} | all-to-all | bytes 3145728 | tf_op jit(solution)/shard_map/all_to_all | solution.py:431
  126.9 2.0 %total.1 = bf16[8,96,1024]{2,1,0:T(8,128)(2,1)} custom-call(bf16[8,96,1024]{2,1,0:T(8,128)(2,1)S(1)} %all_to_all.31.parts_ref), custom_call_target="tpu_custom_call" | custom-call | tf_op jit(solution)/shard_map/total/pallas_call | solution.py:522
  128.9 3.7 %all-to-all-start.5 = ((bf16[8,96,1024]{2,1,0:T(8,128)(2,1)}), bf16[8,96,1024]{2,1,0:T(8,128)(2,1)S(1)}, u32[]{:S(2)}, u32[]{:S(2)}) async-start(bf16[8,96,1024]{2,1,0:T(8,128)(2,1)} %total.1), calls=%async_computation.5 | async-start | bytes 3145728 | tf_op jit(solution)/shard_map/all_to_all | solution.py:431
  132.7 0.8 dynamic_slice.7
  133.4 0.5 and_select_fusion.1
  134.0 0.8 slice.12
  134.8 0.8 select_bitcast_fusion
  135.5 0.1 eq.40
  135.6 1.0 constant_dynamic-slice_fusion
  136.6 0.0 copy-start.12
  136.6 0.1 multiply_convert_fusion.w_ref
  136.7 0.0 copy-done.3
  136.7 0.0 copy-done.7
  136.7 0.1 pad_maximum_fusion
  136.9 0.4 copy-done.12
  137.3 1.1 convolution_convert_fusion
  138.4 16.1 %all-to-all-done.5.yg_ref.yu_ref = bf16[8,96,1024]{2,1,0:T(8,128)(2,1)S(1)} async-done(((bf16[8,96,1024]{2,1,0:T(8,128)(2,1)}), bf16[8,96,1024]{2,1,0:T(8,128)(2,1)S(1)}, u32[]{:S(2)}, u32[]{:S(2)}) %all-to-all-start.5) | async-done | bytes 1572896 | tf_op jit(solution)/shard_map/all_to_all | solution.py:431
  154.5 1.9 %last.1 = (f32[256,512]{1,0:T(8,128)}, f32[256,512]{1,0:T(8,128)}) custom-call(bf16[8,96,1024]{2,1,0:T(8,128)(2,1)S(1)} %all-to-all-done.5.yg_ref.yu_ref, bf16[8,96,1024]{2,1,0:T(8,128)(2,1)S(1)} %all-to-all-done.5.yg_ref.yu_ref, bf16[768,256]{1,0:T(8,128)(2,1)S(1)} %multiply_convert_fusion.w_ref), custom_call_target="tpu_custom_call" | custom-call | tf_op jit(solution)/shard_map/last/pallas_call | solution.py:529
  (16 shorter events, 0.1 us)
Async XLA Ops:
  0.6 27.3 %collective-permute-start.1 = (bf16[512,2048]{1,0:T(8,128)(2,1)}, bf16[512,2048]{1,0:T(8,128)(2,1)S(1)}, u32[]{:S(2)}, u32[]{:S(2)}) collective-permute-start(bf16[512,2048]{1,0:T(8,128)(2,1)} %w0_ref), channel_id=1, source_target_pairs={{0,1},{1,0},{2,3},{3,2},{4,5},{5,4},{6,7},{7,6},{8,9},{9,8},{10,11... | collective-permute-start | bytes 6291464 | tf_op jit(solution)/shard_map/ppermute | solution.py:439
  6.0 1.6 %collective-permute-start = (f32[72,128]{1,0:T(8,128)}, f32[72,128]{1,0:T(8,128)S(1)}, u32[]{:S(2)}, u32[]{:S(2)}) collective-permute-start(f32[72,128]{1,0:T(8,128)} %get-tuple-element.44), channel_id=1, source_target_pairs={{0,1},{1,0},{2,3},{3,2},{4,5},{5,4},{6,7},{7,6},{8,9},{9,8},{10,11... | collective-permute-start | bytes 110600 | tf_op jit(solution)/shard_map/ppermute | solution.py:439
  9.1 13.9 %all-to-all-start = ((f32[8,72,128]{2,1,0:T(8,128)}), f32[8,72,128]{2,1,0:T(8,128)S(1)}, u32[]{:S(2)}, u32[]{:S(2)}) async-start(f32[8,72,128]{2,1,0:T(8,128)} %broadcast_in_dim.24), calls=%async_computation | async-start | bytes 589824 | tf_op jit(solution)/shard_map/all_to_all | solution.py:431
  21.9 19.3 %collective-permute-start.2 = (bf16[768,512]{1,0:T(8,128)(2,1)}, bf16[768,512]{1,0:T(8,128)(2,1)}, u32[]{:S(2)}, u32[]{:S(2)}) collective-permute-start(bf16[768,512]{1,0:T(8,128)(2,1)} %get-tuple-element.56.g0_ref), channel_id=1, source_target_pairs={{0,1},{1,0},{2,3},{3,2},{4,5},{5,4},{6,7},{7,6},{8,9},{9,8},{10,11... | collective-permute-start | bytes 2359304 | tf_op jit(solution)/shard_map/ppermute | solution.py:439
  22.1 19.2 %collective-permute-start.3 = (bf16[768,512]{1,0:T(8,128)(2,1)}, bf16[768,512]{1,0:T(8,128)(2,1)}, u32[]{:S(2)}, u32[]{:S(2)}) collective-permute-start(bf16[768,512]{1,0:T(8,128)(2,1)} %get-tuple-element.57.u0_ref), channel_id=1, source_target_pairs={{0,1},{1,0},{2,3},{3,2},{4,5},{5,4},{6,7},{7,6},{8,9},{9,8},{10,11... | collective-permute-start | bytes 2359304 | tf_op jit(solution)/shard_map/ppermute | solution.py:439
  23.0 0.7 copy-start.4
  27.9 5.2 %copy-start.10 = (bf16[512,2048]{1,0:T(8,128)(2,1)}, bf16[512,2048]{1,0:T(8,128)(2,1)S(1)}, u32[]{:S(2)}) copy-start(bf16[512,2048]{1,0:T(8,128)(2,1)S(1)} %collective-permute-done.1.w1_ref) | copy-start | bytes 6291460
  28.0 18.4 %all-to-all-start.1 = ((bf16[8,64,768]{2,1,0:T(8,128)(2,1)}), bf16[8,64,768]{2,1,0:T(8,128)(2,1)S(1)}, u32[]{:S(2)}, u32[]{:S(2)}) async-start(bf16[8,64,768]{2,1,0:T(8,128)(2,1)} %get-tuple-element.54), calls=%async_computation.1 | async-start | bytes 1572864 | tf_op jit(solution)/shard_map/all_to_all | solution.py:431
  46.3 0.9 copy-start
  53.5 3.7 %copy-start.1 = (bf16[8,64,768]{2,1,0:T(8,128)(2,1)S(1)}, bf16[8,64,768]{2,1,0:T(8,128)(2,1)}, u32[]{:S(2)}) copy-start(bf16[8,64,768]{2,1,0:T(8,128)(2,1)} %copy-done) | copy-start | bytes 2359300
  53.5 16.7 %all-to-all-start.2 = ((bf16[8,64,768]{2,1,0:T(8,128)(2,1)}), bf16[8,64,768]{2,1,0:T(8,128)(2,1)S(1)}, u32[]{:S(2)}, u32[]{:S(2)}) async-start(bf16[8,64,768]{2,1,0:T(8,128)(2,1)} %get-tuple-element.65), calls=%async_computation.2 | async-start | bytes 1572864 | tf_op jit(solution)/shard_map/all_to_all | solution.py:431
  57.5 4.8 %copy-start.5 = (bf16[512,768]{0,1:T(8,128)(2,1)}, bf16[512,768]{0,1:T(8,128)(2,1)S(1)}, u32[]{:S(2)}) copy-start(bf16[512,768]{0,1:T(8,128)(2,1)S(1)} %copy.29) | copy-start | bytes 2359300
  57.5 13.0 %collective-permute-start.6 = (bf16[768,512]{1,0:T(8,128)(2,1)S(1)}, bf16[768,512]{1,0:T(8,128)(2,1)}, u32[]{:S(2)}, u32[]{:S(2)}) collective-permute-start(bf16[768,512]{1,0:T(8,128)(2,1)S(1)} %bitcast.24), channel_id=1, source_target_pairs={{0,1},{1,0},{2,3},{3,2},{4,5},{5,4},{6,7},{7,6},{8,9},{9,8},{10,11... | collective-permute-start | bytes 2359304 | tf_op jit(solution)/shard_map/ppermute | solution.py:439
  62.2 2.8 %copy-start.8 = (bf16[64,2048]{1,0:T(8,128)(2,1)S(1)}, bf16[64,2048]{1,0:T(8,128)(2,1)}, u32[]{:S(2)}) copy-start(bf16[64,2048]{1,0:T(8,128)(2,1)} %get-tuple-element.66) | copy-start | bytes 786436
  62.2 2.8 %copy-start.9 = (bf16[64,768]{1,0:T(8,128)(2,1)S(1)}, bf16[64,768]{1,0:T(8,128)(2,1)}, u32[]{:S(2)}) copy-start(bf16[64,768]{1,0:T(8,128)(2,1)} %get-tuple-element.67) | copy-start | bytes 294916
  64.5 6.0 %collective-permute-start.5 = (bf16[512,512]{1,0:T(8,128)(2,1)S(1)}, bf16[512,512]{1,0:T(8,128)(2,1)S(1)}, u32[]{:S(2)}, u32[]{:S(2)}) collective-permute-start(bf16[512,512]{1,0:T(8,128)(2,1)S(1)} %slice_bitcast_fusion), channel_id=1, source_target_pairs={{0,1},{1,0},{2,3},{3,2},{4,5},{5,4},{6,7},{7,6},{8,9},{9,8},{10,11... | collective-permute-start | bytes 1572872 | tf_op jit(solution)/shard_map/ppermute | solution.py:439
  64.8 5.6 %collective-permute-start.4 = (bf16[512,512]{1,0:T(8,128)(2,1)S(1)}, bf16[512,512]{1,0:T(8,128)(2,1)}, u32[]{:S(2)}, u32[]{:S(2)}) collective-permute-start(bf16[512,512]{1,0:T(8,128)(2,1)S(1)} %slice_bitcast_fusion.1), channel_id=1, source_target_pairs={{0,1},{1,0},{2,3},{3,2},{4,5},{5,4},{6,7},{7,6},{8,9},{9,8},{10,11... | collective-permute-start | bytes 1572872 | tf_op jit(solution)/shard_map/ppermute | solution.py:439
  70.5 0.8 copy-start.11
  87.5 2.3 %copy-start.2 = (bf16[8,64,768]{2,1,0:T(8,128)(2,1)}, bf16[8,64,768]{2,1,0:T(8,128)(2,1)S(1)}, u32[]{:S(2)}) copy-start(bf16[8,64,768]{2,1,0:T(8,128)(2,1)S(1)} %all_to_all.30.e0_ref) | copy-start | bytes 2359300
  87.5 2.3 %collective-permute-start.7 = (bf16[8,64,768]{2,1,0:T(8,128)(2,1)S(1)}, bf16[8,64,768]{2,1,0:T(8,128)(2,1)S(1)}, u32[]{:S(2)}, u32[]{:S(2)}) collective-permute-start(bf16[8,64,768]{2,1,0:T(8,128)(2,1)S(1)} %all_to_all.30.e0_ref), channel_id=1, source_target_pairs={{0,1},{1,0},{2,3},{3,2},{4,5},{5,4},{6,7},{7,6},{8,9},{9,8},{10,11... | collective-permute-start | bytes 2359304 | tf_op jit(solution)/shard_map/ppermute | solution.py:439
  89.8 0.9 copy-start.6
  128.9 7.8 %copy-start.3 = (bf16[8,64,768]{2,1,0:T(8,128)(2,1)S(1)}, bf16[8,64,768]{2,1,0:T(8,128)(2,1)}, u32[]{:S(2)}) copy-start(bf16[8,64,768]{2,1,0:T(8,128)(2,1)} %copy-done.2) | copy-start | bytes 2359300
  128.9 7.8 %copy-start.7 = (bf16[8,64,768]{2,1,0:T(8,128)(2,1)S(1)}, bf16[8,64,768]{2,1,0:T(8,128)(2,1)}, u32[]{:S(2)}) copy-start(bf16[8,64,768]{2,1,0:T(8,128)(2,1)} %copy-done.6) | copy-start | bytes 2359300
  128.9 25.6 %all-to-all-start.5 = ((bf16[8,96,1024]{2,1,0:T(8,128)(2,1)}), bf16[8,96,1024]{2,1,0:T(8,128)(2,1)S(1)}, u32[]{:S(2)}, u32[]{:S(2)}) async-start(bf16[8,96,1024]{2,1,0:T(8,128)(2,1)} %total.1), calls=%async_computation.5 | async-start | bytes 3145728 | tf_op jit(solution)/shard_map/all_to_all | solution.py:431
  136.6 0.7 copy-start.12

commit v4 on v3

--- a/solution.py
+++ b/solution.py
@@ -239,12 +239,14 @@
 
 
 def down_kernel(w0_ref, w1_ref, out_ref, d0_ref, d1_ref, w0b, w1b, outb, sem):
-    copies = fetch((w0_ref, out_ref, w1_ref), (w0b, outb, w1b), sem)
+    copies = fetch((out_ref, w0_ref, w1_ref), (outb, w0b, w1b), sem)
     copies[0].wait()
-    copies[1].wait()
-    d0_ref[...] = dot(w0b[...], outb[...]).astype(BF16)
-    copies[2].wait()
-    d1_ref[...] = dot(w1b[...], outb[...]).astype(BF16)
+    tall = 256
+    for copy, w, d_ref in ((copies[1], w0b, d0_ref), (copies[2], w1b, d1_ref)):
+        copy.wait()
+        for i in range(w.shape[0] // tall):
+            at = pl.ds(i * tall, tall)
+            d_ref[at] = dot(w[at], outb[...]).astype(BF16)
 
 
 def forward_kernel(
@@ -277,11 +279,12 @@
         out.wait()
 
 
-def slopes_kernel(gate_ref, up_ref, a_ref, b_ref):
-    gate, upper = gate_ref[...], up_ref[...]
-    sigma = jax.nn.sigmoid(gate)
-    a_ref[...] = (upper * sigma * (1.0 + gate * (1.0 - sigma))).astype(BF16)
-    b_ref[...] = (gate * sigma).astype(BF16)
+def slopes_kernel(gate_ref, up_ref, a0_ref, b0_ref, a1_ref, b1_ref):
+    for side, (a_ref, b_ref) in enumerate(((a0_ref, b0_ref), (a1_ref, b1_ref))):
+        gate, upper = gate_ref[side], up_ref[side]
+        sigma = jax.nn.sigmoid(gate)
+        a_ref[...] = (upper * sigma * (1.0 + gate * (1.0 - sigma))).astype(BF16)
+        b_ref[...] = (gate * sigma).astype(BF16)
 
 
 def error_kernel(parts_ref, base_ref, err_ref):
@@ -293,33 +296,39 @@
         err_ref[d] = total
 
 
-def backward_kernel(
-    e0_ref, e1_ref, d_ref, a0_ref, b0_ref, a1_ref, b1_ref, x0_ref, x1_ref, y_ref,
-    e0b, e1b, db, a0b, b0b, a1b, b1b, x0b, x1b, grads, sem,
+def hidden_grads(err_buf, down_buf, a_buf, b_buf, copies):
+    copies[0].wait()
+    dpred = (err_buf[...].astype(F32) / 64.0).astype(BF16).reshape(-1, err_buf.shape[-1])
+    copies[1].wait()
+    dact = nt(dpred, down_buf[...])
+    copies[2].wait()
+    dgate = (dact * a_buf[...].astype(F32)).astype(BF16)
+    copies[3].wait()
+    return dgate, (dact * b_buf[...].astype(F32)).astype(BF16)
+
+
+def own_kernel(err_ref, d_ref, a_ref, b_ref, dg_ref, du_ref, errb, db, ab, bb, sem):
+    copies = fetch((err_ref, d_ref, a_ref, b_ref), (errb, db, ab, bb), sem)
+    dg_ref[...], du_ref[...] = hidden_grads(errb, db, ab, bb, copies)
+
+
+def other_kernel(
+    err_ref, d_ref, a_ref, b_ref, x0_ref, dg_ref, du_ref, x1_ref, y_ref,
+    errb, db, ab, bb, x0b, dgb, dub, x1b, sem,
 ):
     copies = fetch(
-        (e0_ref, d_ref, a0_ref.at[0], b0_ref.at[0], e1_ref, a1_ref, b1_ref, x0_ref, x1_ref),
-        (e0b, db, a0b, b0b, e1b, a1b, b1b, x0b, x1b),
+        (err_ref, d_ref, a_ref, b_ref, x0_ref, dg_ref, du_ref, x1_ref),
+        (errb, db, ab, bb, x0b, dgb, dub, x1b),
         sem,
     )
-    width = a0b.shape[1]
-    order = ((e0b, a0b, b0b, 0), (e1b, a1b, b1b, 4))
-    for side, (eb, ab, bb, first) in enumerate(order):
-        for i in range(3 if side else 4):
-            copies[first + i].wait()
-        dpred = (eb[...].astype(F32) / 64.0).astype(BF16).reshape(-1, eb.shape[-1])
-        dact = nt(dpred, db[...])
-        rows = pl.ds(side * dact.shape[0], dact.shape[0])
-        grads[rows, :width] = (dact * ab[...].astype(F32)).astype(BF16)
-        grads[rows, width:] = (dact * bb[...].astype(F32)).astype(BF16)
-    copies[7].wait()
-    copies[8].wait()
-    half = x0b.shape[1]
-    tall = 256
+    dgate, dup = hidden_grads(errb, db, ab, bb, copies)
+    for c in copies[4:]:
+        c.wait()
+    width, tall = dgate.shape[1], 256
     for i in range(y_ref.shape[0] // tall):
         at = pl.ds(i * tall, tall)
-        y = dot(x0b[at], grads[:half]) + dot(x1b[at], grads[half:])
-        y_ref[at] = y.astype(BF16)
+        y_ref[at, :width] = (dot(x0b[at], dgb[...]) + dot(x1b[at], dgate)).astype(BF16)
+        y_ref[at, width:] = (dot(x0b[at], dub[...]) + dot(x1b[at], dup)).astype(BF16)
 
 
 def sum_kernel(parts_ref, out_ref):
@@ -405,10 +414,11 @@
 
 
 PARAMS = pltpu.CompilerParams(vmem_limit_bytes=LIMIT)
+MIDDLE = pltpu.CompilerParams(vmem_limit_bytes=24 * 1024 * 1024)
 SMALL = pltpu.CompilerParams(vmem_limit_bytes=16 * 1024 * 1024)
 
 
-def staged(kernel, name, args, out_shape, scratch, flops, sems, out_specs=VM, bufs=None):
+def staged(kernel, name, args, out_shape, scratch, flops, sems, out_specs=VM, bufs=None, params=PARAMS):
     bufs = [vmem_like(a) for a in args] if bufs is None else bufs
     return pl.pallas_call(
         kernel,
@@ -416,7 +426,7 @@
         in_specs=[HB] * len(args),
         out_specs=out_specs,
         scratch_shapes=bufs + scratch + [pltpu.SemaphoreType.DMA((n,)) for n in sems],
-        compiler_params=PARAMS,
+        compiler_params=params,
         cost_estimate=pl.CostEstimate(flops=flops, bytes_accessed=8000000, transcendentals=0),
         name=name,
     )(*args)
@@ -488,14 +498,16 @@
     )
     part, gate, upper, x_late, w_in_late = lax.optimization_barrier((part, gate, upper, x, w_in_late))
     parts = exchange(part, CHIP)
-    slope = sds(wide.shape, BF16)
-    rows_of = lambda: pl.BlockSpec((2, half // 4, width), lambda i: (0, i, 0))
-    slope_a, slope_b = pl.pallas_call(
-        slopes_kernel, grid=(4,), out_shape=(slope, slope), in_specs=[rows_of(), rows_of()],
-        out_specs=(rows_of(), rows_of()), compiler_params=PARAMS, name="slopes",
+    slope = sds((half, width), BF16)
+    wide_rows = pl.BlockSpec((2, half // 4, width), lambda i: (0, i, 0))
+    slope_rows = pl.BlockSpec((half // 4, width), lambda i: (i, 0))
+    slope_a, slope_b, slope_ao, slope_bo = pl.pallas_call(
+        slopes_kernel, grid=(4,), out_shape=(slope,) * 4, in_specs=[wide_rows] * 2,
+        out_specs=(slope_rows,) * 4, compiler_params=PARAMS, name="slopes",
         cost_estimate=pl.CostEstimate(flops=8000000, bytes_accessed=6000000, transcendentals=1000000),
     )(gate, upper)
-    slope_ao, slope_bo = swap(slope_a[1]), swap(slope_b[1])
+    slope_ao, slope_bo = swap(slope_ao), swap(slope_bo)
+    x_late, slope_a = lax.optimization_barrier((x_late, slope_a))
     x_late = lax.optimization_barrier(x_late.reshape(half, FEATS).T)
     x_other = swap(x_late)
     at = lax.axis_index(GRP)
@@ -508,15 +520,15 @@
         in_specs=[cut(parts.shape, 3), cut(base.shape, 3)], out_specs=cut(parts.shape, 3),
         compiler_params=SMALL, name="error",
     )(parts, base)
-    err_own, slope_ao, slope_bo, x_other = lax.optimization_barrier((err_own, slope_ao, slope_bo, x_other))
+    err_own, slope_ao, slope_bo = lax.optimization_barrier((err_own, slope_ao, slope_bo))
     err = exchange(err_own, CHIP)
     err_other = swap(err)
-    args = (err, err_other, down_w, slope_a, slope_b, slope_ao, slope_bo, x_late, x_other)
-    part_like = pltpu.VMEM((half, width), BF16)
-    bufs = [vmem_like(err)] * 2 + [vmem_like(down_w)] + [part_like] * 4 + [vmem_like(x_late)] * 2
+    dg, du = staged(
+        own_kernel, "own", (err, down_w, slope_a, slope_b), (slope, slope), [], 400000000, (4,), (VM,) * 2, params=MIDDLE,
+    )
     feat_grads = staged(
-        backward_kernel, "backward", args, sds((FEATS, 2 * width), BF16),
-        [pltpu.VMEM((2 * half, 2 * width), BF16)], 2500000000, (9,), bufs=bufs,
+        other_kernel, "other", (err_other, down_w, slope_ao, slope_bo, x_late, dg, du, x_other),
+        sds((FEATS, 2 * width), BF16), [], 2000000000, (8,), params=MIDDLE,
     )
     feat_grads = exchange(feat_grads.reshape(groups, FEATS // groups, 2 * width), GRP)
     feat_grads = pl.pallas_call(

time: 157 us -> 157 us (level)
  blocking collectives: 46.5 us -> 30.4 us
  waiting for transfers between devices: 27.5 us -> 42.3 us
  starting transfers between devices: 20.3 us -> 23.5 us
  Pallas kernels: 45.6 us -> 42.9 us
    all_to_all x4 -> x5, waiting for transfers between devices: 24.2 us -> 41.2 us  [exchange(): return lax.all_to_all(x, axes, split_axis=0, concat_axis=0, tiled=True)]
    all_to_all x2 -> x1, blocking collectives: 46.5 us -> 30.4 us  [exchange(): return lax.all_to_all(x, axes, split_axis=0, concat_axis=0, tiled=True)]
    all_to_all x4 -> x5, starting transfers between devices: 18.4 us -> 21.7 us  [exchange(): return lax.all_to_all(x, axes, split_axis=0, concat_axis=0, tiled=True)]
    pallas_call x4 -> x5, Pallas kernels: 27.3 us -> 24.9 us  [staged(): pl.pallas_call(kernel, out_shape=out_shape, in_specs=[HB] * len(args), ou...]
    ppermute x8, waiting for transfers between devices: 3.37 us -> 1.09 us  [swap(): return lax.ppermute(x, 'core', SWAP)]
    squeeze x2 -> x0, local copies, waits for them, and re-layouts: 2.2 us -> none  [body(): slope_ao, slope_bo = (swap(slope_a[1]), swap(slope_b[1]))]
    unnamed x26 -> x28, local copies, waits for them, and re-layouts: 3.7 us -> 5.35 us
  transfers between devices with their start and end apart: 12 -> 13, of which waited for: 6 -> 6; matrix products, arithmetic and copies ran while one was open for 8% -> 7% of each run, Pallas kernels for 19% -> 20%
where the time goes in v4:
time: 157 us; the launch traced here: 156 us
  Pallas kernels  42.9 us (27%)
  waiting for transfers between devices  42.3 us (27%)
  blocking collectives  30.4 us (19%)
  starting transfers between devices  23.5 us (15%)
  local copies, waits for them, and re-layouts  10.2 us (6%)
  matrix products  3.65 us (2%)
  other arithmetic  2.28 us (1%)
    all_to_all x5, waiting for transfers between devices, exchange(): return lax.all_to_all(x, axes, split_axis=0, concat_axis=0, tiled=True)  41.2 us
    all_to_all x1, blocking collectives, exchange(): return lax.all_to_all(x, axes, split_axis=0, concat_axis=0, tiled=True)  30.4 us
    pallas_call x5, Pallas kernels, staged(): pl.pallas_call(kernel, out_shape=out_shape, in_specs=[HB] * len(args), ou...  24.9 us
    all_to_all x5, starting transfers between devices, exchange(): return lax.all_to_all(x, axes, split_axis=0, concat_axis=0, tiled=True)  21.7 us
    unnamed x28, local copies, waits for them, and re-layouts  5.35 us
    pallas_call x1, Pallas kernels, evolve(): pl.pallas_call(evolve_kernel, out_shape=(sds((ROWS, LANES), F32), sds((2...  5.24 us
    pallas_call x1, Pallas kernels, body(): pl.pallas_call(slopes_kernel, grid=(4,), out_shape=(slope,) * 4, in_specs...  4.35 us
    pallas_call x1, Pallas kernels, finish(): pl.pallas_call(finish_kernel, out_shape=out + (sds(fpos.shape, F32),), in...  4.23 us
  transfers between devices with their start and end apart: 13, of which 6 were waited for; matrix products, arithmetic and copies ran while one was open for 7% of the time, Pallas kernels for 20%

profile of v4, /device:TPU:0, one launch (start us, length us, event | category | flops | bytes accessed | tf_op | source)
XLA Modules:
  0.0 156.1 jit_solution(13739442862946310649)
XLA Ops:
  0.6 0.1 collective-permute-start.1
  0.7 5.2 %evolve.1 = (f32[72,128]{1,0:T(8,128)}, bf16[128,768]{1,0:T(8,128)(2,1)}, f32[24,128]{1,0:T(8,128)}, f32[3,256,128]{2,1,0:T(8,128)}) custom-call(f32[3,256,128]{2,1,0:T(8,128)} %pos_ref.3, f32[3,256,128]{2,1,0:T(8,128)} %vel_ref.3, f32[1,128]{1,0:T(1,128)} %bitcast.25, s32[8,256,128]{2,1,0:T(8,128)} %contact_ref.3, f32[3,128]{1,0:T(4,128)} %off_ref.3, ...), custom_call_target="tpu_custom_call" | custom-call | flops 260000000 | bytes 3000000 | tf_op jit(solution)/shard_map/evolve/pallas_call | solution.py:364
  6.0 0.6 collective-permute-start
  6.5 1.1 collective-permute-done
  7.6 0.8 add.89
  8.4 0.7 broadcast_in_dim.24
  9.1 5.7 %all-to-all-start = ((f32[8,72,128]{2,1,0:T(8,128)}), f32[8,72,128]{2,1,0:T(8,128)S(1)}, u32[]{:S(2)}, u32[]{:S(2)}) async-start(f32[8,72,128]{2,1,0:T(8,128)} %broadcast_in_dim.24), calls=%async_computation | async-start | bytes 589824 | tf_op jit(solution)/shard_map/all_to_all | solution.py:441
  14.9 7.0 %products.1 = (bf16[768,512]{1,0:T(8,128)(2,1)}, bf16[768,512]{1,0:T(8,128)(2,1)}) custom-call(bf16[768,2048]{1,0:T(8,128)(2,1)} %w_in_ref.2, f32[1,2048]{1,0:T(1,128)} %bitcast.32, bf16[2048,512]{1,0:T(8,128)(2,1)} %gate_ref.1, bf16[2048,512]{1,0:T(8,128)(2,1)} %up_ref.1), custom_call_target="tpu_custom_call" | custom-call | flops 3300000000 | bytes 8000000 | tf_op jit(solution)/shard_map/products/pallas_call | solution.py:423
  21.9 0.1 collective-permute-start.2
  22.1 0.4 collective-permute-start.3
  22.5 0.5 all-to-all-done.recv_ref
  23.0 0.7 copy-done.9
  23.7 4.2 %finish.1 = (bf16[8,64,768]{2,1,0:T(8,128)(2,1)}, bf16[64,768]{1,0:T(8,128)(2,1)}, bf16[64,2048]{1,0:T(8,128)(2,1)}, f32[3,128]{1,0:T(4,128)}, f32[3,256,128]{2,1,0:T(8,128)}) custom-call(f32[8,72,128]{2,1,0:T(8,128)} %copy-done.9, f32[24,128]{1,0:T(8,128)} %get-tuple-element.51.bound_ref, ...), custom_call_target="tpu_custom_call", output_to_operand_aliasing={{4}: (18, {})} | custom-call | flops 300000000 | bytes 4000000 | tf_op jit(solution)/shard_map/finish/pallas_call | solution.py:397
  28.0 0.0 collective-permute-done.1.w1_ref
  28.0 0.0 copy-start.12
  28.0 5.2 %all-to-all-start.1 = ((bf16[8,64,768]{2,1,0:T(8,128)(2,1)}), bf16[8,64,768]{2,1,0:T(8,128)(2,1)S(1)}, u32[]{:S(2)}, u32[]{:S(2)}) async-start(bf16[8,64,768]{2,1,0:T(8,128)(2,1)} %get-tuple-element.59), calls=%async_computation.1 | async-start | bytes 1572864 | tf_op jit(solution)/shard_map/all_to_all | solution.py:441
  33.2 0.0 copy-done.12
  33.2 7.0 %down.1 = (bf16[512,768]{1,0:T(8,128)(2,1)}, bf16[512,768]{1,0:T(8,128)(2,1)}) custom-call(bf16[512,2048]{1,0:T(8,128)(2,1)} %w0_ref, bf16[512,2048]{1,0:T(8,128)(2,1)} %copy-done.12, bf16[2048,768]{1,0:T(8,128)(2,1)} %out_ref.1), custom_call_target="tpu_custom_call" | custom-call | flops 3300000000 | bytes 8000000 | tf_op jit(solution)/shard_map/down/pallas_call | solution.py:423
  40.3 0.0 collective-permute-done.2.g1_ref
  40.3 0.0 collective-permute-done.3.u1_ref
  40.3 6.1 %all-to-all-done.1.x_ref = bf16[8,64,768]{2,1,0:T(8,128)(2,1)S(1)} async-done(((bf16[8,64,768]{2,1,0:T(8,128)(2,1)}), bf16[8,64,768]{2,1,0:T(8,128)(2,1)S(1)}, u32[]{:S(2)}, u32[]{:S(2)}) %all-to-all-start.1) | async-done | bytes 786464 | tf_op jit(solution)/shard_map/all_to_all | solution.py:441
  46.4 0.9 copy-done.8
  47.3 6.2 %forward.1 = (bf16[8,64,768]{2,1,0:T(8,128)(2,1)}, f32[2,512,512]{2,1,0:T(8,128)}, f32[2,512,512]{2,1,0:T(8,128)}) custom-call(bf16[8,64,768]{2,1,0:T(8,128)(2,1)} %copy-done.8, bf16[768,512]{1,0:T(8,128)(2,1)} %get-tuple-element.61.g0_ref, bf16[768,512]{1,0:T(8,128)(2,1)} %get-tuple-element.62.u0_ref, bf16[512,768]{1,0:T(8,128)(2,1)} %get-tuple-element.65.d0_ref.d_ref, ...), custom_call_target="tpu_custom_call" | custom-call | flops 2500000000 | bytes 8000000 | tf_op jit(solution)/shard_map/forward/pallas_call | solution.py:423
  53.5 3.6 %all-to-all-start.2 = ((bf16[8,64,768]{2,1,0:T(8,128)(2,1)}), bf16[8,64,768]{2,1,0:T(8,128)(2,1)S(1)}, u32[]{:S(2)}, u32[]{:S(2)}) async-start(bf16[8,64,768]{2,1,0:T(8,128)(2,1)} %get-tuple-element.70), calls=%async_computation.2 | async-start | bytes 1572864 | tf_op jit(solution)/shard_map/all_to_all | solution.py:441
  57.1 4.3 %slopes.1 = (bf16[512,512]{1,0:T(8,128)(2,1)}, bf16[512,512]{1,0:T(8,128)(2,1)}, bf16[512,512]{1,0:T(8,128)(2,1)}, bf16[512,512]{1,0:T(8,128)(2,1)}) custom-call(f32[2,512,512]{2,1,0:T(8,128)} %get-tuple-element.73.gate_ref, f32[2,512,512]{2,1,0:T(8,128)} %get-tuple-element.74.up_ref), custom_call_target="tpu_custom_call" | custom-call | flops 8000000 | bytes 6000000 | tf_op jit(solution)/shard_map/slopes/pallas_call | solution.py:504
  61.5 0.0 collective-permute-start.4
  61.5 0.5 collective-permute-start.5
  62.0 0.0 copy-done.10
  62.0 2.5 %convolution_subtract_fusion.base_ref = f32[64,768]{1,0:T(8,128)S(1)} fusion(bf16[64,2048]{1,0:T(8,128)(2,1)S(1)} %copy-done.10, bf16[2048,768]{1,0:T(8,128)(2,1)} %out_ref.1, bf16[64,768]{1,0:T(8,128)(2,1)S(1)} %copy-done.11), kind=kOutput, calls=%fused_computation.2 | convolution fusion | flops 201424896 | bytes 3702784 | tf_op jit(solution)/shard_map/dot_general | solution.py:445
  64.5 5.6 %all-to-all-done.2.parts_ref = bf16[8,64,768]{2,1,0:T(8,128)(2,1)S(1)} async-done(((bf16[8,64,768]{2,1,0:T(8,128)(2,1)}), bf16[8,64,768]{2,1,0:T(8,128)(2,1)S(1)}, u32[]{:S(2)}, u32[]{:S(2)}) %all-to-all-start.2) | async-done | bytes 786464 | tf_op jit(solution)/shard_map/all_to_all | solution.py:441
  70.1 1.6 %error.1 = bf16[8,64,768]{2,1,0:T(8,128)(2,1)} custom-call(bf16[8,64,768]{2,1,0:T(8,128)(2,1)S(1)} %all-to-all-done.2.parts_ref, f32[64,768]{1,0:T(8,128)S(1)} %convolution_subtract_fusion.base_ref), custom_call_target="tpu_custom_call" | custom-call | tf_op jit(solution)/shard_map/error/pallas_call | solution.py:518
  71.7 0.0 collective-permute-done.4.a_ref
  71.7 0.0 collective-permute-done.5.b_ref
  71.7 3.6 %all-to-all-start.3 = ((bf16[8,64,768]{2,1,0:T(8,128)(2,1)}), bf16[8,64,768]{2,1,0:T(8,128)(2,1)S(1)}, u32[]{:S(2)}, u32[]{:S(2)}) async-start(bf16[8,64,768]{2,1,0:T(8,128)(2,1)} %error.1), calls=%async_computation.3 | async-start | bytes 1572864 | tf_op jit(solution)/shard_map/all_to_all | solution.py:441
  75.3 0.0 copy-done.4
  75.3 1.4 copy.29
  76.7 0.1 collective-permute-start.7
  76.8 11.4 %all-to-all-done.3.err_ref = bf16[8,64,768]{2,1,0:T(8,128)(2,1)S(1)} async-done(((bf16[8,64,768]{2,1,0:T(8,128)(2,1)}), bf16[8,64,768]{2,1,0:T(8,128)(2,1)S(1)}, u32[]{:S(2)}, u32[]{:S(2)}) %all-to-all-start.3) | async-done | bytes 786464 | tf_op jit(solution)/shard_map/all_to_all | solution.py:441
  88.2 0.0 collective-permute-start.6
  88.3 0.0 copy-done.1
  88.3 1.0 copy-done.2
  89.3 1.0 copy-done.3
  90.3 1.3 own.1
  91.6 0.0 collective-permute-done.7.x1_ref
  91.6 0.0 collective-permute-done.6.err_ref
  91.7 3.4 %other.1 = bf16[768,1024]{1,0:T(8,128)(2,1)S(1)} custom-call(bf16[8,64,768]{2,1,0:T(8,128)(2,1)S(1)} %collective-permute-done.6.err_ref, bf16[512,768]{1,0:T(8,128)(2,1)S(1)} %copy-done.1, bf16[512,512]{1,0:T(8,128)(2,1)S(1)} %copy-done.5, bf16[512,512]{1,0:T(8,128)(2,1)S(1)} %copy-done.7, bf16[768,512]{1,0:T(8,128)(2,1)S(1)} %bitcast.19, ...), custom_call_target="tpu_custom_call" | custom-call | flops 2000000000 | bytes 8000000 | tf_op jit(solution)/shard_map/other/pallas_call | solution.py:423
  95.0 30.4 %all_to_all.30.parts_ref = bf16[8,96,1024]{2,1,0:T(8,128)(2,1)S(1)} all-to-all(bf16[8,96,1024]{2,1,0:T(8,128)(2,1)S(1)} %bitcast.17), channel_id=1, replica_groups=mesh['y'=4,'zh'=2,'zl'=2,'x'=4,'core'=2] {'y','zh'}, dimensions={0} | all-to-all | bytes 3145728 | tf_op jit(solution)/shard_map/all_to_all | solution.py:441
  125.5 0.7 total.1
  126.1 0.0 copy-start
  126.1 1.2 copy-done
  127.3 3.6 %all-to-all-start.5 = ((bf16[8,96,1024]{2,1,0:T(8,128)(2,1)}), bf16[8,96,1024]{2,1,0:T(8,128)(2,1)S(1)}, u32[]{:S(2)}, u32[]{:S(2)}) async-start(bf16[8,96,1024]{2,1,0:T(8,128)(2,1)} %copy-done), calls=%async_computation.5 | async-start | bytes 3145728 | tf_op jit(solution)/shard_map/all_to_all | solution.py:441
  130.9 0.8 dynamic_slice.7
  131.7 0.5 and_select_fusion.1
  132.2 0.8 slice.4
  133.0 0.8 select_bitcast_fusion
  133.8 0.1 eq.40
  133.9 1.0 constant_dynamic-slice_fusion
  134.9 0.0 copy-start.13
  134.9 0.1 multiply_convert_fusion.w_ref
  135.0 0.1 pad_maximum_fusion
  135.1 0.4 copy-done.13
  135.5 1.1 convolution_convert_fusion
  136.7 17.6 %all-to-all-done.5.yg_ref.yu_ref = bf16[8,96,1024]{2,1,0:T(8,128)(2,1)S(1)} async-done(((bf16[8,96,1024]{2,1,0:T(8,128)(2,1)}), bf16[8,96,1024]{2,1,0:T(8,128)(2,1)S(1)}, u32[]{:S(2)}, u32[]{:S(2)}) %all-to-all-start.5) | async-done | bytes 1572896 | tf_op jit(solution)/shard_map/all_to_all | solution.py:441
  154.2 1.9 %last.1 = (f32[256,512]{1,0:T(8,128)}, f32[256,512]{1,0:T(8,128)}) custom-call(bf16[8,96,1024]{2,1,0:T(8,128)(2,1)S(1)} %all-to-all-done.5.yg_ref.yu_ref, bf16[8,96,1024]{2,1,0:T(8,128)(2,1)S(1)} %all-to-all-done.5.yg_ref.yu_ref, bf16[768,256]{1,0:T(8,128)(2,1)S(1)} %multiply_convert_fusion.w_ref), custom_call_target="tpu_custom_call" | custom-call | tf_op jit(solution)/shard_map/last/pallas_call | solution.py:541
  (18 shorter events, 0.1 us)
Async XLA Ops:
  0.6 27.4 %collective-permute-start.1 = (bf16[512,2048]{1,0:T(8,128)(2,1)}, bf16[512,2048]{1,0:T(8,128)(2,1)S(1)}, u32[]{:S(2)}, u32[]{:S(2)}) collective-permute-start(bf16[512,2048]{1,0:T(8,128)(2,1)} %w0_ref), channel_id=1, source_target_pairs={{0,1},{1,0},{2,3},{3,2},{4,5},{5,4},{6,7},{7,6},{8,9},{9,8},{10,11... | collective-permute-start | bytes 6291464 | tf_op jit(solution)/shard_map/ppermute | solution.py:449
  6.0 1.6 %collective-permute-start = (f32[72,128]{1,0:T(8,128)}, f32[72,128]{1,0:T(8,128)S(1)}, u32[]{:S(2)}, u32[]{:S(2)}) collective-permute-start(f32[72,128]{1,0:T(8,128)} %get-tuple-element.49), channel_id=1, source_target_pairs={{0,1},{1,0},{2,3},{3,2},{4,5},{5,4},{6,7},{7,6},{8,9},{9,8},{10,11... | collective-permute-start | bytes 110600 | tf_op jit(solution)/shard_map/ppermute | solution.py:449
  9.1 13.9 %all-to-all-start = ((f32[8,72,128]{2,1,0:T(8,128)}), f32[8,72,128]{2,1,0:T(8,128)S(1)}, u32[]{:S(2)}, u32[]{:S(2)}) async-start(f32[8,72,128]{2,1,0:T(8,128)} %broadcast_in_dim.24), calls=%async_computation | async-start | bytes 589824 | tf_op jit(solution)/shard_map/all_to_all | solution.py:441
  21.9 18.4 %collective-permute-start.2 = (bf16[768,512]{1,0:T(8,128)(2,1)}, bf16[768,512]{1,0:T(8,128)(2,1)}, u32[]{:S(2)}, u32[]{:S(2)}) collective-permute-start(bf16[768,512]{1,0:T(8,128)(2,1)} %get-tuple-element.61.g0_ref), channel_id=1, source_target_pairs={{0,1},{1,0},{2,3},{3,2},{4,5},{5,4},{6,7},{7,6},{8,9},{9,8},{10,11... | collective-permute-start | bytes 2359304 | tf_op jit(solution)/shard_map/ppermute | solution.py:449
  22.1 18.2 %collective-permute-start.3 = (bf16[768,512]{1,0:T(8,128)(2,1)}, bf16[768,512]{1,0:T(8,128)(2,1)}, u32[]{:S(2)}, u32[]{:S(2)}) collective-permute-start(bf16[768,512]{1,0:T(8,128)(2,1)} %get-tuple-element.62.u0_ref), channel_id=1, source_target_pairs={{0,1},{1,0},{2,3},{3,2},{4,5},{5,4},{6,7},{7,6},{8,9},{9,8},{10,11... | collective-permute-start | bytes 2359304 | tf_op jit(solution)/shard_map/ppermute | solution.py:449
  23.0 0.7 copy-start.9
  28.0 5.2 %copy-start.12 = (bf16[512,2048]{1,0:T(8,128)(2,1)}, bf16[512,2048]{1,0:T(8,128)(2,1)S(1)}, u32[]{:S(2)}) copy-start(bf16[512,2048]{1,0:T(8,128)(2,1)S(1)} %collective-permute-done.1.w1_ref) | copy-start | bytes 6291460
  28.0 18.4 %all-to-all-start.1 = ((bf16[8,64,768]{2,1,0:T(8,128)(2,1)}), bf16[8,64,768]{2,1,0:T(8,128)(2,1)S(1)}, u32[]{:S(2)}, u32[]{:S(2)}) async-start(bf16[8,64,768]{2,1,0:T(8,128)(2,1)} %get-tuple-element.59), calls=%async_computation.1 | async-start | bytes 1572864 | tf_op jit(solution)/shard_map/all_to_all | solution.py:441
  46.4 0.9 copy-start.8
  53.5 16.5 %all-to-all-start.2 = ((bf16[8,64,768]{2,1,0:T(8,128)(2,1)}), bf16[8,64,768]{2,1,0:T(8,128)(2,1)S(1)}, u32[]{:S(2)}, u32[]{:S(2)}) async-start(bf16[8,64,768]{2,1,0:T(8,128)(2,1)} %get-tuple-element.70), calls=%async_computation.2 | async-start | bytes 1572864 | tf_op jit(solution)/shard_map/all_to_all | solution.py:441
  57.1 4.9 %copy-start.10 = (bf16[64,2048]{1,0:T(8,128)(2,1)S(1)}, bf16[64,2048]{1,0:T(8,128)(2,1)}, u32[]{:S(2)}) copy-start(bf16[64,2048]{1,0:T(8,128)(2,1)} %get-tuple-element.71) | copy-start | bytes 786436
  57.1 4.9 %copy-start.11 = (bf16[64,768]{1,0:T(8,128)(2,1)S(1)}, bf16[64,768]{1,0:T(8,128)(2,1)}, u32[]{:S(2)}) copy-start(bf16[64,768]{1,0:T(8,128)(2,1)} %get-tuple-element.72) | copy-start | bytes 294916
  61.5 10.2 %collective-permute-start.4 = (bf16[512,512]{1,0:T(8,128)(2,1)}, bf16[512,512]{1,0:T(8,128)(2,1)S(1)}, u32[]{:S(2)}, u32[]{:S(2)}) collective-permute-start(bf16[512,512]{1,0:T(8,128)(2,1)} %get-tuple-element.75), channel_id=1, source_target_pairs={{0,1},{1,0},{2,3},{3,2},{4,5},{5,4},{6,7},{7,6},{8,9},{9,8},{10,11... | collective-permute-start | bytes 1572872 | tf_op jit(solution)/shard_map/ppermute | solution.py:449
  61.5 10.2 %collective-permute-start.5 = (bf16[512,512]{1,0:T(8,128)(2,1)}, bf16[512,512]{1,0:T(8,128)(2,1)S(1)}, u32[]{:S(2)}, u32[]{:S(2)}) collective-permute-start(bf16[512,512]{1,0:T(8,128)(2,1)} %get-tuple-element.76), channel_id=1, source_target_pairs={{0,1},{1,0},{2,3},{3,2},{4,5},{5,4},{6,7},{7,6},{8,9},{9,8},{10,11... | collective-permute-start | bytes 1572872 | tf_op jit(solution)/shard_map/ppermute | solution.py:449
  64.5 23.8 %copy-start.1 = (bf16[512,768]{1,0:T(8,128)(2,1)S(1)}, bf16[512,768]{1,0:T(8,128)(2,1)}, u32[]{:S(2)}) copy-start(bf16[512,768]{1,0:T(8,128)(2,1)} %get-tuple-element.65.d0_ref.d_ref) | copy-start | bytes 2359300
  71.7 3.6 %copy-start.4 = (bf16[512,512]{1,0:T(8,128)(2,1)}, bf16[512,512]{1,0:T(8,128)(2,1)S(1)}, u32[]{:S(2)}) copy-start(bf16[512,512]{1,0:T(8,128)(2,1)S(1)} %collective-permute-done.4.a_ref) | copy-start | bytes 1572868
  71.7 5.1 %copy-start.6 = (bf16[512,512]{1,0:T(8,128)(2,1)}, bf16[512,512]{1,0:T(8,128)(2,1)S(1)}, u32[]{:S(2)}) copy-start(bf16[512,512]{1,0:T(8,128)(2,1)S(1)} %collective-permute-done.5.b_ref) | copy-start | bytes 1572868
  71.7 16.5 %all-to-all-start.3 = ((bf16[8,64,768]{2,1,0:T(8,128)(2,1)}), bf16[8,64,768]{2,1,0:T(8,128)(2,1)S(1)}, u32[]{:S(2)}, u32[]{:S(2)}) async-start(bf16[8,64,768]{2,1,0:T(8,128)(2,1)} %error.1), calls=%async_computation.3 | async-start | bytes 1572864 | tf_op jit(solution)/shard_map/all_to_all | solution.py:441
  76.7 14.9 %collective-permute-start.7 = (bf16[768,512]{1,0:T(8,128)(2,1)S(1)}, bf16[768,512]{1,0:T(8,128)(2,1)}, u32[]{:S(2)}, u32[]{:S(2)}) collective-permute-start(bf16[768,512]{1,0:T(8,128)(2,1)S(1)} %bitcast.18), channel_id=1, source_target_pairs={{0,1},{1,0},{2,3},{3,2},{4,5},{5,4},{6,7},{7,6},{8,9},{9,8},{10,11... | collective-permute-start | bytes 2359304 | tf_op jit(solution)/shard_map/ppermute | solution.py:449
  88.2 3.4 %collective-permute-start.6 = (bf16[8,64,768]{2,1,0:T(8,128)(2,1)S(1)}, bf16[8,64,768]{2,1,0:T(8,128)(2,1)S(1)}, u32[]{:S(2)}, u32[]{:S(2)}) collective-permute-start(bf16[8,64,768]{2,1,0:T(8,128)(2,1)S(1)} %all-to-all-done.3.err_ref), channel_id=1, source_target_pairs={{0,1},{1,0},{2,3},{3,2},{4,5},{5,4},{6,7},{7,6},{8,9},{9,8},{10,11... | collective-permute-start | bytes 2359304 | tf_op jit(solution)/shard_map/ppermute | solution.py:449
  88.3 1.0 copy-start.2
  89.3 1.0 copy-start.3
  90.3 1.3 copy-start.5
  90.3 1.3 copy-start.7
  126.1 1.2 copy-start
  127.3 26.9 %all-to-all-start.5 = ((bf16[8,96,1024]{2,1,0:T(8,128)(2,1)}), bf16[8,96,1024]{2,1,0:T(8,128)(2,1)S(1)}, u32[]{:S(2)}, u32[]{:S(2)}) async-start(bf16[8,96,1024]{2,1,0:T(8,128)(2,1)} %copy-done), calls=%async_computation.5 | async-start | bytes 3145728 | tf_op jit(solution)/shard_map/all_to_all | solution.py:441
  134.9 0.7 copy-start.13

commit v5 on v4

--- a/solution.py
+++ b/solution.py
@@ -26,6 +26,9 @@
 ALL = GRP + DEV
 PAIRS = [(s, t) for s in range(2, STEPS) for t in range(1, s)]
 SWAP = [(0, 1), (1, 0)]
+SHIFTS = (1, 3, 2)
+SENT = [(flip, d) for flip in (1, 0) for d in SHIFTS + (0,)]
+GOT = [(0, 0), (1, 0)] + [(flip, d) for flip in (0, 1) for d in SHIFTS]
 
 
 def nt(left, right, precision=None):
@@ -312,10 +315,14 @@
     dg_ref[...], du_ref[...] = hidden_grads(errb, db, ab, bb, copies)
 
 
-def other_kernel(
-    err_ref, d_ref, a_ref, b_ref, x0_ref, dg_ref, du_ref, x1_ref, y_ref,
-    errb, db, ab, bb, x0b, dgb, dub, x1b, sem,
-):
+def group_block(flip, shift):
+    y, zh = lax.axis_index("y"), lax.axis_index("zh")
+    zh = 1 - zh if flip else zh
+    return lax.rem(y + shift + 4, 4) * 2 + zh
+
+
+def other_kernel(err_ref, d_ref, a_ref, b_ref, x0_ref, dg_ref, du_ref, x1_ref, *refs):
+    outs, (errb, db, ab, bb, x0b, dgb, dub, x1b, yb, sem, out_sem) = refs[: len(SENT)], refs[len(SENT) :]
     copies = fetch(
         (err_ref, d_ref, a_ref, b_ref, x0_ref, dg_ref, du_ref, x1_ref),
         (errb, db, ab, bb, x0b, dgb, dub, x1b),
@@ -325,27 +332,31 @@
     for c in copies[4:]:
         c.wait()
     width, tall = dgate.shape[1], 256
-    for i in range(y_ref.shape[0] // tall):
+    for i in range(yb.shape[0] // tall):
         at = pl.ds(i * tall, tall)
-        y_ref[at, :width] = (dot(x0b[at], dgb[...]) + dot(x1b[at], dgate)).astype(BF16)
-        y_ref[at, width:] = (dot(x0b[at], dub[...]) + dot(x1b[at], dup)).astype(BF16)
-
-
-def sum_kernel(parts_ref, out_ref):
-    total = parts_ref[0].astype(F32)
-    for d in range(1, parts_ref.shape[0]):
-        total = total + parts_ref[d].astype(F32)
-    total = total.astype(BF16)
-    for d in range(out_ref.shape[0]):
-        out_ref[d] = total
-
-
-def last_kernel(yg_ref, yu_ref, w_ref, gate_ref, up_ref):
-    for y_ref, out_ref in ((yg_ref, gate_ref), (yu_ref, up_ref)):
-        y = y_ref[...].reshape(w_ref.shape[0], out_ref.shape[1])
-        out_ref[...] = lax.dot_general(
-            w_ref[...], y, (((0,), (0,)), ((), ())), preferred_element_type=F32
-        )
+        yb[at, :width] = (dot(x0b[at], dgb[...]) + dot(x1b[at], dgate)).astype(BF16)
+        yb[at, width:] = (dot(x0b[at], dub[...]) + dot(x1b[at], dup)).astype(BF16)
+    rows, sends = outs[0].shape[0], []
+    for i, (flip, d) in enumerate(SENT):
+        at = pl.ds(pl.multiple_of(group_block(flip, d) * rows, rows), rows)
+        sends.append(pltpu.make_async_copy(yb.at[at], outs[i], out_sem.at[i]))
+        sends[-1].start()
+    for c in sends:
+        c.wait()
+
+
+def last_kernel(w_ref, *refs):
+    parts, (gate_ref, up_ref, wb, yb, sem, y_sem) = refs[: len(GOT)], refs[len(GOT) :]
+    rows = parts[0].shape[0]
+    slots = [pl.ds(i * rows, rows) for i in range(len(GOT))]
+    blocks = [pl.ds(pl.multiple_of(group_block(flip, -d) * rows, rows), rows) for flip, d in GOT]
+    copies = fetch([w_ref.at[b] for b in blocks], [wb.at[i] for i in slots], sem)
+    copies += fetch(parts, [yb.at[i] for i in slots], y_sem)
+    for c in copies:
+        c.wait()
+    width = gate_ref.shape[1]
+    gate_ref[...] = tn(wb[...], yb[:, :width])
+    up_ref[...] = tn(wb[...], yb[:, width:])
 
 
 VM = pl.BlockSpec(memory_space=pltpu.VMEM)
@@ -445,8 +456,23 @@
     return jnp.dot(left, right, preferred_element_type=F32)
 
 
-def swap(x):
-    return lax.ppermute(x, "core", SWAP)
+def tn(left, right):
+    return lax.dot_general(left, right, (((0,), (0,)), ((), ())), preferred_element_type=F32)
+
+
+def swap(x, axis="core"):
+    return lax.ppermute(x, axis, SWAP)
+
+
+def shift(x, d):
+    return lax.ppermute(x, "y", [(i, (i + d) % 4) for i in range(4)])
+
+
+def total(first, *others):
+    out = first.astype(F32)
+    for o in others:
+        out = out + o.astype(F32)
+    return out.astype(BF16)
 
 
 def after(x, *others):
@@ -524,27 +550,25 @@
     err = exchange(err_own, CHIP)
     err_other = swap(err)
     dg, du = staged(
-        own_kernel, "own", (err, down_w, slope_a, slope_b), (slope, slope), [], 400000000, (4,), (VM,) * 2, params=MIDDLE,
-    )
-    feat_grads = staged(
+        own_kernel, "own", (err, down_w, slope_a, slope_b), (slope, slope), [], 400000000, (4,), (VM,) * 2,
+    )
+    piece = sds((FEATS // groups, 2 * width), BF16)
+    pieces = staged(
         other_kernel, "other", (err_other, down_w, slope_ao, slope_bo, x_late, dg, du, x_other),
-        sds((FEATS, 2 * width), BF16), [], 2000000000, (8,), params=MIDDLE,
-    )
-    feat_grads = exchange(feat_grads.reshape(groups, FEATS // groups, 2 * width), GRP)
-    feat_grads = pl.pallas_call(
-        sum_kernel, grid=(4,), out_shape=sds(feat_grads.shape, BF16), in_specs=[cut(feat_grads.shape, 4)],
-        out_specs=cut(feat_grads.shape, 4), compiler_params=SMALL, name="total",
-    )(feat_grads)
-    feat_grads, err_late, err_other = lax.optimization_barrier((feat_grads, err, err_other))
-    feat_grads = exchange(feat_grads, GRP)
+        (piece,) * len(SENT), [pltpu.VMEM((FEATS, 2 * width), BF16)], 2000000000, (8, len(SENT)),
+        (HB,) * len(SENT),
+    )
+    moved = [shift(p, d) if d else p for p, (_, d) in zip(pieces, SENT)]
+    theirs = swap(total(*moved[:4]), "zh")
+    grads = total(*moved[4:], theirs)
+    grads, err_late, err_other = lax.optimization_barrier((grads, err, err_other))
+    twin = swap(grads, "zh")
+    got = [grads, twin] + [shift(v, d) for v in (grads, twin) for d in SHIFTS]
     grad = sds((block, width), F32)
-    grad_gate, grad_up = pl.pallas_call(
-        last_kernel, grid=(2,), out_shape=(grad, grad),
-        in_specs=[
-            cut(feat_grads.shape, 4), cut(feat_grads.shape, 4, 2), pl.BlockSpec(w_own.shape, lambda i: (0, 0))
-        ],
-        out_specs=(cut(grad.shape, 2),) * 2, compiler_params=SMALL, name="last",
-    )(feat_grads, feat_grads, w_own)
+    grad_gate, grad_up = staged(
+        last_kernel, "last", (w_own, *got), (grad, grad), [], 400000000, (len(GOT),) * 2, (VM,) * 2,
+        bufs=[vmem_like(w_own), pltpu.VMEM((FEATS, 2 * width), BF16)], params=MIDDLE,
+    )
     err_all = jnp.concatenate([err_late, err_other], axis=0).reshape(2 * half, FEATS)
     core = lax.axis_index("core")
     codes = recv[:, CODE_ROW : CODE_ROW + 2, :COUNT]

time: 157 us -> 150 us (0.955)
  blocking collectives: 30.4 us -> 0 us
  starting transfers between devices: 23.5 us -> 50.2 us
  waiting for transfers between devices: 42.3 us -> 35.4 us
  Pallas kernels: 42.9 us -> 48.6 us
  local copies, waits for them, and re-layouts: 10.2 us -> 6.33 us
  other arithmetic: 2.28 us -> 3.9 us
    all_to_all x1 -> x0, blocking collectives: 30.4 us -> none  [exchange(): return lax.all_to_all(x, axes, split_axis=0, concat_axis=0, tiled=True)]
    ppermute x8 -> x22, starting transfers between devices: 1.84 us -> 32.1 us  [the longest x12 23.4 us: shift(): return lax.ppermute(x, 'y', [(i, (i + d) % 4) for i in range(4)])]
    all_to_all x5 -> x4, waiting for transfers between devices: 41.2 us -> 24.7 us  [exchange(): return lax.all_to_all(x, axes, split_axis=0, concat_axis=0, tiled=True)]
    ppermute x8 -> x22, waiting for transfers between devices: 1.09 us -> 10.7 us  [the longest x12 8.46 us: shift(): return lax.ppermute(x, 'y', [(i, (i + d) % 4) for i in range(4)])]
    pallas_call x5 -> x6, Pallas kernels: 24.9 us -> 33.2 us  [staged(): pl.pallas_call(kernel, out_shape=out_shape, in_specs=[HB] * len(args), ou...]
    all_to_all x5 -> x4, starting transfers between devices: 21.7 us -> 18.1 us  [exchange(): return lax.all_to_all(x, axes, split_axis=0, concat_axis=0, tiled=True)]
    unnamed x28 -> x26, local copies, waits for them, and re-layouts: 5.35 us -> 2.66 us
    pallas_call x2 -> x0, Pallas kernels: 2.52 us -> none  [the longest x1 1.87 us: body(): pl.pallas_call(last_kernel, grid=(2,), out_shape=(grad, grad), in_specs=[...]
  transfers between devices with their start and end apart: 13 -> 26, of which waited for: 6 -> 13; matrix products, arithmetic and copies ran while one was open for 7% -> 7% of each run, Pallas kernels for 20% -> 22%
where the time goes in v5:
time: 150 us; the launch traced here: 149 us
  starting transfers between devices  50.2 us (33%)
  Pallas kernels  48.6 us (32%)
  waiting for transfers between devices  35.4 us (24%)
  local copies, waits for them, and re-layouts  6.33 us (4%)
  other arithmetic  3.9 us (3%)
  matrix products  3.65 us (2%)
    pallas_call x6, Pallas kernels, staged(): pl.pallas_call(kernel, out_shape=out_shape, in_specs=[HB] * len(args), ou...  33.2 us
    all_to_all x4, waiting for transfers between devices, exchange(): return lax.all_to_all(x, axes, split_axis=0, concat_axis=0, tiled=True)  24.7 us
    ppermute x12, starting transfers between devices, shift(): return lax.ppermute(x, 'y', [(i, (i + d) % 4) for i in range(4)])  23.4 us
    all_to_all x4, starting transfers between devices, exchange(): return lax.all_to_all(x, axes, split_axis=0, concat_axis=0, tiled=True)  18.1 us
    ppermute x10, starting transfers between devices, swap(): return lax.ppermute(x, axis, SWAP)  8.78 us
    ppermute x12, waiting for transfers between devices, shift(): return lax.ppermute(x, 'y', [(i, (i + d) % 4) for i in range(4)])  8.46 us
    pallas_call x1, Pallas kernels, evolve(): pl.pallas_call(evolve_kernel, out_shape=(sds((ROWS, LANES), F32), sds((2...  5.24 us
    pallas_call x1, Pallas kernels, body(): pl.pallas_call(slopes_kernel, grid=(4,), out_shape=(slope,) * 4, in_specs...  4.34 us
  transfers between devices with their start and end apart: 26, of which 13 were waited for; matrix products, arithmetic and copies ran while one was open for 7% of the time, Pallas kernels for 22%

profile of v5, /device:TPU:0, one launch (start us, length us, event | category | flops | bytes accessed | tf_op | source)
XLA Modules:
  0.0 149.3 jit_solution(7804798655450012674)
XLA Ops:
  0.6 0.1 collective-permute-start.1
  0.7 5.2 %evolve.1 = (f32[72,128]{1,0:T(8,128)}, bf16[128,768]{1,0:T(8,128)(2,1)}, f32[24,128]{1,0:T(8,128)}, f32[3,256,128]{2,1,0:T(8,128)}) custom-call(f32[3,256,128]{2,1,0:T(8,128)} %pos_ref.3, f32[3,256,128]{2,1,0:T(8,128)} %vel_ref.3, f32[1,128]{1,0:T(1,128)} %bitcast.23, s32[8,256,128]{2,1,0:T(8,128)} %contact_ref.3, f32[3,128]{1,0:T(4,128)} %off_ref.3, ...), custom_call_target="tpu_custom_call" | custom-call | flops 260000000 | bytes 3000000 | tf_op jit(solution)/shard_map/evolve/pallas_call | solution.py:375
  6.0 0.6 collective-permute-start
  6.5 1.1 collective-permute-done
  7.6 0.8 add.110
  8.4 0.7 broadcast_in_dim.24
  9.1 5.7 %all-to-all-start = ((f32[8,72,128]{2,1,0:T(8,128)}), f32[8,72,128]{2,1,0:T(8,128)S(1)}, u32[]{:S(2)}, u32[]{:S(2)}) async-start(f32[8,72,128]{2,1,0:T(8,128)} %broadcast_in_dim.24), calls=%async_computation | async-start | bytes 589824 | tf_op jit(solution)/shard_map/all_to_all | solution.py:452
  14.9 7.1 %products.1 = (bf16[768,512]{1,0:T(8,128)(2,1)}, bf16[768,512]{1,0:T(8,128)(2,1)}) custom-call(bf16[768,2048]{1,0:T(8,128)(2,1)} %w_in_ref.2, f32[1,2048]{1,0:T(1,128)} %bitcast.30, bf16[2048,512]{1,0:T(8,128)(2,1)} %gate_ref.1, bf16[2048,512]{1,0:T(8,128)(2,1)} %up_ref.1), custom_call_target="tpu_custom_call" | custom-call | flops 3300000000 | bytes 8000000 | tf_op jit(solution)/shard_map/products/pallas_call | solution.py:434
  21.9 0.1 collective-permute-start.2
  22.1 0.4 collective-permute-start.3
  22.5 0.5 all-to-all-done.recv_ref
  23.0 0.7 copy-done.4
  23.7 4.2 %finish.1 = (bf16[8,64,768]{2,1,0:T(8,128)(2,1)}, bf16[64,768]{1,0:T(8,128)(2,1)}, bf16[64,2048]{1,0:T(8,128)(2,1)}, f32[3,128]{1,0:T(4,128)}, f32[3,256,128]{2,1,0:T(8,128)}) custom-call(f32[8,72,128]{2,1,0:T(8,128)} %copy-done.4, f32[24,128]{1,0:T(8,128)} %get-tuple-element.59.bound_ref, ...), custom_call_target="tpu_custom_call", output_to_operand_aliasing={{4}: (18, {})} | custom-call | flops 300000000 | bytes 4000000 | tf_op jit(solution)/shard_map/finish/pallas_call | solution.py:408
  28.0 0.0 collective-permute-done.1.w1_ref
  28.0 5.2 %all-to-all-start.1 = ((bf16[8,64,768]{2,1,0:T(8,128)(2,1)}), bf16[8,64,768]{2,1,0:T(8,128)(2,1)S(1)}, u32[]{:S(2)}, u32[]{:S(2)}) async-start(bf16[8,64,768]{2,1,0:T(8,128)(2,1)} %get-tuple-element.67), calls=%async_computation.1 | async-start | bytes 1572864 | tf_op jit(solution)/shard_map/all_to_all | solution.py:452
  33.2 7.0 %down.1 = (bf16[512,768]{1,0:T(8,128)(2,1)}, bf16[512,768]{1,0:T(8,128)(2,1)}) custom-call(bf16[512,2048]{1,0:T(8,128)(2,1)} %w0_ref, bf16[512,2048]{1,0:T(8,128)(2,1)} %copy-done.10, bf16[2048,768]{1,0:T(8,128)(2,1)} %out_ref.1), custom_call_target="tpu_custom_call" | custom-call | flops 3300000000 | bytes 8000000 | tf_op jit(solution)/shard_map/down/pallas_call | solution.py:434
  40.3 6.1 %all-to-all-done.1.x_ref = bf16[8,64,768]{2,1,0:T(8,128)(2,1)S(1)} async-done(((bf16[8,64,768]{2,1,0:T(8,128)(2,1)}), bf16[8,64,768]{2,1,0:T(8,128)(2,1)S(1)}, u32[]{:S(2)}, u32[]{:S(2)}) %all-to-all-start.1) | async-done | bytes 786464 | tf_op jit(solution)/shard_map/all_to_all | solution.py:452
  46.4 0.9 copy-done.2
  47.3 6.2 %forward.1 = (bf16[8,64,768]{2,1,0:T(8,128)(2,1)}, f32[2,512,512]{2,1,0:T(8,128)}, f32[2,512,512]{2,1,0:T(8,128)}) custom-call(bf16[8,64,768]{2,1,0:T(8,128)(2,1)} %copy-done.2, bf16[768,512]{1,0:T(8,128)(2,1)} %get-tuple-element.69.g0_ref, bf16[768,512]{1,0:T(8,128)(2,1)} %get-tuple-element.70.u0_ref, bf16[512,768]{1,0:T(8,128)(2,1)} %get-tuple-element.73.d0_ref.d_ref, ...), custom_call_target="tpu_custom_call" | custom-call | flops 2500000000 | bytes 8000000 | tf_op jit(solution)/shard_map/forward/pallas_call | solution.py:434
  53.5 3.6 %all-to-all-start.2 = ((bf16[8,64,768]{2,1,0:T(8,128)(2,1)}), bf16[8,64,768]{2,1,0:T(8,128)(2,1)S(1)}, u32[]{:S(2)}, u32[]{:S(2)}) async-start(bf16[8,64,768]{2,1,0:T(8,128)(2,1)} %get-tuple-element.78), calls=%async_computation.2 | async-start | bytes 1572864 | tf_op jit(solution)/shard_map/all_to_all | solution.py:452
  57.1 4.3 %slopes.1 = (bf16[512,512]{1,0:T(8,128)(2,1)}, bf16[512,512]{1,0:T(8,128)(2,1)}, bf16[512,512]{1,0:T(8,128)(2,1)}, bf16[512,512]{1,0:T(8,128)(2,1)}) custom-call(f32[2,512,512]{2,1,0:T(8,128)} %get-tuple-element.81.gate_ref, f32[2,512,512]{2,1,0:T(8,128)} %get-tuple-element.82.up_ref), custom_call_target="tpu_custom_call" | custom-call | flops 8000000 | bytes 6000000 | tf_op jit(solution)/shard_map/slopes/pallas_call | solution.py:530
  61.4 0.5 collective-permute-start.5
  61.9 2.5 %convolution_subtract_fusion.base_ref = f32[64,768]{1,0:T(8,128)S(1)} fusion(bf16[64,2048]{1,0:T(8,128)(2,1)S(1)} %copy-done.8, bf16[2048,768]{1,0:T(8,128)(2,1)} %out_ref.1, bf16[64,768]{1,0:T(8,128)(2,1)S(1)} %copy-done.9), kind=kOutput, calls=%fused_computation.2 | convolution fusion | flops 201424896 | bytes 3702784 | tf_op jit(solution)/shard_map/dot_general | solution.py:456
  64.5 5.6 %all-to-all-done.2.parts_ref = bf16[8,64,768]{2,1,0:T(8,128)(2,1)S(1)} async-done(((bf16[8,64,768]{2,1,0:T(8,128)(2,1)}), bf16[8,64,768]{2,1,0:T(8,128)(2,1)S(1)}, u32[]{:S(2)}, u32[]{:S(2)}) %all-to-all-start.2) | async-done | bytes 786464 | tf_op jit(solution)/shard_map/all_to_all | solution.py:452
  70.0 1.6 %error.1 = bf16[8,64,768]{2,1,0:T(8,128)(2,1)} custom-call(bf16[8,64,768]{2,1,0:T(8,128)(2,1)S(1)} %all-to-all-done.2.parts_ref, f32[64,768]{1,0:T(8,128)S(1)} %convolution_subtract_fusion.base_ref), custom_call_target="tpu_custom_call" | custom-call | tf_op jit(solution)/shard_map/error/pallas_call | solution.py:544
  71.7 3.6 %all-to-all-start.3 = ((bf16[8,64,768]{2,1,0:T(8,128)(2,1)}), bf16[8,64,768]{2,1,0:T(8,128)(2,1)S(1)}, u32[]{:S(2)}, u32[]{:S(2)}) async-start(bf16[8,64,768]{2,1,0:T(8,128)(2,1)} %error.1), calls=%async_computation.3 | async-start | bytes 1572864 | tf_op jit(solution)/shard_map/all_to_all | solution.py:452
  75.2 0.3 copy.29
  75.5 0.1 collective-permute-start.7
  75.6 12.6 %all-to-all-done.3.err_ref = bf16[8,64,768]{2,1,0:T(8,128)(2,1)S(1)} async-done(((bf16[8,64,768]{2,1,0:T(8,128)(2,1)}), bf16[8,64,768]{2,1,0:T(8,128)(2,1)S(1)}, u32[]{:S(2)}, u32[]{:S(2)}) %all-to-all-start.3) | async-done | bytes 786464 | tf_op jit(solution)/shard_map/all_to_all | solution.py:452
  88.2 0.8 dynamic_slice.7
  89.0 0.1 copy-done
  89.1 3.2 %own.1 = (bf16[512,512]{1,0:T(8,128)(2,1)}, bf16[512,512]{1,0:T(8,128)(2,1)}) custom-call(bf16[8,64,768]{2,1,0:T(8,128)(2,1)} %copy-done, bf16[512,768]{1,0:T(8,128)(2,1)} %get-tuple-element.73.d0_ref.d_ref, bf16[512,512]{1,0:T(8,128)(2,1)} %get-tuple-element.91.a_ref, bf16[512,512]{1,0:T(8,128)(2,1)} %get-tuple-element.92.b_ref), custom_call_target="tpu_custom_call" | custom-call | flops 400000000 | bytes 8000000 | tf_op jit(solution)/shard_map/own/pallas_call | solution.py:434
  92.3 0.9 copy-done.6
  93.2 5.5 %other.1 = (bf16[96,1024]{1,0:T(8,128)(2,1)}, bf16[96,1024]{1,0:T(8,128)(2,1)}, bf16[96,1024]{1,0:T(8,128)(2,1)}, bf16[96,1024]{1,0:T(8,128)(2,1)}, bf16[96,1024...) custom-call(bf16[8,64,768]{2,1,0:T(8,128)(2,1)} %copy-done.6, ...), custom_call_target="tpu_custom_call" | custom-call | flops 2000000000 | bytes 8000000 | tf_op jit(solution)/shard_map/other/pallas_call | solution.py:434
  98.8 1.7 %collective-permute-start.11 = (bf16[96,1024]{1,0:T(8,128)(2,1)}, bf16[96,1024]{1,0:T(8,128)(2,1)S(1)}, u32[]{:S(2)}, u32[]{:S(2)}) collective-permute-start(bf16[96,1024]{1,0:T(8,128)(2,1)} %get-tuple-element.99), channel_id=1, source_target_pairs={{0,32},{32,64},{64,96},{96,0},{1,33},{33,65},{65,97},{97,1},{2,34}... | collective-permute-start | bytes 589832 | tf_op jit(solution)/shard_map/ppermute | solution.py:468
  100.4 1.7 %collective-permute-start.12 = (bf16[96,1024]{1,0:T(8,128)(2,1)}, bf16[96,1024]{1,0:T(8,128)(2,1)S(1)}, u32[]{:S(2)}, u32[]{:S(2)}) collective-permute-start(bf16[96,1024]{1,0:T(8,128)(2,1)} %get-tuple-element.100), channel_id=1, source_target_pairs={{0,96},{32,0},{64,32},{96,64},{1,97},{33,1},{65,33},{97,65},{2,98}... | collective-permute-start | bytes 589832 | tf_op jit(solution)/shard_map/ppermute | solution.py:468
  102.1 2.0 %collective-permute-start.13 = (bf16[96,1024]{1,0:T(8,128)(2,1)}, bf16[96,1024]{1,0:T(8,128)(2,1)S(1)}, u32[]{:S(2)}, u32[]{:S(2)}) collective-permute-start(bf16[96,1024]{1,0:T(8,128)(2,1)} %get-tuple-element.101), channel_id=1, source_target_pairs={{0,64},{32,96},{64,0},{96,32},{1,65},{33,97},{65,1},{97,33},{2,66}... | collective-permute-start | bytes 589832 | tf_op jit(solution)/shard_map/ppermute | solution.py:468
  104.1 0.8 slice.4
  104.9 1.0 collective-permute-start.8
  105.8 2.6 %collective-permute-start.9 = (bf16[96,1024]{1,0:T(8,128)(2,1)}, bf16[96,1024]{1,0:T(8,128)(2,1)S(1)}, u32[]{:S(2)}, u32[]{:S(2)}) collective-permute-start(bf16[96,1024]{1,0:T(8,128)(2,1)} %get-tuple-element.96), channel_id=1, source_target_pairs={{0,96},{32,0},{64,32},{96,64},{1,97},{33,1},{65,33},{97,65},{2,98}... | collective-permute-start | bytes 589832 | tf_op jit(solution)/shard_map/ppermute | solution.py:468
  108.4 5.5 %collective-permute-start.10 = (bf16[96,1024]{1,0:T(8,128)(2,1)}, bf16[96,1024]{1,0:T(8,128)(2,1)S(1)}, u32[]{:S(2)}, u32[]{:S(2)}) collective-permute-start(bf16[96,1024]{1,0:T(8,128)(2,1)} %get-tuple-element.97), channel_id=1, source_target_pairs={{0,64},{32,96},{64,0},{96,32},{1,65},{33,97},{65,1},{97,33},{2,66}... | collective-permute-start | bytes 589832 | tf_op jit(solution)/shard_map/ppermute | solution.py:468
  113.9 1.0 add_convert_fusion.1
  114.9 3.7 %collective-permute-start.14 = (bf16[96,1024]{1,0:T(8,128)(2,1)S(1)}, bf16[96,1024]{1,0:T(8,128)(2,1)S(1)}, u32[]{:S(2)}, u32[]{:S(2)}) collective-permute-start(bf16[96,1024]{1,0:T(8,128)(2,1)S(1)} %add_convert_fusion.1), channel_id=1, source_target_pairs={{0,16},{16,0},{1,17},{17,1},{2,18},{18,2},{3,19},{19,3},{4,20},{20... | collective-permute-start | bytes 589832 | tf_op jit(solution)/shard_map/ppermute | solution.py:464
  118.6 0.8 select_bitcast_fusion
  119.4 0.1 eq.40
  119.5 1.0 constant_dynamic-slice_fusion
  120.5 0.8 collective-permute-done.10
  121.4 0.9 collective-permute-done.14
  122.3 1.1 add_convert_fusion.refs_0_
  123.4 0.7 collective-permute-start.18
  124.1 3.2 %collective-permute-start.15 = (bf16[96,1024]{1,0:T(8,128)(2,1)S(1)}, bf16[96,1024]{1,0:T(8,128)(2,1)S(1)}, u32[]{:S(2)}, u32[]{:S(2)}) collective-permute-start(bf16[96,1024]{1,0:T(8,128)(2,1)S(1)} %add_convert_fusion.refs_0_), channel_id=1, source_target_pairs={{0,16},{16,0},{1,17},{17,1},{2,18},{18,2},{3,19},{19,3},{4,20},{20... | collective-permute-start | bytes 589832 | tf_op jit(solution)/shard_map/ppermute | solution.py:464
  127.3 0.1 multiply_convert_fusion.w_ref
  127.4 3.4 %collective-permute-start.17 = (bf16[96,1024]{1,0:T(8,128)(2,1)S(1)}, bf16[96,1024]{1,0:T(8,128)(2,1)S(1)}, u32[]{:S(2)}, u32[]{:S(2)}) collective-permute-start(bf16[96,1024]{1,0:T(8,128)(2,1)S(1)} %add_convert_fusion.refs_0_), channel_id=1, source_target_pairs={{0,96},{32,0},{64,32},{96,64},{1,97},{33,1},{65,33},{97,65},{2,98}... | collective-permute-start | bytes 589832 | tf_op jit(solution)/shard_map/ppermute | solution.py:468
  130.8 0.1 pad_maximum_fusion
  131.0 0.3 collective-permute-done.15.refs_1_
  131.2 2.9 %collective-permute-start.21 = (bf16[96,1024]{1,0:T(8,128)(2,1)S(1)}, bf16[96,1024]{1,0:T(8,128)(2,1)S(1)}, u32[]{:S(2)}, u32[]{:S(2)}) collective-permute-start(bf16[96,1024]{1,0:T(8,128)(2,1)S(1)} %collective-permute-done.15.refs_1_), channel_id=1, source_target_pairs={{0,64},{32,96},{64,0},{96,32},{1,65},{33,97},{65,1},{97,33},{2,66}... | collective-permute-start | bytes 589832 | tf_op jit(solution)/shard_map/ppermute | solution.py:468
  134.1 2.0 %collective-permute-start.20 = (bf16[96,1024]{1,0:T(8,128)(2,1)S(1)}, bf16[96,1024]{1,0:T(8,128)(2,1)S(1)}, u32[]{:S(2)}, u32[]{:S(2)}) collective-permute-start(bf16[96,1024]{1,0:T(8,128)(2,1)S(1)} %collective-permute-done.15.refs_1_), channel_id=1, source_target_pairs={{0,96},{32,0},{64,32},{96,64},{1,97},{33,1},{65,33},{97,65},{2,98}... | collective-permute-start | bytes 589832 | tf_op jit(solution)/shard_map/ppermute | solution.py:468
  136.2 1.1 convolution_convert_fusion
  137.3 0.1 collective-permute-done.17.refs_3_
  137.4 2.5 %collective-permute-done.16.refs_2_ = bf16[96,1024]{1,0:T(8,128)(2,1)S(1)} collective-permute-done((bf16[96,1024]{1,0:T(8,128)(2,1)S(1)}, bf16[96,1024]{1,0:T(8,128)(2,1)S(1)}, u32[]{:S(2)}, u32[]{:S(2)}) %collective-permute-start.16) | collective-permute-done | bytes 196640 | tf_op jit(solution)/shard_map/ppermute | solution.py:468
  139.9 1.9 %collective-permute-done.21.refs_7_ = bf16[96,1024]{1,0:T(8,128)(2,1)S(1)} collective-permute-done((bf16[96,1024]{1,0:T(8,128)(2,1)S(1)}, bf16[96,1024]{1,0:T(8,128)(2,1)S(1)}, u32[]{:S(2)}, u32[]{:S(2)}) %collective-permute-start.21) | collective-permute-done | bytes 196640 | tf_op jit(solution)/shard_map/ppermute | solution.py:468
  141.8 0.8 collective-permute-done.20.refs_6_
  142.6 2.3 %collective-permute-done.19.refs_5_ = bf16[96,1024]{1,0:T(8,128)(2,1)S(1)} collective-permute-done((bf16[96,1024]{1,0:T(8,128)(2,1)S(1)}, bf16[96,1024]{1,0:T(8,128)(2,1)S(1)}, u32[]{:S(2)}, u32[]{:S(2)}) %collective-permute-start.19) | collective-permute-done | bytes 196640 | tf_op jit(solution)/shard_map/ppermute | solution.py:468
  144.9 4.2 %last.1 = (f32[256,512]{1,0:T(8,128)}, f32[256,512]{1,0:T(8,128)}) custom-call(bf16[768,256]{1,0:T(8,128)(2,1)S(1)} %multiply_convert_fusion.w_ref, bf16[96,1024]{1,0:T(8,128)(2,1)S(1)} %add_convert_fusion.refs_0_, bf16[96,1024]{1,0:T(8,128)(2,1)S(1)} %collective-permute-done.15.refs_1_, bf16[96,1024]{1,0:T(8,128)(2,1)S(1)} %collective-permute-done.16.refs_2_, ...), custom_call_target="tpu_custom_call" | custom-call | flops 400000000 | bytes 8000000 | tf_op jit(solution)/shard_map/last/pallas_call | solution.py:434
  (42 shorter events, 0.1 us)
Async XLA Ops:
  0.6 27.3 %collective-permute-start.1 = (bf16[512,2048]{1,0:T(8,128)(2,1)}, bf16[512,2048]{1,0:T(8,128)(2,1)S(1)}, u32[]{:S(2)}, u32[]{:S(2)}) collective-permute-start(bf16[512,2048]{1,0:T(8,128)(2,1)} %w0_ref), channel_id=1, source_target_pairs={{0,1},{1,0},{2,3},{3,2},{4,5},{5,4},{6,7},{7,6},{8,9},{9,8},{10,11... | collective-permute-start | bytes 6291464 | tf_op jit(solution)/shard_map/ppermute | solution.py:464
  6.0 1.6 %collective-permute-start = (f32[72,128]{1,0:T(8,128)}, f32[72,128]{1,0:T(8,128)S(1)}, u32[]{:S(2)}, u32[]{:S(2)}) collective-permute-start(f32[72,128]{1,0:T(8,128)} %get-tuple-element.57), channel_id=1, source_target_pairs={{0,1},{1,0},{2,3},{3,2},{4,5},{5,4},{6,7},{7,6},{8,9},{9,8},{10,11... | collective-permute-start | bytes 110600 | tf_op jit(solution)/shard_map/ppermute | solution.py:464
  9.1 13.9 %all-to-all-start = ((f32[8,72,128]{2,1,0:T(8,128)}), f32[8,72,128]{2,1,0:T(8,128)S(1)}, u32[]{:S(2)}, u32[]{:S(2)}) async-start(f32[8,72,128]{2,1,0:T(8,128)} %broadcast_in_dim.24), calls=%async_computation | async-start | bytes 589824 | tf_op jit(solution)/shard_map/all_to_all | solution.py:452
  21.9 18.3 %collective-permute-start.2 = (bf16[768,512]{1,0:T(8,128)(2,1)}, bf16[768,512]{1,0:T(8,128)(2,1)}, u32[]{:S(2)}, u32[]{:S(2)}) collective-permute-start(bf16[768,512]{1,0:T(8,128)(2,1)} %get-tuple-element.69.g0_ref), channel_id=1, source_target_pairs={{0,1},{1,0},{2,3},{3,2},{4,5},{5,4},{6,7},{7,6},{8,9},{9,8},{10,11... | collective-permute-start | bytes 2359304 | tf_op jit(solution)/shard_map/ppermute | solution.py:464
  22.1 18.2 %collective-permute-start.3 = (bf16[768,512]{1,0:T(8,128)(2,1)}, bf16[768,512]{1,0:T(8,128)(2,1)}, u32[]{:S(2)}, u32[]{:S(2)}) collective-permute-start(bf16[768,512]{1,0:T(8,128)(2,1)} %get-tuple-element.70.u0_ref), channel_id=1, source_target_pairs={{0,1},{1,0},{2,3},{3,2},{4,5},{5,4},{6,7},{7,6},{8,9},{9,8},{10,11... | collective-permute-start | bytes 2359304 | tf_op jit(solution)/shard_map/ppermute | solution.py:464
  23.0 0.7 copy-start.4
  28.0 5.3 %copy-start.10 = (bf16[512,2048]{1,0:T(8,128)(2,1)}, bf16[512,2048]{1,0:T(8,128)(2,1)S(1)}, u32[]{:S(2)}) copy-start(bf16[512,2048]{1,0:T(8,128)(2,1)S(1)} %collective-permute-done.1.w1_ref) | copy-start | bytes 6291460
  28.0 18.4 %all-to-all-start.1 = ((bf16[8,64,768]{2,1,0:T(8,128)(2,1)}), bf16[8,64,768]{2,1,0:T(8,128)(2,1)S(1)}, u32[]{:S(2)}, u32[]{:S(2)}) async-start(bf16[8,64,768]{2,1,0:T(8,128)(2,1)} %get-tuple-element.67), calls=%async_computation.1 | async-start | bytes 1572864 | tf_op jit(solution)/shard_map/all_to_all | solution.py:452
  46.4 0.9 copy-start.2
  53.5 16.5 %all-to-all-start.2 = ((bf16[8,64,768]{2,1,0:T(8,128)(2,1)}), bf16[8,64,768]{2,1,0:T(8,128)(2,1)S(1)}, u32[]{:S(2)}, u32[]{:S(2)}) async-start(bf16[8,64,768]{2,1,0:T(8,128)(2,1)} %get-tuple-element.78), calls=%async_computation.2 | async-start | bytes 1572864 | tf_op jit(solution)/shard_map/all_to_all | solution.py:452
  57.1 4.9 %copy-start.8 = (bf16[64,2048]{1,0:T(8,128)(2,1)S(1)}, bf16[64,2048]{1,0:T(8,128)(2,1)}, u32[]{:S(2)}) copy-start(bf16[64,2048]{1,0:T(8,128)(2,1)} %get-tuple-element.79) | copy-start | bytes 786436
  57.1 4.9 %copy-start.9 = (bf16[64,768]{1,0:T(8,128)(2,1)S(1)}, bf16[64,768]{1,0:T(8,128)(2,1)}, u32[]{:S(2)}) copy-start(bf16[64,768]{1,0:T(8,128)(2,1)} %get-tuple-element.80) | copy-start | bytes 294916
  61.4 10.2 %collective-permute-start.4 = (bf16[512,512]{1,0:T(8,128)(2,1)}, bf16[512,512]{1,0:T(8,128)(2,1)S(1)}, u32[]{:S(2)}, u32[]{:S(2)}) collective-permute-start(bf16[512,512]{1,0:T(8,128)(2,1)} %get-tuple-element.83), channel_id=1, source_target_pairs={{0,1},{1,0},{2,3},{3,2},{4,5},{5,4},{6,7},{7,6},{8,9},{9,8},{10,11... | collective-permute-start | bytes 1572872 | tf_op jit(solution)/shard_map/ppermute | solution.py:464
  61.4 10.2 %collective-permute-start.5 = (bf16[512,512]{1,0:T(8,128)(2,1)}, bf16[512,512]{1,0:T(8,128)(2,1)S(1)}, u32[]{:S(2)}, u32[]{:S(2)}) collective-permute-start(bf16[512,512]{1,0:T(8,128)(2,1)} %get-tuple-element.84), channel_id=1, source_target_pairs={{0,1},{1,0},{2,3},{3,2},{4,5},{5,4},{6,7},{7,6},{8,9},{9,8},{10,11... | collective-permute-start | bytes 1572872 | tf_op jit(solution)/shard_map/ppermute | solution.py:464
  64.5 10.8 %copy-start.3 = (bf16[8,64,768]{2,1,0:T(8,128)(2,1)S(1)}, bf16[8,64,768]{2,1,0:T(8,128)(2,1)}, u32[]{:S(2)}) copy-start(bf16[8,64,768]{2,1,0:T(8,128)(2,1)} %copy-done.2) | copy-start | bytes 2359300
  71.6 20.6 %copy-start.11 = (bf16[512,512]{1,0:T(8,128)(2,1)}, bf16[512,512]{1,0:T(8,128)(2,1)S(1)}, u32[]{:S(2)}) copy-start(bf16[512,512]{1,0:T(8,128)(2,1)S(1)} %collective-permute-done.4.a_ref) | copy-start | bytes 1572868
  71.7 20.6 %copy-start.12 = (bf16[512,512]{1,0:T(8,128)(2,1)}, bf16[512,512]{1,0:T(8,128)(2,1)S(1)}, u32[]{:S(2)}) copy-start(bf16[512,512]{1,0:T(8,128)(2,1)S(1)} %collective-permute-done.5.b_ref) | copy-start | bytes 1572868
  71.7 16.5 %all-to-all-start.3 = ((bf16[8,64,768]{2,1,0:T(8,128)(2,1)}), bf16[8,64,768]{2,1,0:T(8,128)(2,1)S(1)}, u32[]{:S(2)}, u32[]{:S(2)}) async-start(bf16[8,64,768]{2,1,0:T(8,128)(2,1)} %error.1), calls=%async_computation.3 | async-start | bytes 1572864 | tf_op jit(solution)/shard_map/all_to_all | solution.py:452
  75.5 16.8 %copy-start.5 = (bf16[512,768]{0,1:T(8,128)(2,1)}, bf16[512,768]{0,1:T(8,128)(2,1)S(1)}, u32[]{:S(2)}) copy-start(bf16[512,768]{0,1:T(8,128)(2,1)S(1)} %copy.29) | copy-start | bytes 2359300
  75.5 16.8 %collective-permute-start.7 = (bf16[768,512]{1,0:T(8,128)(2,1)S(1)}, bf16[768,512]{1,0:T(8,128)(2,1)}, u32[]{:S(2)}, u32[]{:S(2)}) collective-permute-start(bf16[768,512]{1,0:T(8,128)(2,1)S(1)} %bitcast.18), channel_id=1, source_target_pairs={{0,1},{1,0},{2,3},{3,2},{4,5},{5,4},{6,7},{7,6},{8,9},{9,8},{10,11... | collective-permute-start | bytes 2359304 | tf_op jit(solution)/shard_map/ppermute | solution.py:464
  88.2 0.9 copy-start
  88.2 4.1 %collective-permute-start.6 = (bf16[8,64,768]{2,1,0:T(8,128)(2,1)S(1)}, bf16[8,64,768]{2,1,0:T(8,128)(2,1)S(1)}, u32[]{:S(2)}, u32[]{:S(2)}) collective-permute-start(bf16[8,64,768]{2,1,0:T(8,128)(2,1)S(1)} %all-to-all-done.3.err_ref), channel_id=1, source_target_pairs={{0,1},{1,0},{2,3},{3,2},{4,5},{5,4},{6,7},{7,6},{8,9},{9,8},{10,11... | collective-permute-start | bytes 2359304 | tf_op jit(solution)/shard_map/ppermute | solution.py:464
  92.3 0.9 copy-start.6
  98.7 32.1 %copy-start.1 = (bf16[8,64,768]{2,1,0:T(8,128)(2,1)S(1)}, bf16[8,64,768]{2,1,0:T(8,128)(2,1)}, u32[]{:S(2)}) copy-start(bf16[8,64,768]{2,1,0:T(8,128)(2,1)} %copy-done) | copy-start | bytes 2359300
  98.8 32.1 %copy-start.7 = (bf16[8,64,768]{2,1,0:T(8,128)(2,1)S(1)}, bf16[8,64,768]{2,1,0:T(8,128)(2,1)}, u32[]{:S(2)}) copy-start(bf16[8,64,768]{2,1,0:T(8,128)(2,1)} %copy-done.6) | copy-start | bytes 2359300
  98.8 9.6 %collective-permute-start.11 = (bf16[96,1024]{1,0:T(8,128)(2,1)}, bf16[96,1024]{1,0:T(8,128)(2,1)S(1)}, u32[]{:S(2)}, u32[]{:S(2)}) collective-permute-start(bf16[96,1024]{1,0:T(8,128)(2,1)} %get-tuple-element.99), channel_id=1, source_target_pairs={{0,32},{32,64},{64,96},{96,0},{1,33},{33,65},{65,97},{97,1},{2,34}... | collective-permute-start | bytes 589832 | tf_op jit(solution)/shard_map/ppermute | solution.py:468
  100.4 13.4 %collective-permute-start.12 = (bf16[96,1024]{1,0:T(8,128)(2,1)}, bf16[96,1024]{1,0:T(8,128)(2,1)S(1)}, u32[]{:S(2)}, u32[]{:S(2)}) collective-permute-start(bf16[96,1024]{1,0:T(8,128)(2,1)} %get-tuple-element.100), channel_id=1, source_target_pairs={{0,96},{32,0},{64,32},{96,64},{1,97},{33,1},{65,33},{97,65},{2,98}... | collective-permute-start | bytes 589832 | tf_op jit(solution)/shard_map/ppermute | solution.py:468
  102.1 11.8 %collective-permute-start.13 = (bf16[96,1024]{1,0:T(8,128)(2,1)}, bf16[96,1024]{1,0:T(8,128)(2,1)S(1)}, u32[]{:S(2)}, u32[]{:S(2)}) collective-permute-start(bf16[96,1024]{1,0:T(8,128)(2,1)} %get-tuple-element.101), channel_id=1, source_target_pairs={{0,64},{32,96},{64,0},{96,32},{1,65},{33,97},{65,1},{97,33},{2,66}... | collective-permute-start | bytes 589832 | tf_op jit(solution)/shard_map/ppermute | solution.py:468
  104.9 15.6 %collective-permute-start.8 = (bf16[96,1024]{1,0:T(8,128)(2,1)}, bf16[96,1024]{1,0:T(8,128)(2,1)S(1)}, u32[]{:S(2)}, u32[]{:S(2)}) collective-permute-start(bf16[96,1024]{1,0:T(8,128)(2,1)} %get-tuple-element.95), channel_id=1, source_target_pairs={{0,32},{32,64},{64,96},{96,0},{1,33},{33,65},{65,97},{97,1},{2,34}... | collective-permute-start | bytes 589832 | tf_op jit(solution)/shard_map/ppermute | solution.py:468
  105.8 14.7 %collective-permute-start.9 = (bf16[96,1024]{1,0:T(8,128)(2,1)}, bf16[96,1024]{1,0:T(8,128)(2,1)S(1)}, u32[]{:S(2)}, u32[]{:S(2)}) collective-permute-start(bf16[96,1024]{1,0:T(8,128)(2,1)} %get-tuple-element.96), channel_id=1, source_target_pairs={{0,96},{32,0},{64,32},{96,64},{1,97},{33,1},{65,33},{97,65},{2,98}... | collective-permute-start | bytes 589832 | tf_op jit(solution)/shard_map/ppermute | solution.py:468
  108.4 13.0 %collective-permute-start.10 = (bf16[96,1024]{1,0:T(8,128)(2,1)}, bf16[96,1024]{1,0:T(8,128)(2,1)S(1)}, u32[]{:S(2)}, u32[]{:S(2)}) collective-permute-start(bf16[96,1024]{1,0:T(8,128)(2,1)} %get-tuple-element.97), channel_id=1, source_target_pairs={{0,64},{32,96},{64,0},{96,32},{1,65},{33,97},{65,1},{97,33},{2,66}... | collective-permute-start | bytes 589832 | tf_op jit(solution)/shard_map/ppermute | solution.py:468
  114.9 7.3 %collective-permute-start.14 = (bf16[96,1024]{1,0:T(8,128)(2,1)S(1)}, bf16[96,1024]{1,0:T(8,128)(2,1)S(1)}, u32[]{:S(2)}, u32[]{:S(2)}) collective-permute-start(bf16[96,1024]{1,0:T(8,128)(2,1)S(1)} %add_convert_fusion.1), channel_id=1, source_target_pairs={{0,16},{16,0},{1,17},{17,1},{2,18},{18,2},{3,19},{19,3},{4,20},{20... | collective-permute-start | bytes 589832 | tf_op jit(solution)/shard_map/ppermute | solution.py:464
  123.4 12.8 %collective-permute-start.18 = (bf16[96,1024]{1,0:T(8,128)(2,1)S(1)}, bf16[96,1024]{1,0:T(8,128)(2,1)S(1)}, u32[]{:S(2)}, u32[]{:S(2)}) collective-permute-start(bf16[96,1024]{1,0:T(8,128)(2,1)S(1)} %add_convert_fusion.refs_0_), channel_id=1, source_target_pairs={{0,64},{32,96},{64,0},{96,32},{1,65},{33,97},{65,1},{97,33},{2,66}... | collective-permute-start | bytes 589832 | tf_op jit(solution)/shard_map/ppermute | solution.py:468
  124.1 7.2 %collective-permute-start.15 = (bf16[96,1024]{1,0:T(8,128)(2,1)S(1)}, bf16[96,1024]{1,0:T(8,128)(2,1)S(1)}, u32[]{:S(2)}, u32[]{:S(2)}) collective-permute-start(bf16[96,1024]{1,0:T(8,128)(2,1)S(1)} %add_convert_fusion.refs_0_), channel_id=1, source_target_pairs={{0,16},{16,0},{1,17},{17,1},{2,18},{18,2},{3,19},{19,3},{4,20},{20... | collective-permute-start | bytes 589832 | tf_op jit(solution)/shard_map/ppermute | solution.py:464
  127.4 10.0 %collective-permute-start.17 = (bf16[96,1024]{1,0:T(8,128)(2,1)S(1)}, bf16[96,1024]{1,0:T(8,128)(2,1)S(1)}, u32[]{:S(2)}, u32[]{:S(2)}) collective-permute-start(bf16[96,1024]{1,0:T(8,128)(2,1)S(1)} %add_convert_fusion.refs_0_), channel_id=1, source_target_pairs={{0,96},{32,0},{64,32},{96,64},{1,97},{33,1},{65,33},{97,65},{2,98}... | collective-permute-start | bytes 589832 | tf_op jit(solution)/shard_map/ppermute | solution.py:468
  130.8 9.1 %collective-permute-start.16 = (bf16[96,1024]{1,0:T(8,128)(2,1)S(1)}, bf16[96,1024]{1,0:T(8,128)(2,1)S(1)}, u32[]{:S(2)}, u32[]{:S(2)}) collective-permute-start(bf16[96,1024]{1,0:T(8,128)(2,1)S(1)} %add_convert_fusion.refs_0_), channel_id=1, source_target_pairs={{0,32},{32,64},{64,96},{96,0},{1,33},{33,65},{65,97},{97,1},{2,34}... | collective-permute-start | bytes 589832 | tf_op jit(solution)/shard_map/ppermute | solution.py:468
  131.2 10.5 %collective-permute-start.21 = (bf16[96,1024]{1,0:T(8,128)(2,1)S(1)}, bf16[96,1024]{1,0:T(8,128)(2,1)S(1)}, u32[]{:S(2)}, u32[]{:S(2)}) collective-permute-start(bf16[96,1024]{1,0:T(8,128)(2,1)S(1)} %collective-permute-done.15.refs_1_), channel_id=1, source_target_pairs={{0,64},{32,96},{64,0},{96,32},{1,65},{33,97},{65,1},{97,33},{2,66}... | collective-permute-start | bytes 589832 | tf_op jit(solution)/shard_map/ppermute | solution.py:468
  134.1 8.5 %collective-permute-start.20 = (bf16[96,1024]{1,0:T(8,128)(2,1)S(1)}, bf16[96,1024]{1,0:T(8,128)(2,1)S(1)}, u32[]{:S(2)}, u32[]{:S(2)}) collective-permute-start(bf16[96,1024]{1,0:T(8,128)(2,1)S(1)} %collective-permute-done.15.refs_1_), channel_id=1, source_target_pairs={{0,96},{32,0},{64,32},{96,64},{1,97},{33,1},{65,33},{97,65},{2,98}... | collective-permute-start | bytes 589832 | tf_op jit(solution)/shard_map/ppermute | solution.py:468
  136.2 8.7 %collective-permute-start.19 = (bf16[96,1024]{1,0:T(8,128)(2,1)S(1)}, bf16[96,1024]{1,0:T(8,128)(2,1)S(1)}, u32[]{:S(2)}, u32[]{:S(2)}) collective-permute-start(bf16[96,1024]{1,0:T(8,128)(2,1)S(1)} %collective-permute-done.15.refs_1_), channel_id=1, source_target_pairs={{0,32},{32,64},{64,96},{96,0},{1,33},{33,65},{65,97},{97,1},{2,34}... | collective-permute-start | bytes 589832 | tf_op jit(solution)/shard_map/ppermute | solution.py:468

commit v6 on v5

--- a/solution.py
+++ b/solution.py
@@ -294,25 +294,40 @@
     total = base_ref[...]
     for d in range(parts_ref.shape[0]):
         total = total + parts_ref[d].astype(F32)
-    total = total.astype(BF16)
-    for d in range(err_ref.shape[0]):
-        err_ref[d] = total
-
-
-def hidden_grads(err_buf, down_buf, a_buf, b_buf, copies):
+    err_ref[...] = total.astype(BF16)
+
+
+def chip_block(flip, shift):
+    zl, x = lax.axis_index("zl"), lax.axis_index("x")
+    zl = 1 - zl if flip else zl
+    return zl * 4 + lax.rem(x + shift + 4, 4)
+
+
+def place(pieces, errb, sem):
+    return fetch(pieces, [errb.at[chip_block(flip, -d)] for flip, d in GOT], sem)
+
+
+def hidden_grads(pieces, copies, err_buf, down_buf, a_buf, b_buf, err_ref, err_sem):
+    for c in pieces:
+        c.wait()
+    out = pltpu.make_async_copy(err_buf, err_ref, err_sem.at[0])
+    out.start()
+    dpred = (err_buf[...].astype(F32) / 64.0).astype(BF16).reshape(-1, err_buf.shape[-1])
     copies[0].wait()
-    dpred = (err_buf[...].astype(F32) / 64.0).astype(BF16).reshape(-1, err_buf.shape[-1])
+    dact = nt(dpred, down_buf[...])
     copies[1].wait()
-    dact = nt(dpred, down_buf[...])
+    dgate = (dact * a_buf[...].astype(F32)).astype(BF16)
     copies[2].wait()
-    dgate = (dact * a_buf[...].astype(F32)).astype(BF16)
-    copies[3].wait()
-    return dgate, (dact * b_buf[...].astype(F32)).astype(BF16)
-
-
-def own_kernel(err_ref, d_ref, a_ref, b_ref, dg_ref, du_ref, errb, db, ab, bb, sem):
-    copies = fetch((err_ref, d_ref, a_ref, b_ref), (errb, db, ab, bb), sem)
-    dg_ref[...], du_ref[...] = hidden_grads(errb, db, ab, bb, copies)
+    return dgate, (dact * b_buf[...].astype(F32)).astype(BF16), out
+
+
+def own_kernel(*refs):
+    pieces, refs = refs[: len(GOT)], refs[len(GOT) :]
+    d_ref, a_ref, b_ref, dg_ref, du_ref, err_ref, errb, db, ab, bb, sem, piece_sem, err_sem = refs
+    placed = place(pieces, errb, piece_sem)
+    copies = fetch((d_ref, a_ref, b_ref), (db, ab, bb), sem)
+    dg_ref[...], du_ref[...], out = hidden_grads(placed, copies, errb, db, ab, bb, err_ref, err_sem)
+    out.wait()
 
 
 def group_block(flip, shift):
@@ -321,15 +336,17 @@
     return lax.rem(y + shift + 4, 4) * 2 + zh
 
 
-def other_kernel(err_ref, d_ref, a_ref, b_ref, x0_ref, dg_ref, du_ref, x1_ref, *refs):
-    outs, (errb, db, ab, bb, x0b, dgb, dub, x1b, yb, sem, out_sem) = refs[: len(SENT)], refs[len(SENT) :]
+def other_kernel(*refs):
+    pieces, refs = refs[: len(GOT)], refs[len(GOT) :]
+    (d_ref, a_ref, b_ref, x0_ref, dg_ref, du_ref, x1_ref), refs = refs[:7], refs[7:]
+    outs, refs = refs[: len(SENT)], refs[len(SENT) :]
+    err_ref, errb, db, ab, bb, x0b, dgb, dub, x1b, yb, sem, piece_sem, out_sem, err_sem = refs
+    placed = place(pieces, errb, piece_sem)
     copies = fetch(
-        (err_ref, d_ref, a_ref, b_ref, x0_ref, dg_ref, du_ref, x1_ref),
-        (errb, db, ab, bb, x0b, dgb, dub, x1b),
-        sem,
-    )
-    dgate, dup = hidden_grads(errb, db, ab, bb, copies)
-    for c in copies[4:]:
+        (d_ref, a_ref, b_ref, x0_ref, dg_ref, du_ref, x1_ref), (db, ab, bb, x0b, dgb, dub, x1b), sem
+    )
+    dgate, dup, err_out = hidden_grads(placed, copies, errb, db, ab, bb, err_ref, err_sem)
+    for c in copies[3:]:
         c.wait()
     width, tall = dgate.shape[1], 256
     for i in range(yb.shape[0] // tall):
@@ -343,20 +360,17 @@
         sends[-1].start()
     for c in sends:
         c.wait()
+    err_out.wait()
 
 
 def last_kernel(w_ref, *refs):
-    parts, (gate_ref, up_ref, wb, yb, sem, y_sem) = refs[: len(GOT)], refs[len(GOT) :]
-    rows = parts[0].shape[0]
-    slots = [pl.ds(i * rows, rows) for i in range(len(GOT))]
+    count = len(GOT)
+    rows = refs[0].shape[0]
     blocks = [pl.ds(pl.multiple_of(group_block(flip, -d) * rows, rows), rows) for flip, d in GOT]
-    copies = fetch([w_ref.at[b] for b in blocks], [wb.at[i] for i in slots], sem)
-    copies += fetch(parts, [yb.at[i] for i in slots], y_sem)
-    for c in copies:
-        c.wait()
-    width = gate_ref.shape[1]
-    gate_ref[...] = tn(wb[...], yb[:, :width])
-    up_ref[...] = tn(wb[...], yb[:, width:])
+    w = jnp.concatenate([w_ref[b] for b in blocks], axis=0)
+    for side, out_ref in enumerate(refs[2 * count :]):
+        y = jnp.concatenate([r[...] for r in refs[side * count : (side + 1) * count]], axis=0)
+        out_ref[...] = tn(w, y)
 
 
 VM = pl.BlockSpec(memory_space=pltpu.VMEM)
@@ -464,8 +478,13 @@
     return lax.ppermute(x, axis, SWAP)
 
 
-def shift(x, d):
-    return lax.ppermute(x, "y", [(i, (i + d) % 4) for i in range(4)])
+def shift(x, d, axis):
+    return lax.ppermute(x, axis, [(i, (i + d) % 4) for i in range(4)])
+
+
+def gather(x, pair_axis, ring_axis):
+    twin = swap(x, pair_axis)
+    return [x, twin] + [shift(v, d, ring_axis) for v in (x, twin) for d in SHIFTS]
 
 
 def total(first, *others):
@@ -542,33 +561,38 @@
     gain_own = lax.dynamic_slice_in_dim(gain, at * block, block, 0)
     w_own = lax.optimization_barrier((w_own.astype(F32) * gain_own).astype(BF16))
     err_own = pl.pallas_call(
-        error_kernel, grid=(3,), out_shape=sds((chips, COUNT, FEATS), BF16),
-        in_specs=[cut(parts.shape, 3), cut(base.shape, 3)], out_specs=cut(parts.shape, 3),
+        error_kernel, grid=(3,), out_shape=sds(base.shape, BF16),
+        in_specs=[cut(parts.shape, 3), cut(base.shape, 3)], out_specs=cut(base.shape, 3),
         compiler_params=SMALL, name="error",
     )(parts, base)
     err_own, slope_ao, slope_bo = lax.optimization_barrier((err_own, slope_ao, slope_bo))
-    err = exchange(err_own, CHIP)
-    err_other = swap(err)
-    dg, du = staged(
-        own_kernel, "own", (err, down_w, slope_a, slope_b), (slope, slope), [], 400000000, (4,), (VM,) * 2,
+    err = gather(err_own, "zl", "x")
+    err_swapped = [swap(v) for v in err]
+    rows_err = sds((chips, COUNT, FEATS), BF16)
+    args = (down_w, slope_a, slope_b)
+    dg, du, err = staged(
+        own_kernel, "own", (*err, *args), (slope, slope, rows_err), [], 400000000, (3, len(GOT), 1), (VM, VM, HB),
+        bufs=[pltpu.VMEM(rows_err.shape, BF16)] + [vmem_like(v) for v in args], params=MIDDLE,
     )
     piece = sds((FEATS // groups, 2 * width), BF16)
-    pieces = staged(
-        other_kernel, "other", (err_other, down_w, slope_ao, slope_bo, x_late, dg, du, x_other),
-        (piece,) * len(SENT), [pltpu.VMEM((FEATS, 2 * width), BF16)], 2000000000, (8, len(SENT)),
-        (HB,) * len(SENT),
-    )
-    moved = [shift(p, d) if d else p for p, (_, d) in zip(pieces, SENT)]
+    args = (down_w, slope_ao, slope_bo, x_late, dg, du, x_other)
+    *pieces, err_other = staged(
+        other_kernel, "other", (*err_swapped, *args), (piece,) * len(SENT) + (rows_err,),
+        [pltpu.VMEM((FEATS, 2 * width), BF16)], 2000000000, (7, len(GOT), len(SENT), 1), (HB,) * (len(SENT) + 1),
+        bufs=[pltpu.VMEM(rows_err.shape, BF16)] + [vmem_like(v) for v in args], params=MIDDLE,
+    )
+    moved = [shift(p, d, "y") if d else p for p, (_, d) in zip(pieces, SENT)]
     theirs = swap(total(*moved[:4]), "zh")
     grads = total(*moved[4:], theirs)
     grads, err_late, err_other = lax.optimization_barrier((grads, err, err_other))
-    twin = swap(grads, "zh")
-    got = [grads, twin] + [shift(v, d) for v in (grads, twin) for d in SHIFTS]
+    got = gather(grads, "zh", "y")
     grad = sds((block, width), F32)
-    grad_gate, grad_up = staged(
-        last_kernel, "last", (w_own, *got), (grad, grad), [], 400000000, (len(GOT),) * 2, (VM,) * 2,
-        bufs=[vmem_like(w_own), pltpu.VMEM((FEATS, 2 * width), BF16)], params=MIDDLE,
-    )
+    grad_gate, grad_up = pl.pallas_call(
+        last_kernel, grid=(2,), out_shape=(grad, grad),
+        in_specs=[pl.BlockSpec(w_own.shape, lambda i: (0, 0))]
+        + [cut(piece.shape, 4)] * len(GOT) + [cut(piece.shape, 4, 2)] * len(GOT),
+        out_specs=(cut(grad.shape, 2),) * 2, compiler_params=SMALL, name="last",
+    )(w_own, *got, *got)
     err_all = jnp.concatenate([err_late, err_other], axis=0).reshape(2 * half, FEATS)
     core = lax.axis_index("core")
     codes = recv[:, CODE_ROW : CODE_ROW + 2, :COUNT]

time: 150 us -> 151 us (level)
  starting transfers between devices: 50.2 us -> 55.4 us
  local copies, waits for them, and re-layouts: 6.33 us -> 10.9 us
  waiting for transfers between devices: 35.4 us -> 31.3 us
  Pallas kernels: 48.6 us -> 45.6 us
  other arithmetic: 3.9 us -> 2.04 us
    all_to_all x4 -> x3, waiting for transfers between devices: 24.7 us -> 11.6 us  [exchange(): return lax.all_to_all(x, axes, split_axis=0, concat_axis=0, tiled=True)]
    ppermute x12 -> x18, waiting for transfers between devices: 8.46 us -> 17.5 us  [shift(): return lax.ppermute(x, axis, [(i, (i + d) % 4) for i in range(4)])]
    ppermute x12 -> x18, starting transfers between devices: 23.4 us -> 30.1 us  [shift(): return lax.ppermute(x, axis, [(i, (i + d) % 4) for i in range(4)])]
    unnamed x26 -> x36, local copies, waits for them, and re-layouts: 2.66 us -> 7.22 us
    pallas_call x6 -> x5, Pallas kernels: 33.2 us -> 29.4 us  [staged(): pl.pallas_call(kernel, out_shape=out_shape, in_specs=[HB] * len(args), ou...]
    all_to_all x4 -> x3, starting transfers between devices: 18.1 us -> 14.4 us  [exchange(): return lax.all_to_all(x, axes, split_axis=0, concat_axis=0, tiled=True)]
    ppermute x10 -> x18, starting transfers between devices: 8.78 us -> 10.9 us  [swap(): return lax.ppermute(x, axis, SWAP)]
    convert_element_type x2, other arithmetic: 2.13 us -> 0.28 us  [total(): return out.astype(BF16)]
  transfers between devices with their start and end apart: 26 -> 39, of which waited for: 13 -> 15; matrix products, arithmetic and copies ran while one was open for 7% -> 6% of each run, Pallas kernels for 22% -> 21%
where the time goes in v6:
time: 151 us; the launch traced here: 150 us
  starting transfers between devices  55.4 us (37%)
  Pallas kernels  45.6 us (30%)
  waiting for transfers between devices  31.3 us (21%)
  local copies, waits for them, and re-layouts  10.9 us (7%)
  matrix products  3.74 us (2%)
  other arithmetic  2.04 us (1%)
    ppermute x18, starting transfers between devices, shift(): return lax.ppermute(x, axis, [(i, (i + d) % 4) for i in range(4)])  30.1 us
    pallas_call x5, Pallas kernels, staged(): pl.pallas_call(kernel, out_shape=out_shape, in_specs=[HB] * len(args), ou...  29.4 us
    ppermute x18, waiting for transfers between devices, shift(): return lax.ppermute(x, axis, [(i, (i + d) % 4) for i in range(4)])  17.5 us
    all_to_all x3, starting transfers between devices, exchange(): return lax.all_to_all(x, axes, split_axis=0, concat_axis=0, tiled=True)  14.4 us
    all_to_all x3, waiting for transfers between devices, exchange(): return lax.all_to_all(x, axes, split_axis=0, concat_axis=0, tiled=True)  11.6 us
    ppermute x18, starting transfers between devices, swap(): return lax.ppermute(x, axis, SWAP)  10.9 us
    unnamed x36, local copies, waits for them, and re-layouts  7.22 us
    pallas_call x1, Pallas kernels, evolve(): pl.pallas_call(evolve_kernel, out_shape=(sds((ROWS, LANES), F32), sds((2...  5.24 us
  transfers between devices with their start and end apart: 39, of which 15 were waited for; matrix products, arithmetic and copies ran while one was open for 6% of the time, Pallas kernels for 21%

profile of v6, /device:TPU:0, one launch (start us, length us, event | category | flops | bytes accessed | tf_op | source)
XLA Modules:
  0.0 149.9 jit_solution(1828435464864347550)
XLA Ops:
  0.7 5.2 %evolve.1 = (f32[72,128]{1,0:T(8,128)}, bf16[128,768]{1,0:T(8,128)(2,1)}, f32[24,128]{1,0:T(8,128)}, f32[3,256,128]{2,1,0:T(8,128)}) custom-call(f32[3,256,128]{2,1,0:T(8,128)} %pos_ref.3, f32[3,256,128]{2,1,0:T(8,128)} %vel_ref.3, f32[1,128]{1,0:T(1,128)} %bitcast.23, s32[8,256,128]{2,1,0:T(8,128)} %contact_ref.3, f32[3,128]{1,0:T(4,128)} %off_ref.3, ...), custom_call_target="tpu_custom_call" | custom-call | flops 260000000 | bytes 3000000 | tf_op jit(solution)/shard_map/evolve/pallas_call | solution.py:389
  6.0 0.6 collective-permute-start
  6.5 1.1 collective-permute-done
  7.6 0.8 add.110
  8.4 0.7 broadcast_in_dim.24
  9.1 5.7 %all-to-all-start = ((f32[8,72,128]{2,1,0:T(8,128)}), f32[8,72,128]{2,1,0:T(8,128)}, u32[]{:S(2)}, u32[]{:S(2)}) async-start(f32[8,72,128]{2,1,0:T(8,128)} %broadcast_in_dim.24), calls=%async_computation | async-start | bytes 589824 | tf_op jit(solution)/shard_map/all_to_all | solution.py:466
  14.9 7.1 %products.1 = (bf16[768,512]{1,0:T(8,128)(2,1)}, bf16[768,512]{1,0:T(8,128)(2,1)}) custom-call(bf16[768,2048]{1,0:T(8,128)(2,1)} %w_in_ref.2, f32[1,2048]{1,0:T(1,128)} %bitcast.30, bf16[2048,512]{1,0:T(8,128)(2,1)} %gate_ref.1, bf16[2048,512]{1,0:T(8,128)(2,1)} %up_ref.1), custom_call_target="tpu_custom_call" | custom-call | flops 3300000000 | bytes 8000000 | tf_op jit(solution)/shard_map/products/pallas_call | solution.py:448
  22.5 0.6 all-to-all-done.recv_ref
  23.1 4.2 %finish.1 = (bf16[8,64,768]{2,1,0:T(8,128)(2,1)}, bf16[64,768]{1,0:T(8,128)(2,1)}, bf16[64,2048]{1,0:T(8,128)(2,1)}, f32[3,128]{1,0:T(4,128)}, f32[3,256,128]{2,1,0:T(8,128)}) custom-call(f32[8,72,128]{2,1,0:T(8,128)} %all-to-all-done.recv_ref, f32[24,128]{1,0:T(8,128)} %get-tuple-element.61.bound_ref, ...), custom_call_target="tpu_custom_call", output_to_operand_aliasing={{4}: (18, {})} | custom-call | flops 300000000 | bytes 4000000 | tf_op jit(solution)/shard_map/finish/pallas_call | solution.py:422
  27.4 1.3 copy-done.16
  28.7 5.1 %all-to-all-start.1 = ((bf16[8,64,768]{2,1,0:T(8,128)(2,1)}), bf16[8,64,768]{2,1,0:T(8,128)(2,1)S(1)}, u32[]{:S(2)}, u32[]{:S(2)}) async-start(bf16[8,64,768]{2,1,0:T(8,128)(2,1)} %get-tuple-element.69), calls=%async_computation.1 | async-start | bytes 1572864 | tf_op jit(solution)/shard_map/all_to_all | solution.py:466
  33.8 7.0 %down.1 = (bf16[512,768]{1,0:T(8,128)(2,1)}, bf16[512,768]{1,0:T(8,128)(2,1)}) custom-call(bf16[512,2048]{1,0:T(8,128)(2,1)} %w0_ref, bf16[512,2048]{1,0:T(8,128)(2,1)} %copy-done.16, bf16[2048,768]{1,0:T(8,128)(2,1)} %out_ref.1), custom_call_target="tpu_custom_call" | custom-call | flops 3300000000 | bytes 8000000 | tf_op jit(solution)/shard_map/down/pallas_call | solution.py:448
  40.9 6.1 %all-to-all-done.1.x_ref = bf16[8,64,768]{2,1,0:T(8,128)(2,1)S(1)} async-done(((bf16[8,64,768]{2,1,0:T(8,128)(2,1)}), bf16[8,64,768]{2,1,0:T(8,128)(2,1)S(1)}, u32[]{:S(2)}, u32[]{:S(2)}) %all-to-all-start.1) | async-done | bytes 786464 | tf_op jit(solution)/shard_map/all_to_all | solution.py:466
  47.0 0.9 copy-done.12
  47.9 6.2 %forward.1 = (bf16[8,64,768]{2,1,0:T(8,128)(2,1)}, f32[2,512,512]{2,1,0:T(8,128)}, f32[2,512,512]{2,1,0:T(8,128)}) custom-call(bf16[8,64,768]{2,1,0:T(8,128)(2,1)} %copy-done.12, bf16[768,512]{1,0:T(8,128)(2,1)} %get-tuple-element.71.g0_ref, bf16[768,512]{1,0:T(8,128)(2,1)} %get-tuple-element.72.u0_ref, bf16[512,768]{1,0:T(8,128)(2,1)} %get-tuple-element.75.d0_ref.refs_8_, ...), custom_call_target="tpu_custom_call" | custom-call | flops 2500000000 | bytes 8000000 | tf_op jit(solution)/shard_map/forward/pallas_call | solution.py:448
  54.1 3.6 %all-to-all-start.2 = ((bf16[8,64,768]{2,1,0:T(8,128)(2,1)}), bf16[8,64,768]{2,1,0:T(8,128)(2,1)S(1)}, u32[]{:S(2)}, u32[]{:S(2)}) async-start(bf16[8,64,768]{2,1,0:T(8,128)(2,1)} %get-tuple-element.80), calls=%async_computation.2 | async-start | bytes 1572864 | tf_op jit(solution)/shard_map/all_to_all | solution.py:466
  57.7 4.3 %slopes.1 = (bf16[512,512]{1,0:T(8,128)(2,1)}, bf16[512,512]{1,0:T(8,128)(2,1)}, bf16[512,512]{1,0:T(8,128)(2,1)}, bf16[512,512]{1,0:T(8,128)(2,1)}) custom-call(f32[2,512,512]{2,1,0:T(8,128)} %get-tuple-element.83.gate_ref, f32[2,512,512]{2,1,0:T(8,128)} %get-tuple-element.84.up_ref), custom_call_target="tpu_custom_call" | custom-call | flops 8000000 | bytes 6000000 | tf_op jit(solution)/shard_map/slopes/pallas_call | solution.py:549
  62.4 0.5 collective-permute-start.4
  63.0 2.6 %convolution_subtract_fusion.base_ref = f32[64,768]{1,0:T(8,128)S(1)} fusion(bf16[64,2048]{1,0:T(8,128)(2,1)S(1)} %copy-done.14, bf16[2048,768]{1,0:T(8,128)(2,1)} %out_ref.1, bf16[64,768]{1,0:T(8,128)(2,1)S(1)} %copy-done.15), kind=kOutput, calls=%fused_computation.2 | convolution fusion | flops 201424896 | bytes 3702784 | tf_op jit(solution)/shard_map/dot_general | solution.py:470
  65.7 5.0 %all-to-all-done.2.parts_ref = bf16[8,64,768]{2,1,0:T(8,128)(2,1)S(1)} async-done(((bf16[8,64,768]{2,1,0:T(8,128)(2,1)}), bf16[8,64,768]{2,1,0:T(8,128)(2,1)S(1)}, u32[]{:S(2)}, u32[]{:S(2)}) %all-to-all-start.2) | async-done | bytes 786464 | tf_op jit(solution)/shard_map/all_to_all | solution.py:466
  71.0 0.9 collective-permute-start.13
  71.9 2.7 %collective-permute-start.11 = (bf16[64,768]{1,0:T(8,128)(2,1)S(1)}, bf16[64,768]{1,0:T(8,128)(2,1)S(1)}, u32[]{:S(2)}, u32[]{:S(2)}) collective-permute-start(bf16[64,768]{1,0:T(8,128)(2,1)S(1)} %error.1.refs_0_), channel_id=1, source_target_pairs={{0,6},{2,0},{4,2},{6,4},{1,7},{3,1},{5,3},{7,5},{8,14},{10,8},{12,... | collective-permute-start | bytes 294920 | tf_op jit(solution)/shard_map/ppermute | solution.py:482
  74.6 0.5 collective-permute-start.7
  75.1 2.9 %collective-permute-done.13.refs_4_ = bf16[64,768]{1,0:T(8,128)(2,1)S(1)} collective-permute-done((bf16[64,768]{1,0:T(8,128)(2,1)S(1)}, bf16[64,768]{1,0:T(8,128)(2,1)S(1)}, u32[]{:S(2)}, u32[]{:S(2)}) %collective-permute-start.13) | collective-permute-done | bytes 98336 | tf_op jit(solution)/shard_map/ppermute | solution.py:482
  78.0 0.5 collective-permute-start.14
  78.5 1.9 %collective-permute-done.9.refs_2_ = bf16[64,768]{1,0:T(8,128)(2,1)S(1)} collective-permute-done((bf16[64,768]{1,0:T(8,128)(2,1)S(1)}, bf16[64,768]{1,0:T(8,128)(2,1)S(1)}, u32[]{:S(2)}, u32[]{:S(2)}) %collective-permute-start.9) | collective-permute-done | bytes 98336 | tf_op jit(solution)/shard_map/ppermute | solution.py:482
  80.4 0.8 collective-permute-start.19
  81.2 0.6 copy-done.6
  81.9 1.2 collective-permute-start.17
  83.1 0.9 collective-permute-start.15
  83.9 0.6 copy-done.8
  84.6 0.6 copy-done.10
  85.2 0.5 collective-permute-start.10
  85.7 1.5 collective-permute-done.19.refs_7_
  87.7 1.6 %collective-permute-done.15.refs_5_ = bf16[64,768]{1,0:T(8,128)(2,1)} collective-permute-done((bf16[64,768]{1,0:T(8,128)(2,1)S(1)}, bf16[64,768]{1,0:T(8,128)(2,1)}, u32[]{:S(2)}, u32[]{:S(2)}) %collective-permute-start.15) | collective-permute-done | bytes 98336 | tf_op jit(solution)/shard_map/ppermute | solution.py:482
  89.3 0.8 dynamic_slice.7
  90.1 1.0 copy-done.2
  91.1 2.8 %own.1 = (bf16[512,512]{1,0:T(8,128)(2,1)S(1)}, bf16[512,512]{1,0:T(8,128)(2,1)S(1)}, bf16[8,64,768]{2,1,0:T(8,128)(2,1)S(1)}) custom-call(bf16[64,768]{1,0:T(8,128)(2,1)S(1)} %error.1.refs_0_, bf16[64,768]{1,0:T(8,128)(2,1)S(1)} %collective-permute-done.7.refs_1_, bf16[64,768]{1,0:T(8,128)(2,1)S(1)} %collective-permute-done.9.refs_2_, ...), custom_call_target="tpu_custom_call" | custom-call | flops 400000000 | bytes 8000000 | tf_op jit(solution)/shard_map/own/pallas_call | solution.py:448
  94.0 6.3 %other.1 = (bf16[96,1024]{1,0:T(8,128)(2,1)}, bf16[96,1024]{1,0:T(8,128)(2,1)}, bf16[96,1024]{1,0:T(8,128)(2,1)}, bf16[96,1024]{1,0:T(8,128)(2,1)S(1)}, bf16[96,...) custom-call(bf16[64,768]{1,0:T(8,128)(2,1)S(1)} %copy-done.7, ...), custom_call_target="tpu_custom_call" | custom-call | flops 2000000000 | bytes 8000000 | tf_op jit(solution)/shard_map/other/pallas_call | solution.py:448
  100.3 0.7 copy-done.3
  101.0 0.7 copy-done.4
  101.7 0.7 copy-done.5
  102.4 1.6 %collective-permute-start.25 = (bf16[96,1024]{1,0:T(8,128)(2,1)}, bf16[96,1024]{1,0:T(8,128)(2,1)S(1)}, u32[]{:S(2)}, u32[]{:S(2)}) collective-permute-start(bf16[96,1024]{1,0:T(8,128)(2,1)} %get-tuple-element.101), channel_id=1, source_target_pairs={{0,32},{32,64},{64,96},{96,0},{1,33},{33,65},{65,97},{97,1},{2,34}... | collective-permute-start | bytes 589832 | tf_op jit(solution)/shard_map/ppermute | solution.py:482
  103.9 1.7 %collective-permute-start.26 = (bf16[96,1024]{1,0:T(8,128)(2,1)}, bf16[96,1024]{1,0:T(8,128)(2,1)S(1)}, u32[]{:S(2)}, u32[]{:S(2)}) collective-permute-start(bf16[96,1024]{1,0:T(8,128)(2,1)} %get-tuple-element.102), channel_id=1, source_target_pairs={{0,96},{32,0},{64,32},{96,64},{1,97},{33,1},{65,33},{97,65},{2,98}... | collective-permute-start | bytes 589832 | tf_op jit(solution)/shard_map/ppermute | solution.py:482
  105.6 2.0 %collective-permute-start.27 = (bf16[96,1024]{1,0:T(8,128)(2,1)}, bf16[96,1024]{1,0:T(8,128)(2,1)S(1)}, u32[]{:S(2)}, u32[]{:S(2)}) collective-permute-start(bf16[96,1024]{1,0:T(8,128)(2,1)} %get-tuple-element.103), channel_id=1, source_target_pairs={{0,64},{32,96},{64,0},{96,32},{1,65},{33,97},{65,1},{97,33},{2,66}... | collective-permute-start | bytes 589832 | tf_op jit(solution)/shard_map/ppermute | solution.py:482
  107.6 0.8 slice.4
  108.4 0.7 collective-permute-start.22
  109.1 2.6 %collective-permute-start.23 = (bf16[96,1024]{1,0:T(8,128)(2,1)}, bf16[96,1024]{1,0:T(8,128)(2,1)S(1)}, u32[]{:S(2)}, u32[]{:S(2)}) collective-permute-start(bf16[96,1024]{1,0:T(8,128)(2,1)} %copy-done.4), channel_id=1, source_target_pairs={{0,96},{32,0},{64,32},{96,64},{1,97},{33,1},{65,33},{97,65},{2,98}... | collective-permute-start | bytes 589832 | tf_op jit(solution)/shard_map/ppermute | solution.py:482
  111.7 6.0 %collective-permute-start.24 = (bf16[96,1024]{1,0:T(8,128)(2,1)}, bf16[96,1024]{1,0:T(8,128)(2,1)S(1)}, u32[]{:S(2)}, u32[]{:S(2)}) collective-permute-start(bf16[96,1024]{1,0:T(8,128)(2,1)} %copy-done.3), channel_id=1, source_target_pairs={{0,64},{32,96},{64,0},{96,32},{1,65},{33,97},{65,1},{97,33},{2,66}... | collective-permute-start | bytes 589832 | tf_op jit(solution)/shard_map/ppermute | solution.py:482
  117.8 3.7 %collective-permute-start.28 = (bf16[96,1024]{1,0:T(8,128)(2,1)S(1)}, bf16[96,1024]{1,0:T(8,128)(2,1)S(1)}, u32[]{:S(2)}, u32[]{:S(2)}) collective-permute-start(bf16[96,1024]{1,0:T(8,128)(2,1)S(1)} %add_convert_fusion.1), channel_id=1, source_target_pairs={{0,16},{16,0},{1,17},{17,1},{2,18},{18,2},{3,19},{19,3},{4,20},{20... | collective-permute-start | bytes 589832 | tf_op jit(solution)/shard_map/ppermute | solution.py:478
  121.5 0.8 select_bitcast_fusion
  122.3 1.0 constant_dynamic-slice_fusion
  123.4 1.7 %collective-permute-done.24 = bf16[96,1024]{1,0:T(8,128)(2,1)S(1)} collective-permute-done((bf16[96,1024]{1,0:T(8,128)(2,1)}, bf16[96,1024]{1,0:T(8,128)(2,1)S(1)}, u32[]{:S(2)}, u32[]{:S(2)}) %collective-permute-start.24) | collective-permute-done | bytes 196640 | tf_op jit(solution)/shard_map/ppermute | solution.py:482
  125.3 0.7 collective-permute-start.32
  126.0 3.5 %collective-permute-start.29 = (bf16[96,1024]{1,0:T(8,128)(2,1)S(1)}, bf16[96,1024]{1,0:T(8,128)(2,1)S(1)}, u32[]{:S(2)}, u32[]{:S(2)}) collective-permute-start(bf16[96,1024]{1,0:T(8,128)(2,1)S(1)} %add_convert_fusion.refs_0_.refs_8_), channel_id=1, source_target_pairs={{0,16},{16,0},{1,17},{17,1},{2,18},{18,2},{3,19},{19,3},{4,20},{20... | collective-permute-start | bytes 589832 | tf_op jit(solution)/shard_map/ppermute | solution.py:478
  129.6 3.2 %collective-permute-start.31 = (bf16[96,1024]{1,0:T(8,128)(2,1)S(1)}, bf16[96,1024]{1,0:T(8,128)(2,1)S(1)}, u32[]{:S(2)}, u32[]{:S(2)}) collective-permute-start(bf16[96,1024]{1,0:T(8,128)(2,1)S(1)} %add_convert_fusion.refs_0_.refs_8_), channel_id=1, source_target_pairs={{0,96},{32,0},{64,32},{96,64},{1,97},{33,1},{65,33},{97,65},{2,98}... | collective-permute-start | bytes 589832 | tf_op jit(solution)/shard_map/ppermute | solution.py:482
  132.9 0.8 collective-permute-done.29.refs_1_.refs_9_
  133.7 3.2 %collective-permute-start.35 = (bf16[96,1024]{1,0:T(8,128)(2,1)S(1)}, bf16[96,1024]{1,0:T(8,128)(2,1)S(1)}, u32[]{:S(2)}, u32[]{:S(2)}) collective-permute-start(bf16[96,1024]{1,0:T(8,128)(2,1)S(1)} %collective-permute-done.29.refs_1_.refs_9_), channel_id=1, source_target_pairs={{0,64},{32,96},{64,0},{96,32},{1,65},{33,97},{65,1},{97,33},{2,66}... | collective-permute-start | bytes 589832 | tf_op jit(solution)/shard_map/ppermute | solution.py:482
  136.9 2.0 %collective-permute-start.34 = (bf16[96,1024]{1,0:T(8,128)(2,1)S(1)}, bf16[96,1024]{1,0:T(8,128)(2,1)S(1)}, u32[]{:S(2)}, u32[]{:S(2)}) collective-permute-start(bf16[96,1024]{1,0:T(8,128)(2,1)S(1)} %collective-permute-done.29.refs_1_.refs_9_), channel_id=1, source_target_pairs={{0,96},{32,0},{64,32},{96,64},{1,97},{33,1},{65,33},{97,65},{2,98}... | collective-permute-start | bytes 589832 | tf_op jit(solution)/shard_map/ppermute | solution.py:482
  138.9 1.1 convolution_convert_fusion
  140.0 4.3 %collective-permute-done.30.refs_2_.refs_10_ = bf16[96,1024]{1,0:T(8,128)(2,1)S(1)} collective-permute-done((bf16[96,1024]{1,0:T(8,128)(2,1)S(1)}, bf16[96,1024]{1,0:T(8,128)(2,1)S(1)}, u32[]{:S(2)}, u32[]{:S(2)}) %collective-permute-start.30) | collective-permute-done | bytes 196640 | tf_op jit(solution)/shard_map/ppermute | solution.py:482
  144.3 1.0 collective-permute-done.34.refs_6_.refs_14_
  145.3 2.5 %collective-permute-done.33.refs_5_.refs_13_ = bf16[96,1024]{1,0:T(8,128)(2,1)S(1)} collective-permute-done((bf16[96,1024]{1,0:T(8,128)(2,1)S(1)}, bf16[96,1024]{1,0:T(8,128)(2,1)S(1)}, u32[]{:S(2)}, u32[]{:S(2)}) %collective-permute-start.33) | collective-permute-done | bytes 196640 | tf_op jit(solution)/shard_map/ppermute | solution.py:482
  147.8 2.0 %last.1 = (f32[256,512]{1,0:T(8,128)}, f32[256,512]{1,0:T(8,128)}) custom-call(bf16[768,256]{1,0:T(8,128)(2,1)S(1)} %multiply_convert_fusion.w_ref, bf16[96,1024]{1,0:T(8,128)(2,1)S(1)} %add_convert_fusion.refs_0_.refs_8_, bf16[96,1024]{1,0:T(8,128)(2,1)S(1)} %collective-permute-done.29.refs_1_.refs_9_, ...), custom_call_target="tpu_custom_call" | custom-call | tf_op jit(solution)/shard_map/last/pallas_call | solution.py:590
  (78 shorter events, 2.8 us)
Async XLA Ops:
  0.6 26.7 %collective-permute-start.1 = (bf16[512,2048]{1,0:T(8,128)(2,1)}, bf16[512,2048]{1,0:T(8,128)(2,1)S(1)}, u32[]{:S(2)}, u32[]{:S(2)}) collective-permute-start(bf16[512,2048]{1,0:T(8,128)(2,1)} %w0_ref), channel_id=1, source_target_pairs={{0,1},{1,0},{2,3},{3,2},{4,5},{5,4},{6,7},{7,6},{8,9},{9,8},{10,11... | collective-permute-start | bytes 6291464 | tf_op jit(solution)/shard_map/ppermute | solution.py:478
  6.0 1.6 %collective-permute-start = (f32[72,128]{1,0:T(8,128)}, f32[72,128]{1,0:T(8,128)S(1)}, u32[]{:S(2)}, u32[]{:S(2)}) collective-permute-start(f32[72,128]{1,0:T(8,128)} %get-tuple-element.59), channel_id=1, source_target_pairs={{0,1},{1,0},{2,3},{3,2},{4,5},{5,4},{6,7},{7,6},{8,9},{9,8},{10,11... | collective-permute-start | bytes 110600 | tf_op jit(solution)/shard_map/ppermute | solution.py:478
  9.1 14.0 %all-to-all-start = ((f32[8,72,128]{2,1,0:T(8,128)}), f32[8,72,128]{2,1,0:T(8,128)}, u32[]{:S(2)}, u32[]{:S(2)}) async-start(f32[8,72,128]{2,1,0:T(8,128)} %broadcast_in_dim.24), calls=%async_computation | async-start | bytes 589824 | tf_op jit(solution)/shard_map/all_to_all | solution.py:466
  21.9 19.0 %collective-permute-start.2 = (bf16[768,512]{1,0:T(8,128)(2,1)}, bf16[768,512]{1,0:T(8,128)(2,1)S(1)}, u32[]{:S(2)}, u32[]{:S(2)}) collective-permute-start(bf16[768,512]{1,0:T(8,128)(2,1)} %get-tuple-element.71.g0_ref), channel_id=1, source_target_pairs={{0,1},{1,0},{2,3},{3,2},{4,5},{5,4},{6,7},{7,6},{8,9},{9,8},{10,11... | collective-permute-start | bytes 2359304 | tf_op jit(solution)/shard_map/ppermute | solution.py:478
  22.1 18.8 %collective-permute-start.3 = (bf16[768,512]{1,0:T(8,128)(2,1)}, bf16[768,512]{1,0:T(8,128)(2,1)}, u32[]{:S(2)}, u32[]{:S(2)}) collective-permute-start(bf16[768,512]{1,0:T(8,128)(2,1)} %get-tuple-element.72.u0_ref), channel_id=1, source_target_pairs={{0,1},{1,0},{2,3},{3,2},{4,5},{5,4},{6,7},{7,6},{8,9},{9,8},{10,11... | collective-permute-start | bytes 2359304 | tf_op jit(solution)/shard_map/ppermute | solution.py:478
  27.4 1.3 copy-start.16
  28.7 18.3 %all-to-all-start.1 = ((bf16[8,64,768]{2,1,0:T(8,128)(2,1)}), bf16[8,64,768]{2,1,0:T(8,128)(2,1)S(1)}, u32[]{:S(2)}, u32[]{:S(2)}) async-start(bf16[8,64,768]{2,1,0:T(8,128)(2,1)} %get-tuple-element.69), calls=%async_computation.1 | async-start | bytes 1572864 | tf_op jit(solution)/shard_map/all_to_all | solution.py:466
  40.9 6.1 %copy-start.17 = (bf16[768,512]{1,0:T(8,128)(2,1)}, bf16[768,512]{1,0:T(8,128)(2,1)S(1)}, u32[]{:S(2)}) copy-start(bf16[768,512]{1,0:T(8,128)(2,1)S(1)} %collective-permute-done.2.g1_ref) | copy-start | bytes 2359300
  47.0 0.9 copy-start.12
  54.1 16.5 %all-to-all-start.2 = ((bf16[8,64,768]{2,1,0:T(8,128)(2,1)}), bf16[8,64,768]{2,1,0:T(8,128)(2,1)S(1)}, u32[]{:S(2)}, u32[]{:S(2)}) async-start(bf16[8,64,768]{2,1,0:T(8,128)(2,1)} %get-tuple-element.80), calls=%async_computation.2 | async-start | bytes 1572864 | tf_op jit(solution)/shard_map/all_to_all | solution.py:466
  57.7 4.4 %copy-start.13 = (bf16[8,64,768]{2,1,0:T(8,128)(2,1)S(1)}, bf16[8,64,768]{2,1,0:T(8,128)(2,1)}, u32[]{:S(2)}) copy-start(bf16[8,64,768]{2,1,0:T(8,128)(2,1)} %copy-done.12) | copy-start | bytes 2359300
  57.7 5.3 %copy-start.14 = (bf16[64,2048]{1,0:T(8,128)(2,1)S(1)}, bf16[64,2048]{1,0:T(8,128)(2,1)}, u32[]{:S(2)}) copy-start(bf16[64,2048]{1,0:T(8,128)(2,1)} %get-tuple-element.81) | copy-start | bytes 786436
  57.7 5.3 %copy-start.15 = (bf16[64,768]{1,0:T(8,128)(2,1)S(1)}, bf16[64,768]{1,0:T(8,128)(2,1)}, u32[]{:S(2)}) copy-start(bf16[64,768]{1,0:T(8,128)(2,1)} %get-tuple-element.82) | copy-start | bytes 294916
  62.3 20.7 %collective-permute-start.21 = (bf16[768,512]{1,0:T(8,128)(2,1)S(1)}, bf16[768,512]{1,0:T(8,128)(2,1)}, u32[]{:S(2)}, u32[]{:S(2)}) collective-permute-start(bf16[768,512]{1,0:T(8,128)(2,1)S(1)} %bitcast.16), channel_id=1, source_target_pairs={{0,1},{1,0},{2,3},{3,2},{4,5},{5,4},{6,7},{7,6},{8,9},{9,8},{10,11... | collective-permute-start | bytes 2359304 | tf_op jit(solution)/shard_map/ppermute | solution.py:478
  62.4 8.5 %collective-permute-start.4 = (bf16[512,512]{1,0:T(8,128)(2,1)}, bf16[512,512]{1,0:T(8,128)(2,1)}, u32[]{:S(2)}, u32[]{:S(2)}) collective-permute-start(bf16[512,512]{1,0:T(8,128)(2,1)} %get-tuple-element.85), channel_id=1, source_target_pairs={{0,1},{1,0},{2,3},{3,2},{4,5},{5,4},{6,7},{7,6},{8,9},{9,8},{10,11... | collective-permute-start | bytes 1572872 | tf_op jit(solution)/shard_map/ppermute | solution.py:478
  62.9 8.0 %collective-permute-start.5 = (bf16[512,512]{1,0:T(8,128)(2,1)}, bf16[512,512]{1,0:T(8,128)(2,1)}, u32[]{:S(2)}, u32[]{:S(2)}) collective-permute-start(bf16[512,512]{1,0:T(8,128)(2,1)} %get-tuple-element.86), channel_id=1, source_target_pairs={{0,1},{1,0},{2,3},{3,2},{4,5},{5,4},{6,7},{7,6},{8,9},{9,8},{10,11... | collective-permute-start | bytes 1572872 | tf_op jit(solution)/shard_map/ppermute | solution.py:478
  63.0 27.1 %copy-start = (bf16[512,768]{1,0:T(8,128)(2,1)S(1)}, bf16[512,768]{1,0:T(8,128)(2,1)}, u32[]{:S(2)}) copy-start(bf16[512,768]{1,0:T(8,128)(2,1)} %get-tuple-element.75.d0_ref.refs_8_) | copy-start | bytes 2359300
  63.0 27.1 %copy-start.1 = (bf16[512,512]{1,0:T(8,128)(2,1)S(1)}, bf16[512,512]{1,0:T(8,128)(2,1)}, u32[]{:S(2)}) copy-start(bf16[512,512]{1,0:T(8,128)(2,1)} %get-tuple-element.93.refs_9_) | copy-start | bytes 1572868
  71.0 7.1 %collective-permute-start.13 = (bf16[64,768]{1,0:T(8,128)(2,1)S(1)}, bf16[64,768]{1,0:T(8,128)(2,1)S(1)}, u32[]{:S(2)}, u32[]{:S(2)}) collective-permute-start(bf16[64,768]{1,0:T(8,128)(2,1)S(1)} %error.1.refs_0_), channel_id=1, source_target_pairs={{0,4},{2,6},{4,0},{6,2},{1,5},{3,7},{5,1},{7,3},{8,12},{10,14},{12... | collective-permute-start | bytes 294920 | tf_op jit(solution)/shard_map/ppermute | solution.py:482
  71.9 6.2 %collective-permute-start.11 = (bf16[64,768]{1,0:T(8,128)(2,1)S(1)}, bf16[64,768]{1,0:T(8,128)(2,1)S(1)}, u32[]{:S(2)}, u32[]{:S(2)}) collective-permute-start(bf16[64,768]{1,0:T(8,128)(2,1)S(1)} %error.1.refs_0_), channel_id=1, source_target_pairs={{0,6},{2,0},{4,2},{6,4},{1,7},{3,1},{5,3},{7,5},{8,14},{10,8},{12,... | collective-permute-start | bytes 294920 | tf_op jit(solution)/shard_map/ppermute | solution.py:482
  74.6 5.8 %collective-permute-start.9 = (bf16[64,768]{1,0:T(8,128)(2,1)S(1)}, bf16[64,768]{1,0:T(8,128)(2,1)S(1)}, u32[]{:S(2)}, u32[]{:S(2)}) collective-permute-start(bf16[64,768]{1,0:T(8,128)(2,1)S(1)} %error.1.refs_0_), channel_id=1, source_target_pairs={{0,2},{2,4},{4,6},{6,0},{1,3},{3,5},{5,7},{7,1},{8,10},{10,12},{12... | collective-permute-start | bytes 294920 | tf_op jit(solution)/shard_map/ppermute | solution.py:482
  74.6 5.8 %collective-permute-start.7 = (bf16[64,768]{1,0:T(8,128)(2,1)S(1)}, bf16[64,768]{1,0:T(8,128)(2,1)S(1)}, u32[]{:S(2)}, u32[]{:S(2)}) collective-permute-start(bf16[64,768]{1,0:T(8,128)(2,1)S(1)} %error.1.refs_0_), channel_id=1, source_target_pairs={{0,8},{8,0},{1,9},{9,1},{2,10},{10,2},{3,11},{11,3},{4,12},{12,4},... | collective-permute-start | bytes 294920 | tf_op jit(solution)/shard_map/ppermute | solution.py:478
  78.0 3.2 %collective-permute-start.6 = (bf16[64,768]{1,0:T(8,128)(2,1)S(1)}, bf16[64,768]{1,0:T(8,128)(2,1)S(1)}, u32[]{:S(2)}, u32[]{:S(2)}) collective-permute-start(bf16[64,768]{1,0:T(8,128)(2,1)S(1)} %error.1.refs_0_), channel_id=1, source_target_pairs={{0,1},{1,0},{2,3},{3,2},{4,5},{5,4},{6,7},{7,6},{8,9},{9,8},{10,11... | collective-permute-start | bytes 294920 | tf_op jit(solution)/shard_map/ppermute | solution.py:478
  78.0 5.9 %collective-permute-start.14 = (bf16[64,768]{1,0:T(8,128)(2,1)S(1)}, bf16[64,768]{1,0:T(8,128)(2,1)S(1)}, u32[]{:S(2)}, u32[]{:S(2)}) collective-permute-start(bf16[64,768]{1,0:T(8,128)(2,1)S(1)} %collective-permute-done.13.refs_4_), channel_id=1, source_target_pairs={{0,1},{1,0},{2,3},{3,2},{4,5},{5,4},{6,7},{7,6},{8,9},{9,8},{10,11... | collective-permute-start | bytes 294920 | tf_op jit(solution)/shard_map/ppermute | solution.py:478
  80.4 4.2 %collective-permute-start.12 = (bf16[64,768]{1,0:T(8,128)(2,1)S(1)}, bf16[64,768]{1,0:T(8,128)(2,1)S(1)}, u32[]{:S(2)}, u32[]{:S(2)}) collective-permute-start(bf16[64,768]{1,0:T(8,128)(2,1)S(1)} %collective-permute-done.11.refs_3_), channel_id=1, source_target_pairs={{0,1},{1,0},{2,3},{3,2},{4,5},{5,4},{6,7},{7,6},{8,9},{9,8},{10,11... | collective-permute-start | bytes 294920 | tf_op jit(solution)/shard_map/ppermute | solution.py:478
  80.4 6.8 %collective-permute-start.19 = (bf16[64,768]{1,0:T(8,128)(2,1)S(1)}, bf16[64,768]{1,0:T(8,128)(2,1)S(1)}, u32[]{:S(2)}, u32[]{:S(2)}) collective-permute-start(bf16[64,768]{1,0:T(8,128)(2,1)S(1)} %collective-permute-done.7.refs_1_), channel_id=1, source_target_pairs={{0,4},{2,6},{4,0},{6,2},{1,5},{3,7},{5,1},{7,3},{8,12},{10,14},{12... | collective-permute-start | bytes 294920 | tf_op jit(solution)/shard_map/ppermute | solution.py:482
  81.2 0.6 copy-start.6
  81.9 5.6 %collective-permute-start.17 = (bf16[64,768]{1,0:T(8,128)(2,1)S(1)}, bf16[64,768]{1,0:T(8,128)(2,1)}, u32[]{:S(2)}, u32[]{:S(2)}) collective-permute-start(bf16[64,768]{1,0:T(8,128)(2,1)S(1)} %collective-permute-done.7.refs_1_), channel_id=1, source_target_pairs={{0,6},{2,0},{4,2},{6,4},{1,7},{3,1},{5,3},{7,5},{8,14},{10,8},{12,... | collective-permute-start | bytes 294920 | tf_op jit(solution)/shard_map/ppermute | solution.py:482
  83.1 6.3 %collective-permute-start.15 = (bf16[64,768]{1,0:T(8,128)(2,1)S(1)}, bf16[64,768]{1,0:T(8,128)(2,1)}, u32[]{:S(2)}, u32[]{:S(2)}) collective-permute-start(bf16[64,768]{1,0:T(8,128)(2,1)S(1)} %collective-permute-done.7.refs_1_), channel_id=1, source_target_pairs={{0,2},{2,4},{4,6},{6,0},{1,3},{3,5},{5,7},{7,1},{8,10},{10,12},{12... | collective-permute-start | bytes 294920 | tf_op jit(solution)/shard_map/ppermute | solution.py:482
  83.9 0.6 copy-start.8
  84.6 9.4 %collective-permute-start.8 = (bf16[64,768]{1,0:T(8,128)(2,1)S(1)}, bf16[64,768]{1,0:T(8,128)(2,1)}, u32[]{:S(2)}, u32[]{:S(2)}) collective-permute-start(bf16[64,768]{1,0:T(8,128)(2,1)S(1)} %collective-permute-done.7.refs_1_), channel_id=1, source_target_pairs={{0,1},{1,0},{2,3},{3,2},{4,5},{5,4},{6,7},{7,6},{8,9},{9,8},{10,11... | collective-permute-start | bytes 294920 | tf_op jit(solution)/shard_map/ppermute | solution.py:478
  84.6 0.6 copy-start.10
  85.2 8.7 %collective-permute-start.10 = (bf16[64,768]{1,0:T(8,128)(2,1)S(1)}, bf16[64,768]{1,0:T(8,128)(2,1)}, u32[]{:S(2)}, u32[]{:S(2)}) collective-permute-start(bf16[64,768]{1,0:T(8,128)(2,1)S(1)} %collective-permute-done.9.refs_2_), channel_id=1, source_target_pairs={{0,1},{1,0},{2,3},{3,2},{4,5},{5,4},{6,7},{7,6},{8,9},{9,8},{10,11... | collective-permute-start | bytes 294920 | tf_op jit(solution)/shard_map/ppermute | solution.py:478
  87.2 6.8 %collective-permute-start.20 = (bf16[64,768]{1,0:T(8,128)(2,1)S(1)}, bf16[64,768]{1,0:T(8,128)(2,1)}, u32[]{:S(2)}, u32[]{:S(2)}) collective-permute-start(bf16[64,768]{1,0:T(8,128)(2,1)S(1)} %collective-permute-done.19.refs_7_), channel_id=1, source_target_pairs={{0,1},{1,0},{2,3},{3,2},{4,5},{5,4},{6,7},{7,6},{8,9},{9,8},{10,11... | collective-permute-start | bytes 294920 | tf_op jit(solution)/shard_map/ppermute | solution.py:478
  87.4 6.6 %collective-permute-start.18 = (bf16[64,768]{1,0:T(8,128)(2,1)}, bf16[64,768]{1,0:T(8,128)(2,1)}, u32[]{:S(2)}, u32[]{:S(2)}) collective-permute-start(bf16[64,768]{1,0:T(8,128)(2,1)} %collective-permute-done.17.refs_6_), channel_id=1, source_target_pairs={{0,1},{1,0},{2,3},{3,2},{4,5},{5,4},{6,7},{7,6},{8,9},{9,8},{10,11... | collective-permute-start | bytes 294920 | tf_op jit(solution)/shard_map/ppermute | solution.py:478
  89.3 4.7 %collective-permute-start.16 = (bf16[64,768]{1,0:T(8,128)(2,1)}, bf16[64,768]{1,0:T(8,128)(2,1)}, u32[]{:S(2)}, u32[]{:S(2)}) collective-permute-start(bf16[64,768]{1,0:T(8,128)(2,1)} %collective-permute-done.15.refs_5_), channel_id=1, source_target_pairs={{0,1},{1,0},{2,3},{3,2},{4,5},{5,4},{6,7},{7,6},{8,9},{9,8},{10,11... | collective-permute-start | bytes 294920 | tf_op jit(solution)/shard_map/ppermute | solution.py:478
  90.1 1.0 copy-start.2
  91.1 2.9 %copy-start.7 = (bf16[64,768]{1,0:T(8,128)(2,1)S(1)}, bf16[64,768]{1,0:T(8,128)(2,1)}, u32[]{:S(2)}) copy-start(bf16[64,768]{1,0:T(8,128)(2,1)} %copy-done.6) | copy-start | bytes 294916
  91.1 2.9 %copy-start.9 = (bf16[64,768]{1,0:T(8,128)(2,1)S(1)}, bf16[64,768]{1,0:T(8,128)(2,1)}, u32[]{:S(2)}) copy-start(bf16[64,768]{1,0:T(8,128)(2,1)} %copy-done.8) | copy-start | bytes 294916
  91.1 2.9 %copy-start.11 = (bf16[64,768]{1,0:T(8,128)(2,1)S(1)}, bf16[64,768]{1,0:T(8,128)(2,1)}, u32[]{:S(2)}) copy-start(bf16[64,768]{1,0:T(8,128)(2,1)} %copy-done.10) | copy-start | bytes 294916
  100.3 0.7 copy-start.3
  101.0 0.7 copy-start.4
  101.7 0.7 copy-start.5
  102.4 9.3 %collective-permute-start.25 = (bf16[96,1024]{1,0:T(8,128)(2,1)}, bf16[96,1024]{1,0:T(8,128)(2,1)S(1)}, u32[]{:S(2)}, u32[]{:S(2)}) collective-permute-start(bf16[96,1024]{1,0:T(8,128)(2,1)} %get-tuple-element.101), channel_id=1, source_target_pairs={{0,32},{32,64},{64,96},{96,0},{1,33},{33,65},{65,97},{97,1},{2,34}... | collective-permute-start | bytes 589832 | tf_op jit(solution)/shard_map/ppermute | solution.py:482
  103.9 13.7 %collective-permute-start.26 = (bf16[96,1024]{1,0:T(8,128)(2,1)}, bf16[96,1024]{1,0:T(8,128)(2,1)S(1)}, u32[]{:S(2)}, u32[]{:S(2)}) collective-permute-start(bf16[96,1024]{1,0:T(8,128)(2,1)} %get-tuple-element.102), channel_id=1, source_target_pairs={{0,96},{32,0},{64,32},{96,64},{1,97},{33,1},{65,33},{97,65},{2,98}... | collective-permute-start | bytes 589832 | tf_op jit(solution)/shard_map/ppermute | solution.py:482
  105.6 12.1 %collective-permute-start.27 = (bf16[96,1024]{1,0:T(8,128)(2,1)}, bf16[96,1024]{1,0:T(8,128)(2,1)S(1)}, u32[]{:S(2)}, u32[]{:S(2)}) collective-permute-start(bf16[96,1024]{1,0:T(8,128)(2,1)} %get-tuple-element.103), channel_id=1, source_target_pairs={{0,64},{32,96},{64,0},{96,32},{1,65},{33,97},{65,1},{97,33},{2,66}... | collective-permute-start | bytes 589832 | tf_op jit(solution)/shard_map/ppermute | solution.py:482
  108.4 15.0 %collective-permute-start.22 = (bf16[96,1024]{1,0:T(8,128)(2,1)}, bf16[96,1024]{1,0:T(8,128)(2,1)S(1)}, u32[]{:S(2)}, u32[]{:S(2)}) collective-permute-start(bf16[96,1024]{1,0:T(8,128)(2,1)} %copy-done.5), channel_id=1, source_target_pairs={{0,32},{32,64},{64,96},{96,0},{1,33},{33,65},{65,97},{97,1},{2,34}... | collective-permute-start | bytes 589832 | tf_op jit(solution)/shard_map/ppermute | solution.py:482
  109.1 14.2 %collective-permute-start.23 = (bf16[96,1024]{1,0:T(8,128)(2,1)}, bf16[96,1024]{1,0:T(8,128)(2,1)S(1)}, u32[]{:S(2)}, u32[]{:S(2)}) collective-permute-start(bf16[96,1024]{1,0:T(8,128)(2,1)} %copy-done.4), channel_id=1, source_target_pairs={{0,96},{32,0},{64,32},{96,64},{1,97},{33,1},{65,33},{97,65},{2,98}... | collective-permute-start | bytes 589832 | tf_op jit(solution)/shard_map/ppermute | solution.py:482
  111.7 13.3 %collective-permute-start.24 = (bf16[96,1024]{1,0:T(8,128)(2,1)}, bf16[96,1024]{1,0:T(8,128)(2,1)S(1)}, u32[]{:S(2)}, u32[]{:S(2)}) collective-permute-start(bf16[96,1024]{1,0:T(8,128)(2,1)} %copy-done.3), channel_id=1, source_target_pairs={{0,64},{32,96},{64,0},{96,32},{1,65},{33,97},{65,1},{97,33},{2,66}... | collective-permute-start | bytes 589832 | tf_op jit(solution)/shard_map/ppermute | solution.py:482
  117.8 7.4 %collective-permute-start.28 = (bf16[96,1024]{1,0:T(8,128)(2,1)S(1)}, bf16[96,1024]{1,0:T(8,128)(2,1)S(1)}, u32[]{:S(2)}, u32[]{:S(2)}) collective-permute-start(bf16[96,1024]{1,0:T(8,128)(2,1)S(1)} %add_convert_fusion.1), channel_id=1, source_target_pairs={{0,16},{16,0},{1,17},{17,1},{2,18},{18,2},{3,19},{19,3},{4,20},{20... | collective-permute-start | bytes 589832 | tf_op jit(solution)/shard_map/ppermute | solution.py:478
  125.3 13.6 %collective-permute-start.32 = (bf16[96,1024]{1,0:T(8,128)(2,1)S(1)}, bf16[96,1024]{1,0:T(8,128)(2,1)S(1)}, u32[]{:S(2)}, u32[]{:S(2)}) collective-permute-start(bf16[96,1024]{1,0:T(8,128)(2,1)S(1)} %add_convert_fusion.refs_0_.refs_8_), channel_id=1, source_target_pairs={{0,64},{32,96},{64,0},{96,32},{1,65},{33,97},{65,1},{97,33},{2,66}... | collective-permute-start | bytes 589832 | tf_op jit(solution)/shard_map/ppermute | solution.py:482
  126.0 7.7 %collective-permute-start.29 = (bf16[96,1024]{1,0:T(8,128)(2,1)S(1)}, bf16[96,1024]{1,0:T(8,128)(2,1)S(1)}, u32[]{:S(2)}, u32[]{:S(2)}) collective-permute-start(bf16[96,1024]{1,0:T(8,128)(2,1)S(1)} %add_convert_fusion.refs_0_.refs_8_), channel_id=1, source_target_pairs={{0,16},{16,0},{1,17},{17,1},{2,18},{18,2},{3,19},{19,3},{4,20},{20... | collective-permute-start | bytes 589832 | tf_op jit(solution)/shard_map/ppermute | solution.py:478
  129.6 10.4 %collective-permute-start.31 = (bf16[96,1024]{1,0:T(8,128)(2,1)S(1)}, bf16[96,1024]{1,0:T(8,128)(2,1)S(1)}, u32[]{:S(2)}, u32[]{:S(2)}) collective-permute-start(bf16[96,1024]{1,0:T(8,128)(2,1)S(1)} %add_convert_fusion.refs_0_.refs_8_), channel_id=1, source_target_pairs={{0,96},{32,0},{64,32},{96,64},{1,97},{33,1},{65,33},{97,65},{2,98}... | collective-permute-start | bytes 589832 | tf_op jit(solution)/shard_map/ppermute | solution.py:482
  132.8 11.5 %collective-permute-start.30 = (bf16[96,1024]{1,0:T(8,128)(2,1)S(1)}, bf16[96,1024]{1,0:T(8,128)(2,1)S(1)}, u32[]{:S(2)}, u32[]{:S(2)}) collective-permute-start(bf16[96,1024]{1,0:T(8,128)(2,1)S(1)} %add_convert_fusion.refs_0_.refs_8_), channel_id=1, source_target_pairs={{0,32},{32,64},{64,96},{96,0},{1,33},{33,65},{65,97},{97,1},{2,34}... | collective-permute-start | bytes 589832 | tf_op jit(solution)/shard_map/ppermute | solution.py:482
  133.7 10.6 %collective-permute-start.35 = (bf16[96,1024]{1,0:T(8,128)(2,1)S(1)}, bf16[96,1024]{1,0:T(8,128)(2,1)S(1)}, u32[]{:S(2)}, u32[]{:S(2)}) collective-permute-start(bf16[96,1024]{1,0:T(8,128)(2,1)S(1)} %collective-permute-done.29.refs_1_.refs_9_), channel_id=1, source_target_pairs={{0,64},{32,96},{64,0},{96,32},{1,65},{33,97},{65,1},{97,33},{2,66}... | collective-permute-start | bytes 589832 | tf_op jit(solution)/shard_map/ppermute | solution.py:482
  136.9 8.4 %collective-permute-start.34 = (bf16[96,1024]{1,0:T(8,128)(2,1)S(1)}, bf16[96,1024]{1,0:T(8,128)(2,1)S(1)}, u32[]{:S(2)}, u32[]{:S(2)}) collective-permute-start(bf16[96,1024]{1,0:T(8,128)(2,1)S(1)} %collective-permute-done.29.refs_1_.refs_9_), channel_id=1, source_target_pairs={{0,96},{32,0},{64,32},{96,64},{1,97},{33,1},{65,33},{97,65},{2,98}... | collective-permute-start | bytes 589832 | tf_op jit(solution)/shard_map/ppermute | solution.py:482
  138.9 8.9 %collective-permute-start.33 = (bf16[96,1024]{1,0:T(8,128)(2,1)S(1)}, bf16[96,1024]{1,0:T(8,128)(2,1)S(1)}, u32[]{:S(2)}, u32[]{:S(2)}) collective-permute-start(bf16[96,1024]{1,0:T(8,128)(2,1)S(1)} %collective-permute-done.29.refs_1_.refs_9_), channel_id=1, source_target_pairs={{0,32},{32,64},{64,96},{96,0},{1,33},{33,65},{65,97},{97,1},{2,34}... | collective-permute-start | bytes 589832 | tf_op jit(solution)/shard_map/ppermute | solution.py:482

commit v7 on v5

--- a/solution.py
+++ b/solution.py
@@ -331,32 +331,32 @@
     dgate, dup = hidden_grads(errb, db, ab, bb, copies)
     for c in copies[4:]:
         c.wait()
-    width, tall = dgate.shape[1], 256
-    for i in range(yb.shape[0] // tall):
-        at = pl.ds(i * tall, tall)
-        yb[at, :width] = (dot(x0b[at], dgb[...]) + dot(x1b[at], dgate)).astype(BF16)
-        yb[at, width:] = (dot(x0b[at], dub[...]) + dot(x1b[at], dup)).astype(BF16)
-    rows, sends = outs[0].shape[0], []
-    for i, (flip, d) in enumerate(SENT):
-        at = pl.ds(pl.multiple_of(group_block(flip, d) * rows, rows), rows)
-        sends.append(pltpu.make_async_copy(yb.at[at], outs[i], out_sem.at[i]))
-        sends[-1].start()
+    width, rows = dgate.shape[1], outs[0].shape[0]
+    y, zh = lax.axis_index("y"), lax.axis_index("zh")
+    sends = []
+    for i, d in enumerate(SHIFTS + (0,)):
+        at = pl.ds(pl.multiple_of(lax.rem(y + d, 4) * (2 * rows), 2 * rows), 2 * rows)
+        slot = pl.ds(i * 2 * rows, 2 * rows)
+        left, right = x0b[at], x1b[at]
+        yb[slot, :width] = (dot(left, dgb[...]) + dot(right, dgate)).astype(BF16)
+        yb[slot, width:] = (dot(left, dub[...]) + dot(right, dup)).astype(BF16)
+        for flip in (1, 0):
+            at = pl.ds(pl.multiple_of(i * 2 * rows + (1 - zh if flip else zh) * rows, rows), rows)
+            j = SENT.index((flip, d))
+            sends.append(pltpu.make_async_copy(yb.at[at], outs[j], out_sem.at[j]))
+            sends[-1].start()
     for c in sends:
         c.wait()
 
 
 def last_kernel(w_ref, *refs):
-    parts, (gate_ref, up_ref, wb, yb, sem, y_sem) = refs[: len(GOT)], refs[len(GOT) :]
-    rows = parts[0].shape[0]
-    slots = [pl.ds(i * rows, rows) for i in range(len(GOT))]
+    count = len(GOT)
+    rows = refs[0].shape[0]
     blocks = [pl.ds(pl.multiple_of(group_block(flip, -d) * rows, rows), rows) for flip, d in GOT]
-    copies = fetch([w_ref.at[b] for b in blocks], [wb.at[i] for i in slots], sem)
-    copies += fetch(parts, [yb.at[i] for i in slots], y_sem)
-    for c in copies:
-        c.wait()
-    width = gate_ref.shape[1]
-    gate_ref[...] = tn(wb[...], yb[:, :width])
-    up_ref[...] = tn(wb[...], yb[:, width:])
+    w = jnp.concatenate([w_ref[b] for b in blocks], axis=0)
+    for side, out_ref in enumerate(refs[2 * count :]):
+        y = jnp.concatenate([r[...] for r in refs[side * count : (side + 1) * count]], axis=0)
+        out_ref[...] = tn(w, y)
 
 
 VM = pl.BlockSpec(memory_space=pltpu.VMEM)
@@ -536,11 +536,6 @@
     x_late, slope_a = lax.optimization_barrier((x_late, slope_a))
     x_late = lax.optimization_barrier(x_late.reshape(half, FEATS).T)
     x_other = swap(x_late)
-    at = lax.axis_index(GRP)
-    block = w_in.shape[1] // groups
-    w_own = lax.optimization_barrier(lax.dynamic_slice_in_dim(w_in_late, at * block, block, 1))
-    gain_own = lax.dynamic_slice_in_dim(gain, at * block, block, 0)
-    w_own = lax.optimization_barrier((w_own.astype(F32) * gain_own).astype(BF16))
     err_own = pl.pallas_call(
         error_kernel, grid=(3,), out_shape=sds((chips, COUNT, FEATS), BF16),
         in_specs=[cut(parts.shape, 3), cut(base.shape, 3)], out_specs=cut(parts.shape, 3),
@@ -558,6 +553,13 @@
         (piece,) * len(SENT), [pltpu.VMEM((FEATS, 2 * width), BF16)], 2000000000, (8, len(SENT)),
         (HB,) * len(SENT),
     )
+    pieces = list(pieces)
+    pieces[0], gain_late, w_in_late = lax.optimization_barrier((pieces[0], gain, w_in_late))
+    at = lax.axis_index(GRP)
+    block = w_in.shape[1] // groups
+    w_own = lax.optimization_barrier(lax.dynamic_slice_in_dim(w_in_late, at * block, block, 1))
+    gain_own = lax.dynamic_slice_in_dim(gain_late, at * block, block, 0)
+    w_own = lax.optimization_barrier((w_own.astype(F32) * gain_own).astype(BF16))
     moved = [shift(p, d) if d else p for p, (_, d) in zip(pieces, SENT)]
     theirs = swap(total(*moved[:4]), "zh")
     grads = total(*moved[4:], theirs)
@@ -565,10 +567,12 @@
     twin = swap(grads, "zh")
     got = [grads, twin] + [shift(v, d) for v in (grads, twin) for d in SHIFTS]
     grad = sds((block, width), F32)
-    grad_gate, grad_up = staged(
-        last_kernel, "last", (w_own, *got), (grad, grad), [], 400000000, (len(GOT),) * 2, (VM,) * 2,
-        bufs=[vmem_like(w_own), pltpu.VMEM((FEATS, 2 * width), BF16)], params=MIDDLE,
-    )
+    grad_gate, grad_up = pl.pallas_call(
+        last_kernel, grid=(2,), out_shape=(grad, grad),
+        in_specs=[pl.BlockSpec(w_own.shape, lambda i: (0, 0))]
+        + [cut(piece.shape, 4)] * len(GOT) + [cut(piece.shape, 4, 2)] * len(GOT),
+        out_specs=(cut(grad.shape, 2),) * 2, compiler_params=SMALL, name="last",
+    )(w_own, *got, *got)
     err_all = jnp.concatenate([err_late, err_other], axis=0).reshape(2 * half, FEATS)
     core = lax.axis_index("core")
     codes = recv[:, CODE_ROW : CODE_ROW + 2, :COUNT]

time: 150 us -> 146 us (0.973)
  Pallas kernels: 48.6 us -> 46.1 us
  waiting for transfers between devices: 35.4 us -> 33.7 us
    pallas_call x6 -> x5, Pallas kernels: 33.2 us -> 28.6 us  [staged(): pl.pallas_call(kernel, out_shape=out_shape, in_specs=[HB] * len(args), ou...]
    pallas_call x0 -> x1, Pallas kernels: none -> 2.04 us  [body(): pl.pallas_call(last_kernel, grid=(2,), out_shape=(grad, grad), in_specs=[...]
    ppermute x12, waiting for transfers between devices: 8.46 us -> 6.9 us  [shift(): return lax.ppermute(x, 'y', [(i, (i + d) % 4) for i in range(4)])]
    unnamed x26 -> x28, local copies, waits for them, and re-layouts: 2.66 us -> 3.64 us
  transfers between devices with their start and end apart: 26 -> 26, of which waited for: 13 -> 11; matrix products, arithmetic and copies ran while one was open for 7% -> 7% of each run, Pallas kernels for 22% -> 23%
where the time goes in v7:
time: 146 us; the launch traced here: 145 us
  starting transfers between devices  49.8 us (34%)
  Pallas kernels  46.1 us (32%)
  waiting for transfers between devices  33.7 us (23%)
  local copies, waits for them, and re-layouts  7.3 us (5%)
  other arithmetic  3.9 us (3%)
  matrix products  3.65 us (2%)
    pallas_call x5, Pallas kernels, staged(): pl.pallas_call(kernel, out_shape=out_shape, in_specs=[HB] * len(args), ou...  28.6 us
    all_to_all x4, waiting for transfers between devices, exchange(): return lax.all_to_all(x, axes, split_axis=0, concat_axis=0, tiled=True)  24.7 us
    ppermute x12, starting transfers between devices, shift(): return lax.ppermute(x, 'y', [(i, (i + d) % 4) for i in range(4)])  22.6 us
    all_to_all x4, starting transfers between devices, exchange(): return lax.all_to_all(x, axes, split_axis=0, concat_axis=0, tiled=True)  18.1 us
    ppermute x10, starting transfers between devices, swap(): return lax.ppermute(x, axis, SWAP)  9.02 us
    ppermute x12, waiting for transfers between devices, shift(): return lax.ppermute(x, 'y', [(i, (i + d) % 4) for i in range(4)])  6.9 us
    pallas_call x1, Pallas kernels, evolve(): pl.pallas_call(evolve_kernel, out_shape=(sds((ROWS, LANES), F32), sds((2...  5.24 us
    pallas_call x1, Pallas kernels, body(): pl.pallas_call(slopes_kernel, grid=(4,), out_shape=(slope,) * 4, in_specs...  4.34 us
  transfers between devices with their start and end apart: 26, of which 11 were waited for; matrix products, arithmetic and copies ran while one was open for 7% of the time, Pallas kernels for 23%

profile of v7, /device:TPU:0, one launch (start us, length us, event | category | flops | bytes accessed | tf_op | source)
XLA Modules:
  0.0 145.4 jit_solution(17632624652574680015)
XLA Ops:
  0.6 0.1 collective-permute-start.1
  0.7 5.2 %evolve.1 = (f32[72,128]{1,0:T(8,128)}, bf16[128,768]{1,0:T(8,128)(2,1)}, f32[24,128]{1,0:T(8,128)}, f32[3,256,128]{2,1,0:T(8,128)}) custom-call(f32[3,256,128]{2,1,0:T(8,128)} %pos_ref.3, f32[3,256,128]{2,1,0:T(8,128)} %vel_ref.3, f32[1,128]{1,0:T(1,128)} %bitcast.23, s32[8,256,128]{2,1,0:T(8,128)} %contact_ref.3, f32[3,128]{1,0:T(4,128)} %off_ref.3, ...), custom_call_target="tpu_custom_call" | custom-call | flops 260000000 | bytes 3000000 | tf_op jit(solution)/shard_map/evolve/pallas_call | solution.py:375
  6.0 0.6 collective-permute-start
  6.5 1.1 collective-permute-done
  7.6 0.8 add.110
  8.4 0.7 broadcast_in_dim.24
  9.1 5.7 %all-to-all-start = ((f32[8,72,128]{2,1,0:T(8,128)}), f32[8,72,128]{2,1,0:T(8,128)S(1)}, u32[]{:S(2)}, u32[]{:S(2)}) async-start(f32[8,72,128]{2,1,0:T(8,128)} %broadcast_in_dim.24), calls=%async_computation | async-start | bytes 589824 | tf_op jit(solution)/shard_map/all_to_all | solution.py:452
  14.9 7.1 %products.1 = (bf16[768,512]{1,0:T(8,128)(2,1)}, bf16[768,512]{1,0:T(8,128)(2,1)}) custom-call(bf16[768,2048]{1,0:T(8,128)(2,1)} %w_in_ref.2, f32[1,2048]{1,0:T(1,128)} %bitcast.30, bf16[2048,512]{1,0:T(8,128)(2,1)} %gate_ref.1, bf16[2048,512]{1,0:T(8,128)(2,1)} %up_ref.1), custom_call_target="tpu_custom_call" | custom-call | flops 3300000000 | bytes 8000000 | tf_op jit(solution)/shard_map/products/pallas_call | solution.py:434
  21.9 0.1 collective-permute-start.2
  22.1 0.4 collective-permute-start.3
  22.5 0.5 all-to-all-done.recv_ref
  23.0 0.7 copy-done.4
  23.7 4.2 %finish.1 = (bf16[8,64,768]{2,1,0:T(8,128)(2,1)}, bf16[64,768]{1,0:T(8,128)(2,1)}, bf16[64,2048]{1,0:T(8,128)(2,1)}, f32[3,128]{1,0:T(4,128)}, f32[3,256,128]{2,1,0:T(8,128)}) custom-call(f32[8,72,128]{2,1,0:T(8,128)} %copy-done.4, f32[24,128]{1,0:T(8,128)} %get-tuple-element.62.bound_ref, ...), custom_call_target="tpu_custom_call", output_to_operand_aliasing={{4}: (18, {})} | custom-call | flops 300000000 | bytes 4000000 | tf_op jit(solution)/shard_map/finish/pallas_call | solution.py:408
  28.0 5.2 %all-to-all-start.1 = ((bf16[8,64,768]{2,1,0:T(8,128)(2,1)}), bf16[8,64,768]{2,1,0:T(8,128)(2,1)S(1)}, u32[]{:S(2)}, u32[]{:S(2)}) async-start(bf16[8,64,768]{2,1,0:T(8,128)(2,1)} %get-tuple-element.70), calls=%async_computation.1 | async-start | bytes 1572864 | tf_op jit(solution)/shard_map/all_to_all | solution.py:452
  33.2 7.0 %down.1 = (bf16[512,768]{1,0:T(8,128)(2,1)}, bf16[512,768]{1,0:T(8,128)(2,1)}) custom-call(bf16[512,2048]{1,0:T(8,128)(2,1)} %w0_ref, bf16[512,2048]{1,0:T(8,128)(2,1)} %copy-done.10, bf16[2048,768]{1,0:T(8,128)(2,1)} %out_ref.1), custom_call_target="tpu_custom_call" | custom-call | flops 3300000000 | bytes 8000000 | tf_op jit(solution)/shard_map/down/pallas_call | solution.py:434
  40.2 0.0 collective-permute-done.2.g1_ref
  40.3 6.1 %all-to-all-done.1.x_ref = bf16[8,64,768]{2,1,0:T(8,128)(2,1)S(1)} async-done(((bf16[8,64,768]{2,1,0:T(8,128)(2,1)}), bf16[8,64,768]{2,1,0:T(8,128)(2,1)S(1)}, u32[]{:S(2)}, u32[]{:S(2)}) %all-to-all-start.1) | async-done | bytes 786464 | tf_op jit(solution)/shard_map/all_to_all | solution.py:452
  46.4 0.9 copy-done.2
  47.3 6.2 %forward.1 = (bf16[8,64,768]{2,1,0:T(8,128)(2,1)}, f32[2,512,512]{2,1,0:T(8,128)}, f32[2,512,512]{2,1,0:T(8,128)}) custom-call(bf16[8,64,768]{2,1,0:T(8,128)(2,1)} %copy-done.2, bf16[768,512]{1,0:T(8,128)(2,1)} %get-tuple-element.72.g0_ref, bf16[768,512]{1,0:T(8,128)(2,1)} %get-tuple-element.73.u0_ref, bf16[512,768]{1,0:T(8,128)(2,1)} %get-tuple-element.76.d0_ref.d_ref, ...), custom_call_target="tpu_custom_call" | custom-call | flops 2500000000 | bytes 8000000 | tf_op jit(solution)/shard_map/forward/pallas_call | solution.py:434
  53.5 3.6 %all-to-all-start.2 = ((bf16[8,64,768]{2,1,0:T(8,128)(2,1)}), bf16[8,64,768]{2,1,0:T(8,128)(2,1)S(1)}, u32[]{:S(2)}, u32[]{:S(2)}) async-start(bf16[8,64,768]{2,1,0:T(8,128)(2,1)} %get-tuple-element.81), calls=%async_computation.2 | async-start | bytes 1572864 | tf_op jit(solution)/shard_map/all_to_all | solution.py:452
  57.1 4.3 %slopes.1 = (bf16[512,512]{1,0:T(8,128)(2,1)}, bf16[512,512]{1,0:T(8,128)(2,1)}, bf16[512,512]{1,0:T(8,128)(2,1)}, bf16[512,512]{1,0:T(8,128)(2,1)}) custom-call(f32[2,512,512]{2,1,0:T(8,128)} %get-tuple-element.84.gate_ref, f32[2,512,512]{2,1,0:T(8,128)} %get-tuple-element.85.up_ref), custom_call_target="tpu_custom_call" | custom-call | flops 8000000 | bytes 6000000 | tf_op jit(solution)/shard_map/slopes/pallas_call | solution.py:530
  61.4 0.5 collective-permute-start.5
  61.9 2.5 %convolution_subtract_fusion.base_ref = f32[64,768]{1,0:T(8,128)S(1)} fusion(bf16[64,2048]{1,0:T(8,128)(2,1)S(1)} %copy-done.8, bf16[2048,768]{1,0:T(8,128)(2,1)} %out_ref.1, bf16[64,768]{1,0:T(8,128)(2,1)S(1)} %copy-done.9), kind=kOutput, calls=%fused_computation.2 | convolution fusion | flops 201424896 | bytes 3702784 | tf_op jit(solution)/shard_map/dot_general | solution.py:456
  64.4 5.6 %all-to-all-done.2.parts_ref = bf16[8,64,768]{2,1,0:T(8,128)(2,1)S(1)} async-done(((bf16[8,64,768]{2,1,0:T(8,128)(2,1)}), bf16[8,64,768]{2,1,0:T(8,128)(2,1)S(1)}, u32[]{:S(2)}, u32[]{:S(2)}) %all-to-all-start.2) | async-done | bytes 786464 | tf_op jit(solution)/shard_map/all_to_all | solution.py:452
  70.0 1.6 %error.1 = bf16[8,64,768]{2,1,0:T(8,128)(2,1)} custom-call(bf16[8,64,768]{2,1,0:T(8,128)(2,1)S(1)} %all-to-all-done.2.parts_ref, f32[64,768]{1,0:T(8,128)S(1)} %convolution_subtract_fusion.base_ref), custom_call_target="tpu_custom_call" | custom-call | tf_op jit(solution)/shard_map/error/pallas_call | solution.py:539
  71.7 3.6 %all-to-all-start.3 = ((bf16[8,64,768]{2,1,0:T(8,128)(2,1)}), bf16[8,64,768]{2,1,0:T(8,128)(2,1)S(1)}, u32[]{:S(2)}, u32[]{:S(2)}) async-start(bf16[8,64,768]{2,1,0:T(8,128)(2,1)} %error.1), calls=%async_computation.3 | async-start | bytes 1572864 | tf_op jit(solution)/shard_map/all_to_all | solution.py:452
  75.3 0.3 copy.29
  75.6 0.1 collective-permute-start.7
  75.6 12.5 %all-to-all-done.3.err_ref = bf16[8,64,768]{2,1,0:T(8,128)(2,1)S(1)} async-done(((bf16[8,64,768]{2,1,0:T(8,128)(2,1)}), bf16[8,64,768]{2,1,0:T(8,128)(2,1)S(1)}, u32[]{:S(2)}, u32[]{:S(2)}) %all-to-all-start.3) | async-done | bytes 786464 | tf_op jit(solution)/shard_map/all_to_all | solution.py:452
  88.2 0.9 copy-done
  89.1 3.2 %own.1 = (bf16[512,512]{1,0:T(8,128)(2,1)}, bf16[512,512]{1,0:T(8,128)(2,1)}) custom-call(bf16[8,64,768]{2,1,0:T(8,128)(2,1)} %copy-done, bf16[512,768]{1,0:T(8,128)(2,1)} %get-tuple-element.76.d0_ref.d_ref, bf16[512,512]{1,0:T(8,128)(2,1)} %get-tuple-element.94.a_ref, bf16[512,512]{1,0:T(8,128)(2,1)} %get-tuple-element.95.b_ref), custom_call_target="tpu_custom_call" | custom-call | flops 400000000 | bytes 8000000 | tf_op jit(solution)/shard_map/own/pallas_call | solution.py:434
  92.4 0.8 copy-done.11
  93.2 0.3 copy-done.6
  93.5 5.1 %other.1 = (bf16[96,1024]{1,0:T(8,128)(2,1)}, bf16[96,1024]{1,0:T(8,128)(2,1)}, bf16[96,1024]{1,0:T(8,128)(2,1)}, bf16[96,1024]{1,0:T(8,128)(2,1)}, bf16[96,1024...) custom-call(bf16[8,64,768]{2,1,0:T(8,128)(2,1)} %copy-done.6, ...), custom_call_target="tpu_custom_call" | custom-call | flops 2000000000 | bytes 8000000 | tf_op jit(solution)/shard_map/other/pallas_call | solution.py:434
  98.6 1.7 %collective-permute-start.11 = (bf16[96,1024]{1,0:T(8,128)(2,1)}, bf16[96,1024]{1,0:T(8,128)(2,1)S(1)}, u32[]{:S(2)}, u32[]{:S(2)}) collective-permute-start(bf16[96,1024]{1,0:T(8,128)(2,1)} %get-tuple-element.104), channel_id=1, source_target_pairs={{0,32},{32,64},{64,96},{96,0},{1,33},{33,65},{65,97},{97,1},{2,34}... | collective-permute-start | bytes 589832 | tf_op jit(solution)/shard_map/ppermute | solution.py:468
  100.3 1.7 %collective-permute-start.12 = (bf16[96,1024]{1,0:T(8,128)(2,1)}, bf16[96,1024]{1,0:T(8,128)(2,1)S(1)}, u32[]{:S(2)}, u32[]{:S(2)}) collective-permute-start(bf16[96,1024]{1,0:T(8,128)(2,1)} %get-tuple-element.105), channel_id=1, source_target_pairs={{0,96},{32,0},{64,32},{96,64},{1,97},{33,1},{65,33},{97,65},{2,98}... | collective-permute-start | bytes 589832 | tf_op jit(solution)/shard_map/ppermute | solution.py:468
  101.9 2.0 %collective-permute-start.13 = (bf16[96,1024]{1,0:T(8,128)(2,1)}, bf16[96,1024]{1,0:T(8,128)(2,1)S(1)}, u32[]{:S(2)}, u32[]{:S(2)}) collective-permute-start(bf16[96,1024]{1,0:T(8,128)(2,1)} %get-tuple-element.106), channel_id=1, source_target_pairs={{0,64},{32,96},{64,0},{96,32},{1,65},{33,97},{65,1},{97,33},{2,66}... | collective-permute-start | bytes 589832 | tf_op jit(solution)/shard_map/ppermute | solution.py:468
  103.9 0.8 slice.4
  104.7 1.0 collective-permute-start.8
  105.7 2.6 %collective-permute-start.9 = (bf16[96,1024]{1,0:T(8,128)(2,1)}, bf16[96,1024]{1,0:T(8,128)(2,1)S(1)}, u32[]{:S(2)}, u32[]{:S(2)}) collective-permute-start(bf16[96,1024]{1,0:T(8,128)(2,1)} %get-tuple-element.99), channel_id=1, source_target_pairs={{0,96},{32,0},{64,32},{96,64},{1,97},{33,1},{65,33},{97,65},{2,98}... | collective-permute-start | bytes 589832 | tf_op jit(solution)/shard_map/ppermute | solution.py:468
  108.3 4.8 %collective-permute-start.10 = (bf16[96,1024]{1,0:T(8,128)(2,1)}, bf16[96,1024]{1,0:T(8,128)(2,1)S(1)}, u32[]{:S(2)}, u32[]{:S(2)}) collective-permute-start(bf16[96,1024]{1,0:T(8,128)(2,1)} %get-tuple-element.100), channel_id=1, source_target_pairs={{0,64},{32,96},{64,0},{96,32},{1,65},{33,97},{65,1},{97,33},{2,66}... | collective-permute-start | bytes 589832 | tf_op jit(solution)/shard_map/ppermute | solution.py:468
  113.1 0.4 collective-permute-done.13
  113.4 1.0 add_convert_fusion.1
  114.5 3.7 %collective-permute-start.14 = (bf16[96,1024]{1,0:T(8,128)(2,1)S(1)}, bf16[96,1024]{1,0:T(8,128)(2,1)S(1)}, u32[]{:S(2)}, u32[]{:S(2)}) collective-permute-start(bf16[96,1024]{1,0:T(8,128)(2,1)S(1)} %add_convert_fusion.1), channel_id=1, source_target_pairs={{0,16},{16,0},{1,17},{17,1},{2,18},{18,2},{3,19},{19,3},{4,20},{20... | collective-permute-start | bytes 589832 | tf_op jit(solution)/shard_map/ppermute | solution.py:464
  118.1 0.8 select_bitcast_fusion
  118.9 0.1 eq.40
  119.0 0.8 dynamic_slice.7
  119.7 1.0 constant_dynamic-slice_fusion
  120.8 1.0 collective-permute-done.14
  121.8 1.1 add_convert_fusion.refs_0_.refs_8_
  122.9 0.5 collective-permute-start.18
  123.3 3.5 %collective-permute-start.15 = (bf16[96,1024]{1,0:T(8,128)(2,1)S(1)}, bf16[96,1024]{1,0:T(8,128)(2,1)S(1)}, u32[]{:S(2)}, u32[]{:S(2)}) collective-permute-start(bf16[96,1024]{1,0:T(8,128)(2,1)S(1)} %add_convert_fusion.refs_0_.refs_8_), channel_id=1, source_target_pairs={{0,16},{16,0},{1,17},{17,1},{2,18},{18,2},{3,19},{19,3},{4,20},{20... | collective-permute-start | bytes 589832 | tf_op jit(solution)/shard_map/ppermute | solution.py:464
  126.8 0.1 multiply_convert_fusion.w_ref
  126.9 3.8 %collective-permute-start.17 = (bf16[96,1024]{1,0:T(8,128)(2,1)S(1)}, bf16[96,1024]{1,0:T(8,128)(2,1)S(1)}, u32[]{:S(2)}, u32[]{:S(2)}) collective-permute-start(bf16[96,1024]{1,0:T(8,128)(2,1)S(1)} %add_convert_fusion.refs_0_.refs_8_), channel_id=1, source_target_pairs={{0,96},{32,0},{64,32},{96,64},{1,97},{33,1},{65,33},{97,65},{2,98}... | collective-permute-start | bytes 589832 | tf_op jit(solution)/shard_map/ppermute | solution.py:468
  130.7 0.1 pad_maximum_fusion
  130.9 2.8 %collective-permute-start.21 = (bf16[96,1024]{1,0:T(8,128)(2,1)S(1)}, bf16[96,1024]{1,0:T(8,128)(2,1)S(1)}, u32[]{:S(2)}, u32[]{:S(2)}) collective-permute-start(bf16[96,1024]{1,0:T(8,128)(2,1)S(1)} %collective-permute-done.15.refs_1_.refs_9_), channel_id=1, source_target_pairs={{0,64},{32,96},{64,0},{96,32},{1,65},{33,97},{65,1},{97,33},{2,66}... | collective-permute-start | bytes 589832 | tf_op jit(solution)/shard_map/ppermute | solution.py:468
  133.7 1.8 %collective-permute-start.20 = (bf16[96,1024]{1,0:T(8,128)(2,1)S(1)}, bf16[96,1024]{1,0:T(8,128)(2,1)S(1)}, u32[]{:S(2)}, u32[]{:S(2)}) collective-permute-start(bf16[96,1024]{1,0:T(8,128)(2,1)S(1)} %collective-permute-done.15.refs_1_.refs_9_), channel_id=1, source_target_pairs={{0,96},{32,0},{64,32},{96,64},{1,97},{33,1},{65,33},{97,65},{2,98}... | collective-permute-start | bytes 589832 | tf_op jit(solution)/shard_map/ppermute | solution.py:468
  135.5 0.2 collective-permute-start.19
  135.7 1.1 convolution_convert_fusion
  136.8 2.6 %collective-permute-done.17.refs_3_.refs_11_ = bf16[96,1024]{1,0:T(8,128)(2,1)S(1)} collective-permute-done((bf16[96,1024]{1,0:T(8,128)(2,1)S(1)}, bf16[96,1024]{1,0:T(8,128)(2,1)S(1)}, u32[]{:S(2)}, u32[]{:S(2)}) %collective-permute-start.17) | collective-permute-done | bytes 196640 | tf_op jit(solution)/shard_map/ppermute | solution.py:468
  139.4 1.8 %collective-permute-done.16.refs_2_.refs_10_ = bf16[96,1024]{1,0:T(8,128)(2,1)S(1)} collective-permute-done((bf16[96,1024]{1,0:T(8,128)(2,1)S(1)}, bf16[96,1024]{1,0:T(8,128)(2,1)S(1)}, u32[]{:S(2)}, u32[]{:S(2)}) %collective-permute-start.16) | collective-permute-done | bytes 196640 | tf_op jit(solution)/shard_map/ppermute | solution.py:468
  141.2 0.3 collective-permute-done.20.refs_6_.refs_14_
  141.5 1.8 %collective-permute-done.19.refs_5_.refs_13_ = bf16[96,1024]{1,0:T(8,128)(2,1)S(1)} collective-permute-done((bf16[96,1024]{1,0:T(8,128)(2,1)S(1)}, bf16[96,1024]{1,0:T(8,128)(2,1)S(1)}, u32[]{:S(2)}, u32[]{:S(2)}) %collective-permute-start.19) | collective-permute-done | bytes 196640 | tf_op jit(solution)/shard_map/ppermute | solution.py:468
  143.3 2.0 %last.1 = (f32[256,512]{1,0:T(8,128)}, f32[256,512]{1,0:T(8,128)}) custom-call(bf16[768,256]{1,0:T(8,128)(2,1)S(1)} %multiply_convert_fusion.w_ref, bf16[96,1024]{1,0:T(8,128)(2,1)S(1)} %add_convert_fusion.refs_0_.refs_8_, bf16[96,1024]{1,0:T(8,128)(2,1)S(1)} %collective-permute-done.15.refs_1_.refs_9_, ...), custom_call_target="tpu_custom_call" | custom-call | tf_op jit(solution)/shard_map/last/pallas_call | solution.py:570
  (44 shorter events, 0.1 us)
Async XLA Ops:
  0.6 27.3 %collective-permute-start.1 = (bf16[512,2048]{1,0:T(8,128)(2,1)}, bf16[512,2048]{1,0:T(8,128)(2,1)S(1)}, u32[]{:S(2)}, u32[]{:S(2)}) collective-permute-start(bf16[512,2048]{1,0:T(8,128)(2,1)} %w0_ref), channel_id=1, source_target_pairs={{0,1},{1,0},{2,3},{3,2},{4,5},{5,4},{6,7},{7,6},{8,9},{9,8},{10,11... | collective-permute-start | bytes 6291464 | tf_op jit(solution)/shard_map/ppermute | solution.py:464
  6.0 1.6 %collective-permute-start = (f32[72,128]{1,0:T(8,128)}, f32[72,128]{1,0:T(8,128)S(1)}, u32[]{:S(2)}, u32[]{:S(2)}) collective-permute-start(f32[72,128]{1,0:T(8,128)} %get-tuple-element.60), channel_id=1, source_target_pairs={{0,1},{1,0},{2,3},{3,2},{4,5},{5,4},{6,7},{7,6},{8,9},{9,8},{10,11... | collective-permute-start | bytes 110600 | tf_op jit(solution)/shard_map/ppermute | solution.py:464
  9.1 13.9 %all-to-all-start = ((f32[8,72,128]{2,1,0:T(8,128)}), f32[8,72,128]{2,1,0:T(8,128)S(1)}, u32[]{:S(2)}, u32[]{:S(2)}) async-start(f32[8,72,128]{2,1,0:T(8,128)} %broadcast_in_dim.24), calls=%async_computation | async-start | bytes 589824 | tf_op jit(solution)/shard_map/all_to_all | solution.py:452
  21.9 18.3 %collective-permute-start.2 = (bf16[768,512]{1,0:T(8,128)(2,1)}, bf16[768,512]{1,0:T(8,128)(2,1)}, u32[]{:S(2)}, u32[]{:S(2)}) collective-permute-start(bf16[768,512]{1,0:T(8,128)(2,1)} %get-tuple-element.72.g0_ref), channel_id=1, source_target_pairs={{0,1},{1,0},{2,3},{3,2},{4,5},{5,4},{6,7},{7,6},{8,9},{9,8},{10,11... | collective-permute-start | bytes 2359304 | tf_op jit(solution)/shard_map/ppermute | solution.py:464
  22.1 18.2 %collective-permute-start.3 = (bf16[768,512]{1,0:T(8,128)(2,1)}, bf16[768,512]{1,0:T(8,128)(2,1)}, u32[]{:S(2)}, u32[]{:S(2)}) collective-permute-start(bf16[768,512]{1,0:T(8,128)(2,1)} %get-tuple-element.73.u0_ref), channel_id=1, source_target_pairs={{0,1},{1,0},{2,3},{3,2},{4,5},{5,4},{6,7},{7,6},{8,9},{9,8},{10,11... | collective-permute-start | bytes 2359304 | tf_op jit(solution)/shard_map/ppermute | solution.py:464
  23.0 0.7 copy-start.4
  28.0 5.2 %copy-start.10 = (bf16[512,2048]{1,0:T(8,128)(2,1)}, bf16[512,2048]{1,0:T(8,128)(2,1)S(1)}, u32[]{:S(2)}) copy-start(bf16[512,2048]{1,0:T(8,128)(2,1)S(1)} %collective-permute-done.1.w1_ref) | copy-start | bytes 6291460
  28.0 18.4 %all-to-all-start.1 = ((bf16[8,64,768]{2,1,0:T(8,128)(2,1)}), bf16[8,64,768]{2,1,0:T(8,128)(2,1)S(1)}, u32[]{:S(2)}, u32[]{:S(2)}) async-start(bf16[8,64,768]{2,1,0:T(8,128)(2,1)} %get-tuple-element.70), calls=%async_computation.1 | async-start | bytes 1572864 | tf_op jit(solution)/shard_map/all_to_all | solution.py:452
  46.4 0.9 copy-start.2
  53.5 16.5 %all-to-all-start.2 = ((bf16[8,64,768]{2,1,0:T(8,128)(2,1)}), bf16[8,64,768]{2,1,0:T(8,128)(2,1)S(1)}, u32[]{:S(2)}, u32[]{:S(2)}) async-start(bf16[8,64,768]{2,1,0:T(8,128)(2,1)} %get-tuple-element.81), calls=%async_computation.2 | async-start | bytes 1572864 | tf_op jit(solution)/shard_map/all_to_all | solution.py:452
  57.0 4.9 %copy-start.8 = (bf16[64,2048]{1,0:T(8,128)(2,1)S(1)}, bf16[64,2048]{1,0:T(8,128)(2,1)}, u32[]{:S(2)}) copy-start(bf16[64,2048]{1,0:T(8,128)(2,1)} %get-tuple-element.82) | copy-start | bytes 786436
  57.0 4.9 %copy-start.9 = (bf16[64,768]{1,0:T(8,128)(2,1)S(1)}, bf16[64,768]{1,0:T(8,128)(2,1)}, u32[]{:S(2)}) copy-start(bf16[64,768]{1,0:T(8,128)(2,1)} %get-tuple-element.83) | copy-start | bytes 294916
  61.4 10.3 %collective-permute-start.4 = (bf16[512,512]{1,0:T(8,128)(2,1)}, bf16[512,512]{1,0:T(8,128)(2,1)S(1)}, u32[]{:S(2)}, u32[]{:S(2)}) collective-permute-start(bf16[512,512]{1,0:T(8,128)(2,1)} %get-tuple-element.86), channel_id=1, source_target_pairs={{0,1},{1,0},{2,3},{3,2},{4,5},{5,4},{6,7},{7,6},{8,9},{9,8},{10,11... | collective-permute-start | bytes 1572872 | tf_op jit(solution)/shard_map/ppermute | solution.py:464
  61.4 10.3 %collective-permute-start.5 = (bf16[512,512]{1,0:T(8,128)(2,1)}, bf16[512,512]{1,0:T(8,128)(2,1)S(1)}, u32[]{:S(2)}, u32[]{:S(2)}) collective-permute-start(bf16[512,512]{1,0:T(8,128)(2,1)} %get-tuple-element.87), channel_id=1, source_target_pairs={{0,1},{1,0},{2,3},{3,2},{4,5},{5,4},{6,7},{7,6},{8,9},{9,8},{10,11... | collective-permute-start | bytes 1572872 | tf_op jit(solution)/shard_map/ppermute | solution.py:464
  64.4 10.8 %copy-start.3 = (bf16[8,64,768]{2,1,0:T(8,128)(2,1)S(1)}, bf16[8,64,768]{2,1,0:T(8,128)(2,1)}, u32[]{:S(2)}) copy-start(bf16[8,64,768]{2,1,0:T(8,128)(2,1)} %copy-done.2) | copy-start | bytes 2359300
  71.6 3.6 %copy-start.12 = (bf16[512,512]{1,0:T(8,128)(2,1)}, bf16[512,512]{1,0:T(8,128)(2,1)S(1)}, u32[]{:S(2)}) copy-start(bf16[512,512]{1,0:T(8,128)(2,1)S(1)} %collective-permute-done.4.a_ref) | copy-start | bytes 1572868
  71.7 3.9 %copy-start.13 = (bf16[512,512]{1,0:T(8,128)(2,1)}, bf16[512,512]{1,0:T(8,128)(2,1)S(1)}, u32[]{:S(2)}) copy-start(bf16[512,512]{1,0:T(8,128)(2,1)S(1)} %collective-permute-done.5.b_ref) | copy-start | bytes 1572868
  71.7 16.5 %all-to-all-start.3 = ((bf16[8,64,768]{2,1,0:T(8,128)(2,1)}), bf16[8,64,768]{2,1,0:T(8,128)(2,1)S(1)}, u32[]{:S(2)}, u32[]{:S(2)}) async-start(bf16[8,64,768]{2,1,0:T(8,128)(2,1)} %error.1), calls=%async_computation.3 | async-start | bytes 1572864 | tf_op jit(solution)/shard_map/all_to_all | solution.py:452
  75.5 16.8 %copy-start.5 = (bf16[512,768]{0,1:T(8,128)(2,1)}, bf16[512,768]{0,1:T(8,128)(2,1)S(1)}, u32[]{:S(2)}) copy-start(bf16[512,768]{0,1:T(8,128)(2,1)S(1)} %copy.29) | copy-start | bytes 2359300
  75.6 16.7 %collective-permute-start.7 = (bf16[768,512]{1,0:T(8,128)(2,1)S(1)}, bf16[768,512]{1,0:T(8,128)(2,1)S(1)}, u32[]{:S(2)}, u32[]{:S(2)}) collective-permute-start(bf16[768,512]{1,0:T(8,128)(2,1)S(1)} %bitcast.18), channel_id=1, source_target_pairs={{0,1},{1,0},{2,3},{3,2},{4,5},{5,4},{6,7},{7,6},{8,9},{9,8},{10,11... | collective-permute-start | bytes 2359304 | tf_op jit(solution)/shard_map/ppermute | solution.py:464
  88.2 0.9 copy-start
  88.2 4.1 %collective-permute-start.6 = (bf16[8,64,768]{2,1,0:T(8,128)(2,1)S(1)}, bf16[8,64,768]{2,1,0:T(8,128)(2,1)S(1)}, u32[]{:S(2)}, u32[]{:S(2)}) collective-permute-start(bf16[8,64,768]{2,1,0:T(8,128)(2,1)S(1)} %all-to-all-done.3.err_ref), channel_id=1, source_target_pairs={{0,1},{1,0},{2,3},{3,2},{4,5},{5,4},{6,7},{7,6},{8,9},{9,8},{10,11... | collective-permute-start | bytes 2359304 | tf_op jit(solution)/shard_map/ppermute | solution.py:464
  92.3 0.9 copy-start.11
  92.3 1.1 copy-start.6
  98.6 32.1 %copy-start.1 = (bf16[8,64,768]{2,1,0:T(8,128)(2,1)S(1)}, bf16[8,64,768]{2,1,0:T(8,128)(2,1)}, u32[]{:S(2)}) copy-start(bf16[8,64,768]{2,1,0:T(8,128)(2,1)} %copy-done) | copy-start | bytes 2359300
  98.6 32.1 %copy-start.7 = (bf16[8,64,768]{2,1,0:T(8,128)(2,1)S(1)}, bf16[8,64,768]{2,1,0:T(8,128)(2,1)}, u32[]{:S(2)}) copy-start(bf16[8,64,768]{2,1,0:T(8,128)(2,1)} %copy-done.6) | copy-start | bytes 2359300
  98.6 9.6 %collective-permute-start.11 = (bf16[96,1024]{1,0:T(8,128)(2,1)}, bf16[96,1024]{1,0:T(8,128)(2,1)S(1)}, u32[]{:S(2)}, u32[]{:S(2)}) collective-permute-start(bf16[96,1024]{1,0:T(8,128)(2,1)} %get-tuple-element.104), channel_id=1, source_target_pairs={{0,32},{32,64},{64,96},{96,0},{1,33},{33,65},{65,97},{97,1},{2,34}... | collective-permute-start | bytes 589832 | tf_op jit(solution)/shard_map/ppermute | solution.py:468
  100.3 12.8 %collective-permute-start.12 = (bf16[96,1024]{1,0:T(8,128)(2,1)}, bf16[96,1024]{1,0:T(8,128)(2,1)S(1)}, u32[]{:S(2)}, u32[]{:S(2)}) collective-permute-start(bf16[96,1024]{1,0:T(8,128)(2,1)} %get-tuple-element.105), channel_id=1, source_target_pairs={{0,96},{32,0},{64,32},{96,64},{1,97},{33,1},{65,33},{97,65},{2,98}... | collective-permute-start | bytes 589832 | tf_op jit(solution)/shard_map/ppermute | solution.py:468
  101.9 11.5 %collective-permute-start.13 = (bf16[96,1024]{1,0:T(8,128)(2,1)}, bf16[96,1024]{1,0:T(8,128)(2,1)S(1)}, u32[]{:S(2)}, u32[]{:S(2)}) collective-permute-start(bf16[96,1024]{1,0:T(8,128)(2,1)} %get-tuple-element.106), channel_id=1, source_target_pairs={{0,64},{32,96},{64,0},{96,32},{1,65},{33,97},{65,1},{97,33},{2,66}... | collective-permute-start | bytes 589832 | tf_op jit(solution)/shard_map/ppermute | solution.py:468
  104.7 16.0 %collective-permute-start.8 = (bf16[96,1024]{1,0:T(8,128)(2,1)}, bf16[96,1024]{1,0:T(8,128)(2,1)S(1)}, u32[]{:S(2)}, u32[]{:S(2)}) collective-permute-start(bf16[96,1024]{1,0:T(8,128)(2,1)} %get-tuple-element.98), channel_id=1, source_target_pairs={{0,32},{32,64},{64,96},{96,0},{1,33},{33,65},{65,97},{97,1},{2,34}... | collective-permute-start | bytes 589832 | tf_op jit(solution)/shard_map/ppermute | solution.py:468
  105.7 15.1 %collective-permute-start.9 = (bf16[96,1024]{1,0:T(8,128)(2,1)}, bf16[96,1024]{1,0:T(8,128)(2,1)S(1)}, u32[]{:S(2)}, u32[]{:S(2)}) collective-permute-start(bf16[96,1024]{1,0:T(8,128)(2,1)} %get-tuple-element.99), channel_id=1, source_target_pairs={{0,96},{32,0},{64,32},{96,64},{1,97},{33,1},{65,33},{97,65},{2,98}... | collective-permute-start | bytes 589832 | tf_op jit(solution)/shard_map/ppermute | solution.py:468
  108.3 12.5 %collective-permute-start.10 = (bf16[96,1024]{1,0:T(8,128)(2,1)}, bf16[96,1024]{1,0:T(8,128)(2,1)S(1)}, u32[]{:S(2)}, u32[]{:S(2)}) collective-permute-start(bf16[96,1024]{1,0:T(8,128)(2,1)} %get-tuple-element.100), channel_id=1, source_target_pairs={{0,64},{32,96},{64,0},{96,32},{1,65},{33,97},{65,1},{97,33},{2,66}... | collective-permute-start | bytes 589832 | tf_op jit(solution)/shard_map/ppermute | solution.py:468
  114.5 7.3 %collective-permute-start.14 = (bf16[96,1024]{1,0:T(8,128)(2,1)S(1)}, bf16[96,1024]{1,0:T(8,128)(2,1)S(1)}, u32[]{:S(2)}, u32[]{:S(2)}) collective-permute-start(bf16[96,1024]{1,0:T(8,128)(2,1)S(1)} %add_convert_fusion.1), channel_id=1, source_target_pairs={{0,16},{16,0},{1,17},{17,1},{2,18},{18,2},{3,19},{19,3},{4,20},{20... | collective-permute-start | bytes 589832 | tf_op jit(solution)/shard_map/ppermute | solution.py:464
  122.9 12.6 %collective-permute-start.18 = (bf16[96,1024]{1,0:T(8,128)(2,1)S(1)}, bf16[96,1024]{1,0:T(8,128)(2,1)S(1)}, u32[]{:S(2)}, u32[]{:S(2)}) collective-permute-start(bf16[96,1024]{1,0:T(8,128)(2,1)S(1)} %add_convert_fusion.refs_0_.refs_8_), channel_id=1, source_target_pairs={{0,64},{32,96},{64,0},{96,32},{1,65},{33,97},{65,1},{97,33},{2,66}... | collective-permute-start | bytes 589832 | tf_op jit(solution)/shard_map/ppermute | solution.py:468
  123.3 7.6 %collective-permute-start.15 = (bf16[96,1024]{1,0:T(8,128)(2,1)S(1)}, bf16[96,1024]{1,0:T(8,128)(2,1)S(1)}, u32[]{:S(2)}, u32[]{:S(2)}) collective-permute-start(bf16[96,1024]{1,0:T(8,128)(2,1)S(1)} %add_convert_fusion.refs_0_.refs_8_), channel_id=1, source_target_pairs={{0,16},{16,0},{1,17},{17,1},{2,18},{18,2},{3,19},{19,3},{4,20},{20... | collective-permute-start | bytes 589832 | tf_op jit(solution)/shard_map/ppermute | solution.py:464
  126.9 12.5 %collective-permute-start.17 = (bf16[96,1024]{1,0:T(8,128)(2,1)S(1)}, bf16[96,1024]{1,0:T(8,128)(2,1)S(1)}, u32[]{:S(2)}, u32[]{:S(2)}) collective-permute-start(bf16[96,1024]{1,0:T(8,128)(2,1)S(1)} %add_convert_fusion.refs_0_.refs_8_), channel_id=1, source_target_pairs={{0,96},{32,0},{64,32},{96,64},{1,97},{33,1},{65,33},{97,65},{2,98}... | collective-permute-start | bytes 589832 | tf_op jit(solution)/shard_map/ppermute | solution.py:468
  130.7 10.5 %collective-permute-start.16 = (bf16[96,1024]{1,0:T(8,128)(2,1)S(1)}, bf16[96,1024]{1,0:T(8,128)(2,1)S(1)}, u32[]{:S(2)}, u32[]{:S(2)}) collective-permute-start(bf16[96,1024]{1,0:T(8,128)(2,1)S(1)} %add_convert_fusion.refs_0_.refs_8_), channel_id=1, source_target_pairs={{0,32},{32,64},{64,96},{96,0},{1,33},{33,65},{65,97},{97,1},{2,34}... | collective-permute-start | bytes 589832 | tf_op jit(solution)/shard_map/ppermute | solution.py:468
  130.9 10.3 %collective-permute-start.21 = (bf16[96,1024]{1,0:T(8,128)(2,1)S(1)}, bf16[96,1024]{1,0:T(8,128)(2,1)S(1)}, u32[]{:S(2)}, u32[]{:S(2)}) collective-permute-start(bf16[96,1024]{1,0:T(8,128)(2,1)S(1)} %collective-permute-done.15.refs_1_.refs_9_), channel_id=1, source_target_pairs={{0,64},{32,96},{64,0},{96,32},{1,65},{33,97},{65,1},{97,33},{2,66}... | collective-permute-start | bytes 589832 | tf_op jit(solution)/shard_map/ppermute | solution.py:468
  133.7 7.9 %collective-permute-start.20 = (bf16[96,1024]{1,0:T(8,128)(2,1)S(1)}, bf16[96,1024]{1,0:T(8,128)(2,1)S(1)}, u32[]{:S(2)}, u32[]{:S(2)}) collective-permute-start(bf16[96,1024]{1,0:T(8,128)(2,1)S(1)} %collective-permute-done.15.refs_1_.refs_9_), channel_id=1, source_target_pairs={{0,96},{32,0},{64,32},{96,64},{1,97},{33,1},{65,33},{97,65},{2,98}... | collective-permute-start | bytes 589832 | tf_op jit(solution)/shard_map/ppermute | solution.py:468
  135.5 7.8 %collective-permute-start.19 = (bf16[96,1024]{1,0:T(8,128)(2,1)S(1)}, bf16[96,1024]{1,0:T(8,128)(2,1)S(1)}, u32[]{:S(2)}, u32[]{:S(2)}) collective-permute-start(bf16[96,1024]{1,0:T(8,128)(2,1)S(1)} %collective-permute-done.15.refs_1_.refs_9_), channel_id=1, source_target_pairs={{0,32},{32,64},{64,96},{96,0},{1,33},{33,65},{65,97},{97,1},{2,34}... | collective-permute-start | bytes 589832 | tf_op jit(solution)/shard_map/ppermute | solution.py:468

commit v8 on v7

--- a/solution.py
+++ b/solution.py
@@ -156,7 +156,14 @@
         ),
         sem,
     )
-    for c in copies[:-1]:
+    copies[10].wait()
+    copies[11].wait()
+    picks = pick_matrix(pickb)
+    onehot = (attachb[...] == iota((LANES, LANES), 0)).astype(F32)
+    at = iota((3 * TAIL, FEATS), 0)
+    where = (at // TAIL) * NODES + (NODES - TAIL) + at % TAIL
+    place = (iota((3 * TAIL, FEATS), 1) == where).astype(F32).astype(BF16)
+    for c in copies[:10] + copies[12:-1]:
         c.wait()
     total = recvb[0]
     for d in range(1, recvb.shape[0]):
@@ -183,7 +190,6 @@
         qs.append(q)
     plat_out[...] = q
     k = stiffb[...]
-    onehot = (attachb[...] == iota((LANES, LANES), 0)).astype(F32)
     fair = jnp.dot(jnp.concatenate(qs, axis=0), onehot, precision=HIGH, preferred_element_type=F32)
     trow = iota((TAIL, LANES), 0)
     pos = [posb[c] for c in range(3)]
@@ -207,10 +213,7 @@
             pos[c] = p + vel[c]
     copy = pltpu.make_async_copy(final, fpos_ref.at[:, NODES - TAIL : NODES, :], out_sem)
     copy.start()
-    picked = nt(pick_matrix(pickb), tails[...].astype(BF16)).astype(BF16)
-    at = iota((3 * TAIL, FEATS), 0)
-    where = (at // TAIL) * NODES + (NODES - TAIL) + at % TAIL
-    place = (iota((3 * TAIL, FEATS), 1) == where).astype(F32).astype(BF16)
+    picked = nt(picks, tails[...].astype(BF16)).astype(BF16)
     rows = rowsb[...].astype(F32) + jnp.dot(picked, place, preferred_element_type=F32)
     count = t_ref.shape[0]
     t_ref[...] = rows[count:].astype(BF16)
@@ -261,22 +264,31 @@
     )
     copies[0].wait()
     x = xb[...].reshape(-1, xb.shape[-1])
-    part, outs = None, []
-    for side, (g, u, d) in enumerate(((g0b, u0b, d0b), (g1b, u1b, d1b))):
-        copies[1 + 3 * side].wait()
-        gate = dot(x, g[...])
-        gateb[side] = gate
-        copies[2 + 3 * side].wait()
-        upper = dot(x, u[...])
-        upb[side] = upper
+    outs = []
+
+    def keep(side):
         for i, (buf, ref) in enumerate(((gateb, gate_ref), (upb, up_ref))):
             out = pltpu.make_async_copy(buf.at[side], ref.at[side], out_sem.at[2 * side + i])
             out.start()
             outs.append(out)
-        act = (gate * jax.nn.sigmoid(gate) * upper).astype(BF16)
-        copies[3 + 3 * side].wait()
-        term = dot(act, d[...])
-        part = term if part is None else part + term
+
+    copies[1].wait()
+    gate0 = dot(x, g0b[...])
+    gateb[0] = gate0
+    copies[2].wait()
+    up0 = dot(x, u0b[...])
+    upb[0] = up0
+    keep(0)
+    for c in copies[3:]:
+        c.wait()
+    gate1, up1 = dot(x, g1b[...]), dot(x, u1b[...])
+    gateb[1] = gate1
+    upb[1] = up1
+    act0 = (gate0 * jax.nn.sigmoid(gate0) * up0).astype(BF16)
+    part = dot(act0, d0b[...])
+    keep(1)
+    act1 = (gate1 * jax.nn.sigmoid(gate1) * up1).astype(BF16)
+    part = part + dot(act1, d1b[...])
     part_ref[...] = part.astype(BF16).reshape(part_ref.shape)
     for out in outs:
         out.wait()

time: 146 us -> 146 us (level)
  no operation moved by 1% of the time
where the time goes in v8:
time: 146 us; the launch traced here: 145 us
  starting transfers between devices  49.8 us (34%)
  Pallas kernels  45.8 us (31%)
  waiting for transfers between devices  33.6 us (23%)
  local copies, waits for them, and re-layouts  7.3 us (5%)
  other arithmetic  3.9 us (3%)
  matrix products  3.65 us (2%)
    pallas_call x5, Pallas kernels, staged(): pl.pallas_call(kernel, out_shape=out_shape, in_specs=[HB] * len(args), ou...  28.3 us
    all_to_all x4, waiting for transfers between devices, exchange(): return lax.all_to_all(x, axes, split_axis=0, concat_axis=0, tiled=True)  24.7 us
    ppermute x12, starting transfers between devices, shift(): return lax.ppermute(x, 'y', [(i, (i + d) % 4) for i in range(4)])  22.7 us
    all_to_all x4, starting transfers between devices, exchange(): return lax.all_to_all(x, axes, split_axis=0, concat_axis=0, tiled=True)  18.1 us
    ppermute x10, starting transfers between devices, swap(): return lax.ppermute(x, axis, SWAP)  9.03 us
    ppermute x12, waiting for transfers between devices, shift(): return lax.ppermute(x, 'y', [(i, (i + d) % 4) for i in range(4)])  6.87 us
    pallas_call x1, Pallas kernels, evolve(): pl.pallas_call(evolve_kernel, out_shape=(sds((ROWS, LANES), F32), sds((2...  5.24 us
    pallas_call x1, Pallas kernels, body(): pl.pallas_call(slopes_kernel, grid=(4,), out_shape=(slope,) * 4, in_specs...  4.34 us
  transfers between devices with their start and end apart: 26, of which 11 were waited for; matrix products, arithmetic and copies ran while one was open for 7% of the time, Pallas kernels for 23%

profile of v8, /device:TPU:0, one launch (start us, length us, event | category | flops | bytes accessed | tf_op | source)
XLA Modules:
  0.0 145.0 jit_solution(17988274287013954919)
XLA Ops:
  0.6 0.1 collective-permute-start.1
  0.7 5.2 %evolve.1 = (f32[72,128]{1,0:T(8,128)}, bf16[128,768]{1,0:T(8,128)(2,1)}, f32[24,128]{1,0:T(8,128)}, f32[3,256,128]{2,1,0:T(8,128)}) custom-call(f32[3,256,128]{2,1,0:T(8,128)} %pos_ref.3, f32[3,256,128]{2,1,0:T(8,128)} %vel_ref.3, f32[1,128]{1,0:T(1,128)} %bitcast.23, s32[8,256,128]{2,1,0:T(8,128)} %contact_ref.3, f32[3,128]{1,0:T(4,128)} %off_ref.3, ...), custom_call_target="tpu_custom_call" | custom-call | flops 260000000 | bytes 3000000 | tf_op jit(solution)/shard_map/evolve/pallas_call | solution.py:387
  6.0 0.6 collective-permute-start
  6.5 1.1 collective-permute-done
  7.6 0.8 add.110
  8.4 0.7 broadcast_in_dim.24
  9.1 5.7 %all-to-all-start = ((f32[8,72,128]{2,1,0:T(8,128)}), f32[8,72,128]{2,1,0:T(8,128)S(1)}, u32[]{:S(2)}, u32[]{:S(2)}) async-start(f32[8,72,128]{2,1,0:T(8,128)} %broadcast_in_dim.24), calls=%async_computation | async-start | bytes 589824 | tf_op jit(solution)/shard_map/all_to_all | solution.py:464
  14.9 7.1 %products.1 = (bf16[768,512]{1,0:T(8,128)(2,1)}, bf16[768,512]{1,0:T(8,128)(2,1)}) custom-call(bf16[768,2048]{1,0:T(8,128)(2,1)} %w_in_ref.2, f32[1,2048]{1,0:T(1,128)} %bitcast.30, bf16[2048,512]{1,0:T(8,128)(2,1)} %gate_ref.1, bf16[2048,512]{1,0:T(8,128)(2,1)} %up_ref.1), custom_call_target="tpu_custom_call" | custom-call | flops 3300000000 | bytes 8000000 | tf_op jit(solution)/shard_map/products/pallas_call | solution.py:446
  21.9 0.1 collective-permute-start.2
  22.1 0.4 collective-permute-start.3
  22.5 0.5 all-to-all-done.recv_ref
  23.0 0.7 copy-done.4
  23.7 4.2 %finish.1 = (bf16[8,64,768]{2,1,0:T(8,128)(2,1)}, bf16[64,768]{1,0:T(8,128)(2,1)}, bf16[64,2048]{1,0:T(8,128)(2,1)}, f32[3,128]{1,0:T(4,128)}, f32[3,256,128]{2,1,0:T(8,128)}) custom-call(f32[8,72,128]{2,1,0:T(8,128)} %copy-done.4, f32[24,128]{1,0:T(8,128)} %get-tuple-element.62.bound_ref, ...), custom_call_target="tpu_custom_call", output_to_operand_aliasing={{4}: (18, {})} | custom-call | flops 300000000 | bytes 4000000 | tf_op jit(solution)/shard_map/finish/pallas_call | solution.py:420
  28.0 0.0 collective-permute-done.1.w1_ref
  28.0 5.2 %all-to-all-start.1 = ((bf16[8,64,768]{2,1,0:T(8,128)(2,1)}), bf16[8,64,768]{2,1,0:T(8,128)(2,1)S(1)}, u32[]{:S(2)}, u32[]{:S(2)}) async-start(bf16[8,64,768]{2,1,0:T(8,128)(2,1)} %get-tuple-element.70), calls=%async_computation.1 | async-start | bytes 1572864 | tf_op jit(solution)/shard_map/all_to_all | solution.py:464
  33.2 7.0 %down.1 = (bf16[512,768]{1,0:T(8,128)(2,1)}, bf16[512,768]{1,0:T(8,128)(2,1)}) custom-call(bf16[512,2048]{1,0:T(8,128)(2,1)} %w0_ref, bf16[512,2048]{1,0:T(8,128)(2,1)} %copy-done.10, bf16[2048,768]{1,0:T(8,128)(2,1)} %out_ref.1), custom_call_target="tpu_custom_call" | custom-call | flops 3300000000 | bytes 8000000 | tf_op jit(solution)/shard_map/down/pallas_call | solution.py:446
  40.3 6.1 %all-to-all-done.1.x_ref = bf16[8,64,768]{2,1,0:T(8,128)(2,1)S(1)} async-done(((bf16[8,64,768]{2,1,0:T(8,128)(2,1)}), bf16[8,64,768]{2,1,0:T(8,128)(2,1)S(1)}, u32[]{:S(2)}, u32[]{:S(2)}) %all-to-all-start.1) | async-done | bytes 786464 | tf_op jit(solution)/shard_map/all_to_all | solution.py:464
  46.4 0.9 copy-done.2
  47.3 5.8 %forward.1 = (bf16[8,64,768]{2,1,0:T(8,128)(2,1)}, f32[2,512,512]{2,1,0:T(8,128)}, f32[2,512,512]{2,1,0:T(8,128)}) custom-call(bf16[8,64,768]{2,1,0:T(8,128)(2,1)} %copy-done.2, bf16[768,512]{1,0:T(8,128)(2,1)} %get-tuple-element.72.g0_ref, bf16[768,512]{1,0:T(8,128)(2,1)} %get-tuple-element.73.u0_ref, bf16[512,768]{1,0:T(8,128)(2,1)} %get-tuple-element.76.d0_ref.d_ref, ...), custom_call_target="tpu_custom_call" | custom-call | flops 2500000000 | bytes 8000000 | tf_op jit(solution)/shard_map/forward/pallas_call | solution.py:446
  53.1 3.6 %all-to-all-start.2 = ((bf16[8,64,768]{2,1,0:T(8,128)(2,1)}), bf16[8,64,768]{2,1,0:T(8,128)(2,1)S(1)}, u32[]{:S(2)}, u32[]{:S(2)}) async-start(bf16[8,64,768]{2,1,0:T(8,128)(2,1)} %get-tuple-element.81), calls=%async_computation.2 | async-start | bytes 1572864 | tf_op jit(solution)/shard_map/all_to_all | solution.py:464
  56.7 4.3 %slopes.1 = (bf16[512,512]{1,0:T(8,128)(2,1)}, bf16[512,512]{1,0:T(8,128)(2,1)}, bf16[512,512]{1,0:T(8,128)(2,1)}, bf16[512,512]{1,0:T(8,128)(2,1)}) custom-call(f32[2,512,512]{2,1,0:T(8,128)} %get-tuple-element.84.gate_ref, f32[2,512,512]{2,1,0:T(8,128)} %get-tuple-element.85.up_ref), custom_call_target="tpu_custom_call" | custom-call | flops 8000000 | bytes 6000000 | tf_op jit(solution)/shard_map/slopes/pallas_call | solution.py:542
  61.0 0.5 collective-permute-start.5
  61.5 2.5 %convolution_subtract_fusion.base_ref = f32[64,768]{1,0:T(8,128)S(1)} fusion(bf16[64,2048]{1,0:T(8,128)(2,1)S(1)} %copy-done.8, bf16[2048,768]{1,0:T(8,128)(2,1)} %out_ref.1, bf16[64,768]{1,0:T(8,128)(2,1)S(1)} %copy-done.9), kind=kOutput, calls=%fused_computation.2 | convolution fusion | flops 201424896 | bytes 3702784 | tf_op jit(solution)/shard_map/dot_general | solution.py:468
  64.1 5.6 %all-to-all-done.2.parts_ref = bf16[8,64,768]{2,1,0:T(8,128)(2,1)S(1)} async-done(((bf16[8,64,768]{2,1,0:T(8,128)(2,1)}), bf16[8,64,768]{2,1,0:T(8,128)(2,1)S(1)}, u32[]{:S(2)}, u32[]{:S(2)}) %all-to-all-start.2) | async-done | bytes 786464 | tf_op jit(solution)/shard_map/all_to_all | solution.py:464
  69.6 1.6 %error.1 = bf16[8,64,768]{2,1,0:T(8,128)(2,1)} custom-call(bf16[8,64,768]{2,1,0:T(8,128)(2,1)S(1)} %all-to-all-done.2.parts_ref, f32[64,768]{1,0:T(8,128)S(1)} %convolution_subtract_fusion.base_ref), custom_call_target="tpu_custom_call" | custom-call | tf_op jit(solution)/shard_map/error/pallas_call | solution.py:551
  71.3 3.6 %all-to-all-start.3 = ((bf16[8,64,768]{2,1,0:T(8,128)(2,1)}), bf16[8,64,768]{2,1,0:T(8,128)(2,1)S(1)}, u32[]{:S(2)}, u32[]{:S(2)}) async-start(bf16[8,64,768]{2,1,0:T(8,128)(2,1)} %error.1), calls=%async_computation.3 | async-start | bytes 1572864 | tf_op jit(solution)/shard_map/all_to_all | solution.py:464
  74.9 0.3 copy.29
  75.2 0.1 collective-permute-start.7
  75.3 12.5 %all-to-all-done.3.err_ref = bf16[8,64,768]{2,1,0:T(8,128)(2,1)S(1)} async-done(((bf16[8,64,768]{2,1,0:T(8,128)(2,1)}), bf16[8,64,768]{2,1,0:T(8,128)(2,1)S(1)}, u32[]{:S(2)}, u32[]{:S(2)}) %all-to-all-start.3) | async-done | bytes 786464 | tf_op jit(solution)/shard_map/all_to_all | solution.py:464
  87.8 0.9 copy-done
  88.7 3.2 %own.1 = (bf16[512,512]{1,0:T(8,128)(2,1)}, bf16[512,512]{1,0:T(8,128)(2,1)}) custom-call(bf16[8,64,768]{2,1,0:T(8,128)(2,1)} %copy-done, bf16[512,768]{1,0:T(8,128)(2,1)} %get-tuple-element.76.d0_ref.d_ref, bf16[512,512]{1,0:T(8,128)(2,1)} %get-tuple-element.94.a_ref, bf16[512,512]{1,0:T(8,128)(2,1)} %get-tuple-element.95.b_ref), custom_call_target="tpu_custom_call" | custom-call | flops 400000000 | bytes 8000000 | tf_op jit(solution)/shard_map/own/pallas_call | solution.py:446
  92.0 0.8 copy-done.11
  92.8 0.3 copy-done.6
  93.1 5.1 %other.1 = (bf16[96,1024]{1,0:T(8,128)(2,1)}, bf16[96,1024]{1,0:T(8,128)(2,1)}, bf16[96,1024]{1,0:T(8,128)(2,1)}, bf16[96,1024]{1,0:T(8,128)(2,1)}, bf16[96,1024...) custom-call(bf16[8,64,768]{2,1,0:T(8,128)(2,1)} %copy-done.6, ...), custom_call_target="tpu_custom_call" | custom-call | flops 2000000000 | bytes 8000000 | tf_op jit(solution)/shard_map/other/pallas_call | solution.py:446
  98.3 1.6 %collective-permute-start.11 = (bf16[96,1024]{1,0:T(8,128)(2,1)}, bf16[96,1024]{1,0:T(8,128)(2,1)S(1)}, u32[]{:S(2)}, u32[]{:S(2)}) collective-permute-start(bf16[96,1024]{1,0:T(8,128)(2,1)} %get-tuple-element.104), channel_id=1, source_target_pairs={{0,32},{32,64},{64,96},{96,0},{1,33},{33,65},{65,97},{97,1},{2,34}... | collective-permute-start | bytes 589832 | tf_op jit(solution)/shard_map/ppermute | solution.py:480
  99.9 1.7 %collective-permute-start.12 = (bf16[96,1024]{1,0:T(8,128)(2,1)}, bf16[96,1024]{1,0:T(8,128)(2,1)S(1)}, u32[]{:S(2)}, u32[]{:S(2)}) collective-permute-start(bf16[96,1024]{1,0:T(8,128)(2,1)} %get-tuple-element.105), channel_id=1, source_target_pairs={{0,96},{32,0},{64,32},{96,64},{1,97},{33,1},{65,33},{97,65},{2,98}... | collective-permute-start | bytes 589832 | tf_op jit(solution)/shard_map/ppermute | solution.py:480
  101.6 2.0 %collective-permute-start.13 = (bf16[96,1024]{1,0:T(8,128)(2,1)}, bf16[96,1024]{1,0:T(8,128)(2,1)S(1)}, u32[]{:S(2)}, u32[]{:S(2)}) collective-permute-start(bf16[96,1024]{1,0:T(8,128)(2,1)} %get-tuple-element.106), channel_id=1, source_target_pairs={{0,64},{32,96},{64,0},{96,32},{1,65},{33,97},{65,1},{97,33},{2,66}... | collective-permute-start | bytes 589832 | tf_op jit(solution)/shard_map/ppermute | solution.py:480
  103.6 0.8 slice.4
  104.4 1.0 collective-permute-start.8
  105.3 2.6 %collective-permute-start.9 = (bf16[96,1024]{1,0:T(8,128)(2,1)}, bf16[96,1024]{1,0:T(8,128)(2,1)S(1)}, u32[]{:S(2)}, u32[]{:S(2)}) collective-permute-start(bf16[96,1024]{1,0:T(8,128)(2,1)} %get-tuple-element.99), channel_id=1, source_target_pairs={{0,96},{32,0},{64,32},{96,64},{1,97},{33,1},{65,33},{97,65},{2,98}... | collective-permute-start | bytes 589832 | tf_op jit(solution)/shard_map/ppermute | solution.py:480
  107.9 4.8 %collective-permute-start.10 = (bf16[96,1024]{1,0:T(8,128)(2,1)}, bf16[96,1024]{1,0:T(8,128)(2,1)S(1)}, u32[]{:S(2)}, u32[]{:S(2)}) collective-permute-start(bf16[96,1024]{1,0:T(8,128)(2,1)} %get-tuple-element.100), channel_id=1, source_target_pairs={{0,64},{32,96},{64,0},{96,32},{1,65},{33,97},{65,1},{97,33},{2,66}... | collective-permute-start | bytes 589832 | tf_op jit(solution)/shard_map/ppermute | solution.py:480
  112.7 0.4 collective-permute-done.13
  113.1 1.0 add_convert_fusion.1
  114.1 3.7 %collective-permute-start.14 = (bf16[96,1024]{1,0:T(8,128)(2,1)S(1)}, bf16[96,1024]{1,0:T(8,128)(2,1)S(1)}, u32[]{:S(2)}, u32[]{:S(2)}) collective-permute-start(bf16[96,1024]{1,0:T(8,128)(2,1)S(1)} %add_convert_fusion.1), channel_id=1, source_target_pairs={{0,16},{16,0},{1,17},{17,1},{2,18},{18,2},{3,19},{19,3},{4,20},{20... | collective-permute-start | bytes 589832 | tf_op jit(solution)/shard_map/ppermute | solution.py:476
  117.8 0.8 select_bitcast_fusion
  118.5 0.1 eq.40
  118.6 0.8 dynamic_slice.7
  119.4 1.0 constant_dynamic-slice_fusion
  120.4 1.0 collective-permute-done.14
  121.4 1.1 add_convert_fusion.refs_0_.refs_8_
  122.5 0.4 collective-permute-start.18
  123.0 3.5 %collective-permute-start.15 = (bf16[96,1024]{1,0:T(8,128)(2,1)S(1)}, bf16[96,1024]{1,0:T(8,128)(2,1)S(1)}, u32[]{:S(2)}, u32[]{:S(2)}) collective-permute-start(bf16[96,1024]{1,0:T(8,128)(2,1)S(1)} %add_convert_fusion.refs_0_.refs_8_), channel_id=1, source_target_pairs={{0,16},{16,0},{1,17},{17,1},{2,18},{18,2},{3,19},{19,3},{4,20},{20... | collective-permute-start | bytes 589832 | tf_op jit(solution)/shard_map/ppermute | solution.py:476
  126.5 0.1 multiply_convert_fusion.w_ref
  126.6 3.8 %collective-permute-start.17 = (bf16[96,1024]{1,0:T(8,128)(2,1)S(1)}, bf16[96,1024]{1,0:T(8,128)(2,1)S(1)}, u32[]{:S(2)}, u32[]{:S(2)}) collective-permute-start(bf16[96,1024]{1,0:T(8,128)(2,1)S(1)} %add_convert_fusion.refs_0_.refs_8_), channel_id=1, source_target_pairs={{0,96},{32,0},{64,32},{96,64},{1,97},{33,1},{65,33},{97,65},{2,98}... | collective-permute-start | bytes 589832 | tf_op jit(solution)/shard_map/ppermute | solution.py:480
  130.4 0.1 pad_maximum_fusion
  130.5 2.8 %collective-permute-start.21 = (bf16[96,1024]{1,0:T(8,128)(2,1)S(1)}, bf16[96,1024]{1,0:T(8,128)(2,1)S(1)}, u32[]{:S(2)}, u32[]{:S(2)}) collective-permute-start(bf16[96,1024]{1,0:T(8,128)(2,1)S(1)} %collective-permute-done.15.refs_1_.refs_9_), channel_id=1, source_target_pairs={{0,64},{32,96},{64,0},{96,32},{1,65},{33,97},{65,1},{97,33},{2,66}... | collective-permute-start | bytes 589832 | tf_op jit(solution)/shard_map/ppermute | solution.py:480
  133.3 1.8 %collective-permute-start.20 = (bf16[96,1024]{1,0:T(8,128)(2,1)S(1)}, bf16[96,1024]{1,0:T(8,128)(2,1)S(1)}, u32[]{:S(2)}, u32[]{:S(2)}) collective-permute-start(bf16[96,1024]{1,0:T(8,128)(2,1)S(1)} %collective-permute-done.15.refs_1_.refs_9_), channel_id=1, source_target_pairs={{0,96},{32,0},{64,32},{96,64},{1,97},{33,1},{65,33},{97,65},{2,98}... | collective-permute-start | bytes 589832 | tf_op jit(solution)/shard_map/ppermute | solution.py:480
  135.1 0.2 collective-permute-start.19
  135.3 1.1 convolution_convert_fusion
  136.4 2.6 %collective-permute-done.17.refs_3_.refs_11_ = bf16[96,1024]{1,0:T(8,128)(2,1)S(1)} collective-permute-done((bf16[96,1024]{1,0:T(8,128)(2,1)S(1)}, bf16[96,1024]{1,0:T(8,128)(2,1)S(1)}, u32[]{:S(2)}, u32[]{:S(2)}) %collective-permute-start.17) | collective-permute-done | bytes 196640 | tf_op jit(solution)/shard_map/ppermute | solution.py:480
  139.1 1.8 %collective-permute-done.16.refs_2_.refs_10_ = bf16[96,1024]{1,0:T(8,128)(2,1)S(1)} collective-permute-done((bf16[96,1024]{1,0:T(8,128)(2,1)S(1)}, bf16[96,1024]{1,0:T(8,128)(2,1)S(1)}, u32[]{:S(2)}, u32[]{:S(2)}) %collective-permute-start.16) | collective-permute-done | bytes 196640 | tf_op jit(solution)/shard_map/ppermute | solution.py:480
  140.8 0.3 collective-permute-done.20.refs_6_.refs_14_
  141.2 1.8 %collective-permute-done.19.refs_5_.refs_13_ = bf16[96,1024]{1,0:T(8,128)(2,1)S(1)} collective-permute-done((bf16[96,1024]{1,0:T(8,128)(2,1)S(1)}, bf16[96,1024]{1,0:T(8,128)(2,1)S(1)}, u32[]{:S(2)}, u32[]{:S(2)}) %collective-permute-start.19) | collective-permute-done | bytes 196640 | tf_op jit(solution)/shard_map/ppermute | solution.py:480
  142.9 2.0 %last.1 = (f32[256,512]{1,0:T(8,128)}, f32[256,512]{1,0:T(8,128)}) custom-call(bf16[768,256]{1,0:T(8,128)(2,1)S(1)} %multiply_convert_fusion.w_ref, bf16[96,1024]{1,0:T(8,128)(2,1)S(1)} %add_convert_fusion.refs_0_.refs_8_, bf16[96,1024]{1,0:T(8,128)(2,1)S(1)} %collective-permute-done.15.refs_1_.refs_9_, ...), custom_call_target="tpu_custom_call" | custom-call | tf_op jit(solution)/shard_map/last/pallas_call | solution.py:582
  (44 shorter events, 0.1 us)
Async XLA Ops:
  0.6 27.3 %collective-permute-start.1 = (bf16[512,2048]{1,0:T(8,128)(2,1)}, bf16[512,2048]{1,0:T(8,128)(2,1)S(1)}, u32[]{:S(2)}, u32[]{:S(2)}) collective-permute-start(bf16[512,2048]{1,0:T(8,128)(2,1)} %w0_ref), channel_id=1, source_target_pairs={{0,1},{1,0},{2,3},{3,2},{4,5},{5,4},{6,7},{7,6},{8,9},{9,8},{10,11... | collective-permute-start | bytes 6291464 | tf_op jit(solution)/shard_map/ppermute | solution.py:476
  6.0 1.6 %collective-permute-start = (f32[72,128]{1,0:T(8,128)}, f32[72,128]{1,0:T(8,128)S(1)}, u32[]{:S(2)}, u32[]{:S(2)}) collective-permute-start(f32[72,128]{1,0:T(8,128)} %get-tuple-element.60), channel_id=1, source_target_pairs={{0,1},{1,0},{2,3},{3,2},{4,5},{5,4},{6,7},{7,6},{8,9},{9,8},{10,11... | collective-permute-start | bytes 110600 | tf_op jit(solution)/shard_map/ppermute | solution.py:476
  9.1 13.9 %all-to-all-start = ((f32[8,72,128]{2,1,0:T(8,128)}), f32[8,72,128]{2,1,0:T(8,128)S(1)}, u32[]{:S(2)}, u32[]{:S(2)}) async-start(f32[8,72,128]{2,1,0:T(8,128)} %broadcast_in_dim.24), calls=%async_computation | async-start | bytes 589824 | tf_op jit(solution)/shard_map/all_to_all | solution.py:464
  21.9 18.3 %collective-permute-start.2 = (bf16[768,512]{1,0:T(8,128)(2,1)}, bf16[768,512]{1,0:T(8,128)(2,1)}, u32[]{:S(2)}, u32[]{:S(2)}) collective-permute-start(bf16[768,512]{1,0:T(8,128)(2,1)} %get-tuple-element.72.g0_ref), channel_id=1, source_target_pairs={{0,1},{1,0},{2,3},{3,2},{4,5},{5,4},{6,7},{7,6},{8,9},{9,8},{10,11... | collective-permute-start | bytes 2359304 | tf_op jit(solution)/shard_map/ppermute | solution.py:476
  22.1 18.2 %collective-permute-start.3 = (bf16[768,512]{1,0:T(8,128)(2,1)}, bf16[768,512]{1,0:T(8,128)(2,1)}, u32[]{:S(2)}, u32[]{:S(2)}) collective-permute-start(bf16[768,512]{1,0:T(8,128)(2,1)} %get-tuple-element.73.u0_ref), channel_id=1, source_target_pairs={{0,1},{1,0},{2,3},{3,2},{4,5},{5,4},{6,7},{7,6},{8,9},{9,8},{10,11... | collective-permute-start | bytes 2359304 | tf_op jit(solution)/shard_map/ppermute | solution.py:476
  23.0 0.7 copy-start.4
  28.0 5.2 %copy-start.10 = (bf16[512,2048]{1,0:T(8,128)(2,1)}, bf16[512,2048]{1,0:T(8,128)(2,1)S(1)}, u32[]{:S(2)}) copy-start(bf16[512,2048]{1,0:T(8,128)(2,1)S(1)} %collective-permute-done.1.w1_ref) | copy-start | bytes 6291460
  28.0 18.4 %all-to-all-start.1 = ((bf16[8,64,768]{2,1,0:T(8,128)(2,1)}), bf16[8,64,768]{2,1,0:T(8,128)(2,1)S(1)}, u32[]{:S(2)}, u32[]{:S(2)}) async-start(bf16[8,64,768]{2,1,0:T(8,128)(2,1)} %get-tuple-element.70), calls=%async_computation.1 | async-start | bytes 1572864 | tf_op jit(solution)/shard_map/all_to_all | solution.py:464
  46.4 0.9 copy-start.2
  53.1 16.5 %all-to-all-start.2 = ((bf16[8,64,768]{2,1,0:T(8,128)(2,1)}), bf16[8,64,768]{2,1,0:T(8,128)(2,1)S(1)}, u32[]{:S(2)}, u32[]{:S(2)}) async-start(bf16[8,64,768]{2,1,0:T(8,128)(2,1)} %get-tuple-element.81), calls=%async_computation.2 | async-start | bytes 1572864 | tf_op jit(solution)/shard_map/all_to_all | solution.py:464
  56.7 4.9 %copy-start.8 = (bf16[64,2048]{1,0:T(8,128)(2,1)S(1)}, bf16[64,2048]{1,0:T(8,128)(2,1)}, u32[]{:S(2)}) copy-start(bf16[64,2048]{1,0:T(8,128)(2,1)} %get-tuple-element.82) | copy-start | bytes 786436
  56.7 4.9 %copy-start.9 = (bf16[64,768]{1,0:T(8,128)(2,1)S(1)}, bf16[64,768]{1,0:T(8,128)(2,1)}, u32[]{:S(2)}) copy-start(bf16[64,768]{1,0:T(8,128)(2,1)} %get-tuple-element.83) | copy-start | bytes 294916
  61.0 10.3 %collective-permute-start.4 = (bf16[512,512]{1,0:T(8,128)(2,1)}, bf16[512,512]{1,0:T(8,128)(2,1)S(1)}, u32[]{:S(2)}, u32[]{:S(2)}) collective-permute-start(bf16[512,512]{1,0:T(8,128)(2,1)} %get-tuple-element.86), channel_id=1, source_target_pairs={{0,1},{1,0},{2,3},{3,2},{4,5},{5,4},{6,7},{7,6},{8,9},{9,8},{10,11... | collective-permute-start | bytes 1572872 | tf_op jit(solution)/shard_map/ppermute | solution.py:476
  61.0 10.3 %collective-permute-start.5 = (bf16[512,512]{1,0:T(8,128)(2,1)}, bf16[512,512]{1,0:T(8,128)(2,1)S(1)}, u32[]{:S(2)}, u32[]{:S(2)}) collective-permute-start(bf16[512,512]{1,0:T(8,128)(2,1)} %get-tuple-element.87), channel_id=1, source_target_pairs={{0,1},{1,0},{2,3},{3,2},{4,5},{5,4},{6,7},{7,6},{8,9},{9,8},{10,11... | collective-permute-start | bytes 1572872 | tf_op jit(solution)/shard_map/ppermute | solution.py:476
  64.1 10.8 %copy-start.3 = (bf16[8,64,768]{2,1,0:T(8,128)(2,1)S(1)}, bf16[8,64,768]{2,1,0:T(8,128)(2,1)}, u32[]{:S(2)}) copy-start(bf16[8,64,768]{2,1,0:T(8,128)(2,1)} %copy-done.2) | copy-start | bytes 2359300
  71.3 3.6 %copy-start.12 = (bf16[512,512]{1,0:T(8,128)(2,1)}, bf16[512,512]{1,0:T(8,128)(2,1)S(1)}, u32[]{:S(2)}) copy-start(bf16[512,512]{1,0:T(8,128)(2,1)S(1)} %collective-permute-done.4.a_ref) | copy-start | bytes 1572868
  71.3 3.9 %copy-start.13 = (bf16[512,512]{1,0:T(8,128)(2,1)}, bf16[512,512]{1,0:T(8,128)(2,1)S(1)}, u32[]{:S(2)}) copy-start(bf16[512,512]{1,0:T(8,128)(2,1)S(1)} %collective-permute-done.5.b_ref) | copy-start | bytes 1572868
  71.3 16.5 %all-to-all-start.3 = ((bf16[8,64,768]{2,1,0:T(8,128)(2,1)}), bf16[8,64,768]{2,1,0:T(8,128)(2,1)S(1)}, u32[]{:S(2)}, u32[]{:S(2)}) async-start(bf16[8,64,768]{2,1,0:T(8,128)(2,1)} %error.1), calls=%async_computation.3 | async-start | bytes 1572864 | tf_op jit(solution)/shard_map/all_to_all | solution.py:464
  75.2 16.8 %copy-start.5 = (bf16[512,768]{0,1:T(8,128)(2,1)}, bf16[512,768]{0,1:T(8,128)(2,1)S(1)}, u32[]{:S(2)}) copy-start(bf16[512,768]{0,1:T(8,128)(2,1)S(1)} %copy.29) | copy-start | bytes 2359300
  75.2 16.8 %collective-permute-start.7 = (bf16[768,512]{1,0:T(8,128)(2,1)S(1)}, bf16[768,512]{1,0:T(8,128)(2,1)S(1)}, u32[]{:S(2)}, u32[]{:S(2)}) collective-permute-start(bf16[768,512]{1,0:T(8,128)(2,1)S(1)} %bitcast.18), channel_id=1, source_target_pairs={{0,1},{1,0},{2,3},{3,2},{4,5},{5,4},{6,7},{7,6},{8,9},{9,8},{10,11... | collective-permute-start | bytes 2359304 | tf_op jit(solution)/shard_map/ppermute | solution.py:476
  87.8 0.9 copy-start
  87.8 4.1 %collective-permute-start.6 = (bf16[8,64,768]{2,1,0:T(8,128)(2,1)S(1)}, bf16[8,64,768]{2,1,0:T(8,128)(2,1)S(1)}, u32[]{:S(2)}, u32[]{:S(2)}) collective-permute-start(bf16[8,64,768]{2,1,0:T(8,128)(2,1)S(1)} %all-to-all-done.3.err_ref), channel_id=1, source_target_pairs={{0,1},{1,0},{2,3},{3,2},{4,5},{5,4},{6,7},{7,6},{8,9},{9,8},{10,11... | collective-permute-start | bytes 2359304 | tf_op jit(solution)/shard_map/ppermute | solution.py:476
  91.9 0.9 copy-start.11
  92.0 1.1 copy-start.6
  98.2 32.1 %copy-start.1 = (bf16[8,64,768]{2,1,0:T(8,128)(2,1)S(1)}, bf16[8,64,768]{2,1,0:T(8,128)(2,1)}, u32[]{:S(2)}) copy-start(bf16[8,64,768]{2,1,0:T(8,128)(2,1)} %copy-done) | copy-start | bytes 2359300
  98.3 32.1 %copy-start.7 = (bf16[8,64,768]{2,1,0:T(8,128)(2,1)S(1)}, bf16[8,64,768]{2,1,0:T(8,128)(2,1)}, u32[]{:S(2)}) copy-start(bf16[8,64,768]{2,1,0:T(8,128)(2,1)} %copy-done.6) | copy-start | bytes 2359300
  98.3 9.6 %collective-permute-start.11 = (bf16[96,1024]{1,0:T(8,128)(2,1)}, bf16[96,1024]{1,0:T(8,128)(2,1)S(1)}, u32[]{:S(2)}, u32[]{:S(2)}) collective-permute-start(bf16[96,1024]{1,0:T(8,128)(2,1)} %get-tuple-element.104), channel_id=1, source_target_pairs={{0,32},{32,64},{64,96},{96,0},{1,33},{33,65},{65,97},{97,1},{2,34}... | collective-permute-start | bytes 589832 | tf_op jit(solution)/shard_map/ppermute | solution.py:480
  99.9 12.8 %collective-permute-start.12 = (bf16[96,1024]{1,0:T(8,128)(2,1)}, bf16[96,1024]{1,0:T(8,128)(2,1)S(1)}, u32[]{:S(2)}, u32[]{:S(2)}) collective-permute-start(bf16[96,1024]{1,0:T(8,128)(2,1)} %get-tuple-element.105), channel_id=1, source_target_pairs={{0,96},{32,0},{64,32},{96,64},{1,97},{33,1},{65,33},{97,65},{2,98}... | collective-permute-start | bytes 589832 | tf_op jit(solution)/shard_map/ppermute | solution.py:480
  101.6 11.5 %collective-permute-start.13 = (bf16[96,1024]{1,0:T(8,128)(2,1)}, bf16[96,1024]{1,0:T(8,128)(2,1)S(1)}, u32[]{:S(2)}, u32[]{:S(2)}) collective-permute-start(bf16[96,1024]{1,0:T(8,128)(2,1)} %get-tuple-element.106), channel_id=1, source_target_pairs={{0,64},{32,96},{64,0},{96,32},{1,65},{33,97},{65,1},{97,33},{2,66}... | collective-permute-start | bytes 589832 | tf_op jit(solution)/shard_map/ppermute | solution.py:480
  104.4 16.0 %collective-permute-start.8 = (bf16[96,1024]{1,0:T(8,128)(2,1)}, bf16[96,1024]{1,0:T(8,128)(2,1)S(1)}, u32[]{:S(2)}, u32[]{:S(2)}) collective-permute-start(bf16[96,1024]{1,0:T(8,128)(2,1)} %get-tuple-element.98), channel_id=1, source_target_pairs={{0,32},{32,64},{64,96},{96,0},{1,33},{33,65},{65,97},{97,1},{2,34}... | collective-permute-start | bytes 589832 | tf_op jit(solution)/shard_map/ppermute | solution.py:480
  105.3 15.1 %collective-permute-start.9 = (bf16[96,1024]{1,0:T(8,128)(2,1)}, bf16[96,1024]{1,0:T(8,128)(2,1)S(1)}, u32[]{:S(2)}, u32[]{:S(2)}) collective-permute-start(bf16[96,1024]{1,0:T(8,128)(2,1)} %get-tuple-element.99), channel_id=1, source_target_pairs={{0,96},{32,0},{64,32},{96,64},{1,97},{33,1},{65,33},{97,65},{2,98}... | collective-permute-start | bytes 589832 | tf_op jit(solution)/shard_map/ppermute | solution.py:480
  107.9 12.5 %collective-permute-start.10 = (bf16[96,1024]{1,0:T(8,128)(2,1)}, bf16[96,1024]{1,0:T(8,128)(2,1)S(1)}, u32[]{:S(2)}, u32[]{:S(2)}) collective-permute-start(bf16[96,1024]{1,0:T(8,128)(2,1)} %get-tuple-element.100), channel_id=1, source_target_pairs={{0,64},{32,96},{64,0},{96,32},{1,65},{33,97},{65,1},{97,33},{2,66}... | collective-permute-start | bytes 589832 | tf_op jit(solution)/shard_map/ppermute | solution.py:480
  114.1 7.3 %collective-permute-start.14 = (bf16[96,1024]{1,0:T(8,128)(2,1)S(1)}, bf16[96,1024]{1,0:T(8,128)(2,1)S(1)}, u32[]{:S(2)}, u32[]{:S(2)}) collective-permute-start(bf16[96,1024]{1,0:T(8,128)(2,1)S(1)} %add_convert_fusion.1), channel_id=1, source_target_pairs={{0,16},{16,0},{1,17},{17,1},{2,18},{18,2},{3,19},{19,3},{4,20},{20... | collective-permute-start | bytes 589832 | tf_op jit(solution)/shard_map/ppermute | solution.py:476
  122.5 12.6 %collective-permute-start.18 = (bf16[96,1024]{1,0:T(8,128)(2,1)S(1)}, bf16[96,1024]{1,0:T(8,128)(2,1)S(1)}, u32[]{:S(2)}, u32[]{:S(2)}) collective-permute-start(bf16[96,1024]{1,0:T(8,128)(2,1)S(1)} %add_convert_fusion.refs_0_.refs_8_), channel_id=1, source_target_pairs={{0,64},{32,96},{64,0},{96,32},{1,65},{33,97},{65,1},{97,33},{2,66}... | collective-permute-start | bytes 589832 | tf_op jit(solution)/shard_map/ppermute | solution.py:480
  123.0 7.6 %collective-permute-start.15 = (bf16[96,1024]{1,0:T(8,128)(2,1)S(1)}, bf16[96,1024]{1,0:T(8,128)(2,1)S(1)}, u32[]{:S(2)}, u32[]{:S(2)}) collective-permute-start(bf16[96,1024]{1,0:T(8,128)(2,1)S(1)} %add_convert_fusion.refs_0_.refs_8_), channel_id=1, source_target_pairs={{0,16},{16,0},{1,17},{17,1},{2,18},{18,2},{3,19},{19,3},{4,20},{20... | collective-permute-start | bytes 589832 | tf_op jit(solution)/shard_map/ppermute | solution.py:476
  126.6 12.5 %collective-permute-start.17 = (bf16[96,1024]{1,0:T(8,128)(2,1)S(1)}, bf16[96,1024]{1,0:T(8,128)(2,1)S(1)}, u32[]{:S(2)}, u32[]{:S(2)}) collective-permute-start(bf16[96,1024]{1,0:T(8,128)(2,1)S(1)} %add_convert_fusion.refs_0_.refs_8_), channel_id=1, source_target_pairs={{0,96},{32,0},{64,32},{96,64},{1,97},{33,1},{65,33},{97,65},{2,98}... | collective-permute-start | bytes 589832 | tf_op jit(solution)/shard_map/ppermute | solution.py:480
  130.4 10.5 %collective-permute-start.16 = (bf16[96,1024]{1,0:T(8,128)(2,1)S(1)}, bf16[96,1024]{1,0:T(8,128)(2,1)S(1)}, u32[]{:S(2)}, u32[]{:S(2)}) collective-permute-start(bf16[96,1024]{1,0:T(8,128)(2,1)S(1)} %add_convert_fusion.refs_0_.refs_8_), channel_id=1, source_target_pairs={{0,32},{32,64},{64,96},{96,0},{1,33},{33,65},{65,97},{97,1},{2,34}... | collective-permute-start | bytes 589832 | tf_op jit(solution)/shard_map/ppermute | solution.py:480
  130.5 10.3 %collective-permute-start.21 = (bf16[96,1024]{1,0:T(8,128)(2,1)S(1)}, bf16[96,1024]{1,0:T(8,128)(2,1)S(1)}, u32[]{:S(2)}, u32[]{:S(2)}) collective-permute-start(bf16[96,1024]{1,0:T(8,128)(2,1)S(1)} %collective-permute-done.15.refs_1_.refs_9_), channel_id=1, source_target_pairs={{0,64},{32,96},{64,0},{96,32},{1,65},{33,97},{65,1},{97,33},{2,66}... | collective-permute-start | bytes 589832 | tf_op jit(solution)/shard_map/ppermute | solution.py:480
  133.3 7.9 %collective-permute-start.20 = (bf16[96,1024]{1,0:T(8,128)(2,1)S(1)}, bf16[96,1024]{1,0:T(8,128)(2,1)S(1)}, u32[]{:S(2)}, u32[]{:S(2)}) collective-permute-start(bf16[96,1024]{1,0:T(8,128)(2,1)S(1)} %collective-permute-done.15.refs_1_.refs_9_), channel_id=1, source_target_pairs={{0,96},{32,0},{64,32},{96,64},{1,97},{33,1},{65,33},{97,65},{2,98}... | collective-permute-start | bytes 589832 | tf_op jit(solution)/shard_map/ppermute | solution.py:480
  135.1 7.9 %collective-permute-start.19 = (bf16[96,1024]{1,0:T(8,128)(2,1)S(1)}, bf16[96,1024]{1,0:T(8,128)(2,1)S(1)}, u32[]{:S(2)}, u32[]{:S(2)}) collective-permute-start(bf16[96,1024]{1,0:T(8,128)(2,1)S(1)} %collective-permute-done.15.refs_1_.refs_9_), channel_id=1, source_target_pairs={{0,32},{32,64},{64,96},{96,0},{1,33},{33,65},{65,97},{97,1},{2,34}... | collective-permute-start | bytes 589832 | tf_op jit(solution)/shard_map/ppermute | solution.py:480

commit v9 on v8

--- a/solution.py
+++ b/solution.py
@@ -575,7 +575,7 @@
     moved = [shift(p, d) if d else p for p, (_, d) in zip(pieces, SENT)]
     theirs = swap(total(*moved[:4]), "zh")
     grads = total(*moved[4:], theirs)
-    grads, err_late, err_other = lax.optimization_barrier((grads, err, err_other))
+    grads, err_late, err_other, recv = lax.optimization_barrier((grads, err, err_other, recv))
     twin = swap(grads, "zh")
     got = [grads, twin] + [shift(v, d) for v in (grads, twin) for d in SHIFTS]
     grad = sds((block, width), F32)

time: 146 us -> 146 us (level)
  waiting for transfers between devices: 33.6 us -> 36.1 us
    ppermute x10, waiting for transfers between devices: 2.09 us -> 4.92 us  [swap(): return lax.ppermute(x, axis, SWAP)]
where the time goes in v9:
time: 146 us; the launch traced here: 145 us
  starting transfers between devices  48.5 us (33%)
  Pallas kernels  45.7 us (31%)
  waiting for transfers between devices  36.1 us (25%)
  local copies, waits for them, and re-layouts  7.07 us (5%)
  matrix products  3.65 us (2%)
  other arithmetic  2.97 us (2%)
    pallas_call x5, Pallas kernels, staged(): pl.pallas_call(kernel, out_shape=out_shape, in_specs=[HB] * len(args), ou...  28.2 us
    all_to_all x4, waiting for transfers between devices, exchange(): return lax.all_to_all(x, axes, split_axis=0, concat_axis=0, tiled=True)  24.7 us
    ppermute x12, starting transfers between devices, shift(): return lax.ppermute(x, 'y', [(i, (i + d) % 4) for i in range(4)])  21.3 us
    all_to_all x4, starting transfers between devices, exchange(): return lax.all_to_all(x, axes, split_axis=0, concat_axis=0, tiled=True)  18.1 us
    ppermute x10, starting transfers between devices, swap(): return lax.ppermute(x, axis, SWAP)  9.03 us
    ppermute x12, waiting for transfers between devices, shift(): return lax.ppermute(x, 'y', [(i, (i + d) % 4) for i in range(4)])  6.43 us
    pallas_call x1, Pallas kernels, evolve(): pl.pallas_call(evolve_kernel, out_shape=(sds((ROWS, LANES), F32), sds((2...  5.24 us
    ppermute x10, waiting for transfers between devices, swap(): return lax.ppermute(x, axis, SWAP)  4.92 us
  transfers between devices with their start and end apart: 26, of which 11 were waited for; matrix products, arithmetic and copies ran while one was open for 7% of the time, Pallas kernels for 23%

profile of v9, /device:TPU:0, one launch (start us, length us, event | category | flops | bytes accessed | tf_op | source)
XLA Modules:
  0.0 144.9 jit_solution(17494614856058622295)
XLA Ops:
  0.6 0.1 collective-permute-start.1
  0.7 5.2 %evolve.1 = (f32[72,128]{1,0:T(8,128)}, bf16[128,768]{1,0:T(8,128)(2,1)}, f32[24,128]{1,0:T(8,128)}, f32[3,256,128]{2,1,0:T(8,128)}) custom-call(f32[3,256,128]{2,1,0:T(8,128)} %pos_ref.3, f32[3,256,128]{2,1,0:T(8,128)} %vel_ref.3, f32[1,128]{1,0:T(1,128)} %bitcast.23, s32[8,256,128]{2,1,0:T(8,128)} %contact_ref.3, f32[3,128]{1,0:T(4,128)} %off_ref.3, ...), custom_call_target="tpu_custom_call" | custom-call | flops 260000000 | bytes 3000000 | tf_op jit(solution)/shard_map/evolve/pallas_call | solution.py:387
  6.0 0.6 collective-permute-start
  6.5 1.1 collective-permute-done
  7.6 0.8 add.110
  8.4 0.7 broadcast_in_dim.24
  9.1 5.7 %all-to-all-start = ((f32[8,72,128]{2,1,0:T(8,128)}), f32[8,72,128]{2,1,0:T(8,128)S(1)}, u32[]{:S(2)}, u32[]{:S(2)}) async-start(f32[8,72,128]{2,1,0:T(8,128)} %broadcast_in_dim.24), calls=%async_computation | async-start | bytes 589824 | tf_op jit(solution)/shard_map/all_to_all | solution.py:464
  14.9 7.1 %products.1 = (bf16[768,512]{1,0:T(8,128)(2,1)}, bf16[768,512]{1,0:T(8,128)(2,1)}) custom-call(bf16[768,2048]{1,0:T(8,128)(2,1)} %w_in_ref.2, f32[1,2048]{1,0:T(1,128)} %bitcast.30, bf16[2048,512]{1,0:T(8,128)(2,1)} %gate_ref.1, bf16[2048,512]{1,0:T(8,128)(2,1)} %up_ref.1), custom_call_target="tpu_custom_call" | custom-call | flops 3300000000 | bytes 8000000 | tf_op jit(solution)/shard_map/products/pallas_call | solution.py:446
  21.9 0.1 collective-permute-start.2
  22.1 0.4 collective-permute-start.3
  22.5 0.5 all-to-all-done.recv_ref
  23.0 0.7 copy-done.4
  23.7 4.2 %finish.1 = (bf16[8,64,768]{2,1,0:T(8,128)(2,1)}, bf16[64,768]{1,0:T(8,128)(2,1)}, bf16[64,2048]{1,0:T(8,128)(2,1)}, f32[3,128]{1,0:T(4,128)}, f32[3,256,128]{2,1,0:T(8,128)}) custom-call(f32[8,72,128]{2,1,0:T(8,128)} %copy-done.4, f32[24,128]{1,0:T(8,128)} %get-tuple-element.63.bound_ref, ...), custom_call_target="tpu_custom_call", output_to_operand_aliasing={{4}: (18, {})} | custom-call | flops 300000000 | bytes 4000000 | tf_op jit(solution)/shard_map/finish/pallas_call | solution.py:420
  28.0 0.0 collective-permute-done.1.w1_ref
  28.0 5.2 %all-to-all-start.1 = ((bf16[8,64,768]{2,1,0:T(8,128)(2,1)}), bf16[8,64,768]{2,1,0:T(8,128)(2,1)S(1)}, u32[]{:S(2)}, u32[]{:S(2)}) async-start(bf16[8,64,768]{2,1,0:T(8,128)(2,1)} %get-tuple-element.71), calls=%async_computation.1 | async-start | bytes 1572864 | tf_op jit(solution)/shard_map/all_to_all | solution.py:464
  33.2 7.0 %down.1 = (bf16[512,768]{1,0:T(8,128)(2,1)}, bf16[512,768]{1,0:T(8,128)(2,1)}) custom-call(bf16[512,2048]{1,0:T(8,128)(2,1)} %w0_ref, bf16[512,2048]{1,0:T(8,128)(2,1)} %copy-done.11, bf16[2048,768]{1,0:T(8,128)(2,1)} %out_ref.1), custom_call_target="tpu_custom_call" | custom-call | flops 3300000000 | bytes 8000000 | tf_op jit(solution)/shard_map/down/pallas_call | solution.py:446
  40.3 0.0 collective-permute-done.3.u1_ref
  40.3 6.1 %all-to-all-done.1.x_ref = bf16[8,64,768]{2,1,0:T(8,128)(2,1)S(1)} async-done(((bf16[8,64,768]{2,1,0:T(8,128)(2,1)}), bf16[8,64,768]{2,1,0:T(8,128)(2,1)S(1)}, u32[]{:S(2)}, u32[]{:S(2)}) %all-to-all-start.1) | async-done | bytes 786464 | tf_op jit(solution)/shard_map/all_to_all | solution.py:464
  46.4 0.9 copy-done.2
  47.3 5.8 %forward.1 = (bf16[8,64,768]{2,1,0:T(8,128)(2,1)}, f32[2,512,512]{2,1,0:T(8,128)}, f32[2,512,512]{2,1,0:T(8,128)}) custom-call(bf16[8,64,768]{2,1,0:T(8,128)(2,1)} %copy-done.2, bf16[768,512]{1,0:T(8,128)(2,1)} %get-tuple-element.73.g0_ref, bf16[768,512]{1,0:T(8,128)(2,1)} %get-tuple-element.74.u0_ref, bf16[512,768]{1,0:T(8,128)(2,1)} %get-tuple-element.77.d0_ref.d_ref, ...), custom_call_target="tpu_custom_call" | custom-call | flops 2500000000 | bytes 8000000 | tf_op jit(solution)/shard_map/forward/pallas_call | solution.py:446
  53.1 3.6 %all-to-all-start.2 = ((bf16[8,64,768]{2,1,0:T(8,128)(2,1)}), bf16[8,64,768]{2,1,0:T(8,128)(2,1)S(1)}, u32[]{:S(2)}, u32[]{:S(2)}) async-start(bf16[8,64,768]{2,1,0:T(8,128)(2,1)} %get-tuple-element.82), calls=%async_computation.2 | async-start | bytes 1572864 | tf_op jit(solution)/shard_map/all_to_all | solution.py:464
  56.7 4.3 %slopes.1 = (bf16[512,512]{1,0:T(8,128)(2,1)}, bf16[512,512]{1,0:T(8,128)(2,1)}, bf16[512,512]{1,0:T(8,128)(2,1)}, bf16[512,512]{1,0:T(8,128)(2,1)}) custom-call(f32[2,512,512]{2,1,0:T(8,128)} %get-tuple-element.85.gate_ref, f32[2,512,512]{2,1,0:T(8,128)} %get-tuple-element.86.up_ref), custom_call_target="tpu_custom_call" | custom-call | flops 8000000 | bytes 6000000 | tf_op jit(solution)/shard_map/slopes/pallas_call | solution.py:542
  61.0 0.5 collective-permute-start.5
  61.5 2.5 %convolution_subtract_fusion.base_ref = f32[64,768]{1,0:T(8,128)S(1)} fusion(bf16[64,2048]{1,0:T(8,128)(2,1)S(1)} %copy-done.8, bf16[2048,768]{1,0:T(8,128)(2,1)} %out_ref.1, bf16[64,768]{1,0:T(8,128)(2,1)S(1)} %copy-done.10), kind=kOutput, calls=%fused_computation.2 | convolution fusion | flops 201424896 | bytes 3702784 | tf_op jit(solution)/shard_map/dot_general | solution.py:468
  64.1 5.6 %all-to-all-done.2.parts_ref = bf16[8,64,768]{2,1,0:T(8,128)(2,1)S(1)} async-done(((bf16[8,64,768]{2,1,0:T(8,128)(2,1)}), bf16[8,64,768]{2,1,0:T(8,128)(2,1)S(1)}, u32[]{:S(2)}, u32[]{:S(2)}) %all-to-all-start.2) | async-done | bytes 786464 | tf_op jit(solution)/shard_map/all_to_all | solution.py:464
  69.6 1.6 %error.1 = bf16[8,64,768]{2,1,0:T(8,128)(2,1)} custom-call(bf16[8,64,768]{2,1,0:T(8,128)(2,1)S(1)} %all-to-all-done.2.parts_ref, f32[64,768]{1,0:T(8,128)S(1)} %convolution_subtract_fusion.base_ref), custom_call_target="tpu_custom_call" | custom-call | tf_op jit(solution)/shard_map/error/pallas_call | solution.py:551
  71.3 3.6 %all-to-all-start.3 = ((bf16[8,64,768]{2,1,0:T(8,128)(2,1)}), bf16[8,64,768]{2,1,0:T(8,128)(2,1)S(1)}, u32[]{:S(2)}, u32[]{:S(2)}) async-start(bf16[8,64,768]{2,1,0:T(8,128)(2,1)} %error.1), calls=%async_computation.3 | async-start | bytes 1572864 | tf_op jit(solution)/shard_map/all_to_all | solution.py:464
  74.9 0.3 copy.28
  75.1 0.1 collective-permute-start.7
  75.2 12.6 %all-to-all-done.3.err_ref = bf16[8,64,768]{2,1,0:T(8,128)(2,1)S(1)} async-done(((bf16[8,64,768]{2,1,0:T(8,128)(2,1)}), bf16[8,64,768]{2,1,0:T(8,128)(2,1)S(1)}, u32[]{:S(2)}, u32[]{:S(2)}) %all-to-all-start.3) | async-done | bytes 786464 | tf_op jit(solution)/shard_map/all_to_all | solution.py:464
  87.8 0.9 copy-done
  88.7 3.2 %own.1 = (bf16[512,512]{1,0:T(8,128)(2,1)}, bf16[512,512]{1,0:T(8,128)(2,1)}) custom-call(bf16[8,64,768]{2,1,0:T(8,128)(2,1)} %copy-done, bf16[512,768]{1,0:T(8,128)(2,1)} %get-tuple-element.77.d0_ref.d_ref, bf16[512,512]{1,0:T(8,128)(2,1)} %get-tuple-element.95.a_ref, bf16[512,512]{1,0:T(8,128)(2,1)} %get-tuple-element.96.b_ref), custom_call_target="tpu_custom_call" | custom-call | flops 400000000 | bytes 8000000 | tf_op jit(solution)/shard_map/own/pallas_call | solution.py:446
  91.9 0.9 copy-done.6
  92.8 5.2 %other.1 = (bf16[96,1024]{1,0:T(8,128)(2,1)}, bf16[96,1024]{1,0:T(8,128)(2,1)}, bf16[96,1024]{1,0:T(8,128)(2,1)}, bf16[96,1024]{1,0:T(8,128)(2,1)}, bf16[96,1024...) custom-call(bf16[8,64,768]{2,1,0:T(8,128)(2,1)} %copy-done.6, ...), custom_call_target="tpu_custom_call" | custom-call | flops 2000000000 | bytes 8000000 | tf_op jit(solution)/shard_map/other/pallas_call | solution.py:446
  98.0 1.6 %collective-permute-start.11 = (bf16[96,1024]{1,0:T(8,128)(2,1)}, bf16[96,1024]{1,0:T(8,128)(2,1)S(1)}, u32[]{:S(2)}, u32[]{:S(2)}) collective-permute-start(bf16[96,1024]{1,0:T(8,128)(2,1)} %get-tuple-element.105), channel_id=1, source_target_pairs={{0,32},{32,64},{64,96},{96,0},{1,33},{33,65},{65,97},{97,1},{2,34}... | collective-permute-start | bytes 589832 | tf_op jit(solution)/shard_map/ppermute | solution.py:480
  99.6 1.7 %collective-permute-start.12 = (bf16[96,1024]{1,0:T(8,128)(2,1)}, bf16[96,1024]{1,0:T(8,128)(2,1)S(1)}, u32[]{:S(2)}, u32[]{:S(2)}) collective-permute-start(bf16[96,1024]{1,0:T(8,128)(2,1)} %get-tuple-element.106), channel_id=1, source_target_pairs={{0,96},{32,0},{64,32},{96,64},{1,97},{33,1},{65,33},{97,65},{2,98}... | collective-permute-start | bytes 589832 | tf_op jit(solution)/shard_map/ppermute | solution.py:480
  101.3 2.0 %collective-permute-start.13 = (bf16[96,1024]{1,0:T(8,128)(2,1)}, bf16[96,1024]{1,0:T(8,128)(2,1)S(1)}, u32[]{:S(2)}, u32[]{:S(2)}) collective-permute-start(bf16[96,1024]{1,0:T(8,128)(2,1)} %get-tuple-element.107), channel_id=1, source_target_pairs={{0,64},{32,96},{64,0},{96,32},{1,65},{33,97},{65,1},{97,33},{2,66}... | collective-permute-start | bytes 589832 | tf_op jit(solution)/shard_map/ppermute | solution.py:480
  103.3 0.7 collective-permute-start.8
  104.0 2.6 %collective-permute-start.9 = (bf16[96,1024]{1,0:T(8,128)(2,1)}, bf16[96,1024]{1,0:T(8,128)(2,1)S(1)}, u32[]{:S(2)}, u32[]{:S(2)}) collective-permute-start(bf16[96,1024]{1,0:T(8,128)(2,1)} %get-tuple-element.100), channel_id=1, source_target_pairs={{0,96},{32,0},{64,32},{96,64},{1,97},{33,1},{65,33},{97,65},{2,98}... | collective-permute-start | bytes 589832 | tf_op jit(solution)/shard_map/ppermute | solution.py:480
  106.5 0.8 dynamic_slice.7
  107.3 1.0 constant_dynamic-slice_fusion
  108.3 5.2 %collective-permute-start.10 = (bf16[96,1024]{1,0:T(8,128)(2,1)}, bf16[96,1024]{1,0:T(8,128)(2,1)S(1)}, u32[]{:S(2)}, u32[]{:S(2)}) collective-permute-start(bf16[96,1024]{1,0:T(8,128)(2,1)} %get-tuple-element.101), channel_id=1, source_target_pairs={{0,64},{32,96},{64,0},{96,32},{1,65},{33,97},{65,1},{97,33},{2,66}... | collective-permute-start | bytes 589832 | tf_op jit(solution)/shard_map/ppermute | solution.py:480
  113.5 1.0 add_convert_fusion.1
  114.5 3.7 %collective-permute-start.14 = (bf16[96,1024]{1,0:T(8,128)(2,1)S(1)}, bf16[96,1024]{1,0:T(8,128)(2,1)S(1)}, u32[]{:S(2)}, u32[]{:S(2)}) collective-permute-start(bf16[96,1024]{1,0:T(8,128)(2,1)S(1)} %add_convert_fusion.1), channel_id=1, source_target_pairs={{0,16},{16,0},{1,17},{17,1},{2,18},{18,2},{3,19},{19,3},{4,20},{20... | collective-permute-start | bytes 589832 | tf_op jit(solution)/shard_map/ppermute | solution.py:476
  118.2 0.1 multiply_convert_fusion.w_ref
  118.3 1.6 %collective-permute-done.10 = bf16[96,1024]{1,0:T(8,128)(2,1)S(1)} collective-permute-done((bf16[96,1024]{1,0:T(8,128)(2,1)}, bf16[96,1024]{1,0:T(8,128)(2,1)S(1)}, u32[]{:S(2)}, u32[]{:S(2)}) %collective-permute-start.10) | collective-permute-done | bytes 196640 | tf_op jit(solution)/shard_map/ppermute | solution.py:480
  119.9 2.0 %collective-permute-done.14 = bf16[96,1024]{1,0:T(8,128)(2,1)S(1)} collective-permute-done((bf16[96,1024]{1,0:T(8,128)(2,1)S(1)}, bf16[96,1024]{1,0:T(8,128)(2,1)S(1)}, u32[]{:S(2)}, u32[]{:S(2)}) %collective-permute-start.14) | collective-permute-done | bytes 196640 | tf_op jit(solution)/shard_map/ppermute | solution.py:476
  121.9 0.2 add_convert_fusion.refs_0_.refs_8_
  122.0 0.1 collective-permute-start.18
  122.1 3.4 %collective-permute-start.17 = (bf16[96,1024]{1,0:T(8,128)(2,1)S(1)}, bf16[96,1024]{1,0:T(8,128)(2,1)S(1)}, u32[]{:S(2)}, u32[]{:S(2)}) collective-permute-start(bf16[96,1024]{1,0:T(8,128)(2,1)S(1)} %add_convert_fusion.refs_0_.refs_8_), channel_id=1, source_target_pairs={{0,96},{32,0},{64,32},{96,64},{1,97},{33,1},{65,33},{97,65},{2,98}... | collective-permute-start | bytes 589832 | tf_op jit(solution)/shard_map/ppermute | solution.py:480
  125.5 3.5 %collective-permute-start.15 = (bf16[96,1024]{1,0:T(8,128)(2,1)S(1)}, bf16[96,1024]{1,0:T(8,128)(2,1)S(1)}, u32[]{:S(2)}, u32[]{:S(2)}) collective-permute-start(bf16[96,1024]{1,0:T(8,128)(2,1)S(1)} %add_convert_fusion.refs_0_.refs_8_), channel_id=1, source_target_pairs={{0,16},{16,0},{1,17},{17,1},{2,18},{18,2},{3,19},{19,3},{4,20},{20... | collective-permute-start | bytes 589832 | tf_op jit(solution)/shard_map/ppermute | solution.py:476
  129.0 0.8 slice.3
  129.8 0.8 select_bitcast_fusion
  130.6 0.1 eq.40
  130.7 0.1 pad_maximum_fusion
  130.8 1.9 %collective-permute-done.15.refs_1_.refs_9_ = bf16[96,1024]{1,0:T(8,128)(2,1)S(1)} collective-permute-done((bf16[96,1024]{1,0:T(8,128)(2,1)S(1)}, bf16[96,1024]{1,0:T(8,128)(2,1)S(1)}, u32[]{:S(2)}, u32[]{:S(2)}) %collective-permute-start.15) | collective-permute-done | bytes 196640 | tf_op jit(solution)/shard_map/ppermute | solution.py:476
  132.7 2.2 %collective-permute-start.21 = (bf16[96,1024]{1,0:T(8,128)(2,1)S(1)}, bf16[96,1024]{1,0:T(8,128)(2,1)S(1)}, u32[]{:S(2)}, u32[]{:S(2)}) collective-permute-start(bf16[96,1024]{1,0:T(8,128)(2,1)S(1)} %collective-permute-done.15.refs_1_.refs_9_), channel_id=1, source_target_pairs={{0,64},{32,96},{64,0},{96,32},{1,65},{33,97},{65,1},{97,33},{2,66}... | collective-permute-start | bytes 589832 | tf_op jit(solution)/shard_map/ppermute | solution.py:480
  134.8 1.1 collective-permute-start.20
  135.9 0.9 collective-permute-start.19
  136.9 1.1 convolution_convert_fusion
  138.0 1.9 %collective-permute-done.21.refs_7_.refs_15_ = bf16[96,1024]{1,0:T(8,128)(2,1)S(1)} collective-permute-done((bf16[96,1024]{1,0:T(8,128)(2,1)S(1)}, bf16[96,1024]{1,0:T(8,128)(2,1)S(1)}, u32[]{:S(2)}, u32[]{:S(2)}) %collective-permute-start.21) | collective-permute-done | bytes 196640 | tf_op jit(solution)/shard_map/ppermute | solution.py:480
  139.8 2.7 %collective-permute-done.20.refs_6_.refs_14_ = bf16[96,1024]{1,0:T(8,128)(2,1)S(1)} collective-permute-done((bf16[96,1024]{1,0:T(8,128)(2,1)S(1)}, bf16[96,1024]{1,0:T(8,128)(2,1)S(1)}, u32[]{:S(2)}, u32[]{:S(2)}) %collective-permute-start.20) | collective-permute-done | bytes 196640 | tf_op jit(solution)/shard_map/ppermute | solution.py:480
  142.6 0.3 collective-permute-done.19.refs_5_.refs_13_
  142.8 2.0 %last.1 = (f32[256,512]{1,0:T(8,128)}, f32[256,512]{1,0:T(8,128)}) custom-call(bf16[768,256]{1,0:T(8,128)(2,1)S(1)} %multiply_convert_fusion.w_ref, bf16[96,1024]{1,0:T(8,128)(2,1)S(1)} %add_convert_fusion.refs_0_.refs_8_, bf16[96,1024]{1,0:T(8,128)(2,1)S(1)} %collective-permute-done.15.refs_1_.refs_9_, ...), custom_call_target="tpu_custom_call" | custom-call | tf_op jit(solution)/shard_map/last/pallas_call | solution.py:582
  (44 shorter events, 0.1 us)
Async XLA Ops:
  0.6 27.3 %collective-permute-start.1 = (bf16[512,2048]{1,0:T(8,128)(2,1)}, bf16[512,2048]{1,0:T(8,128)(2,1)S(1)}, u32[]{:S(2)}, u32[]{:S(2)}) collective-permute-start(bf16[512,2048]{1,0:T(8,128)(2,1)} %w0_ref), channel_id=1, source_target_pairs={{0,1},{1,0},{2,3},{3,2},{4,5},{5,4},{6,7},{7,6},{8,9},{9,8},{10,11... | collective-permute-start | bytes 6291464 | tf_op jit(solution)/shard_map/ppermute | solution.py:476
  6.0 1.6 %collective-permute-start = (f32[72,128]{1,0:T(8,128)}, f32[72,128]{1,0:T(8,128)S(1)}, u32[]{:S(2)}, u32[]{:S(2)}) collective-permute-start(f32[72,128]{1,0:T(8,128)} %get-tuple-element.61), channel_id=1, source_target_pairs={{0,1},{1,0},{2,3},{3,2},{4,5},{5,4},{6,7},{7,6},{8,9},{9,8},{10,11... | collective-permute-start | bytes 110600 | tf_op jit(solution)/shard_map/ppermute | solution.py:476
  9.1 13.9 %all-to-all-start = ((f32[8,72,128]{2,1,0:T(8,128)}), f32[8,72,128]{2,1,0:T(8,128)S(1)}, u32[]{:S(2)}, u32[]{:S(2)}) async-start(f32[8,72,128]{2,1,0:T(8,128)} %broadcast_in_dim.24), calls=%async_computation | async-start | bytes 589824 | tf_op jit(solution)/shard_map/all_to_all | solution.py:464
  21.9 18.3 %collective-permute-start.2 = (bf16[768,512]{1,0:T(8,128)(2,1)}, bf16[768,512]{1,0:T(8,128)(2,1)}, u32[]{:S(2)}, u32[]{:S(2)}) collective-permute-start(bf16[768,512]{1,0:T(8,128)(2,1)} %get-tuple-element.73.g0_ref), channel_id=1, source_target_pairs={{0,1},{1,0},{2,3},{3,2},{4,5},{5,4},{6,7},{7,6},{8,9},{9,8},{10,11... | collective-permute-start | bytes 2359304 | tf_op jit(solution)/shard_map/ppermute | solution.py:476
  22.1 18.2 %collective-permute-start.3 = (bf16[768,512]{1,0:T(8,128)(2,1)}, bf16[768,512]{1,0:T(8,128)(2,1)}, u32[]{:S(2)}, u32[]{:S(2)}) collective-permute-start(bf16[768,512]{1,0:T(8,128)(2,1)} %get-tuple-element.74.u0_ref), channel_id=1, source_target_pairs={{0,1},{1,0},{2,3},{3,2},{4,5},{5,4},{6,7},{7,6},{8,9},{9,8},{10,11... | collective-permute-start | bytes 2359304 | tf_op jit(solution)/shard_map/ppermute | solution.py:476
  23.0 0.7 copy-start.4
  28.0 5.2 %copy-start.11 = (bf16[512,2048]{1,0:T(8,128)(2,1)}, bf16[512,2048]{1,0:T(8,128)(2,1)S(1)}, u32[]{:S(2)}) copy-start(bf16[512,2048]{1,0:T(8,128)(2,1)S(1)} %collective-permute-done.1.w1_ref) | copy-start | bytes 6291460
  28.0 18.4 %all-to-all-start.1 = ((bf16[8,64,768]{2,1,0:T(8,128)(2,1)}), bf16[8,64,768]{2,1,0:T(8,128)(2,1)S(1)}, u32[]{:S(2)}, u32[]{:S(2)}) async-start(bf16[8,64,768]{2,1,0:T(8,128)(2,1)} %get-tuple-element.71), calls=%async_computation.1 | async-start | bytes 1572864 | tf_op jit(solution)/shard_map/all_to_all | solution.py:464
  46.4 0.9 copy-start.2
  53.1 16.5 %all-to-all-start.2 = ((bf16[8,64,768]{2,1,0:T(8,128)(2,1)}), bf16[8,64,768]{2,1,0:T(8,128)(2,1)S(1)}, u32[]{:S(2)}, u32[]{:S(2)}) async-start(bf16[8,64,768]{2,1,0:T(8,128)(2,1)} %get-tuple-element.82), calls=%async_computation.2 | async-start | bytes 1572864 | tf_op jit(solution)/shard_map/all_to_all | solution.py:464
  56.7 4.9 %copy-start.8 = (bf16[64,2048]{1,0:T(8,128)(2,1)S(1)}, bf16[64,2048]{1,0:T(8,128)(2,1)}, u32[]{:S(2)}) copy-start(bf16[64,2048]{1,0:T(8,128)(2,1)} %get-tuple-element.83) | copy-start | bytes 786436
  56.7 4.8 %copy-start.10 = (bf16[64,768]{1,0:T(8,128)(2,1)S(1)}, bf16[64,768]{1,0:T(8,128)(2,1)}, u32[]{:S(2)}) copy-start(bf16[64,768]{1,0:T(8,128)(2,1)} %get-tuple-element.84) | copy-start | bytes 294916
  61.0 10.2 %collective-permute-start.4 = (bf16[512,512]{1,0:T(8,128)(2,1)}, bf16[512,512]{1,0:T(8,128)(2,1)S(1)}, u32[]{:S(2)}, u32[]{:S(2)}) collective-permute-start(bf16[512,512]{1,0:T(8,128)(2,1)} %get-tuple-element.87), channel_id=1, source_target_pairs={{0,1},{1,0},{2,3},{3,2},{4,5},{5,4},{6,7},{7,6},{8,9},{9,8},{10,11... | collective-permute-start | bytes 1572872 | tf_op jit(solution)/shard_map/ppermute | solution.py:476
  61.0 10.2 %collective-permute-start.5 = (bf16[512,512]{1,0:T(8,128)(2,1)}, bf16[512,512]{1,0:T(8,128)(2,1)S(1)}, u32[]{:S(2)}, u32[]{:S(2)}) collective-permute-start(bf16[512,512]{1,0:T(8,128)(2,1)} %get-tuple-element.88), channel_id=1, source_target_pairs={{0,1},{1,0},{2,3},{3,2},{4,5},{5,4},{6,7},{7,6},{8,9},{9,8},{10,11... | collective-permute-start | bytes 1572872 | tf_op jit(solution)/shard_map/ppermute | solution.py:476
  64.0 10.8 %copy-start.3 = (bf16[8,64,768]{2,1,0:T(8,128)(2,1)S(1)}, bf16[8,64,768]{2,1,0:T(8,128)(2,1)}, u32[]{:S(2)}) copy-start(bf16[8,64,768]{2,1,0:T(8,128)(2,1)} %copy-done.2) | copy-start | bytes 2359300
  71.2 20.6 %copy-start.12 = (bf16[512,512]{1,0:T(8,128)(2,1)}, bf16[512,512]{1,0:T(8,128)(2,1)S(1)}, u32[]{:S(2)}) copy-start(bf16[512,512]{1,0:T(8,128)(2,1)S(1)} %collective-permute-done.4.a_ref) | copy-start | bytes 1572868
  71.3 3.6 %copy-start.13 = (bf16[512,512]{1,0:T(8,128)(2,1)}, bf16[512,512]{1,0:T(8,128)(2,1)S(1)}, u32[]{:S(2)}) copy-start(bf16[512,512]{1,0:T(8,128)(2,1)S(1)} %collective-permute-done.5.b_ref) | copy-start | bytes 1572868
  71.3 16.5 %all-to-all-start.3 = ((bf16[8,64,768]{2,1,0:T(8,128)(2,1)}), bf16[8,64,768]{2,1,0:T(8,128)(2,1)S(1)}, u32[]{:S(2)}, u32[]{:S(2)}) async-start(bf16[8,64,768]{2,1,0:T(8,128)(2,1)} %error.1), calls=%async_computation.3 | async-start | bytes 1572864 | tf_op jit(solution)/shard_map/all_to_all | solution.py:464
  75.1 16.8 %copy-start.5 = (bf16[512,768]{0,1:T(8,128)(2,1)}, bf16[512,768]{0,1:T(8,128)(2,1)S(1)}, u32[]{:S(2)}) copy-start(bf16[512,768]{0,1:T(8,128)(2,1)S(1)} %copy.28) | copy-start | bytes 2359300
  75.1 16.7 %collective-permute-start.7 = (bf16[768,512]{1,0:T(8,128)(2,1)S(1)}, bf16[768,512]{1,0:T(8,128)(2,1)}, u32[]{:S(2)}, u32[]{:S(2)}) collective-permute-start(bf16[768,512]{1,0:T(8,128)(2,1)S(1)} %bitcast.18), channel_id=1, source_target_pairs={{0,1},{1,0},{2,3},{3,2},{4,5},{5,4},{6,7},{7,6},{8,9},{9,8},{10,11... | collective-permute-start | bytes 2359304 | tf_op jit(solution)/shard_map/ppermute | solution.py:476
  87.8 0.9 copy-start
  87.8 4.1 %collective-permute-start.6 = (bf16[8,64,768]{2,1,0:T(8,128)(2,1)S(1)}, bf16[8,64,768]{2,1,0:T(8,128)(2,1)S(1)}, u32[]{:S(2)}, u32[]{:S(2)}) collective-permute-start(bf16[8,64,768]{2,1,0:T(8,128)(2,1)S(1)} %all-to-all-done.3.err_ref), channel_id=1, source_target_pairs={{0,1},{1,0},{2,3},{3,2},{4,5},{5,4},{6,7},{7,6},{8,9},{9,8},{10,11... | collective-permute-start | bytes 2359304 | tf_op jit(solution)/shard_map/ppermute | solution.py:476
  91.9 0.9 copy-start.6
  98.0 23.9 %copy-start.9 = (bf16[96,1024]{1,0:T(8,128)(2,1)S(1)}, bf16[96,1024]{1,0:T(8,128)(2,1)}, u32[]{:S(2)}) copy-start(bf16[96,1024]{1,0:T(8,128)(2,1)} %get-tuple-element.102) | copy-start | bytes 589828
  98.0 32.7 %copy-start.1 = (bf16[8,64,768]{2,1,0:T(8,128)(2,1)S(1)}, bf16[8,64,768]{2,1,0:T(8,128)(2,1)}, u32[]{:S(2)}) copy-start(bf16[8,64,768]{2,1,0:T(8,128)(2,1)} %copy-done) | copy-start | bytes 2359300
  98.0 32.7 %copy-start.7 = (bf16[8,64,768]{2,1,0:T(8,128)(2,1)S(1)}, bf16[8,64,768]{2,1,0:T(8,128)(2,1)}, u32[]{:S(2)}) copy-start(bf16[8,64,768]{2,1,0:T(8,128)(2,1)} %copy-done.6) | copy-start | bytes 2359300
  98.0 10.3 %collective-permute-start.11 = (bf16[96,1024]{1,0:T(8,128)(2,1)}, bf16[96,1024]{1,0:T(8,128)(2,1)S(1)}, u32[]{:S(2)}, u32[]{:S(2)}) collective-permute-start(bf16[96,1024]{1,0:T(8,128)(2,1)} %get-tuple-element.105), channel_id=1, source_target_pairs={{0,32},{32,64},{64,96},{96,0},{1,33},{33,65},{65,97},{97,1},{2,34}... | collective-permute-start | bytes 589832 | tf_op jit(solution)/shard_map/ppermute | solution.py:480
  99.6 13.9 %collective-permute-start.12 = (bf16[96,1024]{1,0:T(8,128)(2,1)}, bf16[96,1024]{1,0:T(8,128)(2,1)S(1)}, u32[]{:S(2)}, u32[]{:S(2)}) collective-permute-start(bf16[96,1024]{1,0:T(8,128)(2,1)} %get-tuple-element.106), channel_id=1, source_target_pairs={{0,96},{32,0},{64,32},{96,64},{1,97},{33,1},{65,33},{97,65},{2,98}... | collective-permute-start | bytes 589832 | tf_op jit(solution)/shard_map/ppermute | solution.py:480
  101.3 12.2 %collective-permute-start.13 = (bf16[96,1024]{1,0:T(8,128)(2,1)}, bf16[96,1024]{1,0:T(8,128)(2,1)S(1)}, u32[]{:S(2)}, u32[]{:S(2)}) collective-permute-start(bf16[96,1024]{1,0:T(8,128)(2,1)} %get-tuple-element.107), channel_id=1, source_target_pairs={{0,64},{32,96},{64,0},{96,32},{1,65},{33,97},{65,1},{97,33},{2,66}... | collective-permute-start | bytes 589832 | tf_op jit(solution)/shard_map/ppermute | solution.py:480
  103.3 15.0 %collective-permute-start.8 = (bf16[96,1024]{1,0:T(8,128)(2,1)}, bf16[96,1024]{1,0:T(8,128)(2,1)S(1)}, u32[]{:S(2)}, u32[]{:S(2)}) collective-permute-start(bf16[96,1024]{1,0:T(8,128)(2,1)} %get-tuple-element.99), channel_id=1, source_target_pairs={{0,32},{32,64},{64,96},{96,0},{1,33},{33,65},{65,97},{97,1},{2,34}... | collective-permute-start | bytes 589832 | tf_op jit(solution)/shard_map/ppermute | solution.py:480
  104.0 14.3 %collective-permute-start.9 = (bf16[96,1024]{1,0:T(8,128)(2,1)}, bf16[96,1024]{1,0:T(8,128)(2,1)S(1)}, u32[]{:S(2)}, u32[]{:S(2)}) collective-permute-start(bf16[96,1024]{1,0:T(8,128)(2,1)} %get-tuple-element.100), channel_id=1, source_target_pairs={{0,96},{32,0},{64,32},{96,64},{1,97},{33,1},{65,33},{97,65},{2,98}... | collective-permute-start | bytes 589832 | tf_op jit(solution)/shard_map/ppermute | solution.py:480
  108.3 11.6 %collective-permute-start.10 = (bf16[96,1024]{1,0:T(8,128)(2,1)}, bf16[96,1024]{1,0:T(8,128)(2,1)S(1)}, u32[]{:S(2)}, u32[]{:S(2)}) collective-permute-start(bf16[96,1024]{1,0:T(8,128)(2,1)} %get-tuple-element.101), channel_id=1, source_target_pairs={{0,64},{32,96},{64,0},{96,32},{1,65},{33,97},{65,1},{97,33},{2,66}... | collective-permute-start | bytes 589832 | tf_op jit(solution)/shard_map/ppermute | solution.py:480
  114.5 7.3 %collective-permute-start.14 = (bf16[96,1024]{1,0:T(8,128)(2,1)S(1)}, bf16[96,1024]{1,0:T(8,128)(2,1)S(1)}, u32[]{:S(2)}, u32[]{:S(2)}) collective-permute-start(bf16[96,1024]{1,0:T(8,128)(2,1)S(1)} %add_convert_fusion.1), channel_id=1, source_target_pairs={{0,16},{16,0},{1,17},{17,1},{2,18},{18,2},{3,19},{19,3},{4,20},{20... | collective-permute-start | bytes 589832 | tf_op jit(solution)/shard_map/ppermute | solution.py:476
  122.0 13.9 %collective-permute-start.18 = (bf16[96,1024]{1,0:T(8,128)(2,1)S(1)}, bf16[96,1024]{1,0:T(8,128)(2,1)S(1)}, u32[]{:S(2)}, u32[]{:S(2)}) collective-permute-start(bf16[96,1024]{1,0:T(8,128)(2,1)S(1)} %add_convert_fusion.refs_0_.refs_8_), channel_id=1, source_target_pairs={{0,64},{32,96},{64,0},{96,32},{1,65},{33,97},{65,1},{97,33},{2,66}... | collective-permute-start | bytes 589832 | tf_op jit(solution)/shard_map/ppermute | solution.py:480
  122.1 15.9 %collective-permute-start.17 = (bf16[96,1024]{1,0:T(8,128)(2,1)S(1)}, bf16[96,1024]{1,0:T(8,128)(2,1)S(1)}, u32[]{:S(2)}, u32[]{:S(2)}) collective-permute-start(bf16[96,1024]{1,0:T(8,128)(2,1)S(1)} %add_convert_fusion.refs_0_.refs_8_), channel_id=1, source_target_pairs={{0,96},{32,0},{64,32},{96,64},{1,97},{33,1},{65,33},{97,65},{2,98}... | collective-permute-start | bytes 589832 | tf_op jit(solution)/shard_map/ppermute | solution.py:480
  125.5 12.5 %collective-permute-start.16 = (bf16[96,1024]{1,0:T(8,128)(2,1)S(1)}, bf16[96,1024]{1,0:T(8,128)(2,1)S(1)}, u32[]{:S(2)}, u32[]{:S(2)}) collective-permute-start(bf16[96,1024]{1,0:T(8,128)(2,1)S(1)} %add_convert_fusion.refs_0_.refs_8_), channel_id=1, source_target_pairs={{0,32},{32,64},{64,96},{96,0},{1,33},{33,65},{65,97},{97,1},{2,34}... | collective-permute-start | bytes 589832 | tf_op jit(solution)/shard_map/ppermute | solution.py:480
  125.5 7.2 %collective-permute-start.15 = (bf16[96,1024]{1,0:T(8,128)(2,1)S(1)}, bf16[96,1024]{1,0:T(8,128)(2,1)S(1)}, u32[]{:S(2)}, u32[]{:S(2)}) collective-permute-start(bf16[96,1024]{1,0:T(8,128)(2,1)S(1)} %add_convert_fusion.refs_0_.refs_8_), channel_id=1, source_target_pairs={{0,16},{16,0},{1,17},{17,1},{2,18},{18,2},{3,19},{19,3},{4,20},{20... | collective-permute-start | bytes 589832 | tf_op jit(solution)/shard_map/ppermute | solution.py:476
  132.7 7.2 %collective-permute-start.21 = (bf16[96,1024]{1,0:T(8,128)(2,1)S(1)}, bf16[96,1024]{1,0:T(8,128)(2,1)S(1)}, u32[]{:S(2)}, u32[]{:S(2)}) collective-permute-start(bf16[96,1024]{1,0:T(8,128)(2,1)S(1)} %collective-permute-done.15.refs_1_.refs_9_), channel_id=1, source_target_pairs={{0,64},{32,96},{64,0},{96,32},{1,65},{33,97},{65,1},{97,33},{2,66}... | collective-permute-start | bytes 589832 | tf_op jit(solution)/shard_map/ppermute | solution.py:480
  134.8 7.7 %collective-permute-start.20 = (bf16[96,1024]{1,0:T(8,128)(2,1)S(1)}, bf16[96,1024]{1,0:T(8,128)(2,1)S(1)}, u32[]{:S(2)}, u32[]{:S(2)}) collective-permute-start(bf16[96,1024]{1,0:T(8,128)(2,1)S(1)} %collective-permute-done.15.refs_1_.refs_9_), channel_id=1, source_target_pairs={{0,96},{32,0},{64,32},{96,64},{1,97},{33,1},{65,33},{97,65},{2,98}... | collective-permute-start | bytes 589832 | tf_op jit(solution)/shard_map/ppermute | solution.py:480
  135.9 6.9 %collective-permute-start.19 = (bf16[96,1024]{1,0:T(8,128)(2,1)S(1)}, bf16[96,1024]{1,0:T(8,128)(2,1)S(1)}, u32[]{:S(2)}, u32[]{:S(2)}) collective-permute-start(bf16[96,1024]{1,0:T(8,128)(2,1)S(1)} %collective-permute-done.15.refs_1_.refs_9_), channel_id=1, source_target_pairs={{0,32},{32,64},{64,96},{96,0},{1,33},{33,65},{65,97},{97,1},{2,34}... | collective-permute-start | bytes 589832 | tf_op jit(solution)/shard_map/ppermute | solution.py:480
